TPU v7x, 512 devices: a whole 4x4x16 slice. The times are simulated.
512 devices in a mesh: ctx: 64 (over x, z_lo, core), head: 8 (over y, z_hi).
Axes of the slice: x: 4, y: 4, z: 16 (z_hi: 2, z_lo: 8; z = z_hi * 8 + z_lo), core: 2. Of those that a mesh axis runs over, the one named last changes fastest.
Arguments:
- hidden: bfloat16 [12288, 5120], P('ctx', 'head'), may hold values from -64 to 64
- norm_gain: bfloat16 [5120], replicated, may hold values from 0.099609375 to 1.8984375
- query_gain: float32 [128], replicated, may hold values from 1.4 to 6
- key_gain: float32 [128], replicated, may hold values from 1.4 to 6
- weight_store: bfloat16 [5120, 6144], P('ctx', 'head'), may hold values from -0.0559017 to 0.0559017
- documents: int32 [12288], P('ctx'), may hold values from 0 to 63, never falling along the last dimension, each value on 1 to 6144 neighbouring positions
- owners: int32 [64], replicated, may hold values from 0 to 63, each once
Outputs:
- keys_fresh: bfloat16 [12288, 1024], P('ctx', 'head')
- values_fresh: bfloat16 [12288, 1024], P('ctx', 'head')
- context: bfloat16 [12288, 4096], P('ctx', 'head')
Inputs may be any that keep to these rules, and one draw needn't show every extreme that they name: `documents`: segment numbers never fall along the slab; each of the 64 segments holds 1 to 6144 tokens and one holds exactly 6144. `owners`: each slot holds exactly one panel.
All inputs are finite; a program needn't handle non-finite values.
Results may differ from a plain program's by a relative error of at most 0.012.
The roundings to bfloat16 on the way count: a program that leaves them out, or rounds other values in their place, can miss the bound.
Values may be sent and summed in bfloat16 or wider, within the bound.
No kernel may reach another device: no remote copies, remote signals or barrier semaphores. Data moves between devices by JAX's collectives and lax.ppermute only.
A program may use at most 128 MiB of HBM per device.

v0:
```python
import math

import jax
import jax.numpy as jnp
from jax import lax
from jax.sharding import PartitionSpec as P

epsilon = 1e-06
rope_base = 1000000.0


def rms_scale(values, gain_vector):
    mean_square = jnp.mean(values * values, axis=-1, keepdims=True)
    return values * lax.rsqrt(mean_square + epsilon) * gain_vector


def rotate(values, positions):
    half_width = values.shape[-1] // 2
    exponent = jnp.arange(half_width, dtype=jnp.float32) * (2.0 / values.shape[-1])
    frequency = jnp.exp(exponent * -math.log(rope_base))
    angles = positions.astype(jnp.float32)[:, None] * frequency[None, :]
    layout = (values.shape[0],) + (1,) * (values.ndim - 2) + (values.shape[-1],)
    cosine = jnp.concatenate([jnp.cos(angles), jnp.cos(angles)], axis=-1).reshape(layout)
    sine_part = jnp.concatenate([jnp.sin(angles), jnp.sin(angles)], axis=-1).reshape(layout)
    turned = jnp.concatenate([-values[..., half_width:], values[..., :half_width]], axis=-1)
    return values * cosine + turned * sine_part


def document_of(token_index, starts):
    return jnp.sum((starts[None, :] <= token_index[:, None]).astype(jnp.int32), axis=1) - 1


def body(hidden, norm_gain, query_gain, key_gain, weight_store, documents, owners):
    tok_rows = hidden.shape[0]
    head_width = query_gain.shape[0]
    slot_count = lax.axis_size("ctx")
    query_cols = weight_store.shape[1] - 2 * head_width
    per_group = query_cols // head_width
    panel_rows = weight_store.shape[0]
    gathered = lax.all_gather(hidden, "head", axis=1, tiled=True)
    normed = rms_scale(gathered.astype(jnp.float32), norm_gain.astype(jnp.float32)).astype(
        jnp.bfloat16
    )
    slot_table = jnp.arange(slot_count, dtype=jnp.int32)
    one_hot = (documents[:, None] == slot_table[None, :]).astype(jnp.int32)
    counted = lax.psum(jnp.sum(one_hot, axis=0), "ctx")
    starts = jnp.cumsum(counted) - counted
    own_index = lax.axis_index("ctx") * tok_rows + jnp.arange(tok_rows, dtype=jnp.int32)
    positions = own_index - jnp.sum(one_hot * starts[None, :], axis=1)
    panel_of_slot = jnp.sum(
        slot_table[:, None] * (owners[:, None] == slot_table[None, :]).astype(jnp.int32), axis=0
    )
    pieces = lax.all_gather(weight_store, "ctx", axis=0, tiled=True)
    row_index = jnp.arange(pieces.shape[0], dtype=jnp.int32)
    source = jnp.take(panel_of_slot, row_index // panel_rows) * panel_rows + row_index % panel_rows
    selected = jnp.take(normed, source, axis=1)
    projected = jnp.dot(selected, pieces, preferred_element_type=jnp.float32)
    query_proj = projected[:, :query_cols]
    pair_proj = projected[:, query_cols:]
    query_heads = query_proj.reshape(tok_rows, per_group, head_width)
    queries = rotate(rms_scale(query_heads, query_gain), positions).astype(jnp.bfloat16)
    key_part = pair_proj[:, None, :head_width]
    keys_fresh = rotate(rms_scale(key_part, key_gain), positions)[:, 0, :].astype(jnp.bfloat16)
    values_fresh = pair_proj[:, head_width:].astype(jnp.bfloat16)
    inverse_root = 1.0 / math.sqrt(head_width)
    pieces = (
        lax.all_gather(keys_fresh, "ctx", axis=0, tiled=True),
        lax.all_gather(values_fresh, "ctx", axis=0, tiled=True),
    )
    key_rows = pieces[0]
    running_max = jnp.full((tok_rows, per_group), -1e30, jnp.float32)
    key_index = jnp.arange(key_rows.shape[0], dtype=jnp.int32)
    key_docs = document_of(key_index, starts)
    scores = (
        jnp.einsum("thd,sd->ths", queries, key_rows, preferred_element_type=jnp.float32)
        * inverse_root
    )
    allowed = (key_docs[None, :] == documents[:, None]) & (key_index[None, :] <= own_index[:, None])
    allowed = allowed[:, None, :]
    masked = jnp.where(allowed, scores, -1e30)
    new_max = jnp.maximum(running_max, jnp.max(masked, axis=-1))
    expterms = jnp.where(allowed, jnp.exp(masked - new_max[..., None]), 0.0)
    denominator = jnp.sum(expterms, axis=-1)
    product = jnp.einsum(
        "ths,sd->thd", expterms.astype(jnp.bfloat16), pieces[1], preferred_element_type=jnp.float32
    )
    summed = product
    running_max, denominator, summed = (new_max, denominator, summed)
    context = (
        (summed / denominator[..., None])
        .reshape(tok_rows, per_group * head_width)
        .astype(jnp.bfloat16)
    )
    return (keys_fresh, values_fresh, context)


def solution(mesh):
    in_specs = (P("ctx", "head"), P(), P(), P(), P("ctx", "head"), P("ctx"), P())
    out_specs = (P("ctx", "head"), P("ctx", "head"), P("ctx", "head"))
    return jax.shard_map(body, mesh=mesh, in_specs=in_specs, out_specs=out_specs, check_vma=False)
```

profile of v0, /device:TPU:1, one launch (start us, length us, event | category | flops | bytes accessed | tf_op | source)
XLA Modules:
  0.0 543.6 jit_solution(17861181589208213929)
XLA Ops:
  7.2 1.9 copy.25
  9.1 0.7 all-gather.7.cloned.1.call-update
  9.9 0.7 convert_element_type.41
  10.6 0.8 convert_reduce_fusion.1
  11.4 23.4 %psum.7 = s32[64]{0:T(128)S(1)} all-reduce(s32[64]{0:T(128)S(1)} %convert_reduce_fusion.1), channel_id=1, replica_groups=mesh['ctx'=64,'head'=8] {'ctx'}, use_global_device_ids=true, to_apply=%region_4.5 | all-reduce | flops 64 | bytes 512 | tf_op jit(solution)/shard_map/psum | solution.py:46
  43.4 0.8 select_reduce_fusion.1
  44.1 0.7 fusion.55
  44.8 0.7 fusion.52
  45.5 0.7 fusion.53
  46.3 0.7 fusion.54
  47.0 0.8 select_reduce_fusion
  47.8 4.5 compare_select_fusion.2
  52.3 35.9 %compare_and_fusion = (pred[5120]{0:T(1024)(128)(4,1)S(1)}, s32[5120]{0:T(1024)S(1)}) fusion(pred[5120]{0:T(1024)(128)(4,1)S(1)} %compare_reduce_fusion, pred[5120]{0:T(1024)(128)(4,1)S(1)} %compare_reduce_fusion.1, pred[5120]{0:T(1024)(128)(4,1)S(1)} %compare_reduce_fusion.2, pred[5120]{0:T(1024)(128)(4,1)S(1)} %compare_reduce_fusion.3, ...), kind=kLoop, calls=%fused_computation.143 | loop fusion | flops 430080 | bytes 338148 | tf_op jit(solution)/shard_map/jit(_take)/and | solution.py:56
  88.8 54.3 %all-gather.5.cloned.1.call-done = bf16[192,5120]{0,1:T(8,128)(2,1)} async-done(((bf16[192,640]{0,1:T(8,128)(2,1)}), bf16[192,5120]{0,1:T(8,128)(2,1)}) %all-gather.5.cloned.1.call-update) | async-done | bytes 1966096 | tf_op jit(solution)/shard_map/all_gather | solution.py:40
  143.1 2.5 fusion.7
  145.6 3.5 fusion.9
  149.1 20.9 %gather_fusion = bf16[5120,192]{1,0:T(8,128)(2,1)} fusion(bf16[192,5120]{0,1:T(8,128)(2,1)S(1)} %fusion.9, s32[5120]{0:T(1024)S(1)} %broadcast_clamp_fusion), kind=kCustom, calls=%fused_computation | custom fusion | bytes 3952640 | tf_op jit(solution)/shard_map/jit(_take)/gather | solution.py:56
  170.0 102.7 %all-gather.7.cloned.1.call-done = bf16[5120,768]{1,0:T(8,128)(2,1)} async-done(((bf16[80,768]{1,0:T(8,128)(2,1)}), bf16[5120,768]{1,0:T(8,128)(2,1)}) %all-gather.7.cloned.1.call-update) | async-done | bytes 7864336 | tf_op jit(solution)/shard_map/all_gather | solution.py:53
  272.7 6.3 %fusion.13 = f32[192,768]{1,0:T(8,128)S(1)} fusion(bf16[5120,768]{1,0:T(8,128)(2,1)} %all-gather.7.cloned.1.call-done, bf16[5120,192]{1,0:T(8,128)(2,1)} %gather_fusion, pred[5120]{0:T(1024)(128)(4,1)S(1)} %get-tuple-element.3), kind=kOutput, calls=%fused_computation.20 | convolution fusion | flops 1510932480 | bytes 10425344 | tf_op jit(solution)/shard_map/dot_general | solution.py:57
  279.4 0.5 copy-done
  279.9 0.8 pad_maximum_fusion
  280.7 0.5 convert_reduce_fusion
  281.3 1.9 fusion.6
  283.2 1.0 slice.103
  284.2 1.5 slice.118
  286.7 0.5 fusion.33
  287.2 111.2 %all-gather.9.cloned.1.call-done = bf16[12288,128]{1,0:T(8,128)(2,1)} async-done(((bf16[192,128]{1,0:T(8,128)(2,1)}), bf16[12288,128]{1,0:T(8,128)(2,1)}) %all-gather.9.cloned.1.call-update) | async-done | bytes 3145744 | tf_op jit(solution)/shard_map/all_gather | solution.py:67
  398.4 18.0 %fusion = (f32[192,4]{0,1:T(4,128)S(1)}, f32[192,4,12288]{2,0,1:T(8,128)}) fusion(pred[192,12288]{1,0:T(8,128)(4,1)S(1)} %fusion.6, bf16[12288,128]{1,0:T(8,128)(2,1)} %all-gather.9.cloned.1.call-done, bf16[192,4,128]{2,1,0:T(4,128)(2,1)S(1)} %fusion.33), kind=kOutput, calls=%fused_computation.3 | convolution fusion | flops 2444229888 | bytes 43453440 | tf_op jit(solution)/shard_map/thd,sd->ths/dot_general | solution.py:75
  416.4 18.2 %fusion.1 = f32[192,4]{0,1:T(4,128)S(1)} fusion(f32[192,4,12288]{2,0,1:T(8,128)} %get-tuple-element.79, f32[192,4]{0,1:T(4,128)S(1)} %broadcast_maximum_fusion, pred[192,12288]{1,0:T(8,128)(4,1)S(1)} %fusion.6), kind=kLoop, calls=%fused_computation.4 | loop fusion | flops 47185152 | bytes 40114176 | tf_op jit(solution)/shard_map/reduce_sum | solution.py:83
  434.6 84.0 %all-gather.11.cloned.1.call-done = bf16[12288,128]{1,0:T(8,128)(2,1)} async-done(((bf16[192,128]{1,0:T(8,128)(2,1)}), bf16[12288,128]{1,0:T(8,128)(2,1)}) %all-gather.11.cloned.1.call-update) | async-done | bytes 3145744 | tf_op jit(solution)/shard_map/all_gather | solution.py:68
  518.6 17.7 %fusion.27 = bf16[4,24,8,128]{3,2,1,0:T(8,128)(2,1)S(1)} fusion(bf16[12288,128]{1,0:T(8,128)(2,1)} %all-gather.11.cloned.1.call-done, f32[192,4,12288]{2,0,1:T(8,128)} %get-tuple-element.79, f32[192,4]{0,1:T(4,128)S(1)} %broadcast_maximum_fusion, pred[192,12288]{1,0:T(8,128)(4,1)S(1)} %fusion.6, f32[192,4]{0,1:T(4,128)S(1)} %fusion.1), kind=kOutput, calls=%fused_computation.26 | convolution fusion | flops 2463301632 | bytes 43456512 | tf_op jit(solution)/shard_map/ths,sd->thd/dot_general | solution.py:84
  536.4 0.7 copy.38
  (93 shorter events, 10.6 us)
Async XLA Ops:
  7.2 136.0 %all-gather.5.cloned.1.call-start = ((), (), s32[]{:S(2)}) async-start(), calls=%async_computation | async-start | bytes 2949120 | tf_op jit(solution)/shard_map/all_gather | solution.py:40
  9.1 263.6 %all-gather.7.cloned.1.call-start = ((), (), s32[]{:S(2)}) async-start(), calls=%async_computation.1 | async-start | bytes 7987200 | tf_op jit(solution)/shard_map/all_gather | solution.py:53
  9.8 388.5 %all-gather.9.cloned.1.call-start = ((), (), s32[]{:S(2)}) async-start(), calls=%async_computation.2 | async-start | bytes 3194880 | tf_op jit(solution)/shard_map/all_gather | solution.py:67
  272.7 6.5 %copy-start.2 = (f32[128]{0:T(128)S(1)}, f32[128]{0:T(128)}, u32[]{:S(2)}) copy-start(f32[128]{0:T(128)} %param.10) | copy-start | bytes 1540
  272.7 8.6 %copy-start.1 = (s32[192]{0:T(256)S(1)}, s32[192]{0:T(256)}, u32[]{:S(2)}) copy-start(s32[192]{0:T(256)} %param.12) | copy-start | bytes 2308
  279.0 0.8 copy-start
  279.1 7.1 %copy-start.3 = (f32[128]{0:T(128)S(1)}, f32[128]{0:T(128)}, u32[]{:S(2)}) copy-start(f32[128]{0:T(128)} %param.9) | copy-start | bytes 1540
  280.7 238.0 %all-gather.11.cloned.1.call-start = ((), (), s32[]{:S(2)}) async-start(), calls=%async_computation.3 | async-start | bytes 3194880 | tf_op jit(solution)/shard_map/all_gather | solution.py:68
Sparse Core Ops, SparseCore 0:
  11.2 131.9 all-gather.4
  145.3 127.3 all-gather.6
  280.8 117.5 all-gather.8
  401.0 117.6 all-gather.10
where the time goes:
time: 545 us; the launch traced here: 544 us
  waiting for transfers between devices  353 us (65%)
  other arithmetic  81.4 us (15%)
  matrix products  42.1 us (8%)
  local copies, waits for them, and re-layouts  29.6 us (5%)
  blocking collectives  23.4 us (4%)
  between operations  14 us (3%)
    all_gather x1, waiting for transfers between devices, body(): lax.all_gather(keys_fresh, 'ctx', axis=0, tiled=True)  111 us
    all_gather x1, waiting for transfers between devices, body(): pieces = lax.all_gather(weight_store, 'ctx', axis=0, tiled=True)  103 us
    all_gather x1, waiting for transfers between devices, body(): lax.all_gather(values_fresh, 'ctx', axis=0, tiled=True)  84 us
    all_gather x1, waiting for transfers between devices, body(): gathered = lax.all_gather(hidden, 'head', axis=1, tiled=True)  54.3 us
    and x1, other arithmetic, body(): selected = jnp.take(normed, source, axis=1)  35.9 us
    psum x1, blocking collectives, body(): counted = lax.psum(jnp.sum(one_hot, axis=0), 'ctx')  23.4 us
    gather x1, local copies, waits for them, and re-layouts, body(): selected = jnp.take(normed, source, axis=1)  20.9 us
    reduce_sum x1, other arithmetic, body(): denominator = jnp.sum(expterms, axis=-1)  18.2 us
  transfers between devices with their start and end apart: 4, of which 4 were waited for; matrix products, arithmetic and copies ran while one was open for 23% of the time, Pallas kernels for 0%

commit v1 on v0

v1 whole, which is shorter than its diff:
```python
import functools
import math

import jax
import jax.numpy as jnp
from jax import lax
from jax.experimental import pallas as pl
from jax.experimental.pallas import tpu as pltpu
from jax.sharding import Mesh
from jax.sharding import PartitionSpec as P

epsilon = 1e-06
rope_base = 1000000.0
NEG = -1e30
MASKED = -3e38
KEY_BLOCK = 512
VMEM_LIMIT = 48 * 1024 * 1024


def call(kernel, out_shape, n_smem, n_vmem, scratch=(), flops=0):
    specs = [pl.BlockSpec(memory_space=pltpu.SMEM)] * n_smem
    specs += [pl.BlockSpec(memory_space=pltpu.VMEM)] * n_vmem
    n_out = len(out_shape)
    return pl.pallas_call(
        kernel,
        out_shape=out_shape,
        in_specs=specs,
        out_specs=[pl.BlockSpec(memory_space=pltpu.VMEM)] * n_out,
        scratch_shapes=list(scratch),
        compiler_params=pltpu.CompilerParams(vmem_limit_bytes=VMEM_LIMIT),
        cost_estimate=pl.CostEstimate(flops=flops, bytes_accessed=4 << 20, transcendentals=0),
    )


def norm_kernel(where, gain, *refs):
    blocks, out = refs[:-1], refs[-1]
    ny = len(blocks) // 2
    rows, width = blocks[0].shape[1:]
    core, me = where[0], where[1]
    for side in range(2):
        first = pl.multiple_of(rows * (core if side == 0 else 1 - core), rows)
        total = jnp.zeros((rows, 128), jnp.float32)
        for s in range(ny):
            for half in range(2):
                v = blocks[side * ny + s][half].astype(jnp.float32)
                v = v * v
                for k in range(width // 128):
                    total = total + v[:, k * 128 : (k + 1) * 128]
        mean = jnp.sum(total, axis=-1, keepdims=True) * (1.0 / (2 * ny * width))
        scale = lax.rsqrt(mean + epsilon)
        for s in range(ny):
            source = lax.rem(me + ny - s, ny)
            for half in range(2):
                cols = pl.ds(pl.multiple_of((source * 2 + half) * width, 128), width)
                v = blocks[side * ny + s][half].astype(jnp.float32)
                v = v * scale * gain[:, cols]
                out[pl.ds(first, rows), cols] = v.astype(jnp.bfloat16)


def head_norm_rope(v, gain, cosine, sine):
    mean = jnp.mean(v * v, axis=-1, keepdims=True)
    v = v * lax.rsqrt(mean + epsilon) * gain
    return v * cosine + pltpu.roll(v, 64, 1) * sine


def collect(offsets, where, blocks, weights):
    nx = len(blocks)
    nz, both, _ = blocks[0].shape
    panel = both // 2
    for s in range(nx):
        source = lax.rem(where[1] + nx - s, nx)
        for k in range(nz):
            for c in range(2):
                slot = source * (nz * 2) + k * 2 + c
                first = pl.multiple_of(offsets[slot], 16)
                weights[pl.ds(first, panel), :] = blocks[s][k, c * panel : (c + 1) * panel, :]


def pair_kernel(offsets, where, normed, gain, cosine, sine, *refs):
    blocks, out, weights = refs[:-2], refs[-2], refs[-1]
    collect(offsets, where, blocks, weights)
    v = jnp.dot(normed[...], weights[...], preferred_element_type=jnp.float32)
    keys = head_norm_rope(v, gain[...], cosine[...], sine[...])
    out[...] = jnp.where(where[0] == 0, keys, v).astype(jnp.bfloat16)


def query_kernel(offsets, where, normed, gain, cosine, sine, *refs):
    blocks, out, weights = refs[:-2], refs[-2], refs[-1]
    collect(offsets, where, blocks, weights)
    rows = out.shape[2]
    for side in range(2):
        span = pl.ds(side * rows, rows)
        v = jnp.dot(normed[span, :], weights[...], preferred_element_type=jnp.float32)
        for h in range(2):
            q = head_norm_rope(
                v[:, h * 128 : (h + 1) * 128], gain[...], cosine[span, :], sine[span, :]
            )
            out[side, h] = q.astype(jnp.bfloat16)


def attention_kernel(where, starts, mine, other, q0, q1, q2, o0, o1, o2, lse, keys, values, acc, top, total):
    core = where[0]

    @pl.when(core == 0)
    def _():
        keys[...] = mine[...]
        values[...] = other[...]

    @pl.when(core == 1)
    def _():
        keys[...] = other[...]
        values[...] = mine[...]

    rows = starts.shape[1]
    plane = keys.shape[0]
    scale = math.log2(math.e) / math.sqrt(128)
    eye = lax.broadcasted_iota(jnp.int32, (128, 128), 0) == lax.broadcasted_iota(
        jnp.int32, (128, 128), 1
    )
    lse[...] = jnp.full(lse.shape, NEG, jnp.float32)
    for s, (query, out) in enumerate(((q0, o0), (q1, o1), (q2, o2))):
        low, high = where[1 + 2 * s], where[2 + 2 * s]
        acc[...] = jnp.zeros_like(acc)
        top[...] = jnp.full(top.shape, NEG, jnp.float32)
        total[...] = jnp.zeros_like(total)
        index = (
            s * plane
            + where[7]
            + lax.broadcasted_iota(jnp.int32, (rows, 1), 0)
        )
        begin = starts[s]

        def step(b, carry, s=s, query=query, index=index, begin=begin):
            base = pl.multiple_of(b * KEY_BLOCK, KEY_BLOCK)
            key = keys[pl.ds(base, KEY_BLOCK), :]
            value = values[pl.ds(base, KEY_BLOCK), :]
            col = base + lax.broadcasted_iota(jnp.int32, (rows, KEY_BLOCK), 1)
            allowed = col >= begin
            if s == 0:
                allowed = allowed & (col <= index)
            for h in range(query.shape[0] // rows):
                span = pl.ds(h * rows, rows)
                raw = lax.dot_general(
                    query[span, :], key, (((1,), (1,)), ((), ())),
                    preferred_element_type=jnp.float32,
                )
                raw = jnp.where(allowed, raw * scale, MASKED)
                old = top[span, :]
                new = jnp.maximum(old, jnp.max(raw, axis=-1, keepdims=True))
                terms = jnp.exp2(raw - new)
                decay = jnp.exp2(old - new)
                top[span, :] = new
                total[span, :] = total[span, :] * decay + jnp.sum(terms, axis=-1, keepdims=True)
                acc[span, :] = acc[span, :] * decay + jnp.dot(
                    terms.astype(jnp.bfloat16), value, preferred_element_type=jnp.float32
                )
            return carry

        lax.fori_loop(low // KEY_BLOCK, (high + KEY_BLOCK - 1) // KEY_BLOCK, step, 0)
        summed = total[...]
        safe = jnp.where(summed > 0, summed, 1.0)
        out[...] = (acc[...] / safe).astype(out.dtype)
        log = jnp.where(summed > 0, top[...] + jnp.log2(safe), NEG)
        for g in range(log.shape[0] // 128):
            piece = jnp.where(eye, log[g * 128 : (g + 1) * 128, :], 0.0)
            lse[s, g : g + 1, :] = jnp.sum(piece, axis=0, keepdims=True)


def combine_kernel(where, o0, o1, o2, l0, l1, l2, out):
    rows = out.shape[0]
    eye = lax.broadcasted_iota(jnp.int32, (128, 128), 0) == lax.broadcasted_iota(
        jnp.int32, (128, 128), 1
    )

    def column(ref):
        pieces = [
            jnp.sum(jnp.where(eye, ref[g : g + 1, :], 0.0), axis=1, keepdims=True)
            for g in range(o0.shape[0] // 128)
        ]
        return jnp.concatenate(pieces, axis=0)

    a = column(l0)
    b = jnp.where(where[1] == 1, column(l1), NEG)
    c = jnp.where(where[2] == 1, column(l2), NEG)
    top = jnp.maximum(jnp.maximum(a, b), c)
    a, b, c = jnp.exp2(a - top), jnp.exp2(b - top), jnp.exp2(c - top)
    summed = a * o0[...] + b * o1[...].astype(jnp.float32) + c * o2[...].astype(jnp.float32)
    result = (summed / (a + b + c)).astype(jnp.bfloat16)
    for side in range(2):
        first = 256 * (where[0] if side == 0 else 1 - where[0])
        for h in range(2):
            k = side * 2 + h
            cols = pl.ds(pl.multiple_of(first + h * 128, 128), 128)
            out[:, cols] = result[k * rows : (k + 1) * rows, :]


def ring(axis, size, shift):
    return [(i, (i + shift) % size) for i in range(size)]


def body(hidden, norm_gain, query_gain, key_gain, weight_store, documents, owners):
    x, z, c, y = (lax.axis_index(a) for a in ("x", "z", "c", "y"))
    nx, nz, ny = (lax.axis_size(a) for a in ("x", "z", "y"))
    rows, width = hidden.shape
    slots = owners.shape[0]
    panel = weight_store.shape[0]
    swap = [(0, 1), (1, 0)]
    bf16, f32 = jnp.bfloat16, jnp.float32

    both = lax.all_gather(weight_store, "c", axis=0, tiled=True)
    pair_cols = lax.dynamic_slice_in_dim(both, 512 + 128 * c, 128, 1)
    query_cols = lax.dynamic_slice_in_dim(both, 256 * c, 256, 1)
    line = lax.all_gather(jnp.concatenate([pair_cols, query_cols], axis=1), "z", axis=0)
    pair_line, query_line = line[:, :, :128], line[:, :, 128:]
    pair_blocks = [pair_line] + [
        lax.ppermute(pair_line, "x", ring("x", nx, s)) for s in range(1, nx)
    ]
    query_blocks = [query_line] + [
        lax.ppermute(query_line, "x", ring("x", nx, s)) for s in range(1, nx)
    ]

    wide = lax.all_gather(hidden, "w", axis=0)
    own_blocks = [wide] + [lax.ppermute(wide, "y", ring("y", ny, s)) for s in range(1, ny)]
    other_blocks = [lax.ppermute(v, "c", swap) for v in own_blocks]
    where = jnp.stack([c, y]).astype(jnp.int32)
    (normed,) = call(
        norm_kernel,
        [jax.ShapeDtypeStruct((2 * rows, 2 * ny * width), bf16)],
        1,
        1 + 2 * ny,
    )(where, norm_gain.astype(f32)[None, :], *own_blocks, *other_blocks)

    table = jnp.arange(slots, dtype=jnp.int32)
    counted = lax.psum(
        jnp.sum((documents[:, None] == table[None, :]).astype(jnp.int32), axis=0), ("x", "z", "c")
    )
    first = jnp.cumsum(counted) - counted
    pair_docs = lax.all_gather(documents, "c", axis=0, tiled=True)
    begin = jnp.sum(
        (pair_docs[:, None] == table[None, :]).astype(jnp.int32) * first[None, :], axis=1
    )
    plane = nz * 2 * rows
    token = x * plane + z * 2 * rows + jnp.arange(2 * rows, dtype=jnp.int32)
    positions = token - begin
    exponent = jnp.arange(64, dtype=f32) * (2.0 / 128)
    frequency = jnp.exp(exponent * -math.log(rope_base))
    angles = positions.astype(f32)[:, None] * frequency[None, :]
    cosine, sine = jnp.cos(angles), jnp.sin(angles)
    cosine = jnp.concatenate([cosine, cosine], axis=1)
    sine = jnp.concatenate([-sine, sine], axis=1)
    own_begin = lax.dynamic_slice_in_dim(begin, c * rows, rows, 0)
    near_begin = lax.ppermute(own_begin, "x", [(i, i - 1) for i in range(1, nx)])
    far_begin = lax.ppermute(own_begin, "x", [(i, i - 2) for i in range(2, nx)])

    offsets = jnp.sum(
        table[:, None] * (owners[:, None] == table[None, :]).astype(jnp.int32), axis=0
    ) * panel
    spot = jnp.stack([c, x]).astype(jnp.int32)
    (pair,) = call(
        pair_kernel,
        [jax.ShapeDtypeStruct((2 * rows, 128), bf16)],
        2,
        4 + nx,
        [pltpu.VMEM((slots * panel, 128), bf16)],
        2 * 2 * rows * slots * panel * 128,
    )(offsets, spot, normed, key_gain[None, :], cosine, sine, *pair_blocks)
    (query,) = call(
        query_kernel,
        [jax.ShapeDtypeStruct((2, 2, rows, 128), bf16)],
        2,
        4 + nx,
        [pltpu.VMEM((slots * panel, 256), bf16)],
        2 * 2 * rows * slots * panel * 256,
    )(offsets, spot, normed, query_gain[None, :], cosine, sine, *query_blocks)

    mine = lax.all_gather(pair, "z", axis=0, tiled=True)
    other = lax.ppermute(mine, "c", swap)
    own_query = lax.dynamic_index_in_dim(query, c, 0, keepdims=False)
    sent_query = lax.dynamic_index_in_dim(query, 1 - c, 0, keepdims=False)
    q0 = jnp.concatenate([own_query, lax.ppermute(sent_query, "c", swap)], axis=0)
    q0 = q0.reshape(4 * rows, 128)
    q1 = lax.ppermute(q0, "x", [(i, i - 1) for i in range(1, nx)])
    q2 = lax.ppermute(q0, "x", [(i, i - 2) for i in range(2, nx)])

    base = x * plane
    spread = jnp.stack([own_begin, near_begin, far_begin]) - base
    inside = z * 2 * rows + c * rows
    low = [jnp.clip(spread[s, 0], 0, plane) for s in range(3)]
    high = [inside + rows] + [jnp.where(x + s < nx, plane, 0) for s in (1, 2)]
    ranges = jnp.stack(
        [c, low[0], high[0], low[1], high[1], low[2], high[2], inside]
    ).astype(jnp.int32)
    parts = call(
        attention_kernel,
        [
            jax.ShapeDtypeStruct((4 * rows, 128), f32),
            jax.ShapeDtypeStruct((4 * rows, 128), bf16),
            jax.ShapeDtypeStruct((4 * rows, 128), bf16),
            jax.ShapeDtypeStruct((3, 8, 128), f32),
        ],
        1,
        6,
        [
            pltpu.VMEM((plane, 128), bf16),
            pltpu.VMEM((plane, 128), bf16),
            pltpu.VMEM((4 * rows, 128), f32),
            pltpu.VMEM((4 * rows, 1), f32),
            pltpu.VMEM((4 * rows, 1), f32),
        ],
        4 * rows * plane * 128 * 8,
    )(ranges, spread[:, :, None], mine, other, q0, q1, q2)
    o0, o1, o2, lse = parts
    o1 = lax.ppermute(o1, "x", [(i, i + 1) for i in range(nx - 1)])
    o2 = lax.ppermute(o2, "x", [(i, i + 2) for i in range(nx - 2)])
    l1 = lax.ppermute(lse[1], "x", [(i, i + 1) for i in range(nx - 1)])
    l2 = lax.ppermute(lse[2], "x", [(i, i + 2) for i in range(nx - 2)])
    came = jnp.stack([c, (x >= 1).astype(jnp.int32), (x >= 2).astype(jnp.int32)]).astype(jnp.int32)
    (context,) = call(
        combine_kernel, [jax.ShapeDtypeStruct((rows, 512), bf16)], 1, 6
    )(came, o0, o1, o2, lse[0], l1, l2)

    own_part = lax.dynamic_slice_in_dim(mine, inside, rows, 0)
    other_part = lax.dynamic_slice_in_dim(other, inside, rows, 0)
    keys_fresh = jnp.where(c == 0, own_part, other_part)
    values_fresh = jnp.where(c == 0, other_part, own_part)
    return keys_fresh, values_fresh, context


def solution(mesh):
    fine = Mesh(mesh.devices.reshape(4, 8, 2, 4, 2), ("x", "z", "c", "y", "w"))
    ctx, head = ("x", "z", "c"), ("y", "w")
    in_specs = (P(ctx, head), P(), P(), P(), P(ctx, head), P(ctx), P())
    out_specs = (P(ctx, head), P(ctx, head), P(ctx, head))
    return jax.shard_map(body, mesh=fine, in_specs=in_specs, out_specs=out_specs, check_vma=False)
```

time: 545 us -> 306 us (0.56)
  waiting for transfers between devices: 353 us -> 17.5 us
  blocking collectives: 23.4 us -> 150 us
  starting transfers between devices: 0.16 us -> 99.4 us
  other arithmetic: 81.4 us -> 3.85 us
  matrix products: 42.1 us -> 0 us
  Pallas kernels: 0 us -> 18.7 us
  local copies, waits for them, and re-layouts: 29.6 us -> 11 us
  between operations: 14 us -> 3.71 us
    all_gather x4 -> x0, waiting for transfers between devices: 352 us -> none  [the longest x1 111 us: body(): lax.all_gather(keys_fresh, 'ctx', axis=0, tiled=True)]
    all_gather x0 -> x4, blocking collectives: none -> 110 us  [the longest x1 45.6 us: body(): lax.all_gather(jnp.concatenate([pair_cols, query_cols], axis=1), 'z', axi...]
    ppermute x0 -> x23, starting transfers between devices: none -> 99.4 us  [the longest x1 28.3 us: body(): o1 = lax.ppermute(o1, 'x', [(i, i + 1) for i in range(nx - 1)])]
    dot_general x3 -> x0, matrix products: 42.1 us -> none  [the longest x1 18 us: body(): jnp.einsum('thd,sd->ths', queries, key_rows, preferred_element_type=jnp.f...]
    and x2 -> x0, other arithmetic: 37.8 us -> none  [the longest x1 35.9 us: body(): selected = jnp.take(normed, source, axis=1)]
    gather x5 -> x0, local copies, waits for them, and re-layouts: 23.8 us -> none  [the longest x1 20.9 us: body(): selected = jnp.take(normed, source, axis=1)]
    reduce_sum x8 -> x3, other arithmetic: 23.8 us -> 0.98 us  [the longest x1 0.79 us: body(): jnp.sum((documents[:, None] == table[None, :]).astype(jnp.int32), axis=0)]
    pallas_call x0 -> x5, Pallas kernels: none -> 18.7 us  [the longest x1 5.7 us: body(): call(norm_kernel, [jax.ShapeDtypeStruct((2 * rows, 2 * ny * width), bf16)...]
  transfers between devices with their start and end apart: 4 -> 23, of which waited for: 4 -> 6; matrix products, arithmetic and copies ran while one was open for 23% -> 3% of each run, Pallas kernels for 0% -> 4%
where the time goes in v1:
time: 306 us; the launch traced here: 304 us
  blocking collectives  150 us (49%)
  starting transfers between devices  99.4 us (32%)
  Pallas kernels  18.7 us (6%)
  waiting for transfers between devices  17.5 us (6%)
  local copies, waits for them, and re-layouts  11 us (4%)
  other arithmetic  3.85 us (1%)
  between operations  3.71 us (1%)
    all_gather x1, blocking collectives, body(): lax.all_gather(jnp.concatenate([pair_cols, query_cols], axis=1), 'z', axi...  45.6 us
    all_gather x1, blocking collectives, body(): mine = lax.all_gather(pair, 'z', axis=0, tiled=True)  42.3 us
    psum x1, blocking collectives, body(): lax.psum(jnp.sum((documents[:, None] == table[None, :]).astype(jnp.int32)...  33.3 us
    ppermute x1, starting transfers between devices, body(): o1 = lax.ppermute(o1, 'x', [(i, i + 1) for i in range(nx - 1)])  28.3 us
    all_gather x1, blocking collectives, body(): wide = lax.all_gather(hidden, 'w', axis=0)  20.4 us
    ppermute x4, starting transfers between devices, body(): other_blocks = [lax.ppermute(v, 'c', swap) for v in own_blocks]  17.7 us
    ppermute x3, starting transfers between devices, body(): lax.ppermute(pair_line, 'x', ring('x', nx, s))  14.7 us
    ppermute x1, starting transfers between devices, body(): other = lax.ppermute(mine, 'c', swap)  10.4 us
  transfers between devices with their start and end apart: 23, of which 6 were waited for; matrix products, arithmetic and copies ran while one was open for 3% of the time, Pallas kernels for 4%

profile of v1, /device:TPU:1, one launch (start us, length us, event | category | flops | bytes accessed | tf_op | source)
XLA Modules:
  0.0 303.8 jit_solution(18251340253870818357)
XLA Ops:
  0.7 20.4 %all-gather = bf16[384,640]{1,0:T(8,128)(2,1)S(1)} all-gather(bf16[192,640]{1,0:T(8,128)(2,1)} %param.7), channel_id=2, replica_groups=mesh['x'=4,'z'=8,'c'=2,'y'=4,'w'=2] {'w'}, dimensions={0}, use_global_device_ids=true | all-gather | bytes 737280 | tf_op jit(solution)/shard_map/all_gather | solution.py:222
  21.0 4.4 %collective-permute-start.3 = (bf16[2,192,640]{2,1,0:T(8,128)(2,1)S(1)}, bf16[2,192,640]{2,1,0:T(8,128)(2,1)S(1)}, u32[]{:S(2)}, u32[]{:S(2)}) collective-permute-start(bf16[2,192,640]{2,1,0:T(8,128)(2,1)S(1)} %bitcast.36), channel_id=1, source_target_pairs={{0,8},{8,0},{1,9},{9,1},{2,10},{10,2},{3,11},{11,3},{4,12},{12,4},... | collective-permute-start | bytes 1474568 | tf_op jit(solution)/shard_map/ppermute | solution.py:224
  25.4 4.3 %collective-permute-start.2 = (bf16[2,192,640]{2,1,0:T(8,128)(2,1)S(1)}, bf16[2,192,640]{2,1,0:T(8,128)(2,1)S(1)}, u32[]{:S(2)}, u32[]{:S(2)}) collective-permute-start(bf16[2,192,640]{2,1,0:T(8,128)(2,1)S(1)} %bitcast.37), channel_id=1, source_target_pairs={{0,6},{2,0},{4,2},{6,4},{1,7},{3,1},{5,3},{7,5},{8,14},{10,8},{12,... | collective-permute-start | bytes 1474568 | tf_op jit(solution)/shard_map/ppermute | solution.py:223
  29.7 2.3 collective-permute-start.1
  32.0 2.6 collective-permute-start
  35.4 33.3 %psum.7 = s32[64]{0:T(128)S(1)} all-reduce(s32[64]{0:T(128)S(1)} %convert_reduce_fusion), channel_id=1, replica_groups=mesh['x'=4,'z'=8,'c'=2,'y'=4,'w'=2] {'x','z','c'}, use_global_device_ids=true, to_apply=%region_2.0 | all-reduce | flops 64 | bytes 512 | tf_op jit(solution)/shard_map/psum | solution.py:234
  71.4 5.8 %all-reduce = s32[384]{0:T(512)S(1)} all-reduce(s32[384]{0:T(512)S(1)} %dynamic-update-slice), channel_id=1, replica_groups=mesh['x'=4,'z'=8,'c'=2,'y'=4,'w'=2] {'c'}, use_global_device_ids=true, to_apply=%add | all-reduce | flops 384 | bytes 3072
  79.1 2.2 all_gather.24
  81.3 45.6 %all-gather.1 = bf16[1280,384]{1,0:T(8,128)(2,1)} all-gather(bf16[160,384]{1,0:T(8,128)(2,1)S(1)} %pad_maximum_fusion.3), channel_id=3, replica_groups=mesh['x'=4,'z'=8,'c'=2,'y'=4,'w'=2] {'z'}, dimensions={0}, use_global_device_ids=true | all-gather | bytes 1105920 | tf_op jit(solution)/shard_map/all_gather | solution.py:213
  129.0 9.0 %collective-permute-start.6 = (bf16[2,192,640]{2,1,0:T(8,128)(2,1)S(1)}, bf16[2,192,640]{2,1,0:T(8,128)(2,1)S(1)}, u32[]{:S(2)}, u32[]{:S(2)}) collective-permute-start(bf16[2,192,640]{2,1,0:T(8,128)(2,1)S(1)} %collective-permute-done.2.refs_3_), channel_id=1, source_target_pairs={{0,8},{8,0},{1,9},{9,1},{2,10},{10,2},{3,11},{11,3},{4,12},{12,4},... | collective-permute-start | bytes 1474568 | tf_op jit(solution)/shard_map/ppermute | solution.py:224
  138.0 1.9 collective-permute-start.5
  140.0 2.4 collective-permute-start.4
  144.7 6.9 %collective-permute-start.9 = (bf16[8,160,128]{2,1,0:T(8,128)(2,1)S(1)}, bf16[8,160,128]{2,1,0:T(8,128)(2,1)S(1)}, u32[]{:S(2)}, u32[]{:S(2)}) collective-permute-start(bf16[8,160,128]{2,1,0:T(8,128)(2,1)S(1)} %slice.32.refs_0_), channel_id=1, source_target_pairs={{0,384},{128,0},{256,128},{384,256},{1,385},{129,1},{257,129},{385... | collective-permute-start | bytes 983048 | tf_op jit(solution)/shard_map/ppermute | solution.py:216
  151.8 7.0 %collective-permute-done.9.refs_3_ = bf16[8,160,128]{2,1,0:T(8,128)(2,1)S(1)} collective-permute-done((bf16[8,160,128]{2,1,0:T(8,128)(2,1)S(1)}, bf16[8,160,128]{2,1,0:T(8,128)(2,1)S(1)}, u32[]{:S(2)}, u32[]{:S(2)}) %collective-permute-start.9) | collective-permute-done | bytes 327712 | tf_op jit(solution)/shard_map/ppermute | solution.py:216
  159.5 4.0 %collective-permute-start.8 = (bf16[8,160,128]{2,1,0:T(8,128)(2,1)S(1)}, bf16[8,160,128]{2,1,0:T(8,128)(2,1)}, u32[]{:S(2)}, u32[]{:S(2)}) collective-permute-start(bf16[8,160,128]{2,1,0:T(8,128)(2,1)S(1)} %slice.32.refs_0_), channel_id=1, source_target_pairs={{0,256},{128,384},{256,0},{384,128},{1,257},{129,385},{257,1},{385... | collective-permute-start | bytes 983048 | tf_op jit(solution)/shard_map/ppermute | solution.py:216
  163.5 3.8 %collective-permute-start.7 = (bf16[8,160,128]{2,1,0:T(8,128)(2,1)S(1)}, bf16[8,160,128]{2,1,0:T(8,128)(2,1)}, u32[]{:S(2)}, u32[]{:S(2)}) collective-permute-start(bf16[8,160,128]{2,1,0:T(8,128)(2,1)S(1)} %slice.32.refs_0_), channel_id=1, source_target_pairs={{0,128},{128,256},{256,384},{384,0},{1,129},{129,257},{257,385},{3... | collective-permute-start | bytes 983048 | tf_op jit(solution)/shard_map/ppermute | solution.py:216
  168.2 2.7 collective-permute-start.15
  170.9 2.9 collective-permute-start.14
  173.8 1.9 collective-permute-start.13
  177.9 5.7 %shard_map.94.normed = bf16[384,5120]{1,0:T(8,128)(2,1)} custom-call(s32[2]{0:T(128)S(1)} %get-tuple-element.25.where, f32[1,5120]{1,0:T(1,128)S(1)} %bitcast.44, bf16[2,192,640]{2,1,0:T(8,128)(2,1)S(1)} %bitcast.40, bf16[2,192,640]{2,1,0:T(8,128)(2,1)} %collective-permute-done.refs_1_, bf16[2,192,640]{2,1,0:T(8,128)(2,1)} %collective-permute-done.1.refs_2_, ...), custom_call_target="tpu_custom_call" | custom-call | bytes 4194304 | tf_op jit(solution)/shard_map/pallas_call | solution.py:226
  183.7 2.1 copy-done
  185.8 2.6 shard_map.95
  188.4 42.3 %all_gather.27.mine = bf16[3072,128]{1,0:T(8,128)(2,1)S(1)} all-gather(bf16[384,128]{1,0:T(8,128)(2,1)S(1)} %shard_map.95), channel_id=1, replica_groups=mesh['x'=4,'z'=8,'c'=2,'y'=4,'w'=2] {'z'}, dimensions={0}, use_global_device_ids=true | all-gather | bytes 884736 | tf_op jit(solution)/shard_map/all_gather | solution.py:276
  230.7 10.4 %collective-permute-start.10 = (bf16[3072,128]{1,0:T(8,128)(2,1)S(1)}, bf16[3072,128]{1,0:T(8,128)(2,1)}, u32[]{:S(2)}, u32[]{:S(2)}) collective-permute-start(bf16[3072,128]{1,0:T(8,128)(2,1)S(1)} %all_gather.27.mine), channel_id=1, source_target_pairs={{0,8},{8,0},{1,9},{9,1},{2,10},{10,2},{3,11},{11,3},{4,12},{12,4},... | collective-permute-start | bytes 2359304 | tf_op jit(solution)/shard_map/ppermute | solution.py:277
  243.6 4.1 %shard_map.96 = bf16[2,2,192,128]{3,2,1,0:T(8,128)(2,1)S(1)} custom-call(s32[64]{0:T(128)S(1)} %broadcast_multiply_fusion.offsets, s32[2]{0:T(128)S(1)} %get-tuple-element.24.where, bf16[384,5120]{1,0:T(8,128)(2,1)} %shard_map.94.normed, f32[1,128]{1,0:T(1,128)S(1)} %bitcast.46, f32[384,128]{1,0:T(8,128)S(1)} %get-tuple-element.26.cosine, ...), custom_call_target="tpu_custom_call" | custom-call | flops 1006632960 | bytes 4194304 | tf_op jit(solution)/shard_map/pallas_call | solution.py:267
  247.7 1.9 collective-permute-start.16
  253.6 7.3 %collective-permute-done.18.q2 = bf16[768,128]{1,0:T(8,128)(2,1)S(1)} collective-permute-done((bf16[768,128]{1,0:T(8,128)(2,1)S(1)}, bf16[768,128]{1,0:T(8,128)(2,1)S(1)}, u32[]{:S(2)}, u32[]{:S(2)}) %collective-permute-start.18) | collective-permute-done | bytes 196640 | tf_op jit(solution)/shard_map/ppermute | solution.py:283
  261.2 4.2 %shard_map.97 = (f32[768,128]{1,0:T(8,128)S(1)}, bf16[768,128]{1,0:T(8,128)(2,1)S(1)}, bf16[768,128]{1,0:T(8,128)(2,1)S(1)}, f32[3,8,128]{2,1,0:T(8,128)S(1)}) custom-call(s32[8]{0:T(128)S(1)} %stack.98.where, s32[3,192,1]{2,1,0:T(8,128)S(1)} %broadcast_subtract_fusion.starts, bf16[3072,128]{1,0:T(8,128)(2,1)S(1)} %all_gather.27.mine, ...), custom_call_target="tpu_custom_call" | custom-call | flops 2415919104 | bytes 4194304 | tf_op jit(solution)/shard_map/pallas_call | solution.py:293
  265.5 28.3 %collective-permute-start.19 = (bf16[768,128]{1,0:T(8,128)(2,1)S(1)}, bf16[768,128]{1,0:T(8,128)(2,1)S(1)}, u32[]{:S(2)}, u32[]{:S(2)}) collective-permute-start(bf16[768,128]{1,0:T(8,128)(2,1)S(1)} %get-tuple-element.8), channel_id=1, source_target_pairs={{0,128},{128,256},{256,384},{1,129},{129,257},{257,385},{2,130},{1... | collective-permute-start | bytes 589832 | tf_op jit(solution)/shard_map/ppermute | solution.py:313
  296.4 1.9 collective-permute-start.21
  299.8 1.8 collective-permute-done.22.l2
  301.7 2.1 shard_map.98
  (81 shorter events, 22.0 us)
Async XLA Ops:
  0.6 151.0 %copy-start.10 = (s32[64]{0:T(128)S(1)}, s32[64]{0:T(128)}, u32[]{:S(2)}) copy-start(s32[64]{0:T(128)} %param.13) | copy-start | bytes 772
  0.6 175.2 %copy-start.9 = (bf16[5120]{0:T(1024)(128)(2,1)S(1)}, bf16[5120]{0:T(1024)(128)(2,1)}, u32[]{:S(2)}) copy-start(bf16[5120]{0:T(1024)(128)(2,1)} %param.8) | copy-start | bytes 30724
  21.0 142.5 %collective-permute-start.3 = (bf16[2,192,640]{2,1,0:T(8,128)(2,1)S(1)}, bf16[2,192,640]{2,1,0:T(8,128)(2,1)S(1)}, u32[]{:S(2)}, u32[]{:S(2)}) collective-permute-start(bf16[2,192,640]{2,1,0:T(8,128)(2,1)S(1)} %bitcast.36), channel_id=1, source_target_pairs={{0,8},{8,0},{1,9},{9,1},{2,10},{10,2},{3,11},{11,3},{4,12},{12,4},... | collective-permute-start | bytes 1474568 | tf_op jit(solution)/shard_map/ppermute | solution.py:224
  25.4 103.6 %collective-permute-start.2 = (bf16[2,192,640]{2,1,0:T(8,128)(2,1)S(1)}, bf16[2,192,640]{2,1,0:T(8,128)(2,1)S(1)}, u32[]{:S(2)}, u32[]{:S(2)}) collective-permute-start(bf16[2,192,640]{2,1,0:T(8,128)(2,1)S(1)} %bitcast.37), channel_id=1, source_target_pairs={{0,6},{2,0},{4,2},{6,4},{1,7},{3,1},{5,3},{7,5},{8,14},{10,8},{12,... | collective-permute-start | bytes 1474568 | tf_op jit(solution)/shard_map/ppermute | solution.py:223
  29.7 108.3 %collective-permute-start.1 = (bf16[2,192,640]{2,1,0:T(8,128)(2,1)S(1)}, bf16[2,192,640]{2,1,0:T(8,128)(2,1)}, u32[]{:S(2)}, u32[]{:S(2)}) collective-permute-start(bf16[2,192,640]{2,1,0:T(8,128)(2,1)S(1)} %bitcast.38), channel_id=1, source_target_pairs={{0,4},{2,6},{4,0},{6,2},{1,5},{3,7},{5,1},{7,3},{8,12},{10,14},{12... | collective-permute-start | bytes 1474568 | tf_op jit(solution)/shard_map/ppermute | solution.py:223
  32.0 108.0 %collective-permute-start = (bf16[2,192,640]{2,1,0:T(8,128)(2,1)S(1)}, bf16[2,192,640]{2,1,0:T(8,128)(2,1)}, u32[]{:S(2)}, u32[]{:S(2)}) collective-permute-start(bf16[2,192,640]{2,1,0:T(8,128)(2,1)S(1)} %bitcast.39), channel_id=1, source_target_pairs={{0,2},{2,4},{4,6},{6,0},{1,3},{3,5},{5,7},{7,1},{8,10},{10,12},{12... | collective-permute-start | bytes 1474568 | tf_op jit(solution)/shard_map/ppermute | solution.py:223
  77.8 49.9 %collective-permute-start.12 = (s32[192]{0:T(256)S(1)}, s32[192]{0:T(256)S(1)}, u32[]{:S(2)}, u32[]{:S(2)}) collective-permute-start(s32[192]{0:T(256)S(1)} %dynamic_slice.26), channel_id=1, source_target_pairs={{256,0},{384,128},{257,1},{385,129},{258,2},{386,130},{259,3},{387... | collective-permute-start | bytes 2312 | tf_op jit(solution)/shard_map/ppermute | solution.py:253
  127.7 17.0 %collective-permute-start.11 = (s32[192]{0:T(256)S(1)}, s32[192]{0:T(256)S(1)}, u32[]{:S(2)}, u32[]{:S(2)}) collective-permute-start(s32[192]{0:T(256)S(1)} %dynamic_slice.26), channel_id=1, source_target_pairs={{128,0},{256,128},{384,256},{129,1},{257,129},{385,257},{130,2},{2... | collective-permute-start | bytes 2312 | tf_op jit(solution)/shard_map/ppermute | solution.py:252
  129.0 38.4 %copy-start.1 = (bf16[2,192,640]{2,1,0:T(8,128)(2,1)}, bf16[2,192,640]{2,1,0:T(8,128)(2,1)S(1)}, u32[]{:S(2)}) copy-start(bf16[2,192,640]{2,1,0:T(8,128)(2,1)S(1)} %collective-permute-done.2.refs_3_) | copy-start | bytes 1474564
  129.0 38.4 %collective-permute-start.6 = (bf16[2,192,640]{2,1,0:T(8,128)(2,1)S(1)}, bf16[2,192,640]{2,1,0:T(8,128)(2,1)S(1)}, u32[]{:S(2)}, u32[]{:S(2)}) collective-permute-start(bf16[2,192,640]{2,1,0:T(8,128)(2,1)S(1)} %collective-permute-done.2.refs_3_), channel_id=1, source_target_pairs={{0,8},{8,0},{1,9},{9,1},{2,10},{10,2},{3,11},{11,3},{4,12},{12,4},... | collective-permute-start | bytes 1474568 | tf_op jit(solution)/shard_map/ppermute | solution.py:224
  138.0 32.9 %collective-permute-start.5 = (bf16[2,192,640]{2,1,0:T(8,128)(2,1)}, bf16[2,192,640]{2,1,0:T(8,128)(2,1)}, u32[]{:S(2)}, u32[]{:S(2)}) collective-permute-start(bf16[2,192,640]{2,1,0:T(8,128)(2,1)} %collective-permute-done.1.refs_2_), channel_id=1, source_target_pairs={{0,8},{8,0},{1,9},{9,1},{2,10},{10,2},{3,11},{11,3},{4,12},{12,4},... | collective-permute-start | bytes 1474568 | tf_op jit(solution)/shard_map/ppermute | solution.py:224
  140.0 33.9 %collective-permute-start.4 = (bf16[2,192,640]{2,1,0:T(8,128)(2,1)}, bf16[2,192,640]{2,1,0:T(8,128)(2,1)}, u32[]{:S(2)}, u32[]{:S(2)}) collective-permute-start(bf16[2,192,640]{2,1,0:T(8,128)(2,1)} %collective-permute-done.refs_1_), channel_id=1, source_target_pairs={{0,8},{8,0},{1,9},{9,1},{2,10},{10,2},{3,11},{11,3},{4,12},{12,4},... | collective-permute-start | bytes 1474568 | tf_op jit(solution)/shard_map/ppermute | solution.py:224
  144.7 14.1 %collective-permute-start.9 = (bf16[8,160,128]{2,1,0:T(8,128)(2,1)S(1)}, bf16[8,160,128]{2,1,0:T(8,128)(2,1)S(1)}, u32[]{:S(2)}, u32[]{:S(2)}) collective-permute-start(bf16[8,160,128]{2,1,0:T(8,128)(2,1)S(1)} %slice.32.refs_0_), channel_id=1, source_target_pairs={{0,384},{128,0},{256,128},{384,256},{1,385},{129,1},{257,129},{385... | collective-permute-start | bytes 983048 | tf_op jit(solution)/shard_map/ppermute | solution.py:216
  159.5 24.1 %collective-permute-start.8 = (bf16[8,160,128]{2,1,0:T(8,128)(2,1)S(1)}, bf16[8,160,128]{2,1,0:T(8,128)(2,1)}, u32[]{:S(2)}, u32[]{:S(2)}) collective-permute-start(bf16[8,160,128]{2,1,0:T(8,128)(2,1)S(1)} %slice.32.refs_0_), channel_id=1, source_target_pairs={{0,256},{128,384},{256,0},{384,128},{1,257},{129,385},{257,1},{385... | collective-permute-start | bytes 983048 | tf_op jit(solution)/shard_map/ppermute | solution.py:216
  163.5 20.1 %collective-permute-start.7 = (bf16[8,160,128]{2,1,0:T(8,128)(2,1)S(1)}, bf16[8,160,128]{2,1,0:T(8,128)(2,1)}, u32[]{:S(2)}, u32[]{:S(2)}) collective-permute-start(bf16[8,160,128]{2,1,0:T(8,128)(2,1)S(1)} %slice.32.refs_0_), channel_id=1, source_target_pairs={{0,128},{128,256},{256,384},{384,0},{1,129},{129,257},{257,385},{3... | collective-permute-start | bytes 983048 | tf_op jit(solution)/shard_map/ppermute | solution.py:216
  168.2 75.4 %collective-permute-start.15 = (bf16[8,160,256]{2,1,0:T(8,128)(2,1)S(1)}, bf16[8,160,256]{2,1,0:T(8,128)(2,1)S(1)}, u32[]{:S(2)}, u32[]{:S(2)}) collective-permute-start(bf16[8,160,256]{2,1,0:T(8,128)(2,1)S(1)} %slice.36.refs_0_), channel_id=1, source_target_pairs={{0,384},{128,0},{256,128},{384,256},{1,385},{129,1},{257,129},{385... | collective-permute-start | bytes 1966088 | tf_op jit(solution)/shard_map/ppermute | solution.py:219
  170.9 72.7 %collective-permute-start.14 = (bf16[8,160,256]{2,1,0:T(8,128)(2,1)S(1)}, bf16[8,160,256]{2,1,0:T(8,128)(2,1)}, u32[]{:S(2)}, u32[]{:S(2)}) collective-permute-start(bf16[8,160,256]{2,1,0:T(8,128)(2,1)S(1)} %slice.36.refs_0_), channel_id=1, source_target_pairs={{0,256},{128,384},{256,0},{384,128},{1,257},{129,385},{257,1},{385... | collective-permute-start | bytes 1966088 | tf_op jit(solution)/shard_map/ppermute | solution.py:219
  173.8 69.8 %collective-permute-start.13 = (bf16[8,160,256]{2,1,0:T(8,128)(2,1)S(1)}, bf16[8,160,256]{2,1,0:T(8,128)(2,1)}, u32[]{:S(2)}, u32[]{:S(2)}) collective-permute-start(bf16[8,160,256]{2,1,0:T(8,128)(2,1)S(1)} %slice.36.refs_0_), channel_id=1, source_target_pairs={{0,128},{128,256},{256,384},{384,0},{1,129},{129,257},{257,385},{3... | collective-permute-start | bytes 1966088 | tf_op jit(solution)/shard_map/ppermute | solution.py:219
  175.9 1.0 copy-start.2
  176.9 1.0 copy-start.4
  177.9 5.7 %copy-start.6 = (bf16[8,160,128]{2,1,0:T(8,128)(2,1)S(1)}, bf16[8,160,128]{2,1,0:T(8,128)(2,1)}, u32[]{:S(2)}) copy-start(bf16[8,160,128]{2,1,0:T(8,128)(2,1)} %copy-done.5) | copy-start | bytes 983044
  177.9 5.7 %copy-start.7 = (f32[128]{0:T(128)S(1)}, f32[128]{0:T(128)}, u32[]{:S(2)}) copy-start(f32[128]{0:T(128)} %param.10) | copy-start | bytes 1540
  183.6 60.0 %copy-start.8 = (f32[128]{0:T(128)S(1)}, f32[128]{0:T(128)}, u32[]{:S(2)}) copy-start(f32[128]{0:T(128)} %param.9) | copy-start | bytes 1540
  183.7 2.1 copy-start
  230.7 30.6 %collective-permute-start.10 = (bf16[3072,128]{1,0:T(8,128)(2,1)S(1)}, bf16[3072,128]{1,0:T(8,128)(2,1)}, u32[]{:S(2)}, u32[]{:S(2)}) collective-permute-start(bf16[3072,128]{1,0:T(8,128)(2,1)S(1)} %all_gather.27.mine), channel_id=1, source_target_pairs={{0,8},{8,0},{1,9},{9,1},{2,10},{10,2},{3,11},{11,3},{4,12},{12,4},... | collective-permute-start | bytes 2359304 | tf_op jit(solution)/shard_map/ppermute | solution.py:277
  247.7 3.2 %collective-permute-start.16 = (bf16[2,192,128]{2,1,0:T(8,128)(2,1)S(1)}, bf16[2,192,128]{2,1,0:T(8,128)(2,1)S(1)}, u32[]{:S(2)}, u32[]{:S(2)}) collective-permute-start(bf16[2,192,128]{2,1,0:T(8,128)(2,1)S(1)} %get-tuple-element.14), channel_id=1, source_target_pairs={{0,8},{8,0},{1,9},{9,1},{2,10},{10,2},{3,11},{11,3},{4,12},{12,4},... | collective-permute-start | bytes 294920 | tf_op jit(solution)/shard_map/ppermute | solution.py:280
  251.0 9.9 %collective-permute-start.18 = (bf16[768,128]{1,0:T(8,128)(2,1)S(1)}, bf16[768,128]{1,0:T(8,128)(2,1)S(1)}, u32[]{:S(2)}, u32[]{:S(2)}) collective-permute-start(bf16[768,128]{1,0:T(8,128)(2,1)S(1)} %bitcast.41), channel_id=1, source_target_pairs={{256,0},{384,128},{257,1},{385,129},{258,2},{386,130},{259,3},{387... | collective-permute-start | bytes 589832 | tf_op jit(solution)/shard_map/ppermute | solution.py:283
  252.3 9.0 %collective-permute-start.17 = (bf16[768,128]{1,0:T(8,128)(2,1)S(1)}, bf16[768,128]{1,0:T(8,128)(2,1)S(1)}, u32[]{:S(2)}, u32[]{:S(2)}) collective-permute-start(bf16[768,128]{1,0:T(8,128)(2,1)S(1)} %bitcast.42), channel_id=1, source_target_pairs={{128,0},{256,128},{384,256},{129,1},{257,129},{385,257},{130,2},{2... | collective-permute-start | bytes 589832 | tf_op jit(solution)/shard_map/ppermute | solution.py:282
  265.5 36.2 %collective-permute-start.19 = (bf16[768,128]{1,0:T(8,128)(2,1)S(1)}, bf16[768,128]{1,0:T(8,128)(2,1)S(1)}, u32[]{:S(2)}, u32[]{:S(2)}) collective-permute-start(bf16[768,128]{1,0:T(8,128)(2,1)S(1)} %get-tuple-element.8), channel_id=1, source_target_pairs={{0,128},{128,256},{256,384},{1,129},{129,257},{257,385},{2,130},{1... | collective-permute-start | bytes 589832 | tf_op jit(solution)/shard_map/ppermute | solution.py:313
  293.8 7.9 %collective-permute-start.20 = (bf16[768,128]{1,0:T(8,128)(2,1)S(1)}, bf16[768,128]{1,0:T(8,128)(2,1)S(1)}, u32[]{:S(2)}, u32[]{:S(2)}) collective-permute-start(bf16[768,128]{1,0:T(8,128)(2,1)S(1)} %get-tuple-element.9), channel_id=1, source_target_pairs={{0,256},{128,384},{1,257},{129,385},{2,258},{130,386},{3,259},{131... | collective-permute-start | bytes 589832 | tf_op jit(solution)/shard_map/ppermute | solution.py:314
  295.1 6.5 %collective-permute-start.22 = (f32[8,128]{1,0:T(8,128)S(1)}, f32[8,128]{1,0:T(8,128)S(1)}, u32[]{:S(2)}, u32[]{:S(2)}) collective-permute-start(f32[8,128]{1,0:T(8,128)S(1)} %get-tuple-element.15), channel_id=1, source_target_pairs={{0,256},{128,384},{1,257},{129,385},{2,258},{130,386},{3,259},{131... | collective-permute-start | bytes 12296 | tf_op jit(solution)/shard_map/ppermute | solution.py:316
  296.4 5.3 %collective-permute-start.21 = (f32[8,128]{1,0:T(8,128)S(1)}, f32[8,128]{1,0:T(8,128)S(1)}, u32[]{:S(2)}, u32[]{:S(2)}) collective-permute-start(f32[8,128]{1,0:T(8,128)S(1)} %get-tuple-element.16), channel_id=1, source_target_pairs={{0,128},{128,256},{256,384},{1,129},{129,257},{257,385},{2,130},{1... | collective-permute-start | bytes 12296 | tf_op jit(solution)/shard_map/ppermute | solution.py:315
  (2 other events, 1.5 us)

commit v2 on v0

v2 whole, which is shorter than its diff:
```python
import functools
import math

import jax
import jax.numpy as jnp
from jax import lax
from jax.experimental import pallas as pl
from jax.experimental.pallas import tpu as pltpu
from jax.sharding import Mesh
from jax.sharding import PartitionSpec as P

epsilon = 1e-06
rope_base = 1000000.0
NEG = -1e30
MASKED = -3e38
KEY_BLOCK = 512
NO_SEGMENT = 100.0
VMEM_LIMIT = 48 * 1024 * 1024


def call(kernel, out_shape, n_smem, n_vmem, scratch=(), flops=0):
    specs = [pl.BlockSpec(memory_space=pltpu.SMEM)] * n_smem
    specs += [pl.BlockSpec(memory_space=pltpu.VMEM)] * n_vmem
    n_out = len(out_shape)
    return pl.pallas_call(
        kernel,
        out_shape=out_shape,
        in_specs=specs,
        out_specs=[pl.BlockSpec(memory_space=pltpu.VMEM)] * n_out,
        scratch_shapes=list(scratch),
        compiler_params=pltpu.CompilerParams(vmem_limit_bytes=VMEM_LIMIT),
        cost_estimate=pl.CostEstimate(flops=flops, bytes_accessed=4 << 20, transcendentals=0),
    )


PEER = (0, 4, 2, 6, 1, 5, 3, 7)


def head_norm_rope(v, gain, cosine, sine):
    mean = jnp.mean(v * v, axis=-1, keepdims=True)
    v = v * lax.rsqrt(mean + epsilon) * gain
    return v * cosine + pltpu.roll(v, 64, 1) * sine


def collect(offsets, where, blocks, weights, panel):
    nx = len(blocks)
    nz = blocks[0].shape[0]
    for s in range(nx):
        source = lax.rem(where[2] + nx - s, nx)
        for k in range(nz):
            for c in range(2):
                slot = source * (nz * 2) + (where[1] ^ PEER[k]) * 2 + c
                first = pl.multiple_of(offsets[slot], 16)
                weights[pl.ds(first, panel), :] = blocks[s][k, c * panel : (c + 1) * panel, :]


def pair_kernel(panel, offsets, where, norm_gain, gain, cosine, sine, *refs):
    hidden, blocks = refs[:4], refs[4:-3]
    normed, out, weights = refs[-3:]
    collect(offsets, where, blocks, weights, panel)
    ny, rows, width = hidden[0].shape
    for side in range(2):
        first = pl.multiple_of(rows * (where[0] if side == 0 else 1 - where[0]), rows)
        total = jnp.zeros((rows, 128), jnp.float32)
        for half in range(2):
            for s in range(ny):
                v = hidden[side * 2 + half][s].astype(jnp.float32)
                v = v * v
                for k in range(width // 128):
                    total = total + v[:, k * 128 : (k + 1) * 128]
        mean = jnp.sum(total, axis=-1, keepdims=True) * (1.0 / (2 * ny * width))
        scale = lax.rsqrt(mean + epsilon)
        for half in range(2):
            for s in range(ny):
                source = lax.rem(where[3] + ny - s, ny) * 2 + (where[4] ^ half)
                cols = pl.ds(pl.multiple_of(source * width, 128), width)
                v = hidden[side * 2 + half][s].astype(jnp.float32)
                v = v * scale * norm_gain[:, cols]
                normed[pl.ds(first, rows), cols] = v.astype(jnp.bfloat16)
    v = jnp.dot(normed[...], weights[...], preferred_element_type=jnp.float32)
    keys = head_norm_rope(v, gain[...], cosine[...], sine[...])
    out[...] = jnp.where(where[0] == 0, keys, v).astype(jnp.bfloat16)


def query_kernel(panel, offsets, where, normed, gain, cosine, sine, *refs):
    blocks, out, weights = refs[:-2], refs[-2], refs[-1]
    collect(offsets, where, blocks, weights, panel)
    rows = out.shape[2]
    for side in range(2):
        span = pl.ds(side * rows, rows)
        v = jnp.dot(normed[span, :], weights[...], preferred_element_type=jnp.float32)
        for h in range(2):
            q = head_norm_rope(
                v[:, h * 128 : (h + 1) * 128], gain[...], cosine[span, :], sine[span, :]
            )
            out[side, h] = q.astype(jnp.bfloat16)


def identity_mask():
    shape = (128, 128)
    return lax.broadcasted_iota(jnp.int32, shape, 0) == lax.broadcasted_iota(jnp.int32, shape, 1)


def attend(query, keys, values, begin, index, low, high, acc, top, total):
    rows = begin.shape[0]
    scale = math.log2(math.e) / math.sqrt(128)
    acc[...] = jnp.zeros_like(acc)
    top[...] = jnp.full(top.shape, NEG, jnp.float32)
    total[...] = jnp.zeros_like(total)

    def step(b, carry):
        base = pl.multiple_of(b * KEY_BLOCK, KEY_BLOCK)
        key = keys[pl.ds(base, KEY_BLOCK), :]
        value = values[pl.ds(base, KEY_BLOCK), :]
        col = base + lax.broadcasted_iota(jnp.int32, (rows, KEY_BLOCK), 1)
        allowed = col >= begin
        if index is not None:
            allowed = allowed & (col <= index)
        for h in range(query.shape[0] // rows):
            span = pl.ds(h * rows, rows)
            raw = lax.dot_general(
                query[span, :], key, (((1,), (1,)), ((), ())), preferred_element_type=jnp.float32
            )
            raw = jnp.where(allowed, raw * scale, MASKED)
            old = top[span, :]
            new = jnp.maximum(old, jnp.max(raw, axis=-1, keepdims=True))
            terms = jnp.exp2(raw - new)
            decay = jnp.exp2(old - new)
            top[span, :] = new
            total[span, :] = total[span, :] * decay + jnp.sum(terms, axis=-1, keepdims=True)
            acc[span, :] = acc[span, :] * decay + jnp.dot(
                terms.astype(jnp.bfloat16), value, preferred_element_type=jnp.float32
            )
        return carry

    lax.fori_loop(low // KEY_BLOCK, (high + KEY_BLOCK - 1) // KEY_BLOCK, step, 0)
    summed = total[...]
    safe = jnp.where(summed > 0, summed, 1.0)
    return acc[...] / safe, jnp.where(summed > 0, top[...] + jnp.log2(safe), NEG)


def remote_kernel(where, begins, near, far, mine0, mine1, other0, other1, out1, out2, keys, values, acc, top, total):
    block = mine0.shape[1]
    for core, (first, second) in enumerate((((mine0, mine1), (other0, other1)), ((other0, other1), (mine0, mine1)))):

        @pl.when(where[0] == core)
        def _(first=first, second=second):
            for k in range(8):
                spot = pl.ds(pl.multiple_of((where[1] ^ PEER[k]) * block, block), block)
                keys[spot, :] = first[k // 4][k % 4]
                values[spot, :] = second[k // 4][k % 4]

    eye = identity_mask()
    size = near.shape[0]
    for s, query, out in ((1, near, out1), (2, far, out2)):
        low, high = where[2 + 2 * s], where[3 + 2 * s]
        result, log = attend(query, keys, values, begins[s], None, low, high, acc, top, total)
        out[0:size, :] = result.astype(jnp.bfloat16)
        rest = jnp.concatenate(
            [
                jnp.sum(jnp.where(eye, log[g * 128 : (g + 1) * 128, :], 0.0), axis=0, keepdims=True)
                for g in range(size // 128)
            ]
            + [jnp.zeros((16 - size // 128, 128), jnp.float32)],
            axis=0,
        )
        for part in range(3):
            piece = rest.astype(jnp.bfloat16)
            out[size + 16 * part : size + 16 * (part + 1), :] = piece
            rest = rest - piece.astype(jnp.float32)


def own_kernel(where, begins, query, keys, values, out, log, acc, top, total):
    rows = begins.shape[1]
    index = where[8] + lax.broadcasted_iota(jnp.int32, (rows, 1), 0)
    result, level = attend(
        query, keys, values, begins[0], index, where[2], where[3], acc, top, total
    )
    out[...] = result
    log[...] = level


def combine_kernel(where, o0, l0, r1, r2, out):
    rows = out.shape[0]
    size = o0.shape[0]
    eye = identity_mask()

    def column(ref):
        level = sum(
            ref[size + 16 * part : size + 16 * (part + 1), :].astype(jnp.float32)
            for part in (2, 1, 0)
        )
        pieces = [
            jnp.sum(jnp.where(eye, level[g : g + 1, :], 0.0), axis=1, keepdims=True)
            for g in range(size // 128)
        ]
        return jnp.concatenate(pieces, axis=0)

    a = l0[...]
    b = jnp.where(where[1] == 1, column(r1), NEG)
    c = jnp.where(where[2] == 1, column(r2), NEG)
    top = jnp.maximum(jnp.maximum(a, b), c)
    a, b, c = jnp.exp2(a - top), jnp.exp2(b - top), jnp.exp2(c - top)
    summed = a * o0[...]
    summed = summed + b * r1[0:size, :].astype(jnp.float32) + c * r2[0:size, :].astype(jnp.float32)
    result = (summed / (a + b + c)).astype(jnp.bfloat16)
    for side in range(2):
        first = 256 * (where[0] if side == 0 else 1 - where[0])
        for h in range(2):
            k = side * 2 + h
            cols = pl.ds(pl.multiple_of(first + h * 128, 128), 128)
            out[:, cols] = result[k * rows : (k + 1) * rows, :]


def ring(size, shift):
    return [(i, (i + shift) % size) for i in range(size)]


def across(v, bit):
    return lax.ppermute(v, "z", [(i, i ^ bit) for i in range(8)])


def after(v, *earlier):
    return lax.optimization_barrier((v, *earlier))[0]


def body(hidden, norm_gain, query_gain, key_gain, weight_store, documents, owners):
    x, z, c, y, w = (lax.axis_index(a) for a in ("x", "z", "c", "y", "w"))
    nx, nz, ny = (lax.axis_size(a) for a in ("x", "z", "y"))
    rows = hidden.shape[0]
    slots = owners.shape[0]
    panel = weight_store.shape[0]
    swap = [(0, 1), (1, 0)]
    bf16, f32 = jnp.bfloat16, jnp.float32
    table = jnp.arange(slots, dtype=jnp.int32)

    far_half = lax.ppermute(hidden, "w", swap)

    both = lax.all_gather(weight_store, "c", axis=0, tiled=True)
    pair_docs = lax.all_gather(documents, "c", axis=0)
    riders = jnp.pad(
        pair_docs.astype(bf16), ((0, 0), (0, 256 - rows)), constant_values=NO_SEGMENT
    ).reshape(4, 128)
    pair_cols = jnp.concatenate(
        [
            lax.dynamic_slice_in_dim(both, 512 + 128 * c, 128, 1),
            riders,
            jnp.zeros((12, 128), bf16),
        ],
        axis=0,
    )
    query_cols = lax.dynamic_slice_in_dim(both, 256 * c, 256, 1)

    def spread_z(v, bits):
        for bit in bits:
            v = jnp.concatenate([v, across(v, bit)], axis=0)
        return v

    pair_two = spread_z(pair_cols[None], (4, 2))
    query_one = spread_z(query_cols[None], (4,))
    pair_line = spread_z(pair_two, (1,))
    query_line = spread_z(query_one, (2, 1))
    pair_blocks = [pair_line] + [lax.ppermute(pair_line, "x", ring(nx, s)) for s in (1, 3, 2)]
    pair_blocks = [pair_blocks[i] for i in (0, 1, 3, 2)]
    query_blocks = [query_line] + [lax.ppermute(query_line, "x", ring(nx, s)) for s in (1, 3, 2)]
    query_blocks = [query_blocks[i] for i in (0, 1, 3, 2)]

    def spread_y(v):
        parts = {s: lax.ppermute(v, "y", ring(ny, s)) for s in (1, 3, 2)}
        return jnp.stack([v, parts[1], parts[2], parts[3]])

    own_near = spread_y(hidden)
    other_near = lax.ppermute(own_near, "c", swap)
    own_far = spread_y(far_half)
    other_far = lax.ppermute(own_far, "c", swap)

    riding = jnp.stack([v[:, 2 * panel : 2 * panel + 4, :] for v in pair_blocks]).astype(f32)
    starts = jnp.sum(
        (riding.reshape(-1, 1) < table.astype(f32)[None, :]).astype(f32), axis=0
    ).astype(jnp.int32)

    def begin_of(docs):
        return jnp.sum(
            (docs[:, None] == table[None, :]).astype(jnp.int32) * starts[None, :], axis=1
        )

    pair_begin = begin_of(pair_docs.reshape(-1))
    plane = nz * 2 * rows
    token = x * plane + z * 2 * rows + jnp.arange(2 * rows, dtype=jnp.int32)
    positions = token - pair_begin
    exponent = jnp.arange(64, dtype=f32) * (2.0 / 128)
    frequency = jnp.exp(exponent * -math.log(rope_base))
    angles = positions.astype(f32)[:, None] * frequency[None, :]
    cosine, sine = jnp.cos(angles), jnp.sin(angles)
    cosine = jnp.concatenate([cosine, cosine], axis=1)
    sine = jnp.concatenate([-sine, sine], axis=1)
    spread = [lax.dynamic_slice_in_dim(pair_begin, c * rows, rows, 0)]
    for s in (1, 2):
        docs = lax.dynamic_slice_in_dim(riding[nx - s, 0], 2 * c, 2, 0).reshape(-1)[:rows]
        spread.append(begin_of(docs.astype(jnp.int32)))
    spread = jnp.stack(spread) - x * plane

    offsets = panel * jnp.sum(
        table[:, None] * (owners[:, None] == table[None, :]).astype(jnp.int32), axis=0
    )
    spot = jnp.stack([c, z, x, y, w]).astype(jnp.int32)
    features = norm_gain.shape[0]
    normed, pair = call(
        functools.partial(pair_kernel, panel),
        [
            jax.ShapeDtypeStruct((2 * rows, features), bf16),
            jax.ShapeDtypeStruct((2 * rows, 128), bf16),
        ],
        2,
        8 + nx,
        [pltpu.VMEM((features, 128), bf16)],
        4 * 10**9,
    )(
        offsets, spot, norm_gain.astype(f32)[None, :], key_gain[None, :], cosine, sine,
        own_near, own_far, other_near, other_far, *pair_blocks,
    )
    (query,) = call(
        functools.partial(query_kernel, panel),
        [jax.ShapeDtypeStruct((2, 2, rows, 128), bf16)],
        2,
        4 + nx,
        [pltpu.VMEM((features, 256), bf16)],
        4 * 10**9,
    )(offsets, spot, normed, query_gain[None, :], cosine, sine, *query_blocks)

    mine0 = spread_z(pair[None], (4, 2))
    mine1 = across(mine0, 1)
    other0 = lax.ppermute(mine0, "c", swap)
    other1 = lax.ppermute(mine1, "c", swap)
    own_query = lax.dynamic_index_in_dim(query, c, 0, keepdims=False)
    sent_query = lax.dynamic_index_in_dim(query, 1 - c, 0, keepdims=False)
    q0 = jnp.concatenate([own_query, lax.ppermute(sent_query, "c", swap)], axis=0)
    q0 = q0.reshape(4 * rows, 128)
    q1 = lax.ppermute(q0, "x", [(i, i - 1) for i in range(1, nx)])
    q2 = lax.ppermute(q0, "x", [(i, i - 2) for i in range(2, nx)])

    inside = z * 2 * rows + c * rows
    low = [jnp.clip(spread[s, 0], 0, plane) for s in range(3)]
    high = [inside + rows] + [jnp.where(x + s < nx, plane, 0) for s in (1, 2)]
    ranges = jnp.stack(
        [c, z, low[0], high[0], low[1], high[1], low[2], high[2], inside]
    ).astype(jnp.int32)
    state = [
        pltpu.VMEM((4 * rows, 128), f32),
        pltpu.VMEM((4 * rows, 1), f32),
        pltpu.VMEM((4 * rows, 1), f32),
    ]
    r1, r2, keys, values = call(
        remote_kernel,
        [jax.ShapeDtypeStruct((4 * rows + 48, 128), bf16)] * 2
        + [jax.ShapeDtypeStruct((plane, 128), bf16)] * 2,
        1,
        7,
        state,
        10**10,
    )(ranges, spread[:, :, None], q1, q2, mine0, mine1, other0, other1)
    r1 = lax.ppermute(r1, "x", [(i, i + 1) for i in range(nx - 1)])
    r2 = lax.ppermute(r2, "x", [(i, i + 2) for i in range(nx - 2)])
    o0, l0 = call(
        own_kernel,
        [
            jax.ShapeDtypeStruct((4 * rows, 128), f32),
            jax.ShapeDtypeStruct((4 * rows, 1), f32),
        ],
        1,
        4,
        state,
        10**10,
    )(ranges, spread[:, :, None], q0, keys, values)
    came = jnp.stack([c, (x >= 1).astype(jnp.int32), (x >= 2).astype(jnp.int32)]).astype(jnp.int32)
    (context,) = call(combine_kernel, [jax.ShapeDtypeStruct((rows, 512), bf16)], 1, 4)(
        came, o0, l0, r1, r2
    )

    own_part = lax.dynamic_slice_in_dim(pair, c * rows, rows, 0)
    other_part = lax.dynamic_slice_in_dim(other0[0], c * rows, rows, 0)
    keys_fresh = jnp.where(c == 0, own_part, other_part)
    values_fresh = jnp.where(c == 0, other_part, own_part)
    return keys_fresh, values_fresh, context


def solution(mesh):
    fine = Mesh(mesh.devices.reshape(4, 8, 2, 4, 2), ("x", "z", "c", "y", "w"))
    ctx, head = ("x", "z", "c"), ("y", "w")
    in_specs = (P(ctx, head), P(), P(), P(), P(ctx, head), P(ctx), P())
    out_specs = (P(ctx, head), P(ctx, head), P(ctx, head))
    return jax.shard_map(body, mesh=fine, in_specs=in_specs, out_specs=out_specs, check_vma=False)
```

time: 545 us -> 212 us (0.39)
  waiting for transfers between devices: 353 us -> 60.9 us
  starting transfers between devices: 0.16 us -> 113 us
  other arithmetic: 81.4 us -> 5.77 us
  matrix products: 42.1 us -> 0 us
  local copies, waits for them, and re-layouts: 29.6 us -> 3.42 us
  blocking collectives: 23.4 us -> 5.46 us
  Pallas kernels: 0 us -> 16.2 us
  between operations: 14 us -> 4.04 us
    all_gather x4 -> x0, waiting for transfers between devices: 352 us -> none  [the longest x1 111 us: body(): lax.all_gather(keys_fresh, 'ctx', axis=0, tiled=True)]
    ppermute x0 -> x31, starting transfers between devices: none -> 113 us  [the longest x9 25.2 us: across(): return lax.ppermute(v, 'z', [(i, i ^ bit) for i in range(8)])]
    ppermute x0 -> x31, waiting for transfers between devices: none -> 60.9 us  [the longest x9 44.3 us: across(): return lax.ppermute(v, 'z', [(i, i ^ bit) for i in range(8)])]
    dot_general x3 -> x0, matrix products: 42.1 us -> none  [the longest x1 18 us: body(): jnp.einsum('thd,sd->ths', queries, key_rows, preferred_element_type=jnp.f...]
    and x2 -> x0, other arithmetic: 37.8 us -> none  [the longest x1 35.9 us: body(): selected = jnp.take(normed, source, axis=1)]
    gather x5 -> x0, local copies, waits for them, and re-layouts: 23.8 us -> none  [the longest x1 20.9 us: body(): selected = jnp.take(normed, source, axis=1)]
    psum x1 -> x0, blocking collectives: 23.4 us -> none  [body(): counted = lax.psum(jnp.sum(one_hot, axis=0), 'ctx')]
    reduce_sum x8 -> x4, other arithmetic: 23.8 us -> 1.65 us  [the longest x1 0.75 us: body(): jnp.sum(table[:, None] * (owners[:, None] == table[None, :]).astype(jnp.i...]
  transfers between devices with their start and end apart: 4 -> 31, of which waited for: 4 -> 12; matrix products, arithmetic and copies ran while one was open for 23% -> 4% of each run, Pallas kernels for 0% -> 6%
where the time goes in v2:
time: 212 us; the launch traced here: 209 us
  starting transfers between devices  113 us (53%)
  waiting for transfers between devices  60.9 us (29%)
  Pallas kernels  16.2 us (8%)
  other arithmetic  5.77 us (3%)
  blocking collectives  5.46 us (3%)
  between operations  4.04 us (2%)
  local copies, waits for them, and re-layouts  3.42 us (2%)
    ppermute x9, waiting for transfers between devices, across(): return lax.ppermute(v, 'z', [(i, i ^ bit) for i in range(8)])  44.3 us
    ppermute x9, starting transfers between devices, across(): return lax.ppermute(v, 'z', [(i, i ^ bit) for i in range(8)])  25.2 us
    ppermute x6, starting transfers between devices, spread_y(): parts = {s: lax.ppermute(v, 'y', ring(ny, s)) for s in (1, 3, 2)}  19.2 us
    ppermute x1, starting transfers between devices, body(): far_half = lax.ppermute(hidden, 'w', swap)  16.3 us
    ppermute x1, starting transfers between devices, body(): r1 = lax.ppermute(r1, 'x', [(i, i + 1) for i in range(nx - 1)])  11.5 us
    ppermute x3, starting transfers between devices, body(): lax.ppermute(pair_line, 'x', ring(nx, s))  9.33 us
    ppermute x1, starting transfers between devices, body(): other_near = lax.ppermute(own_near, 'c', swap)  9.23 us
    ppermute x3, waiting for transfers between devices, body(): lax.ppermute(pair_line, 'x', ring(nx, s))  7.88 us
  transfers between devices with their start and end apart: 31, of which 12 were waited for; matrix products, arithmetic and copies ran while one was open for 4% of the time, Pallas kernels for 6%

profile of v2, /device:TPU:1, one launch (start us, length us, event | category | flops | bytes accessed | tf_op | source)
XLA Modules:
  0.0 209.0 jit_solution(7750056208046868700)
XLA Ops:
  0.6 16.3 %collective-permute-start.9 = (bf16[192,640]{1,0:T(8,128)(2,1)}, bf16[192,640]{1,0:T(8,128)(2,1)S(1)}, u32[]{:S(2)}, u32[]{:S(2)}) collective-permute-start(bf16[192,640]{1,0:T(8,128)(2,1)} %param.7), channel_id=1, source_target_pairs={{0,1},{1,0},{2,3},{3,2},{4,5},{5,4},{6,7},{7,6},{8,9},{9,8},{10,11... | collective-permute-start | bytes 737288 | tf_op jit(solution)/shard_map/ppermute | solution.py:237
  16.9 3.2 %collective-permute-start.6 = (bf16[192,640]{1,0:T(8,128)(2,1)}, bf16[192,640]{1,0:T(8,128)(2,1)S(1)}, u32[]{:S(2)}, u32[]{:S(2)}) collective-permute-start(bf16[192,640]{1,0:T(8,128)(2,1)} %param.7), channel_id=1, source_target_pairs={{0,2},{2,4},{4,6},{6,0},{1,3},{3,5},{5,7},{7,1},{8,10},{10,12},{12... | collective-permute-start | bytes 737288 | tf_op jit(solution)/shard_map/ppermute | solution.py:269
  20.1 4.5 %collective-permute-start.7 = (bf16[192,640]{1,0:T(8,128)(2,1)}, bf16[192,640]{1,0:T(8,128)(2,1)S(1)}, u32[]{:S(2)}, u32[]{:S(2)}) collective-permute-start(bf16[192,640]{1,0:T(8,128)(2,1)} %param.7), channel_id=1, source_target_pairs={{0,4},{2,6},{4,0},{6,2},{1,5},{3,7},{5,1},{7,3},{8,12},{10,14},{12... | collective-permute-start | bytes 737288 | tf_op jit(solution)/shard_map/ppermute | solution.py:269
  24.7 3.0 %collective-permute-start.8 = (bf16[192,640]{1,0:T(8,128)(2,1)}, bf16[192,640]{1,0:T(8,128)(2,1)S(1)}, u32[]{:S(2)}, u32[]{:S(2)}) collective-permute-start(bf16[192,640]{1,0:T(8,128)(2,1)} %param.7), channel_id=1, source_target_pairs={{0,6},{2,0},{4,2},{6,4},{1,7},{3,1},{5,3},{7,5},{8,14},{10,8},{12,... | collective-permute-start | bytes 737288 | tf_op jit(solution)/shard_map/ppermute | solution.py:269
  27.7 3.6 %all_gather.11 = bf16[160,768]{1,0:T(8,128)(2,1)S(1)} all-gather(bf16[80,768]{1,0:T(8,128)(2,1)} %param.11), channel_id=1, replica_groups=mesh['x'=4,'z'=8,'c'=2,'y'=4,'w'=2] {'c'}, dimensions={0}, use_global_device_ids=true | all-gather | bytes 368640 | tf_op jit(solution)/shard_map/all_gather | solution.py:239
  36.3 4.0 %collective-permute-start = (bf16[1,176,128]{2,1,0:T(8,128)(2,1)S(1)}, bf16[1,176,128]{2,1,0:T(8,128)(2,1)S(1)}, u32[]{:S(2)}, u32[]{:S(2)}) collective-permute-start(bf16[1,176,128]{2,1,0:T(8,128)(2,1)S(1)} %maximum_bitcast_fusion), channel_id=1, source_target_pairs={{0,64},{16,80},{32,96},{48,112},{64,0},{80,16},{96,32},{112,48},{1... | collective-permute-start | bytes 135176 | tf_op jit(solution)/shard_map/ppermute | solution.py:220
  41.1 3.9 %collective-permute-done = bf16[1,176,128]{2,1,0:T(8,128)(2,1)S(1)} collective-permute-done((bf16[1,176,128]{2,1,0:T(8,128)(2,1)S(1)}, bf16[1,176,128]{2,1,0:T(8,128)(2,1)S(1)}, u32[]{:S(2)}, u32[]{:S(2)}) %collective-permute-start) | collective-permute-done | bytes 45088 | tf_op jit(solution)/shard_map/ppermute | solution.py:220
  45.0 4.2 %collective-permute-start.18 = (bf16[1,160,256]{2,1,0:T(8,128)(2,1)S(1)}, bf16[1,160,256]{2,1,0:T(8,128)(2,1)S(1)}, u32[]{:S(2)}, u32[]{:S(2)}) collective-permute-start(bf16[1,160,256]{2,1,0:T(8,128)(2,1)S(1)} %dynamic-slice_bitcast_fusion.2), channel_id=1, source_target_pairs={{0,64},{16,80},{32,96},{48,112},{64,0},{80,16},{96,32},{112,48},{1... | collective-permute-start | bytes 245768 | tf_op jit(solution)/shard_map/ppermute | solution.py:220
  49.2 7.4 %collective-permute-done.18 = bf16[1,160,256]{2,1,0:T(8,128)(2,1)S(1)} collective-permute-done((bf16[1,160,256]{2,1,0:T(8,128)(2,1)S(1)}, bf16[1,160,256]{2,1,0:T(8,128)(2,1)S(1)}, u32[]{:S(2)}, u32[]{:S(2)}) %collective-permute-start.18) | collective-permute-done | bytes 81952 | tf_op jit(solution)/shard_map/ppermute | solution.py:220
  58.6 4.9 %collective-permute-done.1 = bf16[2,176,128]{2,1,0:T(8,128)(2,1)S(1)} collective-permute-done((bf16[2,176,128]{2,1,0:T(8,128)(2,1)S(1)}, bf16[2,176,128]{2,1,0:T(8,128)(2,1)S(1)}, u32[]{:S(2)}, u32[]{:S(2)}) %collective-permute-start.1) | collective-permute-done | bytes 90144 | tf_op jit(solution)/shard_map/ppermute | solution.py:220
  66.3 5.0 %collective-permute-done.19 = bf16[2,160,256]{2,1,0:T(8,128)(2,1)S(1)} collective-permute-done((bf16[2,160,256]{2,1,0:T(8,128)(2,1)S(1)}, bf16[2,160,256]{2,1,0:T(8,128)(2,1)S(1)}, u32[]{:S(2)}, u32[]{:S(2)}) %collective-permute-start.19) | collective-permute-done | bytes 163872 | tf_op jit(solution)/shard_map/ppermute | solution.py:220
  73.3 3.4 %collective-permute-start.20 = (bf16[4,160,256]{2,1,0:T(8,128)(2,1)S(1)}, bf16[4,160,256]{2,1,0:T(8,128)(2,1)S(1)}, u32[]{:S(2)}, u32[]{:S(2)}) collective-permute-start(bf16[4,160,256]{2,1,0:T(8,128)(2,1)S(1)} %pad_maximum_fusion.5), channel_id=1, source_target_pairs={{0,16},{16,0},{32,48},{48,32},{64,80},{80,64},{96,112},{112,96},{1... | collective-permute-start | bytes 983048 | tf_op jit(solution)/shard_map/ppermute | solution.py:220
  79.0 3.4 %collective-permute-start.11 = (bf16[192,640]{1,0:T(8,128)(2,1)S(1)}, bf16[192,640]{1,0:T(8,128)(2,1)S(1)}, u32[]{:S(2)}, u32[]{:S(2)}) collective-permute-start(bf16[192,640]{1,0:T(8,128)(2,1)S(1)} %collective-permute-done.9), channel_id=1, source_target_pairs={{0,4},{2,6},{4,0},{6,2},{1,5},{3,7},{5,1},{7,3},{8,12},{10,14},{12... | collective-permute-start | bytes 737288 | tf_op jit(solution)/shard_map/ppermute | solution.py:269
  82.4 2.8 %collective-permute-start.12 = (bf16[192,640]{1,0:T(8,128)(2,1)S(1)}, bf16[192,640]{1,0:T(8,128)(2,1)S(1)}, u32[]{:S(2)}, u32[]{:S(2)}) collective-permute-start(bf16[192,640]{1,0:T(8,128)(2,1)S(1)} %collective-permute-done.9), channel_id=1, source_target_pairs={{0,6},{2,0},{4,2},{6,4},{1,7},{3,1},{5,3},{7,5},{8,14},{10,8},{12,... | collective-permute-start | bytes 737288 | tf_op jit(solution)/shard_map/ppermute | solution.py:269
  86.4 4.4 %collective-permute-start.5 = (bf16[8,176,128]{2,1,0:T(8,128)(2,1)S(1)}, bf16[8,176,128]{2,1,0:T(8,128)(2,1)S(1)}, u32[]{:S(2)}, u32[]{:S(2)}) collective-permute-start(bf16[8,176,128]{2,1,0:T(8,128)(2,1)S(1)} %pad_maximum_fusion.4.refs_4_), channel_id=1, source_target_pairs={{0,384},{128,0},{256,128},{384,256},{1,385},{129,1},{257,129},{385... | collective-permute-start | bytes 1081352 | tf_op jit(solution)/shard_map/ppermute | solution.py:263
  90.8 9.2 %collective-permute-start.13 = (bf16[4,192,640]{2,1,0:T(8,128)(2,1)S(1)}, bf16[4,192,640]{2,1,0:T(8,128)(2,1)S(1)}, u32[]{:S(2)}, u32[]{:S(2)}) collective-permute-start(bf16[4,192,640]{2,1,0:T(8,128)(2,1)S(1)} %pad_maximum_fusion.refs_0_), channel_id=1, source_target_pairs={{0,8},{8,0},{1,9},{9,1},{2,10},{10,2},{3,11},{11,3},{4,12},{12,4},... | collective-permute-start | bytes 2949128 | tf_op jit(solution)/shard_map/ppermute | solution.py:273
  100.1 2.4 %collective-permute-start.4 = (bf16[8,176,128]{2,1,0:T(8,128)(2,1)S(1)}, bf16[8,176,128]{2,1,0:T(8,128)(2,1)S(1)}, u32[]{:S(2)}, u32[]{:S(2)}) collective-permute-start(bf16[8,176,128]{2,1,0:T(8,128)(2,1)S(1)} %pad_maximum_fusion.4.refs_4_), channel_id=1, source_target_pairs={{0,256},{128,384},{256,0},{384,128},{1,257},{129,385},{257,1},{385... | collective-permute-start | bytes 1081352 | tf_op jit(solution)/shard_map/ppermute | solution.py:263
  102.5 2.5 %collective-permute-start.3 = (bf16[8,176,128]{2,1,0:T(8,128)(2,1)S(1)}, bf16[8,176,128]{2,1,0:T(8,128)(2,1)S(1)}, u32[]{:S(2)}, u32[]{:S(2)}) collective-permute-start(bf16[8,176,128]{2,1,0:T(8,128)(2,1)S(1)} %pad_maximum_fusion.4.refs_4_), channel_id=1, source_target_pairs={{0,128},{128,256},{256,384},{384,0},{1,129},{129,257},{257,385},{3... | collective-permute-start | bytes 1081352 | tf_op jit(solution)/shard_map/ppermute | solution.py:263
  105.2 2.5 %collective-permute-start.14 = (bf16[4,192,640]{2,1,0:T(8,128)(2,1)S(1)}, bf16[4,192,640]{2,1,0:T(8,128)(2,1)S(1)}, u32[]{:S(2)}, u32[]{:S(2)}) collective-permute-start(bf16[4,192,640]{2,1,0:T(8,128)(2,1)S(1)} %pad_maximum_fusion.1.refs_1_), channel_id=1, source_target_pairs={{0,8},{8,0},{1,9},{9,1},{2,10},{10,2},{3,11},{11,3},{4,12},{12,4},... | collective-permute-start | bytes 2949128 | tf_op jit(solution)/shard_map/ppermute | solution.py:275
  107.8 3.4 %collective-permute-start.21 = (bf16[8,160,256]{2,1,0:T(8,128)(2,1)S(1)}, bf16[8,160,256]{2,1,0:T(8,128)(2,1)S(1)}, u32[]{:S(2)}, u32[]{:S(2)}) collective-permute-start(bf16[8,160,256]{2,1,0:T(8,128)(2,1)S(1)} %pad_maximum_fusion.2.refs_0_), channel_id=1, source_target_pairs={{0,128},{128,256},{256,384},{384,0},{1,129},{129,257},{257,385},{3... | collective-permute-start | bytes 1966088 | tf_op jit(solution)/shard_map/ppermute | solution.py:265
  116.0 5.6 %collective-permute-done.3.refs_5_ = bf16[8,176,128]{2,1,0:T(8,128)(2,1)S(1)} collective-permute-done((bf16[8,176,128]{2,1,0:T(8,128)(2,1)S(1)}, bf16[8,176,128]{2,1,0:T(8,128)(2,1)S(1)}, u32[]{:S(2)}, u32[]{:S(2)}) %collective-permute-start.3) | collective-permute-done | bytes 360480 | tf_op jit(solution)/shard_map/ppermute | solution.py:263
  125.6 6.2 %shard_map.94 = (bf16[384,5120]{1,0:T(8,128)(2,1)}, bf16[384,128]{1,0:T(8,128)(2,1)S(1)}) custom-call(s32[64]{0:T(128)S(1)} %broadcast_multiply_fusion.offsets, s32[5]{0:T(128)S(1)} %stack.130.where, f32[1,5120]{1,0:T(1,128)S(1)} %bitcast.64, f32[1,128]{1,0:T(1,128)S(1)} %bitcast.65, f32[384,128]{1,0:T(8,128)S(1)} %get-tuple-element.33.cosine, ...), custom_call_target="tpu_custom_call" | custom-call | flops 4000000000 | bytes 4194304 | tf_op jit(solution)/shard_map/pallas_call | solution.py:308
  131.8 4.0 %collective-permute-start.15 = (bf16[1,384,128]{2,1,0:T(8,128)(2,1)S(1)}, bf16[1,384,128]{2,1,0:T(8,128)(2,1)S(1)}, u32[]{:S(2)}, u32[]{:S(2)}) collective-permute-start(bf16[1,384,128]{2,1,0:T(8,128)(2,1)S(1)} %bitcast.58), channel_id=1, source_target_pairs={{0,64},{16,80},{32,96},{48,112},{64,0},{80,16},{96,32},{112,48},{1... | collective-permute-start | bytes 294920 | tf_op jit(solution)/shard_map/ppermute | solution.py:220
  136.0 11.5 %collective-permute-done.15 = bf16[1,384,128]{2,1,0:T(8,128)(2,1)S(1)} collective-permute-done((bf16[1,384,128]{2,1,0:T(8,128)(2,1)S(1)}, bf16[1,384,128]{2,1,0:T(8,128)(2,1)S(1)}, u32[]{:S(2)}, u32[]{:S(2)}) %collective-permute-start.15) | collective-permute-done | bytes 98336 | tf_op jit(solution)/shard_map/ppermute | solution.py:220
  149.5 9.8 %collective-permute-done.16 = bf16[2,384,128]{2,1,0:T(8,128)(2,1)S(1)} collective-permute-done((bf16[2,384,128]{2,1,0:T(8,128)(2,1)S(1)}, bf16[2,384,128]{2,1,0:T(8,128)(2,1)S(1)}, u32[]{:S(2)}, u32[]{:S(2)}) %collective-permute-start.16) | collective-permute-done | bytes 196640 | tf_op jit(solution)/shard_map/ppermute | solution.py:220
  161.3 3.9 %shard_map.95 = bf16[2,2,192,128]{3,2,1,0:T(8,128)(2,1)S(1)} custom-call(s32[64]{0:T(128)S(1)} %broadcast_multiply_fusion.offsets, s32[5]{0:T(128)S(1)} %stack.130.where, bf16[384,5120]{1,0:T(8,128)(2,1)} %get-tuple-element.12.normed, f32[1,128]{1,0:T(1,128)S(1)} %bitcast.66, f32[384,128]{1,0:T(8,128)S(1)} %get-tuple-element.33.cosine, ...), custom_call_target="tpu_custom_call" | custom-call | flops 4000000000 | bytes 4194304 | tf_op jit(solution)/shard_map/pallas_call | solution.py:322
  171.4 3.2 %collective-permute-start.28 = (bf16[4,384,128]{2,1,0:T(8,128)(2,1)S(1)}, bf16[4,384,128]{2,1,0:T(8,128)(2,1)S(1)}, u32[]{:S(2)}, u32[]{:S(2)}) collective-permute-start(bf16[4,384,128]{2,1,0:T(8,128)(2,1)S(1)} %collective-permute-done.27.mine1), channel_id=1, source_target_pairs={{0,8},{8,0},{1,9},{9,1},{2,10},{10,2},{3,11},{11,3},{4,12},{12,4},... | collective-permute-start | bytes 1179656 | tf_op jit(solution)/shard_map/ppermute | solution.py:334
  180.6 2.6 %collective-permute-done.25.near = bf16[768,128]{1,0:T(8,128)(2,1)S(1)} collective-permute-done((bf16[768,128]{1,0:T(8,128)(2,1)S(1)}, bf16[768,128]{1,0:T(8,128)(2,1)S(1)}, u32[]{:S(2)}, u32[]{:S(2)}) %collective-permute-start.25) | collective-permute-done | bytes 196640 | tf_op jit(solution)/shard_map/ppermute | solution.py:339
  183.2 3.1 %collective-permute-done.26.far = bf16[768,128]{1,0:T(8,128)(2,1)S(1)} collective-permute-done((bf16[768,128]{1,0:T(8,128)(2,1)S(1)}, bf16[768,128]{1,0:T(8,128)(2,1)S(1)}, u32[]{:S(2)}, u32[]{:S(2)}) %collective-permute-start.26) | collective-permute-done | bytes 196640 | tf_op jit(solution)/shard_map/ppermute | solution.py:340
  187.8 11.5 %collective-permute-start.29 = (bf16[816,128]{1,0:T(8,128)(2,1)S(1)}, bf16[816,128]{1,0:T(8,128)(2,1)S(1)}, u32[]{:S(2)}, u32[]{:S(2)}) collective-permute-start(bf16[816,128]{1,0:T(8,128)(2,1)S(1)} %get-tuple-element.17), channel_id=1, source_target_pairs={{0,128},{128,256},{256,384},{1,129},{129,257},{257,385},{2,130},{1... | collective-permute-start | bytes 626696 | tf_op jit(solution)/shard_map/ppermute | solution.py:362
  201.3 2.6 %shard_map.97 = (f32[768,128]{1,0:T(8,128)S(1)}, f32[768,1]{1,0:T(8,128)S(1)}) custom-call(s32[9]{0:T(128)S(1)} %stack.162.where, s32[3,192,1]{2,1,0:T(8,128)S(1)} %broadcast_subtract_fusion.begins, bf16[768,128]{1,0:T(8,128)(2,1)S(1)} %bitcast.63, bf16[3072,128]{1,0:T(8,128)(2,1)S(1)} %get-tuple-element.13.keys, bf16[3072,128]{1,0:T(8,128)(2,1)S(1)} %get-tuple-element.14.values), custom_call_target="tpu_custom_call" | custom-call | flops 10000000000 | bytes 4194304 | tf_op jit(solution)/shard_map/pallas_call | solution.py:364
  203.9 3.0 %collective-permute-done.30.r2 = bf16[816,128]{1,0:T(8,128)(2,1)S(1)} collective-permute-done((bf16[816,128]{1,0:T(8,128)(2,1)S(1)}, bf16[816,128]{1,0:T(8,128)(2,1)S(1)}, u32[]{:S(2)}, u32[]{:S(2)}) %collective-permute-start.30) | collective-permute-done | bytes 208928 | tf_op jit(solution)/shard_map/ppermute | solution.py:363
  (109 shorter events, 44.0 us)
Async XLA Ops:
  0.6 72.7 %collective-permute-start.9 = (bf16[192,640]{1,0:T(8,128)(2,1)}, bf16[192,640]{1,0:T(8,128)(2,1)S(1)}, u32[]{:S(2)}, u32[]{:S(2)}) collective-permute-start(bf16[192,640]{1,0:T(8,128)(2,1)} %param.7), channel_id=1, source_target_pairs={{0,1},{1,0},{2,3},{3,2},{4,5},{5,4},{6,7},{7,6},{8,9},{9,8},{10,11... | collective-permute-start | bytes 737288 | tf_op jit(solution)/shard_map/ppermute | solution.py:237
  16.9 59.8 %collective-permute-start.6 = (bf16[192,640]{1,0:T(8,128)(2,1)}, bf16[192,640]{1,0:T(8,128)(2,1)S(1)}, u32[]{:S(2)}, u32[]{:S(2)}) collective-permute-start(bf16[192,640]{1,0:T(8,128)(2,1)} %param.7), channel_id=1, source_target_pairs={{0,2},{2,4},{4,6},{6,0},{1,3},{3,5},{5,7},{7,1},{8,10},{10,12},{12... | collective-permute-start | bytes 737288 | tf_op jit(solution)/shard_map/ppermute | solution.py:269
  20.1 58.9 %collective-permute-start.7 = (bf16[192,640]{1,0:T(8,128)(2,1)}, bf16[192,640]{1,0:T(8,128)(2,1)S(1)}, u32[]{:S(2)}, u32[]{:S(2)}) collective-permute-start(bf16[192,640]{1,0:T(8,128)(2,1)} %param.7), channel_id=1, source_target_pairs={{0,4},{2,6},{4,0},{6,2},{1,5},{3,7},{5,1},{7,3},{8,12},{10,14},{12... | collective-permute-start | bytes 737288 | tf_op jit(solution)/shard_map/ppermute | solution.py:269
  24.7 57.8 %collective-permute-start.8 = (bf16[192,640]{1,0:T(8,128)(2,1)}, bf16[192,640]{1,0:T(8,128)(2,1)S(1)}, u32[]{:S(2)}, u32[]{:S(2)}) collective-permute-start(bf16[192,640]{1,0:T(8,128)(2,1)} %param.7), channel_id=1, source_target_pairs={{0,6},{2,0},{4,2},{6,4},{1,7},{3,1},{5,3},{7,5},{8,14},{10,8},{12,... | collective-permute-start | bytes 737288 | tf_op jit(solution)/shard_map/ppermute | solution.py:269
  36.3 8.7 %collective-permute-start = (bf16[1,176,128]{2,1,0:T(8,128)(2,1)S(1)}, bf16[1,176,128]{2,1,0:T(8,128)(2,1)S(1)}, u32[]{:S(2)}, u32[]{:S(2)}) collective-permute-start(bf16[1,176,128]{2,1,0:T(8,128)(2,1)S(1)} %maximum_bitcast_fusion), channel_id=1, source_target_pairs={{0,64},{16,80},{32,96},{48,112},{64,0},{80,16},{96,32},{112,48},{1... | collective-permute-start | bytes 135176 | tf_op jit(solution)/shard_map/ppermute | solution.py:220
  45.0 11.7 %collective-permute-start.18 = (bf16[1,160,256]{2,1,0:T(8,128)(2,1)S(1)}, bf16[1,160,256]{2,1,0:T(8,128)(2,1)S(1)}, u32[]{:S(2)}, u32[]{:S(2)}) collective-permute-start(bf16[1,160,256]{2,1,0:T(8,128)(2,1)S(1)} %dynamic-slice_bitcast_fusion.2), channel_id=1, source_target_pairs={{0,64},{16,80},{32,96},{48,112},{64,0},{80,16},{96,32},{112,48},{1... | collective-permute-start | bytes 245768 | tf_op jit(solution)/shard_map/ppermute | solution.py:220
  56.7 6.8 %collective-permute-start.1 = (bf16[2,176,128]{2,1,0:T(8,128)(2,1)S(1)}, bf16[2,176,128]{2,1,0:T(8,128)(2,1)S(1)}, u32[]{:S(2)}, u32[]{:S(2)}) collective-permute-start(bf16[2,176,128]{2,1,0:T(8,128)(2,1)S(1)} %pad_maximum_fusion.12), channel_id=1, source_target_pairs={{0,32},{16,48},{32,0},{48,16},{64,96},{80,112},{96,64},{112,80},{1... | collective-permute-start | bytes 270344 | tf_op jit(solution)/shard_map/ppermute | solution.py:220
  63.5 7.8 %collective-permute-start.19 = (bf16[2,160,256]{2,1,0:T(8,128)(2,1)S(1)}, bf16[2,160,256]{2,1,0:T(8,128)(2,1)S(1)}, u32[]{:S(2)}, u32[]{:S(2)}) collective-permute-start(bf16[2,160,256]{2,1,0:T(8,128)(2,1)S(1)} %pad_maximum_fusion.11), channel_id=1, source_target_pairs={{0,32},{16,48},{32,0},{48,16},{64,96},{80,112},{96,64},{112,80},{1... | collective-permute-start | bytes 491528 | tf_op jit(solution)/shard_map/ppermute | solution.py:220
  71.3 15.0 %collective-permute-start.2 = (bf16[4,176,128]{2,1,0:T(8,128)(2,1)S(1)}, bf16[4,176,128]{2,1,0:T(8,128)(2,1)S(1)}, u32[]{:S(2)}, u32[]{:S(2)}) collective-permute-start(bf16[4,176,128]{2,1,0:T(8,128)(2,1)S(1)} %pad_maximum_fusion.10), channel_id=1, source_target_pairs={{0,16},{16,0},{32,48},{48,32},{64,80},{80,64},{96,112},{112,96},{1... | collective-permute-start | bytes 540680 | tf_op jit(solution)/shard_map/ppermute | solution.py:220
  73.3 52.3 %copy-start = (f32[128]{0:T(128)S(1)}, f32[128]{0:T(128)}, u32[]{:S(2)}) copy-start(f32[128]{0:T(128)} %param.10) | copy-start | bytes 1540
  73.3 31.9 %collective-permute-start.20 = (bf16[4,160,256]{2,1,0:T(8,128)(2,1)S(1)}, bf16[4,160,256]{2,1,0:T(8,128)(2,1)S(1)}, u32[]{:S(2)}, u32[]{:S(2)}) collective-permute-start(bf16[4,160,256]{2,1,0:T(8,128)(2,1)S(1)} %pad_maximum_fusion.5), channel_id=1, source_target_pairs={{0,16},{16,0},{32,48},{48,32},{64,80},{80,64},{96,112},{112,96},{1... | collective-permute-start | bytes 983048 | tf_op jit(solution)/shard_map/ppermute | solution.py:220
  76.7 14.1 %collective-permute-start.10 = (bf16[192,640]{1,0:T(8,128)(2,1)S(1)}, bf16[192,640]{1,0:T(8,128)(2,1)S(1)}, u32[]{:S(2)}, u32[]{:S(2)}) collective-permute-start(bf16[192,640]{1,0:T(8,128)(2,1)S(1)} %collective-permute-done.9), channel_id=1, source_target_pairs={{0,2},{2,4},{4,6},{6,0},{1,3},{3,5},{5,7},{7,1},{8,10},{10,12},{12... | collective-permute-start | bytes 737288 | tf_op jit(solution)/shard_map/ppermute | solution.py:269
  79.0 21.1 %collective-permute-start.11 = (bf16[192,640]{1,0:T(8,128)(2,1)S(1)}, bf16[192,640]{1,0:T(8,128)(2,1)S(1)}, u32[]{:S(2)}, u32[]{:S(2)}) collective-permute-start(bf16[192,640]{1,0:T(8,128)(2,1)S(1)} %collective-permute-done.9), channel_id=1, source_target_pairs={{0,4},{2,6},{4,0},{6,2},{1,5},{3,7},{5,1},{7,3},{8,12},{10,14},{12... | collective-permute-start | bytes 737288 | tf_op jit(solution)/shard_map/ppermute | solution.py:269
  82.4 20.1 %collective-permute-start.12 = (bf16[192,640]{1,0:T(8,128)(2,1)S(1)}, bf16[192,640]{1,0:T(8,128)(2,1)S(1)}, u32[]{:S(2)}, u32[]{:S(2)}) collective-permute-start(bf16[192,640]{1,0:T(8,128)(2,1)S(1)} %collective-permute-done.9), channel_id=1, source_target_pairs={{0,6},{2,0},{4,2},{6,4},{1,7},{3,1},{5,3},{7,5},{8,14},{10,8},{12,... | collective-permute-start | bytes 737288 | tf_op jit(solution)/shard_map/ppermute | solution.py:269
  86.4 21.4 %collective-permute-start.5 = (bf16[8,176,128]{2,1,0:T(8,128)(2,1)S(1)}, bf16[8,176,128]{2,1,0:T(8,128)(2,1)S(1)}, u32[]{:S(2)}, u32[]{:S(2)}) collective-permute-start(bf16[8,176,128]{2,1,0:T(8,128)(2,1)S(1)} %pad_maximum_fusion.4.refs_4_), channel_id=1, source_target_pairs={{0,384},{128,0},{256,128},{384,256},{1,385},{129,1},{257,129},{385... | collective-permute-start | bytes 1081352 | tf_op jit(solution)/shard_map/ppermute | solution.py:263
  90.8 34.7 %collective-permute-start.13 = (bf16[4,192,640]{2,1,0:T(8,128)(2,1)S(1)}, bf16[4,192,640]{2,1,0:T(8,128)(2,1)S(1)}, u32[]{:S(2)}, u32[]{:S(2)}) collective-permute-start(bf16[4,192,640]{2,1,0:T(8,128)(2,1)S(1)} %pad_maximum_fusion.refs_0_), channel_id=1, source_target_pairs={{0,8},{8,0},{1,9},{9,1},{2,10},{10,2},{3,11},{11,3},{4,12},{12,4},... | collective-permute-start | bytes 2949128 | tf_op jit(solution)/shard_map/ppermute | solution.py:273
  100.1 13.5 %collective-permute-start.4 = (bf16[8,176,128]{2,1,0:T(8,128)(2,1)S(1)}, bf16[8,176,128]{2,1,0:T(8,128)(2,1)S(1)}, u32[]{:S(2)}, u32[]{:S(2)}) collective-permute-start(bf16[8,176,128]{2,1,0:T(8,128)(2,1)S(1)} %pad_maximum_fusion.4.refs_4_), channel_id=1, source_target_pairs={{0,256},{128,384},{256,0},{384,128},{1,257},{129,385},{257,1},{385... | collective-permute-start | bytes 1081352 | tf_op jit(solution)/shard_map/ppermute | solution.py:263
  102.5 19.0 %collective-permute-start.3 = (bf16[8,176,128]{2,1,0:T(8,128)(2,1)S(1)}, bf16[8,176,128]{2,1,0:T(8,128)(2,1)S(1)}, u32[]{:S(2)}, u32[]{:S(2)}) collective-permute-start(bf16[8,176,128]{2,1,0:T(8,128)(2,1)S(1)} %pad_maximum_fusion.4.refs_4_), channel_id=1, source_target_pairs={{0,128},{128,256},{256,384},{384,0},{1,129},{129,257},{257,385},{3... | collective-permute-start | bytes 1081352 | tf_op jit(solution)/shard_map/ppermute | solution.py:263
  105.2 20.3 %collective-permute-start.14 = (bf16[4,192,640]{2,1,0:T(8,128)(2,1)S(1)}, bf16[4,192,640]{2,1,0:T(8,128)(2,1)S(1)}, u32[]{:S(2)}, u32[]{:S(2)}) collective-permute-start(bf16[4,192,640]{2,1,0:T(8,128)(2,1)S(1)} %pad_maximum_fusion.1.refs_1_), channel_id=1, source_target_pairs={{0,8},{8,0},{1,9},{9,1},{2,10},{10,2},{3,11},{11,3},{4,12},{12,4},... | collective-permute-start | bytes 2949128 | tf_op jit(solution)/shard_map/ppermute | solution.py:275
  107.8 53.5 %collective-permute-start.21 = (bf16[8,160,256]{2,1,0:T(8,128)(2,1)S(1)}, bf16[8,160,256]{2,1,0:T(8,128)(2,1)S(1)}, u32[]{:S(2)}, u32[]{:S(2)}) collective-permute-start(bf16[8,160,256]{2,1,0:T(8,128)(2,1)S(1)} %pad_maximum_fusion.2.refs_0_), channel_id=1, source_target_pairs={{0,128},{128,256},{256,384},{384,0},{1,129},{129,257},{257,385},{3... | collective-permute-start | bytes 1966088 | tf_op jit(solution)/shard_map/ppermute | solution.py:265
  113.6 47.7 %collective-permute-start.22 = (bf16[8,160,256]{2,1,0:T(8,128)(2,1)S(1)}, bf16[8,160,256]{2,1,0:T(8,128)(2,1)S(1)}, u32[]{:S(2)}, u32[]{:S(2)}) collective-permute-start(bf16[8,160,256]{2,1,0:T(8,128)(2,1)S(1)} %pad_maximum_fusion.2.refs_0_), channel_id=1, source_target_pairs={{0,256},{128,384},{256,0},{384,128},{1,257},{129,385},{257,1},{385... | collective-permute-start | bytes 1966088 | tf_op jit(solution)/shard_map/ppermute | solution.py:265
  121.6 39.7 %collective-permute-start.23 = (bf16[8,160,256]{2,1,0:T(8,128)(2,1)S(1)}, bf16[8,160,256]{2,1,0:T(8,128)(2,1)}, u32[]{:S(2)}, u32[]{:S(2)}) collective-permute-start(bf16[8,160,256]{2,1,0:T(8,128)(2,1)S(1)} %pad_maximum_fusion.2.refs_0_), channel_id=1, source_target_pairs={{0,384},{128,0},{256,128},{384,256},{1,385},{129,1},{257,129},{385... | collective-permute-start | bytes 1966088 | tf_op jit(solution)/shard_map/ppermute | solution.py:265
  131.8 15.7 %collective-permute-start.15 = (bf16[1,384,128]{2,1,0:T(8,128)(2,1)S(1)}, bf16[1,384,128]{2,1,0:T(8,128)(2,1)S(1)}, u32[]{:S(2)}, u32[]{:S(2)}) collective-permute-start(bf16[1,384,128]{2,1,0:T(8,128)(2,1)S(1)} %bitcast.58), channel_id=1, source_target_pairs={{0,64},{16,80},{32,96},{48,112},{64,0},{80,16},{96,32},{112,48},{1... | collective-permute-start | bytes 294920 | tf_op jit(solution)/shard_map/ppermute | solution.py:220
  147.5 11.8 %collective-permute-start.16 = (bf16[2,384,128]{2,1,0:T(8,128)(2,1)S(1)}, bf16[2,384,128]{2,1,0:T(8,128)(2,1)S(1)}, u32[]{:S(2)}, u32[]{:S(2)}) collective-permute-start(bf16[2,384,128]{2,1,0:T(8,128)(2,1)S(1)} %pad_maximum_fusion.8), channel_id=1, source_target_pairs={{0,32},{16,48},{32,0},{48,16},{64,96},{80,112},{96,64},{112,80},{1... | collective-permute-start | bytes 589832 | tf_op jit(solution)/shard_map/ppermute | solution.py:220
  159.3 12.1 %collective-permute-start.27 = (bf16[4,384,128]{2,1,0:T(8,128)(2,1)S(1)}, bf16[4,384,128]{2,1,0:T(8,128)(2,1)S(1)}, u32[]{:S(2)}, u32[]{:S(2)}) collective-permute-start(bf16[4,384,128]{2,1,0:T(8,128)(2,1)S(1)} %pad_maximum_fusion.3.mine0), channel_id=1, source_target_pairs={{0,16},{16,0},{32,48},{48,32},{64,80},{80,64},{96,112},{112,96},{1... | collective-permute-start | bytes 1179656 | tf_op jit(solution)/shard_map/ppermute | solution.py:220
  165.2 14.7 %collective-permute-start.17 = (bf16[4,384,128]{2,1,0:T(8,128)(2,1)S(1)}, bf16[4,384,128]{2,1,0:T(8,128)(2,1)S(1)}, u32[]{:S(2)}, u32[]{:S(2)}) collective-permute-start(bf16[4,384,128]{2,1,0:T(8,128)(2,1)S(1)} %pad_maximum_fusion.3.mine0), channel_id=1, source_target_pairs={{0,8},{8,0},{1,9},{9,1},{2,10},{10,2},{3,11},{11,3},{4,12},{12,4},... | collective-permute-start | bytes 1179656 | tf_op jit(solution)/shard_map/ppermute | solution.py:333
  167.7 7.0 %collective-permute-start.24 = (bf16[2,192,128]{2,1,0:T(8,128)(2,1)S(1)}, bf16[2,192,128]{2,1,0:T(8,128)(2,1)S(1)}, u32[]{:S(2)}, u32[]{:S(2)}) collective-permute-start(bf16[2,192,128]{2,1,0:T(8,128)(2,1)S(1)} %get-tuple-element.22), channel_id=1, source_target_pairs={{0,8},{8,0},{1,9},{9,1},{2,10},{10,2},{3,11},{11,3},{4,12},{12,4},... | collective-permute-start | bytes 294920 | tf_op jit(solution)/shard_map/ppermute | solution.py:337
  171.4 14.8 %collective-permute-start.28 = (bf16[4,384,128]{2,1,0:T(8,128)(2,1)S(1)}, bf16[4,384,128]{2,1,0:T(8,128)(2,1)S(1)}, u32[]{:S(2)}, u32[]{:S(2)}) collective-permute-start(bf16[4,384,128]{2,1,0:T(8,128)(2,1)S(1)} %collective-permute-done.27.mine1), channel_id=1, source_target_pairs={{0,8},{8,0},{1,9},{9,1},{2,10},{10,2},{3,11},{11,3},{4,12},{12,4},... | collective-permute-start | bytes 1179656 | tf_op jit(solution)/shard_map/ppermute | solution.py:334
  174.7 8.4 %collective-permute-start.25 = (bf16[768,128]{1,0:T(8,128)(2,1)S(1)}, bf16[768,128]{1,0:T(8,128)(2,1)S(1)}, u32[]{:S(2)}, u32[]{:S(2)}) collective-permute-start(bf16[768,128]{1,0:T(8,128)(2,1)S(1)} %bitcast.61), channel_id=1, source_target_pairs={{128,0},{256,128},{384,256},{129,1},{257,129},{385,257},{130,2},{2... | collective-permute-start | bytes 589832 | tf_op jit(solution)/shard_map/ppermute | solution.py:339
  176.0 10.2 %collective-permute-start.26 = (bf16[768,128]{1,0:T(8,128)(2,1)S(1)}, bf16[768,128]{1,0:T(8,128)(2,1)S(1)}, u32[]{:S(2)}, u32[]{:S(2)}) collective-permute-start(bf16[768,128]{1,0:T(8,128)(2,1)S(1)} %bitcast.62), channel_id=1, source_target_pairs={{256,0},{384,128},{257,1},{385,129},{258,2},{386,130},{259,3},{387... | collective-permute-start | bytes 589832 | tf_op jit(solution)/shard_map/ppermute | solution.py:340
  187.8 16.1 %collective-permute-start.29 = (bf16[816,128]{1,0:T(8,128)(2,1)S(1)}, bf16[816,128]{1,0:T(8,128)(2,1)S(1)}, u32[]{:S(2)}, u32[]{:S(2)}) collective-permute-start(bf16[816,128]{1,0:T(8,128)(2,1)S(1)} %get-tuple-element.17), channel_id=1, source_target_pairs={{0,128},{128,256},{256,384},{1,129},{129,257},{257,385},{2,130},{1... | collective-permute-start | bytes 626696 | tf_op jit(solution)/shard_map/ppermute | solution.py:362
  199.3 7.7 %collective-permute-start.30 = (bf16[816,128]{1,0:T(8,128)(2,1)S(1)}, bf16[816,128]{1,0:T(8,128)(2,1)S(1)}, u32[]{:S(2)}, u32[]{:S(2)}) collective-permute-start(bf16[816,128]{1,0:T(8,128)(2,1)S(1)} %get-tuple-element.18), channel_id=1, source_target_pairs={{0,256},{128,384},{1,257},{129,385},{2,258},{130,386},{3,259},{131... | collective-permute-start | bytes 626696 | tf_op jit(solution)/shard_map/ppermute | solution.py:363
  (7 other events, 109.5 us)

commit v3 on v2

--- a/solution.py
+++ b/solution.py
@@ -13,7 +13,7 @@
 rope_base = 1000000.0
 NEG = -1e30
 MASKED = -3e38
-KEY_BLOCK = 512
+KEY_BLOCK = 1024
 NO_SEGMENT = 100.0
 VMEM_LIMIT = 48 * 1024 * 1024
 
@@ -33,7 +33,7 @@
     )
 
 
-PEER = (0, 4, 2, 6, 1, 5, 3, 7)
+PEER = (0, 4, 1, 5, 2, 6, 3, 7)
 
 
 def head_norm_rope(v, gain, cosine, sine):
@@ -101,60 +101,78 @@
     return lax.broadcasted_iota(jnp.int32, shape, 0) == lax.broadcasted_iota(jnp.int32, shape, 1)
 
 
-def attend(query, keys, values, begin, index, low, high, acc, top, total):
+def attend(query, keys, values, begin, index, low, high, clear, acc, top):
     rows = begin.shape[0]
     scale = math.log2(math.e) / math.sqrt(128)
     acc[...] = jnp.zeros_like(acc)
     top[...] = jnp.full(top.shape, NEG, jnp.float32)
-    total[...] = jnp.zeros_like(total)
-
-    def step(b, carry):
-        base = pl.multiple_of(b * KEY_BLOCK, KEY_BLOCK)
+
+    def block(base, masked):
         key = keys[pl.ds(base, KEY_BLOCK), :]
         value = values[pl.ds(base, KEY_BLOCK), :]
-        col = base + lax.broadcasted_iota(jnp.int32, (rows, KEY_BLOCK), 1)
-        allowed = col >= begin
-        if index is not None:
-            allowed = allowed & (col <= index)
+        if masked:
+            col = base + lax.broadcasted_iota(jnp.int32, (rows, KEY_BLOCK), 1)
+            allowed = col >= begin
+            if index is not None:
+                allowed = allowed & (col <= index)
         for h in range(query.shape[0] // rows):
             span = pl.ds(h * rows, rows)
             raw = lax.dot_general(
                 query[span, :], key, (((1,), (1,)), ((), ())), preferred_element_type=jnp.float32
             )
-            raw = jnp.where(allowed, raw * scale, MASKED)
+            if masked:
+                raw = jnp.where(allowed, raw, MASKED)
             old = top[span, :]
             new = jnp.maximum(old, jnp.max(raw, axis=-1, keepdims=True))
-            terms = jnp.exp2(raw - new)
-            decay = jnp.exp2(old - new)
+            terms = jnp.exp2(raw * scale - new * scale)
+            decay = jnp.exp2((old - new) * scale)
             top[span, :] = new
-            total[span, :] = total[span, :] * decay + jnp.sum(terms, axis=-1, keepdims=True)
             acc[span, :] = acc[span, :] * decay + jnp.dot(
                 terms.astype(jnp.bfloat16), value, preferred_element_type=jnp.float32
             )
+
+    def step(b, carry):
+        base = pl.multiple_of(b * KEY_BLOCK, KEY_BLOCK)
+        plain = base >= clear
+        if index is not None:
+            plain = plain & (base + KEY_BLOCK <= high - rows)
+
+        @pl.when(plain)
+        def _():
+            block(base, False)
+
+        @pl.when(jnp.logical_not(plain))
+        def _():
+            block(base, True)
+
         return carry
 
     lax.fori_loop(low // KEY_BLOCK, (high + KEY_BLOCK - 1) // KEY_BLOCK, step, 0)
-    summed = total[...]
+    summed = acc[:, 128:]
     safe = jnp.where(summed > 0, summed, 1.0)
-    return acc[...] / safe, jnp.where(summed > 0, top[...] + jnp.log2(safe), NEG)
-
-
-def remote_kernel(where, begins, near, far, mine0, mine1, other0, other1, out1, out2, keys, values, acc, top, total):
-    block = mine0.shape[1]
-    for core, (first, second) in enumerate((((mine0, mine1), (other0, other1)), ((other0, other1), (mine0, mine1)))):
+    one = safe[:, 0:1]
+    return acc[:, :128] / safe, jnp.where(one > 0, top[...] * scale + jnp.log2(one), NEG)
+
+
+def remote_kernel(where, begins, near, far, *refs):
+    mine, other = refs[:4], refs[4:8]
+    out1, out2, keys, values, acc, top = refs[8:]
+    block = mine[0].shape[1]
+    values[:, 128:] = jnp.ones((values.shape[0], 128), values.dtype)
+    for core, (first, second) in enumerate(((mine, other), (other, mine))):
 
         @pl.when(where[0] == core)
         def _(first=first, second=second):
             for k in range(8):
                 spot = pl.ds(pl.multiple_of((where[1] ^ PEER[k]) * block, block), block)
-                keys[spot, :] = first[k // 4][k % 4]
-                values[spot, :] = second[k // 4][k % 4]
+                keys[spot, :] = first[k // 2][k % 2]
+                values[spot, :128] = second[k // 2][k % 2]
 
     eye = identity_mask()
     size = near.shape[0]
     for s, query, out in ((1, near, out1), (2, far, out2)):
-        low, high = where[2 + 2 * s], where[3 + 2 * s]
-        result, log = attend(query, keys, values, begins[s], None, low, high, acc, top, total)
+        limits = [where[3 + 3 * s + i] for i in range(3)]
+        result, log = attend(query, keys, values, begins[s], None, *limits, acc, top)
         out[0:size, :] = result.astype(jnp.bfloat16)
         rest = jnp.concatenate(
             [
@@ -170,12 +188,11 @@
             rest = rest - piece.astype(jnp.float32)
 
 
-def own_kernel(where, begins, query, keys, values, out, log, acc, top, total):
+def own_kernel(where, begins, query, keys, values, out, log, acc, top):
     rows = begins.shape[1]
-    index = where[8] + lax.broadcasted_iota(jnp.int32, (rows, 1), 0)
-    result, level = attend(
-        query, keys, values, begins[0], index, where[2], where[3], acc, top, total
-    )
+    index = where[2] + lax.broadcasted_iota(jnp.int32, (rows, 1), 0)
+    limits = [where[3 + i] for i in range(3)]
+    result, level = attend(query, keys, values, begins[0], index, *limits, acc, top)
     out[...] = result
     log[...] = level
 
@@ -237,7 +254,10 @@
     far_half = lax.ppermute(hidden, "w", swap)
 
     both = lax.all_gather(weight_store, "c", axis=0, tiled=True)
-    pair_docs = lax.all_gather(documents, "c", axis=0)
+    twin_docs = lax.ppermute(documents, "c", swap)
+    pair_docs = jnp.where(
+        c == 0, jnp.stack([documents, twin_docs]), jnp.stack([twin_docs, documents])
+    )
     riders = jnp.pad(
         pair_docs.astype(bf16), ((0, 0), (0, 256 - rows)), constant_values=NO_SEGMENT
     ).reshape(4, 128)
@@ -251,15 +271,13 @@
     )
     query_cols = lax.dynamic_slice_in_dim(both, 256 * c, 256, 1)
 
-    def spread_z(v, bits):
-        for bit in bits:
-            v = jnp.concatenate([v, across(v, bit)], axis=0)
-        return v
-
-    pair_two = spread_z(pair_cols[None], (4, 2))
-    query_one = spread_z(query_cols[None], (4,))
-    pair_line = spread_z(pair_two, (1,))
-    query_line = spread_z(query_one, (2, 1))
+    def spread_z(half):
+        return jnp.concatenate([half] + [across(half, bit) for bit in (1, 2, 3)], axis=0)
+
+    pair_half = jnp.stack([pair_cols, across(pair_cols, 4)])
+    pair_line = spread_z(pair_half)
+    query_cols = after(query_cols, pair_half)
+    query_line = spread_z(jnp.stack([query_cols, across(query_cols, 4)]))
     pair_blocks = [pair_line] + [lax.ppermute(pair_line, "x", ring(nx, s)) for s in (1, 3, 2)]
     pair_blocks = [pair_blocks[i] for i in (0, 1, 3, 2)]
     query_blocks = [query_line] + [lax.ppermute(query_line, "x", ring(nx, s)) for s in (1, 3, 2)]
@@ -328,10 +346,9 @@
         4 * 10**9,
     )(offsets, spot, normed, query_gain[None, :], cosine, sine, *query_blocks)
 
-    mine0 = spread_z(pair[None], (4, 2))
-    mine1 = across(mine0, 1)
-    other0 = lax.ppermute(mine0, "c", swap)
-    other1 = lax.ppermute(mine1, "c", swap)
+    half = jnp.stack([pair, across(pair, 4)])
+    mine = [half] + [across(half, bit) for bit in (1, 2, 3)]
+    other = [lax.ppermute(v, "c", swap) for v in mine]
     own_query = lax.dynamic_index_in_dim(query, c, 0, keepdims=False)
     sent_query = lax.dynamic_index_in_dim(query, 1 - c, 0, keepdims=False)
     q0 = jnp.concatenate([own_query, lax.ppermute(sent_query, "c", swap)], axis=0)
@@ -342,23 +359,18 @@
     inside = z * 2 * rows + c * rows
     low = [jnp.clip(spread[s, 0], 0, plane) for s in range(3)]
     high = [inside + rows] + [jnp.where(x + s < nx, plane, 0) for s in (1, 2)]
-    ranges = jnp.stack(
-        [c, z, low[0], high[0], low[1], high[1], low[2], high[2], inside]
-    ).astype(jnp.int32)
-    state = [
-        pltpu.VMEM((4 * rows, 128), f32),
-        pltpu.VMEM((4 * rows, 1), f32),
-        pltpu.VMEM((4 * rows, 1), f32),
-    ]
+    limits = [v for s in range(3) for v in (low[s], high[s], spread[s, rows - 1])]
+    ranges = jnp.stack([c, z, inside] + limits).astype(jnp.int32)
+    state = [pltpu.VMEM((4 * rows, 256), f32), pltpu.VMEM((4 * rows, 1), f32)]
     r1, r2, keys, values = call(
         remote_kernel,
         [jax.ShapeDtypeStruct((4 * rows + 48, 128), bf16)] * 2
-        + [jax.ShapeDtypeStruct((plane, 128), bf16)] * 2,
+        + [jax.ShapeDtypeStruct((plane, 128 * k), bf16) for k in (1, 2)],
         1,
-        7,
+        11,
         state,
         10**10,
-    )(ranges, spread[:, :, None], q1, q2, mine0, mine1, other0, other1)
+    )(ranges, spread[:, :, None], q1, q2, *mine, *other)
     r1 = lax.ppermute(r1, "x", [(i, i + 1) for i in range(nx - 1)])
     r2 = lax.ppermute(r2, "x", [(i, i + 2) for i in range(nx - 2)])
     o0, l0 = call(
@@ -378,7 +390,7 @@
     )
 
     own_part = lax.dynamic_slice_in_dim(pair, c * rows, rows, 0)
-    other_part = lax.dynamic_slice_in_dim(other0[0], c * rows, rows, 0)
+    other_part = lax.dynamic_slice_in_dim(other[0][0], c * rows, rows, 0)
     keys_fresh = jnp.where(c == 0, own_part, other_part)
     values_fresh = jnp.where(c == 0, other_part, own_part)
     return keys_fresh, values_fresh, context

time: 212 us -> 224 us (1.057)
  starting transfers between devices: 113 us -> 132 us
  waiting for transfers between devices: 60.9 us -> 49.5 us
  local copies, waits for them, and re-layouts: 3.42 us -> 7.99 us
  blocking collectives: 5.46 us -> 2.18 us
    ppermute x9 -> x12, starting transfers between devices: 25.2 us -> 34.4 us  [across(): return lax.ppermute(v, 'z', [(i, i ^ bit) for i in range(8)])]
    ppermute x2 -> x5, starting transfers between devices: 5.62 us -> 14 us  [the longest x4 10.3 us: body(): other = [lax.ppermute(v, 'c', swap) for v in mine]]
    ppermute x3, waiting for transfers between devices: 7.88 us -> 0.01 us  [body(): lax.ppermute(pair_line, 'x', ring(nx, s))]
    ppermute x1, starting transfers between devices: 11.5 us -> 5.97 us  [body(): r1 = lax.ppermute(r1, 'x', [(i, i + 1) for i in range(nx - 1)])]
    ppermute x1, starting transfers between devices: 2.06 us -> 5.49 us  [body(): r2 = lax.ppermute(r2, 'x', [(i, i + 2) for i in range(nx - 2)])]
    ppermute x1, starting transfers between devices: 1.93 us -> 5.28 us  [body(): lax.ppermute(sent_query, 'c', swap)]
    ppermute x1, waiting for transfers between devices: 3.08 us -> 0.01 us  [body(): q2 = lax.ppermute(q0, 'x', [(i, i - 2) for i in range(2, nx)])]
    ppermute x1, starting transfers between devices: 9.23 us -> 6.31 us  [body(): other_near = lax.ppermute(own_near, 'c', swap)]
  transfers between devices with their start and end apart: 31 -> 37, of which waited for: 12 -> 10; matrix products, arithmetic and copies ran while one was open for 4% -> 5% of each run, Pallas kernels for 6% -> 6%
where the time goes in v3:
time: 224 us; the launch traced here: 221 us
  starting transfers between devices  132 us (59%)
  waiting for transfers between devices  49.5 us (22%)
  Pallas kernels  17.6 us (8%)
  local copies, waits for them, and re-layouts  7.99 us (4%)
  other arithmetic  7.39 us (3%)
  between operations  3.33 us (1%)
    ppermute x12, waiting for transfers between devices, across(): return lax.ppermute(v, 'z', [(i, i ^ bit) for i in range(8)])  46 us
    ppermute x12, starting transfers between devices, across(): return lax.ppermute(v, 'z', [(i, i ^ bit) for i in range(8)])  34.4 us
    ppermute x6, starting transfers between devices, spread_y(): parts = {s: lax.ppermute(v, 'y', ring(ny, s)) for s in (1, 3, 2)}  19.5 us
    ppermute x1, starting transfers between devices, body(): far_half = lax.ppermute(hidden, 'w', swap)  15.4 us
    ppermute x4, starting transfers between devices, body(): other = [lax.ppermute(v, 'c', swap) for v in mine]  10.3 us
    ppermute x3, starting transfers between devices, body(): lax.ppermute(query_line, 'x', ring(nx, s))  9.66 us
    ppermute x3, starting transfers between devices, body(): lax.ppermute(pair_line, 'x', ring(nx, s))  9.33 us
    pallas_call x1, Pallas kernels, body(): call(functools.partial(pair_kernel, panel), [jax.ShapeDtypeStruct((2 * ro...  7.13 us
  transfers between devices with their start and end apart: 37, of which 10 were waited for; matrix products, arithmetic and copies ran while one was open for 5% of the time, Pallas kernels for 6%

profile of v3, /device:TPU:1, one launch (start us, length us, event | category | flops | bytes accessed | tf_op | source)
XLA Modules:
  0.0 220.5 jit_solution(1526768444898051670)
XLA Ops:
  0.6 5.5 %collective-permute-start.10 = (bf16[192,640]{1,0:T(8,128)(2,1)}, bf16[192,640]{1,0:T(8,128)(2,1)S(1)}, u32[]{:S(2)}, u32[]{:S(2)}) collective-permute-start(bf16[192,640]{1,0:T(8,128)(2,1)} %param.7), channel_id=1, source_target_pairs={{0,6},{2,0},{4,2},{6,4},{1,7},{3,1},{5,3},{7,5},{8,14},{10,8},{12,... | collective-permute-start | bytes 737288 | tf_op jit(solution)/shard_map/ppermute | solution.py:287
  8.4 2.6 %collective-permute-start.8 = (bf16[192,640]{1,0:T(8,128)(2,1)}, bf16[192,640]{1,0:T(8,128)(2,1)S(1)}, u32[]{:S(2)}, u32[]{:S(2)}) collective-permute-start(bf16[192,640]{1,0:T(8,128)(2,1)} %param.7), channel_id=1, source_target_pairs={{0,2},{2,4},{4,6},{6,0},{1,3},{3,5},{5,7},{7,1},{8,10},{10,12},{12... | collective-permute-start | bytes 737288 | tf_op jit(solution)/shard_map/ppermute | solution.py:287
  11.0 15.4 %collective-permute-start.11 = (bf16[192,640]{1,0:T(8,128)(2,1)}, bf16[192,640]{1,0:T(8,128)(2,1)S(1)}, u32[]{:S(2)}, u32[]{:S(2)}) collective-permute-start(bf16[192,640]{1,0:T(8,128)(2,1)} %param.7), channel_id=1, source_target_pairs={{0,1},{1,0},{2,3},{3,2},{4,5},{5,4},{6,7},{7,6},{8,9},{9,8},{10,11... | collective-permute-start | bytes 737288 | tf_op jit(solution)/shard_map/ppermute | solution.py:254
  26.4 3.7 %collective-permute-start = (s32[192]{0:T(256)}, s32[192]{0:T(256)S(1)}, u32[]{:S(2)}, u32[]{:S(2)}) collective-permute-start(s32[192]{0:T(256)} %param.12), channel_id=1, source_target_pairs={{0,8},{8,0},{1,9},{9,1},{2,10},{10,2},{3,11},{11,3},{4,12},{12,4},... | collective-permute-start | bytes 2312 | tf_op jit(solution)/shard_map/ppermute | solution.py:257
  35.0 4.0 %collective-permute-start.1 = (bf16[176,128]{1,0:T(8,128)(2,1)S(1)}, bf16[176,128]{1,0:T(8,128)(2,1)S(1)}, u32[]{:S(2)}, u32[]{:S(2)}) collective-permute-start(bf16[176,128]{1,0:T(8,128)(2,1)S(1)} %get-tuple-element.32), channel_id=1, source_target_pairs={{0,64},{16,80},{32,96},{48,112},{64,0},{80,16},{96,32},{112,48},{1... | collective-permute-start | bytes 135176 | tf_op jit(solution)/shard_map/ppermute | solution.py:237
  39.2 14.0 %collective-permute-done.1 = bf16[176,128]{1,0:T(8,128)(2,1)S(1)} collective-permute-done((bf16[176,128]{1,0:T(8,128)(2,1)S(1)}, bf16[176,128]{1,0:T(8,128)(2,1)S(1)}, u32[]{:S(2)}, u32[]{:S(2)}) %collective-permute-start.1) | collective-permute-done | bytes 45088 | tf_op jit(solution)/shard_map/ppermute | solution.py:237
  55.5 11.4 %collective-permute-done.19 = bf16[160,256]{1,0:T(8,128)(2,1)S(1)} collective-permute-done((bf16[160,256]{1,0:T(8,128)(2,1)S(1)}, bf16[160,256]{1,0:T(8,128)(2,1)S(1)}, u32[]{:S(2)}, u32[]{:S(2)}) %collective-permute-start.19) | collective-permute-done | bytes 81952 | tf_op jit(solution)/shard_map/ppermute | solution.py:237
  68.8 3.6 %collective-permute-done.2 = bf16[2,176,128]{2,1,0:T(8,128)(2,1)S(1)} collective-permute-done((bf16[2,176,128]{2,1,0:T(8,128)(2,1)S(1)}, bf16[2,176,128]{2,1,0:T(8,128)(2,1)S(1)}, u32[]{:S(2)}, u32[]{:S(2)}) %collective-permute-start.2) | collective-permute-done | bytes 90144 | tf_op jit(solution)/shard_map/ppermute | solution.py:237
  74.4 6.8 %collective-permute-done.3 = bf16[2,176,128]{2,1,0:T(8,128)(2,1)S(1)} collective-permute-done((bf16[2,176,128]{2,1,0:T(8,128)(2,1)S(1)}, bf16[2,176,128]{2,1,0:T(8,128)(2,1)S(1)}, u32[]{:S(2)}, u32[]{:S(2)}) %collective-permute-start.3) | collective-permute-done | bytes 90144 | tf_op jit(solution)/shard_map/ppermute | solution.py:237
  83.2 5.1 %collective-permute-done.4 = bf16[2,176,128]{2,1,0:T(8,128)(2,1)S(1)} collective-permute-done((bf16[2,176,128]{2,1,0:T(8,128)(2,1)S(1)}, bf16[2,176,128]{2,1,0:T(8,128)(2,1)S(1)}, u32[]{:S(2)}, u32[]{:S(2)}) %collective-permute-start.4) | collective-permute-done | bytes 90144 | tf_op jit(solution)/shard_map/ppermute | solution.py:237
  92.6 5.1 %collective-permute-start.22 = (bf16[2,160,256]{2,1,0:T(8,128)(2,1)S(1)}, bf16[2,160,256]{2,1,0:T(8,128)(2,1)S(1)}, u32[]{:S(2)}, u32[]{:S(2)}) collective-permute-start(bf16[2,160,256]{2,1,0:T(8,128)(2,1)S(1)} %pad_maximum_fusion.6), channel_id=1, source_target_pairs={{0,48},{16,32},{32,16},{48,0},{64,112},{80,96},{96,80},{112,64},{1... | collective-permute-start | bytes 491528 | tf_op jit(solution)/shard_map/ppermute | solution.py:237
  98.7 3.9 %collective-permute-start.14 = (bf16[192,640]{1,0:T(8,128)(2,1)S(1)}, bf16[192,640]{1,0:T(8,128)(2,1)S(1)}, u32[]{:S(2)}, u32[]{:S(2)}) collective-permute-start(bf16[192,640]{1,0:T(8,128)(2,1)S(1)} %collective-permute-done.11), channel_id=1, source_target_pairs={{0,6},{2,0},{4,2},{6,4},{1,7},{3,1},{5,3},{7,5},{8,14},{10,8},{12,... | collective-permute-start | bytes 737288 | tf_op jit(solution)/shard_map/ppermute | solution.py:287
  102.6 3.3 %collective-permute-start.13 = (bf16[192,640]{1,0:T(8,128)(2,1)S(1)}, bf16[192,640]{1,0:T(8,128)(2,1)S(1)}, u32[]{:S(2)}, u32[]{:S(2)}) collective-permute-start(bf16[192,640]{1,0:T(8,128)(2,1)S(1)} %collective-permute-done.11), channel_id=1, source_target_pairs={{0,4},{2,6},{4,0},{6,2},{1,5},{3,7},{5,1},{7,3},{8,12},{10,14},{12... | collective-permute-start | bytes 737288 | tf_op jit(solution)/shard_map/ppermute | solution.py:287
  107.9 4.4 %collective-permute-start.7 = (bf16[8,176,128]{2,1,0:T(8,128)(2,1)S(1)}, bf16[8,176,128]{2,1,0:T(8,128)(2,1)S(1)}, u32[]{:S(2)}, u32[]{:S(2)}) collective-permute-start(bf16[8,176,128]{2,1,0:T(8,128)(2,1)S(1)} %constant_dynamic-update-slice_fusion.refs_4_), channel_id=1, source_target_pairs={{0,384},{128,0},{256,128},{384,256},{1,385},{129,1},{257,129},{385... | collective-permute-start | bytes 1081352 | tf_op jit(solution)/shard_map/ppermute | solution.py:281
  112.4 2.4 %collective-permute-start.6 = (bf16[8,176,128]{2,1,0:T(8,128)(2,1)S(1)}, bf16[8,176,128]{2,1,0:T(8,128)(2,1)S(1)}, u32[]{:S(2)}, u32[]{:S(2)}) collective-permute-start(bf16[8,176,128]{2,1,0:T(8,128)(2,1)S(1)} %constant_dynamic-update-slice_fusion.refs_4_), channel_id=1, source_target_pairs={{0,256},{128,384},{256,0},{384,128},{1,257},{129,385},{257,1},{385... | collective-permute-start | bytes 1081352 | tf_op jit(solution)/shard_map/ppermute | solution.py:281
  114.8 2.5 %collective-permute-start.5 = (bf16[8,176,128]{2,1,0:T(8,128)(2,1)S(1)}, bf16[8,176,128]{2,1,0:T(8,128)(2,1)S(1)}, u32[]{:S(2)}, u32[]{:S(2)}) collective-permute-start(bf16[8,176,128]{2,1,0:T(8,128)(2,1)S(1)} %constant_dynamic-update-slice_fusion.refs_4_), channel_id=1, source_target_pairs={{0,128},{128,256},{256,384},{384,0},{1,129},{129,257},{257,385},{3... | collective-permute-start | bytes 1081352 | tf_op jit(solution)/shard_map/ppermute | solution.py:281
  117.4 6.3 %collective-permute-start.15 = (bf16[4,192,640]{2,1,0:T(8,128)(2,1)S(1)}, bf16[4,192,640]{2,1,0:T(8,128)(2,1)}, u32[]{:S(2)}, u32[]{:S(2)}) collective-permute-start(bf16[4,192,640]{2,1,0:T(8,128)(2,1)S(1)} %pad_maximum_fusion.refs_0_), channel_id=1, source_target_pairs={{0,8},{8,0},{1,9},{9,1},{2,10},{10,2},{3,11},{11,3},{4,12},{12,4},... | collective-permute-start | bytes 2949128 | tf_op jit(solution)/shard_map/ppermute | solution.py:291
  123.7 3.4 %collective-permute-start.23 = (bf16[8,160,256]{2,1,0:T(8,128)(2,1)S(1)}, bf16[8,160,256]{2,1,0:T(8,128)(2,1)}, u32[]{:S(2)}, u32[]{:S(2)}) collective-permute-start(bf16[8,160,256]{2,1,0:T(8,128)(2,1)S(1)} %constant_dynamic-update-slice_fusion.5.refs_0_), channel_id=1, source_target_pairs={{0,128},{128,256},{256,384},{384,0},{1,129},{129,257},{257,385},{3... | collective-permute-start | bytes 1966088 | tf_op jit(solution)/shard_map/ppermute | solution.py:283
  127.3 3.6 %collective-permute-start.24 = (bf16[8,160,256]{2,1,0:T(8,128)(2,1)S(1)}, bf16[8,160,256]{2,1,0:T(8,128)(2,1)}, u32[]{:S(2)}, u32[]{:S(2)}) collective-permute-start(bf16[8,160,256]{2,1,0:T(8,128)(2,1)S(1)} %constant_dynamic-update-slice_fusion.5.refs_0_), channel_id=1, source_target_pairs={{0,256},{128,384},{256,0},{384,128},{1,257},{129,385},{257,1},{385... | collective-permute-start | bytes 1966088 | tf_op jit(solution)/shard_map/ppermute | solution.py:283
  131.0 2.6 %collective-permute-start.25 = (bf16[8,160,256]{2,1,0:T(8,128)(2,1)S(1)}, bf16[8,160,256]{2,1,0:T(8,128)(2,1)}, u32[]{:S(2)}, u32[]{:S(2)}) collective-permute-start(bf16[8,160,256]{2,1,0:T(8,128)(2,1)S(1)} %constant_dynamic-update-slice_fusion.5.refs_0_), channel_id=1, source_target_pairs={{0,384},{128,0},{256,128},{384,256},{1,385},{129,1},{257,129},{385... | collective-permute-start | bytes 1966088 | tf_op jit(solution)/shard_map/ppermute | solution.py:283
  133.6 4.5 %collective-permute-start.16 = (bf16[4,192,640]{2,1,0:T(8,128)(2,1)S(1)}, bf16[4,192,640]{2,1,0:T(8,128)(2,1)}, u32[]{:S(2)}, u32[]{:S(2)}) collective-permute-start(bf16[4,192,640]{2,1,0:T(8,128)(2,1)S(1)} %pad_maximum_fusion.1.refs_1_), channel_id=1, source_target_pairs={{0,8},{8,0},{1,9},{9,1},{2,10},{10,2},{3,11},{11,3},{4,12},{12,4},... | collective-permute-start | bytes 2949128 | tf_op jit(solution)/shard_map/ppermute | solution.py:293
  146.1 7.1 %shard_map.94 = (bf16[384,5120]{1,0:T(8,128)(2,1)}, bf16[384,128]{1,0:T(8,128)(2,1)S(1)}) custom-call(s32[64]{0:T(128)S(1)} %broadcast_multiply_fusion.offsets, s32[5]{0:T(128)S(1)} %stack.171.where, f32[1,5120]{1,0:T(1,128)S(1)} %bitcast.72, f32[1,128]{1,0:T(1,128)S(1)} %bitcast.73, f32[384,128]{1,0:T(8,128)S(1)} %get-tuple-element.42.cosine, ...), custom_call_target="tpu_custom_call" | custom-call | flops 4000000000 | bytes 4194304 | tf_op jit(solution)/shard_map/pallas_call | solution.py:326
  153.3 3.9 %collective-permute-start.17 = (bf16[384,128]{1,0:T(8,128)(2,1)S(1)}, bf16[384,128]{1,0:T(8,128)(2,1)S(1)}, u32[]{:S(2)}, u32[]{:S(2)}) collective-permute-start(bf16[384,128]{1,0:T(8,128)(2,1)S(1)} %get-tuple-element.12), channel_id=1, source_target_pairs={{0,64},{16,80},{32,96},{48,112},{64,0},{80,16},{96,32},{112,48},{1... | collective-permute-start | bytes 294920 | tf_op jit(solution)/shard_map/ppermute | solution.py:237
  159.2 4.3 %shard_map.95 = bf16[2,2,192,128]{3,2,1,0:T(8,128)(2,1)S(1)} custom-call(s32[64]{0:T(128)S(1)} %broadcast_multiply_fusion.offsets, s32[5]{0:T(128)S(1)} %stack.171.where, bf16[384,5120]{1,0:T(8,128)(2,1)} %get-tuple-element.13.normed, f32[1,128]{1,0:T(1,128)S(1)} %bitcast.74, f32[384,128]{1,0:T(8,128)S(1)} %get-tuple-element.42.cosine, ...), custom_call_target="tpu_custom_call" | custom-call | flops 4000000000 | bytes 4194304 | tf_op jit(solution)/shard_map/pallas_call | solution.py:340
  163.5 5.3 %collective-permute-start.26 = (bf16[2,192,128]{2,1,0:T(8,128)(2,1)S(1)}, bf16[2,192,128]{2,1,0:T(8,128)(2,1)S(1)}, u32[]{:S(2)}, u32[]{:S(2)}) collective-permute-start(bf16[2,192,128]{2,1,0:T(8,128)(2,1)S(1)} %get-tuple-element.26), channel_id=1, source_target_pairs={{0,8},{8,0},{1,9},{9,1},{2,10},{10,2},{3,11},{11,3},{4,12},{12,4},... | collective-permute-start | bytes 294920 | tf_op jit(solution)/shard_map/ppermute | solution.py:354
  175.2 5.4 %collective-permute-start.31 = (bf16[2,384,128]{2,1,0:T(8,128)(2,1)S(1)}, bf16[2,384,128]{2,1,0:T(8,128)(2,1)S(1)}, u32[]{:S(2)}, u32[]{:S(2)}) collective-permute-start(bf16[2,384,128]{2,1,0:T(8,128)(2,1)S(1)} %pad_maximum_fusion.4.refs_0_), channel_id=1, source_target_pairs={{0,48},{16,32},{32,16},{48,0},{64,112},{80,96},{96,80},{112,64},{1... | collective-permute-start | bytes 589832 | tf_op jit(solution)/shard_map/ppermute | solution.py:237
  183.3 2.8 %collective-permute-start.32 = (bf16[2,384,128]{2,1,0:T(8,128)(2,1)S(1)}, bf16[2,384,128]{2,1,0:T(8,128)(2,1)S(1)}, u32[]{:S(2)}, u32[]{:S(2)}) collective-permute-start(bf16[2,384,128]{2,1,0:T(8,128)(2,1)S(1)} %collective-permute-done.29.refs_1_), channel_id=1, source_target_pairs={{0,8},{8,0},{1,9},{9,1},{2,10},{10,2},{3,11},{11,3},{4,12},{12,4},... | collective-permute-start | bytes 589832 | tf_op jit(solution)/shard_map/ppermute | solution.py:351
  186.2 4.8 %collective-permute-done.30.refs_2_ = bf16[2,384,128]{2,1,0:T(8,128)(2,1)S(1)} collective-permute-done((bf16[2,384,128]{2,1,0:T(8,128)(2,1)S(1)}, bf16[2,384,128]{2,1,0:T(8,128)(2,1)S(1)}, u32[]{:S(2)}, u32[]{:S(2)}) %collective-permute-start.30) | collective-permute-done | bytes 196640 | tf_op jit(solution)/shard_map/ppermute | solution.py:237
  191.0 3.2 %collective-permute-start.33 = (bf16[2,384,128]{2,1,0:T(8,128)(2,1)S(1)}, bf16[2,384,128]{2,1,0:T(8,128)(2,1)S(1)}, u32[]{:S(2)}, u32[]{:S(2)}) collective-permute-start(bf16[2,384,128]{2,1,0:T(8,128)(2,1)S(1)} %collective-permute-done.30.refs_2_), channel_id=1, source_target_pairs={{0,8},{8,0},{1,9},{9,1},{2,10},{10,2},{3,11},{11,3},{4,12},{12,4},... | collective-permute-start | bytes 589832 | tf_op jit(solution)/shard_map/ppermute | solution.py:351
  202.9 6.0 %collective-permute-start.35 = (bf16[816,128]{1,0:T(8,128)(2,1)S(1)}, bf16[816,128]{1,0:T(8,128)(2,1)S(1)}, u32[]{:S(2)}, u32[]{:S(2)}) collective-permute-start(bf16[816,128]{1,0:T(8,128)(2,1)S(1)} %get-tuple-element.19), channel_id=1, source_target_pairs={{0,128},{128,256},{256,384},{1,129},{129,257},{257,385},{2,130},{1... | collective-permute-start | bytes 626696 | tf_op jit(solution)/shard_map/ppermute | solution.py:374
  208.9 5.5 %collective-permute-start.36 = (bf16[816,128]{1,0:T(8,128)(2,1)S(1)}, bf16[816,128]{1,0:T(8,128)(2,1)S(1)}, u32[]{:S(2)}, u32[]{:S(2)}) collective-permute-start(bf16[816,128]{1,0:T(8,128)(2,1)S(1)} %get-tuple-element.20), channel_id=1, source_target_pairs={{0,256},{128,384},{1,257},{129,385},{2,258},{130,386},{3,259},{131... | collective-permute-start | bytes 626696 | tf_op jit(solution)/shard_map/ppermute | solution.py:375
  214.4 2.6 %shard_map.97 = (f32[768,128]{1,0:T(8,128)S(1)}, f32[768,1]{1,0:T(8,128)S(1)}) custom-call(s32[12]{0:T(128)S(1)} %stack.213.where, s32[3,192,1]{2,1,0:T(8,128)S(1)} %broadcast_subtract_fusion.begins, bf16[768,128]{1,0:T(8,128)(2,1)S(1)} %bitcast.71, bf16[3072,128]{1,0:T(8,128)(2,1)S(1)} %get-tuple-element.15.keys, bf16[3072,256]{1,0:T(8,128)(2,1)S(1)} %get-tuple-element.16.values), custom_call_target="tpu_custom_call" | custom-call | flops 10000000000 | bytes 4194304 | tf_op jit(solution)/shard_map/pallas_call | solution.py:376
  (126 shorter events, 51.9 us)
Async XLA Ops:
  0.6 89.6 %collective-permute-start.10 = (bf16[192,640]{1,0:T(8,128)(2,1)}, bf16[192,640]{1,0:T(8,128)(2,1)S(1)}, u32[]{:S(2)}, u32[]{:S(2)}) collective-permute-start(bf16[192,640]{1,0:T(8,128)(2,1)} %param.7), channel_id=1, source_target_pairs={{0,6},{2,0},{4,2},{6,4},{1,7},{3,1},{5,3},{7,5},{8,14},{10,8},{12,... | collective-permute-start | bytes 737288 | tf_op jit(solution)/shard_map/ppermute | solution.py:287
  6.1 86.4 %collective-permute-start.9 = (bf16[192,640]{1,0:T(8,128)(2,1)}, bf16[192,640]{1,0:T(8,128)(2,1)S(1)}, u32[]{:S(2)}, u32[]{:S(2)}) collective-permute-start(bf16[192,640]{1,0:T(8,128)(2,1)} %param.7), channel_id=1, source_target_pairs={{0,4},{2,6},{4,0},{6,2},{1,5},{3,7},{5,1},{7,3},{8,12},{10,14},{12... | collective-permute-start | bytes 737288 | tf_op jit(solution)/shard_map/ppermute | solution.py:287
  8.4 89.2 %collective-permute-start.8 = (bf16[192,640]{1,0:T(8,128)(2,1)}, bf16[192,640]{1,0:T(8,128)(2,1)S(1)}, u32[]{:S(2)}, u32[]{:S(2)}) collective-permute-start(bf16[192,640]{1,0:T(8,128)(2,1)} %param.7), channel_id=1, source_target_pairs={{0,2},{2,4},{4,6},{6,0},{1,3},{3,5},{5,7},{7,1},{8,10},{10,12},{12... | collective-permute-start | bytes 737288 | tf_op jit(solution)/shard_map/ppermute | solution.py:287
  11.0 87.7 %collective-permute-start.11 = (bf16[192,640]{1,0:T(8,128)(2,1)}, bf16[192,640]{1,0:T(8,128)(2,1)S(1)}, u32[]{:S(2)}, u32[]{:S(2)}) collective-permute-start(bf16[192,640]{1,0:T(8,128)(2,1)} %param.7), channel_id=1, source_target_pairs={{0,1},{1,0},{2,3},{3,2},{4,5},{5,4},{6,7},{7,6},{8,9},{9,8},{10,11... | collective-permute-start | bytes 737288 | tf_op jit(solution)/shard_map/ppermute | solution.py:254
  35.0 18.2 %collective-permute-start.1 = (bf16[176,128]{1,0:T(8,128)(2,1)S(1)}, bf16[176,128]{1,0:T(8,128)(2,1)S(1)}, u32[]{:S(2)}, u32[]{:S(2)}) collective-permute-start(bf16[176,128]{1,0:T(8,128)(2,1)S(1)} %get-tuple-element.32), channel_id=1, source_target_pairs={{0,64},{16,80},{32,96},{48,112},{64,0},{80,16},{96,32},{112,48},{1... | collective-permute-start | bytes 135176 | tf_op jit(solution)/shard_map/ppermute | solution.py:237
  53.3 13.6 %collective-permute-start.19 = (bf16[160,256]{1,0:T(8,128)(2,1)S(1)}, bf16[160,256]{1,0:T(8,128)(2,1)S(1)}, u32[]{:S(2)}, u32[]{:S(2)}) collective-permute-start(bf16[160,256]{1,0:T(8,128)(2,1)S(1)} %constant_dynamic-slice_fusion), channel_id=1, source_target_pairs={{0,64},{16,80},{32,96},{48,112},{64,0},{80,16},{96,32},{112,48},{1... | collective-permute-start | bytes 245768 | tf_op jit(solution)/shard_map/ppermute | solution.py:237
  72.5 8.7 %collective-permute-start.3 = (bf16[2,176,128]{2,1,0:T(8,128)(2,1)S(1)}, bf16[2,176,128]{2,1,0:T(8,128)(2,1)S(1)}, u32[]{:S(2)}, u32[]{:S(2)}) collective-permute-start(bf16[2,176,128]{2,1,0:T(8,128)(2,1)S(1)} %pad_maximum_fusion.7), channel_id=1, source_target_pairs={{0,32},{16,48},{32,0},{48,16},{64,96},{80,112},{96,64},{112,80},{1... | collective-permute-start | bytes 270344 | tf_op jit(solution)/shard_map/ppermute | solution.py:237
  88.3 17.7 %collective-permute-start.20 = (bf16[2,160,256]{2,1,0:T(8,128)(2,1)S(1)}, bf16[2,160,256]{2,1,0:T(8,128)(2,1)S(1)}, u32[]{:S(2)}, u32[]{:S(2)}) collective-permute-start(bf16[2,160,256]{2,1,0:T(8,128)(2,1)S(1)} %pad_maximum_fusion.6), channel_id=1, source_target_pairs={{0,16},{16,0},{32,48},{48,32},{64,80},{80,64},{96,112},{112,96},{1... | collective-permute-start | bytes 491528 | tf_op jit(solution)/shard_map/ppermute | solution.py:237
  90.2 17.7 %collective-permute-start.21 = (bf16[2,160,256]{2,1,0:T(8,128)(2,1)S(1)}, bf16[2,160,256]{2,1,0:T(8,128)(2,1)S(1)}, u32[]{:S(2)}, u32[]{:S(2)}) collective-permute-start(bf16[2,160,256]{2,1,0:T(8,128)(2,1)S(1)} %pad_maximum_fusion.6), channel_id=1, source_target_pairs={{0,32},{16,48},{32,0},{48,16},{64,96},{80,112},{96,64},{112,80},{1... | collective-permute-start | bytes 491528 | tf_op jit(solution)/shard_map/ppermute | solution.py:237
  92.6 19.8 %collective-permute-start.22 = (bf16[2,160,256]{2,1,0:T(8,128)(2,1)S(1)}, bf16[2,160,256]{2,1,0:T(8,128)(2,1)S(1)}, u32[]{:S(2)}, u32[]{:S(2)}) collective-permute-start(bf16[2,160,256]{2,1,0:T(8,128)(2,1)S(1)} %pad_maximum_fusion.6), channel_id=1, source_target_pairs={{0,48},{16,32},{32,16},{48,0},{64,112},{80,96},{96,80},{112,64},{1... | collective-permute-start | bytes 491528 | tf_op jit(solution)/shard_map/ppermute | solution.py:237
  98.7 16.1 %collective-permute-start.14 = (bf16[192,640]{1,0:T(8,128)(2,1)S(1)}, bf16[192,640]{1,0:T(8,128)(2,1)S(1)}, u32[]{:S(2)}, u32[]{:S(2)}) collective-permute-start(bf16[192,640]{1,0:T(8,128)(2,1)S(1)} %collective-permute-done.11), channel_id=1, source_target_pairs={{0,6},{2,0},{4,2},{6,4},{1,7},{3,1},{5,3},{7,5},{8,14},{10,8},{12,... | collective-permute-start | bytes 737288 | tf_op jit(solution)/shard_map/ppermute | solution.py:287
  102.6 14.7 %collective-permute-start.13 = (bf16[192,640]{1,0:T(8,128)(2,1)S(1)}, bf16[192,640]{1,0:T(8,128)(2,1)S(1)}, u32[]{:S(2)}, u32[]{:S(2)}) collective-permute-start(bf16[192,640]{1,0:T(8,128)(2,1)S(1)} %collective-permute-done.11), channel_id=1, source_target_pairs={{0,4},{2,6},{4,0},{6,2},{1,5},{3,7},{5,1},{7,3},{8,12},{10,14},{12... | collective-permute-start | bytes 737288 | tf_op jit(solution)/shard_map/ppermute | solution.py:287
  106.0 17.7 %collective-permute-start.12 = (bf16[192,640]{1,0:T(8,128)(2,1)S(1)}, bf16[192,640]{1,0:T(8,128)(2,1)S(1)}, u32[]{:S(2)}, u32[]{:S(2)}) collective-permute-start(bf16[192,640]{1,0:T(8,128)(2,1)S(1)} %collective-permute-done.11), channel_id=1, source_target_pairs={{0,2},{2,4},{4,6},{6,0},{1,3},{3,5},{5,7},{7,1},{8,10},{10,12},{12... | collective-permute-start | bytes 737288 | tf_op jit(solution)/shard_map/ppermute | solution.py:287
  107.9 19.4 %collective-permute-start.7 = (bf16[8,176,128]{2,1,0:T(8,128)(2,1)S(1)}, bf16[8,176,128]{2,1,0:T(8,128)(2,1)S(1)}, u32[]{:S(2)}, u32[]{:S(2)}) collective-permute-start(bf16[8,176,128]{2,1,0:T(8,128)(2,1)S(1)} %constant_dynamic-update-slice_fusion.refs_4_), channel_id=1, source_target_pairs={{0,384},{128,0},{256,128},{384,256},{1,385},{129,1},{257,129},{385... | collective-permute-start | bytes 1081352 | tf_op jit(solution)/shard_map/ppermute | solution.py:281
  112.4 18.6 %collective-permute-start.6 = (bf16[8,176,128]{2,1,0:T(8,128)(2,1)S(1)}, bf16[8,176,128]{2,1,0:T(8,128)(2,1)S(1)}, u32[]{:S(2)}, u32[]{:S(2)}) collective-permute-start(bf16[8,176,128]{2,1,0:T(8,128)(2,1)S(1)} %constant_dynamic-update-slice_fusion.refs_4_), channel_id=1, source_target_pairs={{0,256},{128,384},{256,0},{384,128},{1,257},{129,385},{257,1},{385... | collective-permute-start | bytes 1081352 | tf_op jit(solution)/shard_map/ppermute | solution.py:281
  114.8 18.8 %collective-permute-start.5 = (bf16[8,176,128]{2,1,0:T(8,128)(2,1)S(1)}, bf16[8,176,128]{2,1,0:T(8,128)(2,1)S(1)}, u32[]{:S(2)}, u32[]{:S(2)}) collective-permute-start(bf16[8,176,128]{2,1,0:T(8,128)(2,1)S(1)} %constant_dynamic-update-slice_fusion.refs_4_), channel_id=1, source_target_pairs={{0,128},{128,256},{256,384},{384,0},{1,129},{129,257},{257,385},{3... | collective-permute-start | bytes 1081352 | tf_op jit(solution)/shard_map/ppermute | solution.py:281
  117.4 24.8 %collective-permute-start.15 = (bf16[4,192,640]{2,1,0:T(8,128)(2,1)S(1)}, bf16[4,192,640]{2,1,0:T(8,128)(2,1)}, u32[]{:S(2)}, u32[]{:S(2)}) collective-permute-start(bf16[4,192,640]{2,1,0:T(8,128)(2,1)S(1)} %pad_maximum_fusion.refs_0_), channel_id=1, source_target_pairs={{0,8},{8,0},{1,9},{9,1},{2,10},{10,2},{3,11},{11,3},{4,12},{12,4},... | collective-permute-start | bytes 2949128 | tf_op jit(solution)/shard_map/ppermute | solution.py:291
  123.7 33.5 %collective-permute-start.23 = (bf16[8,160,256]{2,1,0:T(8,128)(2,1)S(1)}, bf16[8,160,256]{2,1,0:T(8,128)(2,1)}, u32[]{:S(2)}, u32[]{:S(2)}) collective-permute-start(bf16[8,160,256]{2,1,0:T(8,128)(2,1)S(1)} %constant_dynamic-update-slice_fusion.5.refs_0_), channel_id=1, source_target_pairs={{0,128},{128,256},{256,384},{384,0},{1,129},{129,257},{257,385},{3... | collective-permute-start | bytes 1966088 | tf_op jit(solution)/shard_map/ppermute | solution.py:283
  127.3 31.0 %collective-permute-start.24 = (bf16[8,160,256]{2,1,0:T(8,128)(2,1)S(1)}, bf16[8,160,256]{2,1,0:T(8,128)(2,1)}, u32[]{:S(2)}, u32[]{:S(2)}) collective-permute-start(bf16[8,160,256]{2,1,0:T(8,128)(2,1)S(1)} %constant_dynamic-update-slice_fusion.5.refs_0_), channel_id=1, source_target_pairs={{0,256},{128,384},{256,0},{384,128},{1,257},{129,385},{257,1},{385... | collective-permute-start | bytes 1966088 | tf_op jit(solution)/shard_map/ppermute | solution.py:283
  131.0 28.2 %collective-permute-start.25 = (bf16[8,160,256]{2,1,0:T(8,128)(2,1)S(1)}, bf16[8,160,256]{2,1,0:T(8,128)(2,1)}, u32[]{:S(2)}, u32[]{:S(2)}) collective-permute-start(bf16[8,160,256]{2,1,0:T(8,128)(2,1)S(1)} %constant_dynamic-update-slice_fusion.5.refs_0_), channel_id=1, source_target_pairs={{0,384},{128,0},{256,128},{384,256},{1,385},{129,1},{257,129},{385... | collective-permute-start | bytes 1966088 | tf_op jit(solution)/shard_map/ppermute | solution.py:283
  153.3 15.7 %collective-permute-start.17 = (bf16[384,128]{1,0:T(8,128)(2,1)S(1)}, bf16[384,128]{1,0:T(8,128)(2,1)S(1)}, u32[]{:S(2)}, u32[]{:S(2)}) collective-permute-start(bf16[384,128]{1,0:T(8,128)(2,1)S(1)} %get-tuple-element.12), channel_id=1, source_target_pairs={{0,64},{16,80},{32,96},{48,112},{64,0},{80,16},{96,32},{112,48},{1... | collective-permute-start | bytes 294920 | tf_op jit(solution)/shard_map/ppermute | solution.py:237
  163.5 17.2 %collective-permute-start.26 = (bf16[2,192,128]{2,1,0:T(8,128)(2,1)S(1)}, bf16[2,192,128]{2,1,0:T(8,128)(2,1)S(1)}, u32[]{:S(2)}, u32[]{:S(2)}) collective-permute-start(bf16[2,192,128]{2,1,0:T(8,128)(2,1)S(1)} %get-tuple-element.26), channel_id=1, source_target_pairs={{0,8},{8,0},{1,9},{9,1},{2,10},{10,2},{3,11},{11,3},{4,12},{12,4},... | collective-permute-start | bytes 294920 | tf_op jit(solution)/shard_map/ppermute | solution.py:354
  169.0 13.0 %collective-permute-start.18 = (bf16[2,384,128]{2,1,0:T(8,128)(2,1)S(1)}, bf16[2,384,128]{2,1,0:T(8,128)(2,1)S(1)}, u32[]{:S(2)}, u32[]{:S(2)}) collective-permute-start(bf16[2,384,128]{2,1,0:T(8,128)(2,1)S(1)} %pad_maximum_fusion.4.refs_0_), channel_id=1, source_target_pairs={{0,8},{8,0},{1,9},{9,1},{2,10},{10,2},{3,11},{11,3},{4,12},{12,4},... | collective-permute-start | bytes 589832 | tf_op jit(solution)/shard_map/ppermute | solution.py:351
  171.4 12.0 %collective-permute-start.29 = (bf16[2,384,128]{2,1,0:T(8,128)(2,1)S(1)}, bf16[2,384,128]{2,1,0:T(8,128)(2,1)S(1)}, u32[]{:S(2)}, u32[]{:S(2)}) collective-permute-start(bf16[2,384,128]{2,1,0:T(8,128)(2,1)S(1)} %pad_maximum_fusion.4.refs_0_), channel_id=1, source_target_pairs={{0,16},{16,0},{32,48},{48,32},{64,80},{80,64},{96,112},{112,96},{1... | collective-permute-start | bytes 589832 | tf_op jit(solution)/shard_map/ppermute | solution.py:237
  173.3 17.7 %collective-permute-start.30 = (bf16[2,384,128]{2,1,0:T(8,128)(2,1)S(1)}, bf16[2,384,128]{2,1,0:T(8,128)(2,1)S(1)}, u32[]{:S(2)}, u32[]{:S(2)}) collective-permute-start(bf16[2,384,128]{2,1,0:T(8,128)(2,1)S(1)} %pad_maximum_fusion.4.refs_0_), channel_id=1, source_target_pairs={{0,32},{16,48},{32,0},{48,16},{64,96},{80,112},{96,64},{112,80},{1... | collective-permute-start | bytes 589832 | tf_op jit(solution)/shard_map/ppermute | solution.py:237
  175.2 19.0 %collective-permute-start.31 = (bf16[2,384,128]{2,1,0:T(8,128)(2,1)S(1)}, bf16[2,384,128]{2,1,0:T(8,128)(2,1)S(1)}, u32[]{:S(2)}, u32[]{:S(2)}) collective-permute-start(bf16[2,384,128]{2,1,0:T(8,128)(2,1)S(1)} %pad_maximum_fusion.4.refs_0_), channel_id=1, source_target_pairs={{0,48},{16,32},{32,16},{48,0},{64,112},{80,96},{96,80},{112,64},{1... | collective-permute-start | bytes 589832 | tf_op jit(solution)/shard_map/ppermute | solution.py:237
  180.7 20.6 %collective-permute-start.27 = (bf16[768,128]{1,0:T(8,128)(2,1)S(1)}, bf16[768,128]{1,0:T(8,128)(2,1)S(1)}, u32[]{:S(2)}, u32[]{:S(2)}) collective-permute-start(bf16[768,128]{1,0:T(8,128)(2,1)S(1)} %bitcast.69), channel_id=1, source_target_pairs={{128,0},{256,128},{384,256},{129,1},{257,129},{385,257},{130,2},{2... | collective-permute-start | bytes 589832 | tf_op jit(solution)/shard_map/ppermute | solution.py:356
  182.0 19.3 %collective-permute-start.28 = (bf16[768,128]{1,0:T(8,128)(2,1)S(1)}, bf16[768,128]{1,0:T(8,128)(2,1)S(1)}, u32[]{:S(2)}, u32[]{:S(2)}) collective-permute-start(bf16[768,128]{1,0:T(8,128)(2,1)S(1)} %bitcast.70), channel_id=1, source_target_pairs={{256,0},{384,128},{257,1},{385,129},{258,2},{386,130},{259,3},{387... | collective-permute-start | bytes 589832 | tf_op jit(solution)/shard_map/ppermute | solution.py:357
  183.3 18.0 %collective-permute-start.32 = (bf16[2,384,128]{2,1,0:T(8,128)(2,1)S(1)}, bf16[2,384,128]{2,1,0:T(8,128)(2,1)S(1)}, u32[]{:S(2)}, u32[]{:S(2)}) collective-permute-start(bf16[2,384,128]{2,1,0:T(8,128)(2,1)S(1)} %collective-permute-done.29.refs_1_), channel_id=1, source_target_pairs={{0,8},{8,0},{1,9},{9,1},{2,10},{10,2},{3,11},{11,3},{4,12},{12,4},... | collective-permute-start | bytes 589832 | tf_op jit(solution)/shard_map/ppermute | solution.py:351
  191.0 10.3 %collective-permute-start.33 = (bf16[2,384,128]{2,1,0:T(8,128)(2,1)S(1)}, bf16[2,384,128]{2,1,0:T(8,128)(2,1)S(1)}, u32[]{:S(2)}, u32[]{:S(2)}) collective-permute-start(bf16[2,384,128]{2,1,0:T(8,128)(2,1)S(1)} %collective-permute-done.30.refs_2_), channel_id=1, source_target_pairs={{0,8},{8,0},{1,9},{9,1},{2,10},{10,2},{3,11},{11,3},{4,12},{12,4},... | collective-permute-start | bytes 589832 | tf_op jit(solution)/shard_map/ppermute | solution.py:351
  202.9 14.1 %collective-permute-start.35 = (bf16[816,128]{1,0:T(8,128)(2,1)S(1)}, bf16[816,128]{1,0:T(8,128)(2,1)S(1)}, u32[]{:S(2)}, u32[]{:S(2)}) collective-permute-start(bf16[816,128]{1,0:T(8,128)(2,1)S(1)} %get-tuple-element.19), channel_id=1, source_target_pairs={{0,128},{128,256},{256,384},{1,129},{129,257},{257,385},{2,130},{1... | collective-permute-start | bytes 626696 | tf_op jit(solution)/shard_map/ppermute | solution.py:374
  208.9 9.6 %collective-permute-start.36 = (bf16[816,128]{1,0:T(8,128)(2,1)S(1)}, bf16[816,128]{1,0:T(8,128)(2,1)S(1)}, u32[]{:S(2)}, u32[]{:S(2)}) collective-permute-start(bf16[816,128]{1,0:T(8,128)(2,1)S(1)} %get-tuple-element.20), channel_id=1, source_target_pairs={{0,256},{128,384},{1,257},{129,385},{2,258},{130,386},{3,259},{131... | collective-permute-start | bytes 626696 | tf_op jit(solution)/shard_map/ppermute | solution.py:375
  (15 other events, 190.5 us)

commit v4 on v3

--- a/solution.py
+++ b/solution.py
@@ -15,7 +15,7 @@
 MASKED = -3e38
 KEY_BLOCK = 1024
 NO_SEGMENT = 100.0
-VMEM_LIMIT = 48 * 1024 * 1024
+VMEM_LIMIT = 20 * 1024 * 1024
 
 
 def call(kernel, out_shape, n_smem, n_vmem, scratch=(), flops=0):
@@ -33,7 +33,7 @@
     )
 
 
-PEER = (0, 4, 1, 5, 2, 6, 3, 7)
+PEER = (0, 4, 2, 6, 1, 5, 3, 7)
 
 
 def head_norm_rope(v, gain, cosine, sine):
@@ -43,21 +43,21 @@
 
 
 def collect(offsets, where, blocks, weights, panel):
-    nx = len(blocks)
-    nz = blocks[0].shape[0]
+    per = blocks[0].shape[0]
+    parts = len(PEER) // per
+    nx = len(blocks) // parts
     for s in range(nx):
         source = lax.rem(where[2] + nx - s, nx)
-        for k in range(nz):
+        for k, peer in enumerate(PEER):
             for c in range(2):
-                slot = source * (nz * 2) + (where[1] ^ PEER[k]) * 2 + c
+                slot = source * (2 * len(PEER)) + (where[1] ^ peer) * 2 + c
                 first = pl.multiple_of(offsets[slot], 16)
-                weights[pl.ds(first, panel), :] = blocks[s][k, c * panel : (c + 1) * panel, :]
-
-
-def pair_kernel(panel, offsets, where, norm_gain, gain, cosine, sine, *refs):
-    hidden, blocks = refs[:4], refs[4:-3]
-    normed, out, weights = refs[-3:]
-    collect(offsets, where, blocks, weights, panel)
+                block = blocks[s * parts + k // per]
+                weights[pl.ds(first, panel), :] = block[k % per, c * panel : (c + 1) * panel, :]
+
+
+def norm_kernel(where, norm_gain, *refs):
+    hidden, normed = refs[:-1], refs[-1]
     ny, rows, width = hidden[0].shape
     for side in range(2):
         first = pl.multiple_of(rows * (where[0] if side == 0 else 1 - where[0]), rows)
@@ -77,6 +77,11 @@
                 v = hidden[side * 2 + half][s].astype(jnp.float32)
                 v = v * scale * norm_gain[:, cols]
                 normed[pl.ds(first, rows), cols] = v.astype(jnp.bfloat16)
+
+
+def pair_kernel(panel, offsets, where, normed, gain, cosine, sine, *refs):
+    blocks, out, weights = refs[:-2], refs[-2], refs[-1]
+    collect(offsets, where, blocks, weights, panel)
     v = jnp.dot(normed[...], weights[...], preferred_element_type=jnp.float32)
     keys = head_norm_rope(v, gain[...], cosine[...], sine[...])
     out[...] = jnp.where(where[0] == 0, keys, v).astype(jnp.bfloat16)
@@ -155,8 +160,8 @@
 
 
 def remote_kernel(where, begins, near, far, *refs):
-    mine, other = refs[:4], refs[4:8]
-    out1, out2, keys, values, acc, top = refs[8:]
+    mine, other = refs[:2], refs[2:4]
+    out1, out2, keys, values, acc, top = refs[4:]
     block = mine[0].shape[1]
     values[:, 128:] = jnp.ones((values.shape[0], 128), values.dtype)
     for core, (first, second) in enumerate(((mine, other), (other, mine))):
@@ -165,8 +170,8 @@
         def _(first=first, second=second):
             for k in range(8):
                 spot = pl.ds(pl.multiple_of((where[1] ^ PEER[k]) * block, block), block)
-                keys[spot, :] = first[k // 2][k % 2]
-                values[spot, :128] = second[k // 2][k % 2]
+                keys[spot, :] = first[k // 4][k % 4]
+                values[spot, :128] = second[k // 4][k % 4]
 
     eye = identity_mask()
     size = near.shape[0]
@@ -251,48 +256,64 @@
     bf16, f32 = jnp.bfloat16, jnp.float32
     table = jnp.arange(slots, dtype=jnp.int32)
 
-    far_half = lax.ppermute(hidden, "w", swap)
-
-    both = lax.all_gather(weight_store, "c", axis=0, tiled=True)
-    twin_docs = lax.ppermute(documents, "c", swap)
-    pair_docs = jnp.where(
-        c == 0, jnp.stack([documents, twin_docs]), jnp.stack([twin_docs, documents])
+    def turn(v, axis, size):
+        return [lax.ppermute(v, axis, ring(size, s)) for s in range(1, size)]
+
+    riders = jnp.pad(documents.astype(bf16), (0, 256 - rows), constant_values=NO_SEGMENT)
+    riders = jnp.pad(riders[None], ((0, 15), (0, weight_store.shape[1] - 256)))
+    both = lax.all_gather(jnp.concatenate([weight_store, riders], axis=0), "c", axis=0)
+    pair_docs = both[:, panel, :256]
+    columns = both[:, :panel].reshape(2 * panel, -1)
+    columns = jnp.concatenate(
+        [
+            lax.dynamic_slice_in_dim(columns, 512 + 128 * c, 128, 1),
+            lax.dynamic_slice_in_dim(columns, 256 * c, 256, 1),
+        ],
+        axis=1,
     )
-    riders = jnp.pad(
-        pair_docs.astype(bf16), ((0, 0), (0, 256 - rows)), constant_values=NO_SEGMENT
-    ).reshape(4, 128)
-    pair_cols = jnp.concatenate(
-        [
-            lax.dynamic_slice_in_dim(both, 512 + 128 * c, 128, 1),
-            riders,
-            jnp.zeros((12, 128), bf16),
-        ],
-        axis=0,
-    )
-    query_cols = lax.dynamic_slice_in_dim(both, 256 * c, 256, 1)
-
-    def spread_z(half):
-        return jnp.concatenate([half] + [across(half, bit) for bit in (1, 2, 3)], axis=0)
-
-    pair_half = jnp.stack([pair_cols, across(pair_cols, 4)])
-    pair_line = spread_z(pair_half)
-    query_cols = after(query_cols, pair_half)
-    query_line = spread_z(jnp.stack([query_cols, across(query_cols, 4)]))
-    pair_blocks = [pair_line] + [lax.ppermute(pair_line, "x", ring(nx, s)) for s in (1, 3, 2)]
-    pair_blocks = [pair_blocks[i] for i in (0, 1, 3, 2)]
-    query_blocks = [query_line] + [lax.ppermute(query_line, "x", ring(nx, s)) for s in (1, 3, 2)]
-    query_blocks = [query_blocks[i] for i in (0, 1, 3, 2)]
-
-    def spread_y(v):
-        parts = {s: lax.ppermute(v, "y", ring(ny, s)) for s in (1, 3, 2)}
-        return jnp.stack([v, parts[1], parts[2], parts[3]])
-
-    own_near = spread_y(hidden)
+    tail = jnp.pad(pair_docs.reshape(4, 128), ((0, 12), (0, 256)))
+    line = jnp.concatenate([columns, tail], axis=0)[None]
+    pair_docs = pair_docs[:, :rows].astype(jnp.int32)
+
+    far = lax.ppermute(hidden, "w", swap)
+    near_parts = turn(hidden, "y", ny)
+    step = across(line, 4)
+    far, step, *near_parts = lax.optimization_barrier((far, step, *near_parts))
+
+    line = jnp.concatenate([line, step], axis=0)
+    own_near = jnp.stack([hidden] + near_parts)
+    far_parts = turn(far, "y", ny)
+    step = across(line, 2)
     other_near = lax.ppermute(own_near, "c", swap)
-    own_far = spread_y(far_half)
+    step, other_near, *far_parts = lax.optimization_barrier((step, other_near, *far_parts))
+
+    line = jnp.concatenate([line, step], axis=0)
+    own_far = jnp.stack([far] + far_parts)
+    step = across(line, 1)
     other_far = lax.ppermute(own_far, "c", swap)
+    first_parts = turn(line[:, :, :128], "x", nx)
+    step, other_far, *first_parts = lax.optimization_barrier((step, other_far, *first_parts))
+
+    second_parts = turn(step[:, :, :128], "x", nx)
+    pair_blocks = [
+        v
+        for both in zip(
+            [line[:, :, :128]] + first_parts, [step[:, :, :128]] + second_parts, strict=True
+        )
+        for v in both
+    ]
+    query_line = jnp.concatenate([line, step], axis=0)[:, : 2 * panel, 128:]
+    query_line = after(query_line, second_parts[0])
+    query_blocks = [query_line] + turn(query_line, "x", nx)
+
+    spot = jnp.stack([c, z, x, y, w]).astype(jnp.int32)
+    features = norm_gain.shape[0]
+    (normed,) = call(
+        norm_kernel, [jax.ShapeDtypeStruct((2 * rows, features), bf16)], 1, 5, (), 4 * 10**9
+    )(spot, norm_gain.astype(f32)[None, :], own_near, own_far, other_near, other_far)
 
     riding = jnp.stack([v[:, 2 * panel : 2 * panel + 4, :] for v in pair_blocks]).astype(f32)
+    riding = riding.reshape(nx, nz, 4, 128)
     starts = jnp.sum(
         (riding.reshape(-1, 1) < table.astype(f32)[None, :]).astype(f32), axis=0
     ).astype(jnp.int32)
@@ -321,22 +342,30 @@
     offsets = panel * jnp.sum(
         table[:, None] * (owners[:, None] == table[None, :]).astype(jnp.int32), axis=0
     )
-    spot = jnp.stack([c, z, x, y, w]).astype(jnp.int32)
-    features = norm_gain.shape[0]
-    normed, pair = call(
+    (pair,) = call(
         functools.partial(pair_kernel, panel),
-        [
-            jax.ShapeDtypeStruct((2 * rows, features), bf16),
-            jax.ShapeDtypeStruct((2 * rows, 128), bf16),
-        ],
+        [jax.ShapeDtypeStruct((2 * rows, 128), bf16)],
         2,
-        8 + nx,
+        4 + 2 * nx,
         [pltpu.VMEM((features, 128), bf16)],
-        4 * 10**9,
-    )(
-        offsets, spot, norm_gain.astype(f32)[None, :], key_gain[None, :], cosine, sine,
-        own_near, own_far, other_near, other_far, *pair_blocks,
-    )
+        2 * 10**9,
+    )(offsets, spot, normed, key_gain[None, :], cosine, sine, *pair_blocks)
+
+    inside = z * 2 * rows + c * rows
+    low = [jnp.clip(spread[s, 0], 0, plane) for s in range(3)]
+    high = [inside + rows] + [jnp.where(x + s < nx, plane, 0) for s in (1, 2)]
+    limits = [v for s in range(3) for v in (low[s], high[s], spread[s, rows - 1])]
+    ranges = jnp.stack([c, z, inside] + limits).astype(jnp.int32)
+    begins = spread[:, :, None]
+
+    mine0 = jnp.stack([pair, across(pair, 4)])
+    mine0, ranges, begins = lax.optimization_barrier((mine0, ranges, begins))
+    mine0 = jnp.concatenate([mine0, across(mine0, 2)], axis=0)
+    mine1 = across(mine0, 1)
+    mine = [mine0, mine1]
+    other = [lax.ppermute(v, "c", swap) for v in mine]
+
+    normed = after(normed, mine0)
     (query,) = call(
         functools.partial(query_kernel, panel),
         [jax.ShapeDtypeStruct((2, 2, rows, 128), bf16)],
@@ -346,9 +375,6 @@
         4 * 10**9,
     )(offsets, spot, normed, query_gain[None, :], cosine, sine, *query_blocks)
 
-    half = jnp.stack([pair, across(pair, 4)])
-    mine = [half] + [across(half, bit) for bit in (1, 2, 3)]
-    other = [lax.ppermute(v, "c", swap) for v in mine]
     own_query = lax.dynamic_index_in_dim(query, c, 0, keepdims=False)
     sent_query = lax.dynamic_index_in_dim(query, 1 - c, 0, keepdims=False)
     q0 = jnp.concatenate([own_query, lax.ppermute(sent_query, "c", swap)], axis=0)
@@ -356,21 +382,16 @@
     q1 = lax.ppermute(q0, "x", [(i, i - 1) for i in range(1, nx)])
     q2 = lax.ppermute(q0, "x", [(i, i - 2) for i in range(2, nx)])
 
-    inside = z * 2 * rows + c * rows
-    low = [jnp.clip(spread[s, 0], 0, plane) for s in range(3)]
-    high = [inside + rows] + [jnp.where(x + s < nx, plane, 0) for s in (1, 2)]
-    limits = [v for s in range(3) for v in (low[s], high[s], spread[s, rows - 1])]
-    ranges = jnp.stack([c, z, inside] + limits).astype(jnp.int32)
     state = [pltpu.VMEM((4 * rows, 256), f32), pltpu.VMEM((4 * rows, 1), f32)]
     r1, r2, keys, values = call(
         remote_kernel,
         [jax.ShapeDtypeStruct((4 * rows + 48, 128), bf16)] * 2
         + [jax.ShapeDtypeStruct((plane, 128 * k), bf16) for k in (1, 2)],
         1,
-        11,
+        7,
         state,
         10**10,
-    )(ranges, spread[:, :, None], q1, q2, *mine, *other)
+    )(ranges, begins, q1, q2, *mine, *other)
     r1 = lax.ppermute(r1, "x", [(i, i + 1) for i in range(nx - 1)])
     r2 = lax.ppermute(r2, "x", [(i, i + 2) for i in range(nx - 2)])
     o0, l0 = call(
@@ -383,7 +404,7 @@
         4,
         state,
         10**10,
-    )(ranges, spread[:, :, None], q0, keys, values)
+    )(ranges, begins, q0, keys, values)
     came = jnp.stack([c, (x >= 1).astype(jnp.int32), (x >= 2).astype(jnp.int32)]).astype(jnp.int32)
     (context,) = call(combine_kernel, [jax.ShapeDtypeStruct((rows, 512), bf16)], 1, 4)(
         came, o0, l0, r1, r2

time: 224 us -> 219 us (0.978)
  starting transfers between devices: 132 us -> 102 us
  waiting for transfers between devices: 49.5 us -> 65.8 us
  local copies, waits for them, and re-layouts: 7.99 us -> 12.4 us
  Pallas kernels: 17.6 us -> 21.5 us
    ppermute x14 -> x16, waiting for transfers between devices: 2.01 us -> 21.9 us  [the longest x15 21.9 us: turn(): return [lax.ppermute(v, axis, ring(size, s)) for s in range(1, size)]]
    ppermute x12 -> x6, starting transfers between devices: 34.4 us -> 20.3 us  [across(): return lax.ppermute(v, 'z', [(i, i ^ bit) for i in range(8)])]
    ppermute x12 -> x6, waiting for transfers between devices: 46 us -> 32.6 us  [across(): return lax.ppermute(v, 'z', [(i, i ^ bit) for i in range(8)])]
    pallas_call x1, Pallas kernels: 1.61 us -> 8.26 us  [body(): call(remote_kernel, [jax.ShapeDtypeStruct((4 * rows + 48, 128), bf16)] *...]
    ppermute x1, waiting for transfers between devices: 0.01 us -> 6.56 us  [body(): q2 = lax.ppermute(q0, 'x', [(i, i - 2) for i in range(2, nx)])]
    unnamed x27 -> x44, local copies, waits for them, and re-layouts: 4.04 us -> 9.16 us
    pallas_call x1, Pallas kernels: 7.13 us -> 2.07 us  [body(): call(functools.partial(pair_kernel, panel), [jax.ShapeDtypeStruct((2 * ro...]
    ppermute x4 -> x2, starting transfers between devices: 10.3 us -> 5.63 us  [body(): other = [lax.ppermute(v, 'c', swap) for v in mine]]
  transfers between devices with their start and end apart: 37 -> 31, of which waited for: 10 -> 13; matrix products, arithmetic and copies ran while one was open for 5% -> 5% of each run, Pallas kernels for 6% -> 5%
where the time goes in v4:
time: 219 us; the launch traced here: 217 us
  starting transfers between devices  102 us (47%)
  waiting for transfers between devices  65.8 us (30%)
  Pallas kernels  21.5 us (10%)
  local copies, waits for them, and re-layouts  12.4 us (6%)
  other arithmetic  8.07 us (4%)
  blocking collectives  3.45 us (2%)
  between operations  3.36 us (2%)
    ppermute x15, starting transfers between devices, turn(): return [lax.ppermute(v, axis, ring(size, s)) for s in range(1, size)]  44.3 us
    ppermute x6, waiting for transfers between devices, across(): return lax.ppermute(v, 'z', [(i, i ^ bit) for i in range(8)])  32.6 us
    ppermute x15, waiting for transfers between devices, turn(): return [lax.ppermute(v, axis, ring(size, s)) for s in range(1, size)]  21.9 us
    ppermute x6, starting transfers between devices, across(): return lax.ppermute(v, 'z', [(i, i ^ bit) for i in range(8)])  20.3 us
    ppermute x1, starting transfers between devices, body(): far = lax.ppermute(hidden, 'w', swap)  15.4 us
    unnamed x44, local copies, waits for them, and re-layouts  9.16 us
    pallas_call x1, Pallas kernels, body(): call(remote_kernel, [jax.ShapeDtypeStruct((4 * rows + 48, 128), bf16)] *...  8.26 us
    ppermute x1, waiting for transfers between devices, body(): q2 = lax.ppermute(q0, 'x', [(i, i - 2) for i in range(2, nx)])  6.56 us
  transfers between devices with their start and end apart: 31, of which 13 were waited for; matrix products, arithmetic and copies ran while one was open for 5% of the time, Pallas kernels for 5%

profile of v4, /device:TPU:1, one launch (start us, length us, event | category | flops | bytes accessed | tf_op | source)
XLA Modules:
  0.0 216.7 jit_solution(2038128805090581100)
XLA Ops:
  0.6 4.2 %collective-permute-start.2 = (bf16[192,640]{1,0:T(8,128)(2,1)}, bf16[192,640]{1,0:T(8,128)(2,1)S(1)}, u32[]{:S(2)}, u32[]{:S(2)}) collective-permute-start(bf16[192,640]{1,0:T(8,128)(2,1)} %param.7), channel_id=1, source_target_pairs={{0,2},{2,4},{4,6},{6,0},{1,3},{3,5},{5,7},{7,1},{8,10},{10,12},{12... | collective-permute-start | bytes 737288 | tf_op jit(solution)/shard_map/ppermute | solution.py:260
  4.8 15.4 %collective-permute-start = (bf16[192,640]{1,0:T(8,128)(2,1)}, bf16[192,640]{1,0:T(8,128)(2,1)S(1)}, u32[]{:S(2)}, u32[]{:S(2)}) collective-permute-start(bf16[192,640]{1,0:T(8,128)(2,1)} %param.7), channel_id=1, source_target_pairs={{0,1},{1,0},{2,3},{3,2},{4,5},{5,4},{6,7},{7,6},{8,9},{9,8},{10,11... | collective-permute-start | bytes 737288 | tf_op jit(solution)/shard_map/ppermute | solution.py:278
  20.3 3.4 %collective-permute-start.4 = (bf16[192,640]{1,0:T(8,128)(2,1)}, bf16[192,640]{1,0:T(8,128)(2,1)S(1)}, u32[]{:S(2)}, u32[]{:S(2)}) collective-permute-start(bf16[192,640]{1,0:T(8,128)(2,1)} %param.7), channel_id=1, source_target_pairs={{0,6},{2,0},{4,2},{6,4},{1,7},{3,1},{5,3},{7,5},{8,14},{10,8},{12,... | collective-permute-start | bytes 737288 | tf_op jit(solution)/shard_map/ppermute | solution.py:260
  23.6 3.5 %collective-permute-start.3 = (bf16[192,640]{1,0:T(8,128)(2,1)}, bf16[192,640]{1,0:T(8,128)(2,1)S(1)}, u32[]{:S(2)}, u32[]{:S(2)}) collective-permute-start(bf16[192,640]{1,0:T(8,128)(2,1)} %param.7), channel_id=1, source_target_pairs={{0,4},{2,6},{4,0},{6,2},{1,5},{3,7},{5,1},{7,3},{8,12},{10,14},{12... | collective-permute-start | bytes 737288 | tf_op jit(solution)/shard_map/ppermute | solution.py:260
  28.8 3.4 %all-gather = bf16[192,768]{1,0:T(8,128)(2,1)S(1)} all-gather(bf16[96,768]{1,0:T(8,128)(2,1)S(1)} %fusion.2), channel_id=2, replica_groups=mesh['x'=4,'z'=8,'c'=2,'y'=4,'w'=2] {'c'}, dimensions={0}, use_global_device_ids=true | all-gather | bytes 442368 | tf_op jit(solution)/shard_map/all_gather | solution.py:264
  32.4 4.0 %collective-permute-start.1 = (bf16[1,176,384]{2,1,0:T(8,128)(2,1)S(1)}, bf16[1,176,384]{2,1,0:T(8,128)(2,1)S(1)}, u32[]{:S(2)}, u32[]{:S(2)}) collective-permute-start(bf16[1,176,384]{2,1,0:T(8,128)(2,1)S(1)} %fusion.4), channel_id=1, source_target_pairs={{0,64},{16,80},{32,96},{48,112},{64,0},{80,16},{96,32},{112,48},{1... | collective-permute-start | bytes 405512 | tf_op jit(solution)/shard_map/ppermute | solution.py:242
  36.4 18.4 %collective-permute-done.1 = bf16[1,176,384]{2,1,0:T(8,128)(2,1)S(1)} collective-permute-done((bf16[1,176,384]{2,1,0:T(8,128)(2,1)S(1)}, bf16[1,176,384]{2,1,0:T(8,128)(2,1)S(1)}, u32[]{:S(2)}, u32[]{:S(2)}) %collective-permute-start.1) | collective-permute-done | bytes 135200 | tf_op jit(solution)/shard_map/ppermute | solution.py:242
  59.4 3.4 %collective-permute-start.9 = (bf16[192,640]{1,0:T(8,128)(2,1)S(1)}, bf16[192,640]{1,0:T(8,128)(2,1)S(1)}, u32[]{:S(2)}, u32[]{:S(2)}) collective-permute-start(bf16[192,640]{1,0:T(8,128)(2,1)S(1)} %collective-permute-done), channel_id=1, source_target_pairs={{0,6},{2,0},{4,2},{6,4},{1,7},{3,1},{5,3},{7,5},{8,14},{10,8},{12,... | collective-permute-start | bytes 737288 | tf_op jit(solution)/shard_map/ppermute | solution.py:260
  62.7 3.5 %collective-permute-start.8 = (bf16[192,640]{1,0:T(8,128)(2,1)S(1)}, bf16[192,640]{1,0:T(8,128)(2,1)S(1)}, u32[]{:S(2)}, u32[]{:S(2)}) collective-permute-start(bf16[192,640]{1,0:T(8,128)(2,1)S(1)} %collective-permute-done), channel_id=1, source_target_pairs={{0,4},{2,6},{4,0},{6,2},{1,5},{3,7},{5,1},{7,3},{8,12},{10,14},{12... | collective-permute-start | bytes 737288 | tf_op jit(solution)/shard_map/ppermute | solution.py:260
  68.9 4.5 %collective-permute-done.8 = bf16[192,640]{1,0:T(8,128)(2,1)S(1)} collective-permute-done((bf16[192,640]{1,0:T(8,128)(2,1)S(1)}, bf16[192,640]{1,0:T(8,128)(2,1)S(1)}, u32[]{:S(2)}, u32[]{:S(2)}) %collective-permute-start.8) | collective-permute-done | bytes 245792 | tf_op jit(solution)/shard_map/ppermute | solution.py:260
  73.4 5.9 %collective-permute-done.7 = bf16[192,640]{1,0:T(8,128)(2,1)S(1)} collective-permute-done((bf16[192,640]{1,0:T(8,128)(2,1)S(1)}, bf16[192,640]{1,0:T(8,128)(2,1)S(1)}, u32[]{:S(2)}, u32[]{:S(2)}) %collective-permute-start.7) | collective-permute-done | bytes 245792 | tf_op jit(solution)/shard_map/ppermute | solution.py:260
  84.2 2.5 %collective-permute-start.10 = (bf16[4,176,384]{2,1,0:T(8,128)(2,1)S(1)}, bf16[4,176,384]{2,1,0:T(8,128)(2,1)S(1)}, u32[]{:S(2)}, u32[]{:S(2)}) collective-permute-start(bf16[4,176,384]{2,1,0:T(8,128)(2,1)S(1)} %pad_maximum_fusion.5), channel_id=1, source_target_pairs={{0,16},{16,0},{32,48},{48,32},{64,80},{80,64},{96,112},{112,96},{1... | collective-permute-start | bytes 1622024 | tf_op jit(solution)/shard_map/ppermute | solution.py:242
  87.3 4.4 %collective-permute-start.14 = (bf16[4,176,128]{2,1,0:T(8,128)(2,1)S(1)}, bf16[4,176,128]{2,1,0:T(8,128)(2,1)S(1)}, u32[]{:S(2)}, u32[]{:S(2)}) collective-permute-start(bf16[4,176,128]{2,1,0:T(8,128)(2,1)S(1)} %slice.106.refs_0_), channel_id=1, source_target_pairs={{0,384},{128,0},{256,128},{384,256},{1,385},{129,1},{257,129},{385... | collective-permute-start | bytes 540680 | tf_op jit(solution)/shard_map/ppermute | solution.py:260
  91.7 2.4 %collective-permute-start.13 = (bf16[4,176,128]{2,1,0:T(8,128)(2,1)S(1)}, bf16[4,176,128]{2,1,0:T(8,128)(2,1)S(1)}, u32[]{:S(2)}, u32[]{:S(2)}) collective-permute-start(bf16[4,176,128]{2,1,0:T(8,128)(2,1)S(1)} %slice.106.refs_0_), channel_id=1, source_target_pairs={{0,256},{128,384},{256,0},{384,128},{1,257},{129,385},{257,1},{385... | collective-permute-start | bytes 540680 | tf_op jit(solution)/shard_map/ppermute | solution.py:260
  94.1 2.5 %collective-permute-start.12 = (bf16[4,176,128]{2,1,0:T(8,128)(2,1)S(1)}, bf16[4,176,128]{2,1,0:T(8,128)(2,1)S(1)}, u32[]{:S(2)}, u32[]{:S(2)}) collective-permute-start(bf16[4,176,128]{2,1,0:T(8,128)(2,1)S(1)} %slice.106.refs_0_), channel_id=1, source_target_pairs={{0,128},{128,256},{256,384},{384,0},{1,129},{129,257},{257,385},{3... | collective-permute-start | bytes 540680 | tf_op jit(solution)/shard_map/ppermute | solution.py:260
  96.7 4.0 %collective-permute-done.13.refs_4_ = bf16[4,176,128]{2,1,0:T(8,128)(2,1)S(1)} collective-permute-done((bf16[4,176,128]{2,1,0:T(8,128)(2,1)S(1)}, bf16[4,176,128]{2,1,0:T(8,128)(2,1)S(1)}, u32[]{:S(2)}, u32[]{:S(2)}) %collective-permute-start.13) | collective-permute-done | bytes 180256 | tf_op jit(solution)/shard_map/ppermute | solution.py:260
  100.6 4.6 %collective-permute-done.12.refs_2_ = bf16[4,176,128]{2,1,0:T(8,128)(2,1)S(1)} collective-permute-done((bf16[4,176,128]{2,1,0:T(8,128)(2,1)S(1)}, bf16[4,176,128]{2,1,0:T(8,128)(2,1)S(1)}, u32[]{:S(2)}, u32[]{:S(2)}) %collective-permute-start.12) | collective-permute-done | bytes 180256 | tf_op jit(solution)/shard_map/ppermute | solution.py:260
  110.3 3.2 %collective-permute-start.15 = (bf16[4,176,128]{2,1,0:T(8,128)(2,1)S(1)}, bf16[4,176,128]{2,1,0:T(8,128)(2,1)S(1)}, u32[]{:S(2)}, u32[]{:S(2)}) collective-permute-start(bf16[4,176,128]{2,1,0:T(8,128)(2,1)S(1)} %slice.86.refs_1_), channel_id=1, source_target_pairs={{0,128},{128,256},{256,384},{384,0},{1,129},{129,257},{257,385},{3... | collective-permute-start | bytes 540680 | tf_op jit(solution)/shard_map/ppermute | solution.py:260
  113.6 3.5 %shard_map.94.normed = bf16[384,5120]{1,0:T(8,128)(2,1)S(1)} custom-call(s32[5]{0:T(128)S(1)} %stack.151.where, f32[1,5120]{1,0:T(1,128)S(1)} %bitcast.87, bf16[4,192,640]{2,1,0:T(8,128)(2,1)S(1)} %pad_maximum_fusion.refs_0_, bf16[4,192,640]{2,1,0:T(8,128)(2,1)S(1)} %pad_maximum_fusion.1.refs_1_, bf16[4,192,640]{2,1,0:T(8,128)(2,1)S(1)} %copy-done.7, ...), custom_call_target="tpu_custom_call" | custom-call | flops 4000000000 | bytes 4194304 | tf_op jit(solution)/shard_map/pallas_call | solution.py:311
  118.9 2.7 %collective-permute-done.15.refs_3_ = bf16[4,176,128]{2,1,0:T(8,128)(2,1)S(1)} collective-permute-done((bf16[4,176,128]{2,1,0:T(8,128)(2,1)S(1)}, bf16[4,176,128]{2,1,0:T(8,128)(2,1)S(1)}, u32[]{:S(2)}, u32[]{:S(2)}) %collective-permute-start.15) | collective-permute-done | bytes 180256 | tf_op jit(solution)/shard_map/ppermute | solution.py:260
  123.5 2.8 %collective-permute-start.22 = (bf16[8,160,256]{2,1,0:T(8,128)(2,1)S(1)}, bf16[8,160,256]{2,1,0:T(8,128)(2,1)}, u32[]{:S(2)}, u32[]{:S(2)}) collective-permute-start(bf16[8,160,256]{2,1,0:T(8,128)(2,1)S(1)} %pad_maximum_fusion.2.refs_0_), channel_id=1, source_target_pairs={{0,256},{128,384},{256,0},{384,128},{1,257},{129,385},{257,1},{385... | collective-permute-start | bytes 1966088 | tf_op jit(solution)/shard_map/ppermute | solution.py:260
  126.3 2.8 %collective-permute-start.21 = (bf16[8,160,256]{2,1,0:T(8,128)(2,1)S(1)}, bf16[8,160,256]{2,1,0:T(8,128)(2,1)}, u32[]{:S(2)}, u32[]{:S(2)}) collective-permute-start(bf16[8,160,256]{2,1,0:T(8,128)(2,1)S(1)} %pad_maximum_fusion.2.refs_0_), channel_id=1, source_target_pairs={{0,128},{128,256},{256,384},{384,0},{1,129},{129,257},{257,385},{3... | collective-permute-start | bytes 1966088 | tf_op jit(solution)/shard_map/ppermute | solution.py:260
  138.3 8.0 %collective-permute-start.18 = (bf16[384,128]{1,0:T(8,128)(2,1)S(1)}, bf16[384,128]{1,0:T(8,128)(2,1)S(1)}, u32[]{:S(2)}, u32[]{:S(2)}) collective-permute-start(bf16[384,128]{1,0:T(8,128)(2,1)S(1)} %shard_map.95), channel_id=1, source_target_pairs={{0,64},{16,80},{32,96},{48,112},{64,0},{80,16},{96,32},{112,48},{1... | collective-permute-start | bytes 294920 | tf_op jit(solution)/shard_map/ppermute | solution.py:242
  150.9 5.0 %collective-permute-done.18 = bf16[384,128]{1,0:T(8,128)(2,1)S(1)} collective-permute-done((bf16[384,128]{1,0:T(8,128)(2,1)S(1)}, bf16[384,128]{1,0:T(8,128)(2,1)S(1)}, u32[]{:S(2)}, u32[]{:S(2)}) %collective-permute-start.18) | collective-permute-done | bytes 98336 | tf_op jit(solution)/shard_map/ppermute | solution.py:242
  157.9 8.7 %collective-permute-done.19 = bf16[2,384,128]{2,1,0:T(8,128)(2,1)S(1)} collective-permute-done((bf16[2,384,128]{2,1,0:T(8,128)(2,1)S(1)}, bf16[2,384,128]{2,1,0:T(8,128)(2,1)S(1)}, u32[]{:S(2)}, u32[]{:S(2)}) %collective-permute-start.19) | collective-permute-done | bytes 196640 | tf_op jit(solution)/shard_map/ppermute | solution.py:242
  173.1 3.1 %shard_map.96 = bf16[2,2,192,128]{3,2,1,0:T(8,128)(2,1)S(1)} custom-call(s32[64]{0:T(128)S(1)} %broadcast_multiply_fusion.offsets, s32[5]{0:T(128)S(1)} %stack.151.where, bf16[384,5120]{1,0:T(8,128)(2,1)S(1)} %copy-done.12, f32[1,128]{1,0:T(1,128)S(1)} %bitcast.89, f32[384,128]{1,0:T(8,128)S(1)} %get-tuple-element.72.cosine, ...), custom_call_target="tpu_custom_call" | custom-call | flops 4000000000 | bytes 4194304 | tf_op jit(solution)/shard_map/pallas_call | solution.py:369
  178.7 3.2 %collective-permute-start.28 = (bf16[4,384,128]{2,1,0:T(8,128)(2,1)S(1)}, bf16[4,384,128]{2,1,0:T(8,128)(2,1)S(1)}, u32[]{:S(2)}, u32[]{:S(2)}) collective-permute-start(bf16[4,384,128]{2,1,0:T(8,128)(2,1)S(1)} %collective-permute-done.27.refs_1_), channel_id=1, source_target_pairs={{0,8},{8,0},{1,9},{9,1},{2,10},{10,2},{3,11},{11,3},{4,12},{12,4},... | collective-permute-start | bytes 1179656 | tf_op jit(solution)/shard_map/ppermute | solution.py:366
  185.4 6.6 %collective-permute-done.26.far = bf16[768,128]{1,0:T(8,128)(2,1)S(1)} collective-permute-done((bf16[768,128]{1,0:T(8,128)(2,1)S(1)}, bf16[768,128]{1,0:T(8,128)(2,1)S(1)}, u32[]{:S(2)}, u32[]{:S(2)}) %collective-permute-start.26) | collective-permute-done | bytes 196640 | tf_op jit(solution)/shard_map/ppermute | solution.py:383
  191.9 8.3 %shard_map.97 = (bf16[816,128]{1,0:T(8,128)(2,1)S(1)}, bf16[816,128]{1,0:T(8,128)(2,1)S(1)}, bf16[3072,128]{1,0:T(8,128)(2,1)S(1)}, bf16[3072,256]{1,0:T(8,128)(2,1)S(1)}) custom-call(s32[12]{0:T(128)S(1)} %stack.185.where, s32[3,192,1]{2,1,0:T(8,128)S(1)} %broadcast_subtract_fusion.begins, bf16[768,128]{1,0:T(8,128)(2,1)S(1)} %collective-permute-done.25.near, ...), custom_call_target="tpu_custom_call" | custom-call | flops 10000000000 | bytes 4194304 | tf_op jit(solution)/shard_map/pallas_call | solution.py:386
  200.2 5.9 %collective-permute-start.29 = (bf16[816,128]{1,0:T(8,128)(2,1)S(1)}, bf16[816,128]{1,0:T(8,128)(2,1)S(1)}, u32[]{:S(2)}, u32[]{:S(2)}) collective-permute-start(bf16[816,128]{1,0:T(8,128)(2,1)S(1)} %get-tuple-element.53), channel_id=1, source_target_pairs={{0,128},{128,256},{256,384},{1,129},{129,257},{257,385},{2,130},{1... | collective-permute-start | bytes 626696 | tf_op jit(solution)/shard_map/ppermute | solution.py:395
  207.4 2.5 %shard_map.98 = (f32[768,128]{1,0:T(8,128)S(1)}, f32[768,1]{1,0:T(8,128)S(1)}) custom-call(s32[12]{0:T(128)S(1)} %stack.185.where, s32[3,192,1]{2,1,0:T(8,128)S(1)} %broadcast_subtract_fusion.begins, bf16[768,128]{1,0:T(8,128)(2,1)S(1)} %bitcast.86, bf16[3072,128]{1,0:T(8,128)(2,1)S(1)} %get-tuple-element.49.keys, bf16[3072,256]{1,0:T(8,128)(2,1)S(1)} %get-tuple-element.50.values), custom_call_target="tpu_custom_call" | custom-call | flops 10000000000 | bytes 4194304 | tf_op jit(solution)/shard_map/pallas_call | solution.py:397
  210.1 4.5 %collective-permute-done.30.r2 = bf16[816,128]{1,0:T(8,128)(2,1)S(1)} collective-permute-done((bf16[816,128]{1,0:T(8,128)(2,1)S(1)}, bf16[816,128]{1,0:T(8,128)(2,1)S(1)}, u32[]{:S(2)}, u32[]{:S(2)}) %collective-permute-start.30) | collective-permute-done | bytes 208928 | tf_op jit(solution)/shard_map/ppermute | solution.py:396
  (133 shorter events, 52.7 us)
Async XLA Ops:
  0.6 54.2 %copy-start.14 = (bf16[192,640]{1,0:T(8,128)(2,1)S(1)}, bf16[192,640]{1,0:T(8,128)(2,1)}, u32[]{:S(2)}) copy-start(bf16[192,640]{1,0:T(8,128)(2,1)} %param.7) | copy-start | bytes 737284
  0.6 54.1 %collective-permute-start.2 = (bf16[192,640]{1,0:T(8,128)(2,1)}, bf16[192,640]{1,0:T(8,128)(2,1)S(1)}, u32[]{:S(2)}, u32[]{:S(2)}) collective-permute-start(bf16[192,640]{1,0:T(8,128)(2,1)} %param.7), channel_id=1, source_target_pairs={{0,2},{2,4},{4,6},{6,0},{1,3},{3,5},{5,7},{7,1},{8,10},{10,12},{12... | collective-permute-start | bytes 737288 | tf_op jit(solution)/shard_map/ppermute | solution.py:260
  4.8 50.0 %collective-permute-start = (bf16[192,640]{1,0:T(8,128)(2,1)}, bf16[192,640]{1,0:T(8,128)(2,1)S(1)}, u32[]{:S(2)}, u32[]{:S(2)}) collective-permute-start(bf16[192,640]{1,0:T(8,128)(2,1)} %param.7), channel_id=1, source_target_pairs={{0,1},{1,0},{2,3},{3,2},{4,5},{5,4},{6,7},{7,6},{8,9},{9,8},{10,11... | collective-permute-start | bytes 737288 | tf_op jit(solution)/shard_map/ppermute | solution.py:278
  20.3 34.5 %collective-permute-start.4 = (bf16[192,640]{1,0:T(8,128)(2,1)}, bf16[192,640]{1,0:T(8,128)(2,1)S(1)}, u32[]{:S(2)}, u32[]{:S(2)}) collective-permute-start(bf16[192,640]{1,0:T(8,128)(2,1)} %param.7), channel_id=1, source_target_pairs={{0,6},{2,0},{4,2},{6,4},{1,7},{3,1},{5,3},{7,5},{8,14},{10,8},{12,... | collective-permute-start | bytes 737288 | tf_op jit(solution)/shard_map/ppermute | solution.py:260
  23.6 31.2 %collective-permute-start.3 = (bf16[192,640]{1,0:T(8,128)(2,1)}, bf16[192,640]{1,0:T(8,128)(2,1)S(1)}, u32[]{:S(2)}, u32[]{:S(2)}) collective-permute-start(bf16[192,640]{1,0:T(8,128)(2,1)} %param.7), channel_id=1, source_target_pairs={{0,4},{2,6},{4,0},{6,2},{1,5},{3,7},{5,1},{7,3},{8,12},{10,14},{12... | collective-permute-start | bytes 737288 | tf_op jit(solution)/shard_map/ppermute | solution.py:260
  32.4 22.4 %collective-permute-start.1 = (bf16[1,176,384]{2,1,0:T(8,128)(2,1)S(1)}, bf16[1,176,384]{2,1,0:T(8,128)(2,1)S(1)}, u32[]{:S(2)}, u32[]{:S(2)}) collective-permute-start(bf16[1,176,384]{2,1,0:T(8,128)(2,1)S(1)} %fusion.4), channel_id=1, source_target_pairs={{0,64},{16,80},{32,96},{48,112},{64,0},{80,16},{96,32},{112,48},{1... | collective-permute-start | bytes 405512 | tf_op jit(solution)/shard_map/ppermute | solution.py:242
  55.0 24.3 %collective-permute-start.6 = (bf16[4,192,640]{2,1,0:T(8,128)(2,1)S(1)}, bf16[4,192,640]{2,1,0:T(8,128)(2,1)S(1)}, u32[]{:S(2)}, u32[]{:S(2)}) collective-permute-start(bf16[4,192,640]{2,1,0:T(8,128)(2,1)S(1)} %pad_maximum_fusion.refs_0_), channel_id=1, source_target_pairs={{0,8},{8,0},{1,9},{9,1},{2,10},{10,2},{3,11},{11,3},{4,12},{12,4},... | collective-permute-start | bytes 2949128 | tf_op jit(solution)/shard_map/ppermute | solution.py:287
  57.4 21.8 %collective-permute-start.5 = (bf16[2,176,384]{2,1,0:T(8,128)(2,1)S(1)}, bf16[2,176,384]{2,1,0:T(8,128)(2,1)}, u32[]{:S(2)}, u32[]{:S(2)}) collective-permute-start(bf16[2,176,384]{2,1,0:T(8,128)(2,1)S(1)} %pad_maximum_fusion.6), channel_id=1, source_target_pairs={{0,32},{16,48},{32,0},{48,16},{64,96},{80,112},{96,64},{112,80},{1... | collective-permute-start | bytes 811016 | tf_op jit(solution)/shard_map/ppermute | solution.py:242
  59.4 9.5 %collective-permute-start.9 = (bf16[192,640]{1,0:T(8,128)(2,1)S(1)}, bf16[192,640]{1,0:T(8,128)(2,1)S(1)}, u32[]{:S(2)}, u32[]{:S(2)}) collective-permute-start(bf16[192,640]{1,0:T(8,128)(2,1)S(1)} %collective-permute-done), channel_id=1, source_target_pairs={{0,6},{2,0},{4,2},{6,4},{1,7},{3,1},{5,3},{7,5},{8,14},{10,8},{12,... | collective-permute-start | bytes 737288 | tf_op jit(solution)/shard_map/ppermute | solution.py:260
  62.7 10.6 %collective-permute-start.8 = (bf16[192,640]{1,0:T(8,128)(2,1)S(1)}, bf16[192,640]{1,0:T(8,128)(2,1)S(1)}, u32[]{:S(2)}, u32[]{:S(2)}) collective-permute-start(bf16[192,640]{1,0:T(8,128)(2,1)S(1)} %collective-permute-done), channel_id=1, source_target_pairs={{0,4},{2,6},{4,0},{6,2},{1,5},{3,7},{5,1},{7,3},{8,12},{10,14},{12... | collective-permute-start | bytes 737288 | tf_op jit(solution)/shard_map/ppermute | solution.py:260
  66.3 13.0 %collective-permute-start.7 = (bf16[192,640]{1,0:T(8,128)(2,1)S(1)}, bf16[192,640]{1,0:T(8,128)(2,1)S(1)}, u32[]{:S(2)}, u32[]{:S(2)}) collective-permute-start(bf16[192,640]{1,0:T(8,128)(2,1)S(1)} %collective-permute-done), channel_id=1, source_target_pairs={{0,2},{2,4},{4,6},{6,0},{1,3},{3,5},{5,7},{7,1},{8,10},{10,12},{12... | collective-permute-start | bytes 737288 | tf_op jit(solution)/shard_map/ppermute | solution.py:260
  80.4 24.8 %collective-permute-start.11 = (bf16[4,192,640]{2,1,0:T(8,128)(2,1)S(1)}, bf16[4,192,640]{2,1,0:T(8,128)(2,1)}, u32[]{:S(2)}, u32[]{:S(2)}) collective-permute-start(bf16[4,192,640]{2,1,0:T(8,128)(2,1)S(1)} %pad_maximum_fusion.1.refs_1_), channel_id=1, source_target_pairs={{0,8},{8,0},{1,9},{9,1},{2,10},{10,2},{3,11},{11,3},{4,12},{12,4},... | collective-permute-start | bytes 2949128 | tf_op jit(solution)/shard_map/ppermute | solution.py:293
  84.2 21.1 %collective-permute-start.10 = (bf16[4,176,384]{2,1,0:T(8,128)(2,1)S(1)}, bf16[4,176,384]{2,1,0:T(8,128)(2,1)S(1)}, u32[]{:S(2)}, u32[]{:S(2)}) collective-permute-start(bf16[4,176,384]{2,1,0:T(8,128)(2,1)S(1)} %pad_maximum_fusion.5), channel_id=1, source_target_pairs={{0,16},{16,0},{32,48},{48,32},{64,80},{80,64},{96,112},{112,96},{1... | collective-permute-start | bytes 1622024 | tf_op jit(solution)/shard_map/ppermute | solution.py:242
  87.3 9.4 %collective-permute-start.14 = (bf16[4,176,128]{2,1,0:T(8,128)(2,1)S(1)}, bf16[4,176,128]{2,1,0:T(8,128)(2,1)S(1)}, u32[]{:S(2)}, u32[]{:S(2)}) collective-permute-start(bf16[4,176,128]{2,1,0:T(8,128)(2,1)S(1)} %slice.106.refs_0_), channel_id=1, source_target_pairs={{0,384},{128,0},{256,128},{384,256},{1,385},{129,1},{257,129},{385... | collective-permute-start | bytes 540680 | tf_op jit(solution)/shard_map/ppermute | solution.py:260
  91.7 8.9 %collective-permute-start.13 = (bf16[4,176,128]{2,1,0:T(8,128)(2,1)S(1)}, bf16[4,176,128]{2,1,0:T(8,128)(2,1)S(1)}, u32[]{:S(2)}, u32[]{:S(2)}) collective-permute-start(bf16[4,176,128]{2,1,0:T(8,128)(2,1)S(1)} %slice.106.refs_0_), channel_id=1, source_target_pairs={{0,256},{128,384},{256,0},{384,128},{1,257},{129,385},{257,1},{385... | collective-permute-start | bytes 540680 | tf_op jit(solution)/shard_map/ppermute | solution.py:260
  94.1 11.1 %collective-permute-start.12 = (bf16[4,176,128]{2,1,0:T(8,128)(2,1)S(1)}, bf16[4,176,128]{2,1,0:T(8,128)(2,1)S(1)}, u32[]{:S(2)}, u32[]{:S(2)}) collective-permute-start(bf16[4,176,128]{2,1,0:T(8,128)(2,1)S(1)} %slice.106.refs_0_), channel_id=1, source_target_pairs={{0,128},{128,256},{256,384},{384,0},{1,129},{129,257},{257,385},{3... | collective-permute-start | bytes 540680 | tf_op jit(solution)/shard_map/ppermute | solution.py:260
  106.3 24.2 %collective-permute-start.17 = (bf16[4,176,128]{2,1,0:T(8,128)(2,1)S(1)}, bf16[4,176,128]{2,1,0:T(8,128)(2,1)S(1)}, u32[]{:S(2)}, u32[]{:S(2)}) collective-permute-start(bf16[4,176,128]{2,1,0:T(8,128)(2,1)S(1)} %slice.86.refs_1_), channel_id=1, source_target_pairs={{0,384},{128,0},{256,128},{384,256},{1,385},{129,1},{257,129},{385... | collective-permute-start | bytes 540680 | tf_op jit(solution)/shard_map/ppermute | solution.py:260
  108.2 21.6 %collective-permute-start.16 = (bf16[4,176,128]{2,1,0:T(8,128)(2,1)S(1)}, bf16[4,176,128]{2,1,0:T(8,128)(2,1)S(1)}, u32[]{:S(2)}, u32[]{:S(2)}) collective-permute-start(bf16[4,176,128]{2,1,0:T(8,128)(2,1)S(1)} %slice.86.refs_1_), channel_id=1, source_target_pairs={{0,256},{128,384},{256,0},{384,128},{1,257},{129,385},{257,1},{385... | collective-permute-start | bytes 540680 | tf_op jit(solution)/shard_map/ppermute | solution.py:260
  110.3 11.3 %collective-permute-start.15 = (bf16[4,176,128]{2,1,0:T(8,128)(2,1)S(1)}, bf16[4,176,128]{2,1,0:T(8,128)(2,1)S(1)}, u32[]{:S(2)}, u32[]{:S(2)}) collective-permute-start(bf16[4,176,128]{2,1,0:T(8,128)(2,1)S(1)} %slice.86.refs_1_), channel_id=1, source_target_pairs={{0,128},{128,256},{256,384},{384,0},{1,129},{129,257},{257,385},{3... | collective-permute-start | bytes 540680 | tf_op jit(solution)/shard_map/ppermute | solution.py:260
  121.6 49.3 %collective-permute-start.23 = (bf16[8,160,256]{2,1,0:T(8,128)(2,1)S(1)}, bf16[8,160,256]{2,1,0:T(8,128)(2,1)}, u32[]{:S(2)}, u32[]{:S(2)}) collective-permute-start(bf16[8,160,256]{2,1,0:T(8,128)(2,1)S(1)} %pad_maximum_fusion.2.refs_0_), channel_id=1, source_target_pairs={{0,384},{128,0},{256,128},{384,256},{1,385},{129,1},{257,129},{385... | collective-permute-start | bytes 1966088 | tf_op jit(solution)/shard_map/ppermute | solution.py:260
  123.5 47.4 %collective-permute-start.22 = (bf16[8,160,256]{2,1,0:T(8,128)(2,1)S(1)}, bf16[8,160,256]{2,1,0:T(8,128)(2,1)}, u32[]{:S(2)}, u32[]{:S(2)}) collective-permute-start(bf16[8,160,256]{2,1,0:T(8,128)(2,1)S(1)} %pad_maximum_fusion.2.refs_0_), channel_id=1, source_target_pairs={{0,256},{128,384},{256,0},{384,128},{1,257},{129,385},{257,1},{385... | collective-permute-start | bytes 1966088 | tf_op jit(solution)/shard_map/ppermute | solution.py:260
  126.3 44.6 %collective-permute-start.21 = (bf16[8,160,256]{2,1,0:T(8,128)(2,1)S(1)}, bf16[8,160,256]{2,1,0:T(8,128)(2,1)}, u32[]{:S(2)}, u32[]{:S(2)}) collective-permute-start(bf16[8,160,256]{2,1,0:T(8,128)(2,1)S(1)} %pad_maximum_fusion.2.refs_0_), channel_id=1, source_target_pairs={{0,128},{128,256},{256,384},{384,0},{1,129},{129,257},{257,385},{3... | collective-permute-start | bytes 1966088 | tf_op jit(solution)/shard_map/ppermute | solution.py:260
  138.3 17.6 %collective-permute-start.18 = (bf16[384,128]{1,0:T(8,128)(2,1)S(1)}, bf16[384,128]{1,0:T(8,128)(2,1)S(1)}, u32[]{:S(2)}, u32[]{:S(2)}) collective-permute-start(bf16[384,128]{1,0:T(8,128)(2,1)S(1)} %shard_map.95), channel_id=1, source_target_pairs={{0,64},{16,80},{32,96},{48,112},{64,0},{80,16},{96,32},{112,48},{1... | collective-permute-start | bytes 294920 | tf_op jit(solution)/shard_map/ppermute | solution.py:242
  155.9 10.7 %collective-permute-start.19 = (bf16[2,384,128]{2,1,0:T(8,128)(2,1)S(1)}, bf16[2,384,128]{2,1,0:T(8,128)(2,1)S(1)}, u32[]{:S(2)}, u32[]{:S(2)}) collective-permute-start(bf16[2,384,128]{2,1,0:T(8,128)(2,1)S(1)} %pad_maximum_fusion.9), channel_id=1, source_target_pairs={{0,32},{16,48},{32,0},{48,16},{64,96},{80,112},{96,64},{112,80},{1... | collective-permute-start | bytes 589832 | tf_op jit(solution)/shard_map/ppermute | solution.py:242
  166.6 12.1 %collective-permute-start.27 = (bf16[4,384,128]{2,1,0:T(8,128)(2,1)S(1)}, bf16[4,384,128]{2,1,0:T(8,128)(2,1)S(1)}, u32[]{:S(2)}, u32[]{:S(2)}) collective-permute-start(bf16[4,384,128]{2,1,0:T(8,128)(2,1)S(1)} %constant_dynamic-update-slice_fusion.8.refs_0_), channel_id=1, source_target_pairs={{0,16},{16,0},{32,48},{48,32},{64,80},{80,64},{96,112},{112,96},{1... | collective-permute-start | bytes 1179656 | tf_op jit(solution)/shard_map/ppermute | solution.py:242
  168.5 16.1 %collective-permute-start.20 = (bf16[4,384,128]{2,1,0:T(8,128)(2,1)S(1)}, bf16[4,384,128]{2,1,0:T(8,128)(2,1)S(1)}, u32[]{:S(2)}, u32[]{:S(2)}) collective-permute-start(bf16[4,384,128]{2,1,0:T(8,128)(2,1)S(1)} %constant_dynamic-update-slice_fusion.8.refs_0_), channel_id=1, source_target_pairs={{0,8},{8,0},{1,9},{9,1},{2,10},{10,2},{3,11},{11,3},{4,12},{12,4},... | collective-permute-start | bytes 1179656 | tf_op jit(solution)/shard_map/ppermute | solution.py:366
  176.2 5.7 %collective-permute-start.24 = (bf16[2,192,128]{2,1,0:T(8,128)(2,1)S(1)}, bf16[2,192,128]{2,1,0:T(8,128)(2,1)S(1)}, u32[]{:S(2)}, u32[]{:S(2)}) collective-permute-start(bf16[2,192,128]{2,1,0:T(8,128)(2,1)S(1)} %get-tuple-element.58), channel_id=1, source_target_pairs={{0,8},{8,0},{1,9},{9,1},{2,10},{10,2},{3,11},{11,3},{4,12},{12,4},... | collective-permute-start | bytes 294920 | tf_op jit(solution)/shard_map/ppermute | solution.py:380
  178.7 13.2 %collective-permute-start.28 = (bf16[4,384,128]{2,1,0:T(8,128)(2,1)S(1)}, bf16[4,384,128]{2,1,0:T(8,128)(2,1)S(1)}, u32[]{:S(2)}, u32[]{:S(2)}) collective-permute-start(bf16[4,384,128]{2,1,0:T(8,128)(2,1)S(1)} %collective-permute-done.27.refs_1_), channel_id=1, source_target_pairs={{0,8},{8,0},{1,9},{9,1},{2,10},{10,2},{3,11},{11,3},{4,12},{12,4},... | collective-permute-start | bytes 1179656 | tf_op jit(solution)/shard_map/ppermute | solution.py:366
  182.0 9.9 %collective-permute-start.26 = (bf16[768,128]{1,0:T(8,128)(2,1)S(1)}, bf16[768,128]{1,0:T(8,128)(2,1)S(1)}, u32[]{:S(2)}, u32[]{:S(2)}) collective-permute-start(bf16[768,128]{1,0:T(8,128)(2,1)S(1)} %bitcast.84), channel_id=1, source_target_pairs={{256,0},{384,128},{257,1},{385,129},{258,2},{386,130},{259,3},{387... | collective-permute-start | bytes 589832 | tf_op jit(solution)/shard_map/ppermute | solution.py:383
  183.3 8.6 %collective-permute-start.25 = (bf16[768,128]{1,0:T(8,128)(2,1)S(1)}, bf16[768,128]{1,0:T(8,128)(2,1)S(1)}, u32[]{:S(2)}, u32[]{:S(2)}) collective-permute-start(bf16[768,128]{1,0:T(8,128)(2,1)S(1)} %bitcast.85), channel_id=1, source_target_pairs={{128,0},{256,128},{384,256},{129,1},{257,129},{385,257},{130,2},{2... | collective-permute-start | bytes 589832 | tf_op jit(solution)/shard_map/ppermute | solution.py:382
  200.2 9.9 %collective-permute-start.29 = (bf16[816,128]{1,0:T(8,128)(2,1)S(1)}, bf16[816,128]{1,0:T(8,128)(2,1)S(1)}, u32[]{:S(2)}, u32[]{:S(2)}) collective-permute-start(bf16[816,128]{1,0:T(8,128)(2,1)S(1)} %get-tuple-element.53), channel_id=1, source_target_pairs={{0,128},{128,256},{256,384},{1,129},{129,257},{257,385},{2,130},{1... | collective-permute-start | bytes 626696 | tf_op jit(solution)/shard_map/ppermute | solution.py:395
  206.1 8.6 %collective-permute-start.30 = (bf16[816,128]{1,0:T(8,128)(2,1)S(1)}, bf16[816,128]{1,0:T(8,128)(2,1)S(1)}, u32[]{:S(2)}, u32[]{:S(2)}) collective-permute-start(bf16[816,128]{1,0:T(8,128)(2,1)S(1)} %get-tuple-element.54), channel_id=1, source_target_pairs={{0,256},{128,384},{1,257},{129,385},{2,258},{130,386},{3,259},{131... | collective-permute-start | bytes 626696 | tf_op jit(solution)/shard_map/ppermute | solution.py:396
  (16 other events, 191.2 us)

commit v5 on v4

--- a/solution.py
+++ b/solution.py
@@ -18,15 +18,16 @@
 VMEM_LIMIT = 20 * 1024 * 1024
 
 
-def call(kernel, out_shape, n_smem, n_vmem, scratch=(), flops=0):
+def call(kernel, out_shape, n_smem, n_vmem, scratch=(), flops=0, n_hbm=0, out_hbm=False):
     specs = [pl.BlockSpec(memory_space=pltpu.SMEM)] * n_smem
+    specs += [pl.BlockSpec(memory_space=pltpu.HBM)] * n_hbm
     specs += [pl.BlockSpec(memory_space=pltpu.VMEM)] * n_vmem
-    n_out = len(out_shape)
+    out = pl.BlockSpec(memory_space=pltpu.HBM if out_hbm else pltpu.VMEM)
     return pl.pallas_call(
         kernel,
         out_shape=out_shape,
         in_specs=specs,
-        out_specs=[pl.BlockSpec(memory_space=pltpu.VMEM)] * n_out,
+        out_specs=[out] * len(out_shape),
         scratch_shapes=list(scratch),
         compiler_params=pltpu.CompilerParams(vmem_limit_bytes=VMEM_LIMIT),
         cost_estimate=pl.CostEstimate(flops=flops, bytes_accessed=4 << 20, transcendentals=0),
@@ -42,22 +43,16 @@
     return v * cosine + pltpu.roll(v, 64, 1) * sine
 
 
-def collect(offsets, where, blocks, weights, panel):
-    per = blocks[0].shape[0]
-    parts = len(PEER) // per
-    nx = len(blocks) // parts
-    for s in range(nx):
-        source = lax.rem(where[2] + nx - s, nx)
-        for k, peer in enumerate(PEER):
-            for c in range(2):
-                slot = source * (2 * len(PEER)) + (where[1] ^ peer) * 2 + c
-                first = pl.multiple_of(offsets[slot], 16)
-                block = blocks[s * parts + k // per]
-                weights[pl.ds(first, panel), :] = block[k % per, c * panel : (c + 1) * panel, :]
+def collect(offsets, block, source, weights, panel):
+    for k in range(block.shape[0]):
+        for c in range(2):
+            slot = (source * block.shape[0] + k) * 2 + c
+            first = pl.multiple_of(offsets[slot], 16)
+            weights[pl.ds(first, panel), :] = block[k, c * panel : (c + 1) * panel, :]
 
 
 def norm_kernel(where, norm_gain, *refs):
-    hidden, normed = refs[:-1], refs[-1]
+    hidden, out, normed, sem = refs[:-3], refs[-3], refs[-2], refs[-1]
     ny, rows, width = hidden[0].shape
     for side in range(2):
         first = pl.multiple_of(rows * (where[0] if side == 0 else 1 - where[0]), rows)
@@ -72,24 +67,34 @@
         scale = lax.rsqrt(mean + epsilon)
         for half in range(2):
             for s in range(ny):
-                source = lax.rem(where[3] + ny - s, ny) * 2 + (where[4] ^ half)
-                cols = pl.ds(pl.multiple_of(source * width, 128), width)
+                cols = pl.ds((s * 2 + half) * width, width)
                 v = hidden[side * 2 + half][s].astype(jnp.float32)
                 v = v * scale * norm_gain[:, cols]
                 normed[pl.ds(first, rows), cols] = v.astype(jnp.bfloat16)
-
-
-def pair_kernel(panel, offsets, where, normed, gain, cosine, sine, *refs):
-    blocks, out, weights = refs[:-2], refs[-2], refs[-1]
-    collect(offsets, where, blocks, weights, panel)
+    copy = pltpu.make_async_copy(normed, out, sem)
+    copy.start()
+    copy.wait()
+
+
+def pair_kernel(panel, offsets, where, source, gain, cosine, sine, blocks, out, normed, weights, sem):
+    copy = pltpu.make_async_copy(source, normed, sem)
+    copy.start()
+    for s in range(blocks.shape[0]):
+        collect(offsets, blocks.at[s], s, weights, panel)
+    copy.wait()
     v = jnp.dot(normed[...], weights[...], preferred_element_type=jnp.float32)
     keys = head_norm_rope(v, gain[...], cosine[...], sine[...])
     out[...] = jnp.where(where[0] == 0, keys, v).astype(jnp.bfloat16)
 
 
-def query_kernel(panel, offsets, where, normed, gain, cosine, sine, *refs):
-    blocks, out, weights = refs[:-2], refs[-2], refs[-1]
-    collect(offsets, where, blocks, weights, panel)
+def query_kernel(panel, offsets, where, source, gain, cosine, sine, *refs):
+    blocks, (out, normed, weights, sem) = refs[:-4], refs[-4:]
+    copy = pltpu.make_async_copy(source, normed, sem)
+    copy.start()
+    nx = len(blocks)
+    for s in range(nx):
+        collect(offsets, blocks[s], lax.rem(where[2] + nx - s, nx), weights, panel)
+    copy.wait()
     rows = out.shape[2]
     for side in range(2):
         span = pl.ds(side * rows, rows)
@@ -159,9 +164,9 @@
     return acc[:, :128] / safe, jnp.where(one > 0, top[...] * scale + jnp.log2(one), NEG)
 
 
-def remote_kernel(where, begins, near, far, *refs):
+def own_kernel(where, begins, query, *refs):
     mine, other = refs[:2], refs[2:4]
-    out1, out2, keys, values, acc, top = refs[4:]
+    out, log, keys, values, acc, top = refs[4:]
     block = mine[0].shape[1]
     values[:, 128:] = jnp.ones((values.shape[0], 128), values.dtype)
     for core, (first, second) in enumerate(((mine, other), (other, mine))):
@@ -173,6 +178,15 @@
                 keys[spot, :] = first[k // 4][k % 4]
                 values[spot, :128] = second[k // 4][k % 4]
 
+    rows = begins.shape[1]
+    index = where[2] + lax.broadcasted_iota(jnp.int32, (rows, 1), 0)
+    limits = [where[3 + i] for i in range(3)]
+    result, level = attend(query, keys, values, begins[0], index, *limits, acc, top)
+    out[...] = result
+    log[...] = level
+
+
+def remote_kernel(where, begins, near, far, keys, values, out1, out2, acc, top):
     eye = identity_mask()
     size = near.shape[0]
     for s, query, out in ((1, near, out1), (2, far, out2)):
@@ -193,15 +207,6 @@
             rest = rest - piece.astype(jnp.float32)
 
 
-def own_kernel(where, begins, query, keys, values, out, log, acc, top):
-    rows = begins.shape[1]
-    index = where[2] + lax.broadcasted_iota(jnp.int32, (rows, 1), 0)
-    limits = [where[3 + i] for i in range(3)]
-    result, level = attend(query, keys, values, begins[0], index, *limits, acc, top)
-    out[...] = result
-    log[...] = level
-
-
 def combine_kernel(where, o0, l0, r1, r2, out):
     rows = out.shape[0]
     size = o0.shape[0]
@@ -247,17 +252,14 @@
 
 
 def body(hidden, norm_gain, query_gain, key_gain, weight_store, documents, owners):
-    x, z, c, y, w = (lax.axis_index(a) for a in ("x", "z", "c", "y", "w"))
-    nx, nz, ny = (lax.axis_size(a) for a in ("x", "z", "y"))
+    x, z, c = (lax.axis_index(a) for a in ("x", "z", "c"))
+    nx, nz = (lax.axis_size(a) for a in ("x", "z"))
     rows = hidden.shape[0]
     slots = owners.shape[0]
     panel = weight_store.shape[0]
     swap = [(0, 1), (1, 0)]
     bf16, f32 = jnp.bfloat16, jnp.float32
     table = jnp.arange(slots, dtype=jnp.int32)
-
-    def turn(v, axis, size):
-        return [lax.ppermute(v, axis, ring(size, s)) for s in range(1, size)]
 
     riders = jnp.pad(documents.astype(bf16), (0, 256 - rows), constant_values=NO_SEGMENT)
     riders = jnp.pad(riders[None], ((0, 15), (0, weight_store.shape[1] - 256)))
@@ -272,48 +274,31 @@
         axis=1,
     )
     tail = jnp.pad(pair_docs.reshape(4, 128), ((0, 12), (0, 256)))
-    line = jnp.concatenate([columns, tail], axis=0)[None]
+    line = jnp.concatenate([columns, tail], axis=0)
     pair_docs = pair_docs[:, :rows].astype(jnp.int32)
 
-    far = lax.ppermute(hidden, "w", swap)
-    near_parts = turn(hidden, "y", ny)
-    step = across(line, 4)
-    far, step, *near_parts = lax.optimization_barrier((far, step, *near_parts))
-
-    line = jnp.concatenate([line, step], axis=0)
-    own_near = jnp.stack([hidden] + near_parts)
-    far_parts = turn(far, "y", ny)
-    step = across(line, 2)
-    other_near = lax.ppermute(own_near, "c", swap)
-    step, other_near, *far_parts = lax.optimization_barrier((step, other_near, *far_parts))
-
-    line = jnp.concatenate([line, step], axis=0)
-    own_far = jnp.stack([far] + far_parts)
-    step = across(line, 1)
-    other_far = lax.ppermute(own_far, "c", swap)
-    first_parts = turn(line[:, :, :128], "x", nx)
-    step, other_far, *first_parts = lax.optimization_barrier((step, other_far, *first_parts))
-
-    second_parts = turn(step[:, :, :128], "x", nx)
-    pair_blocks = [
-        v
-        for both in zip(
-            [line[:, :, :128]] + first_parts, [step[:, :, :128]] + second_parts, strict=True
-        )
-        for v in both
-    ]
-    query_line = jnp.concatenate([line, step], axis=0)[:, : 2 * panel, 128:]
-    query_line = after(query_line, second_parts[0])
-    query_blocks = [query_line] + turn(query_line, "x", nx)
-
-    spot = jnp.stack([c, z, x, y, w]).astype(jnp.int32)
+    hidden, line = lax.optimization_barrier((hidden, line))
+    line = lax.all_gather(line, "z", axis=0)
+    pair_line = jnp.broadcast_to(line[None, :, :, :128], (nx, nz, *line.shape[1:2], 128))
+    pair_blocks = lax.all_to_all(pair_line, "x", 0, 0)
+    query_line = line[:, : 2 * panel, 128:]
+
+    halves = lax.all_gather(hidden, "w", axis=0)
+    own = [lax.all_gather(halves[i], "y", axis=0) for i in range(2)]
+    other = [lax.ppermute(v, "c", swap) for v in own]
+    spot = jnp.stack([c, z, x]).astype(jnp.int32)
     features = norm_gain.shape[0]
     (normed,) = call(
-        norm_kernel, [jax.ShapeDtypeStruct((2 * rows, features), bf16)], 1, 5, (), 4 * 10**9
-    )(spot, norm_gain.astype(f32)[None, :], own_near, own_far, other_near, other_far)
-
-    riding = jnp.stack([v[:, 2 * panel : 2 * panel + 4, :] for v in pair_blocks]).astype(f32)
-    riding = riding.reshape(nx, nz, 4, 128)
+        norm_kernel,
+        [jax.ShapeDtypeStruct((2 * rows, features), bf16)],
+        1,
+        5,
+        [pltpu.VMEM((2 * rows, features), bf16), pltpu.SemaphoreType.DMA],
+        4 * 10**9,
+        out_hbm=True,
+    )(spot, norm_gain.astype(f32)[None, :], *own, *other)
+
+    riding = pair_blocks[:, :, 2 * panel : 2 * panel + 4, :].astype(f32)
     starts = jnp.sum(
         (riding.reshape(-1, 1) < table.astype(f32)[None, :]).astype(f32), axis=0
     ).astype(jnp.int32)
@@ -335,7 +320,8 @@
     sine = jnp.concatenate([-sine, sine], axis=1)
     spread = [lax.dynamic_slice_in_dim(pair_begin, c * rows, rows, 0)]
     for s in (1, 2):
-        docs = lax.dynamic_slice_in_dim(riding[nx - s, 0], 2 * c, 2, 0).reshape(-1)[:rows]
+        place = (jnp.minimum(x + s, nx - 1), z, 2 * c, 0)
+        docs = lax.dynamic_slice(riding, place, (1, 1, 2, 128)).reshape(-1)[:rows]
         spread.append(begin_of(docs.astype(jnp.int32)))
     spread = jnp.stack(spread) - x * plane
 
@@ -346,10 +332,19 @@
         functools.partial(pair_kernel, panel),
         [jax.ShapeDtypeStruct((2 * rows, 128), bf16)],
         2,
-        4 + 2 * nx,
-        [pltpu.VMEM((features, 128), bf16)],
+        4,
+        [
+            pltpu.VMEM((2 * rows, features), bf16),
+            pltpu.VMEM((features, 128), bf16),
+            pltpu.SemaphoreType.DMA,
+        ],
         2 * 10**9,
-    )(offsets, spot, normed, key_gain[None, :], cosine, sine, *pair_blocks)
+        n_hbm=1,
+    )(offsets, spot, normed, key_gain[None, :], cosine, sine, pair_blocks)
+    query_line = after(query_line, pair)
+    query_blocks = [query_line] + [
+        lax.ppermute(query_line, "x", ring(nx, s)) for s in range(1, nx)
+    ]
 
     inside = z * 2 * rows + c * rows
     low = [jnp.clip(spread[s, 0], 0, plane) for s in range(3)]
@@ -370,9 +365,14 @@
         functools.partial(query_kernel, panel),
         [jax.ShapeDtypeStruct((2, 2, rows, 128), bf16)],
         2,
-        4 + nx,
-        [pltpu.VMEM((features, 256), bf16)],
+        3 + nx,
+        [
+            pltpu.VMEM((2 * rows, features), bf16),
+            pltpu.VMEM((features, 256), bf16),
+            pltpu.SemaphoreType.DMA,
+        ],
         4 * 10**9,
+        n_hbm=1,
     )(offsets, spot, normed, query_gain[None, :], cosine, sine, *query_blocks)
 
     own_query = lax.dynamic_index_in_dim(query, c, 0, keepdims=False)
@@ -383,28 +383,29 @@
     q2 = lax.ppermute(q0, "x", [(i, i - 2) for i in range(2, nx)])
 
     state = [pltpu.VMEM((4 * rows, 256), f32), pltpu.VMEM((4 * rows, 1), f32)]
-    r1, r2, keys, values = call(
-        remote_kernel,
-        [jax.ShapeDtypeStruct((4 * rows + 48, 128), bf16)] * 2
-        + [jax.ShapeDtypeStruct((plane, 128 * k), bf16) for k in (1, 2)],
-        1,
-        7,
-        state,
-        10**10,
-    )(ranges, begins, q1, q2, *mine, *other)
-    r1 = lax.ppermute(r1, "x", [(i, i + 1) for i in range(nx - 1)])
-    r2 = lax.ppermute(r2, "x", [(i, i + 2) for i in range(nx - 2)])
-    o0, l0 = call(
+    o0, l0, keys, values = call(
         own_kernel,
         [
             jax.ShapeDtypeStruct((4 * rows, 128), f32),
             jax.ShapeDtypeStruct((4 * rows, 1), f32),
+            jax.ShapeDtypeStruct((plane, 128), bf16),
+            jax.ShapeDtypeStruct((plane, 256), bf16),
         ],
         1,
-        4,
+        6,
         state,
         10**10,
-    )(ranges, begins, q0, keys, values)
+    )(ranges, begins, q0, *mine, *other)
+    r1, r2 = call(
+        remote_kernel,
+        [jax.ShapeDtypeStruct((4 * rows + 48, 128), bf16)] * 2,
+        1,
+        5,
+        state,
+        10**10,
+    )(ranges, begins, q1, q2, keys, values)
+    r1 = lax.ppermute(r1, "x", [(i, i + 1) for i in range(nx - 1)])
+    r2 = lax.ppermute(r2, "x", [(i, i + 2) for i in range(nx - 2)])
     came = jnp.stack([c, (x >= 1).astype(jnp.int32), (x >= 2).astype(jnp.int32)]).astype(jnp.int32)
     (context,) = call(combine_kernel, [jax.ShapeDtypeStruct((rows, 512), bf16)], 1, 4)(
         came, o0, l0, r1, r2

time: 219 us -> 220 us (level)
  blocking collectives: 3.45 us -> 58.8 us
  starting transfers between devices: 102 us -> 64.8 us
  waiting for transfers between devices: 65.8 us -> 40 us
  between operations: 3.36 us -> 16.4 us
  other arithmetic: 8.07 us -> 5.24 us
    all_gather x0 -> x3, blocking collectives: none -> 50.3 us  [the longest x2 25.4 us: body(): own = [lax.all_gather(halves[i], 'y', axis=0) for i in range(2)]]
    ppermute x18 -> x5, starting transfers between devices: 64.5 us -> 18.4 us  [the longest x2 9.94 us: body(): other = [lax.ppermute(v, 'c', swap) for v in own]]
    ppermute x6 -> x3, waiting for transfers between devices: 32.6 us -> 3.33 us  [across(): return lax.ppermute(v, 'z', [(i, i ^ bit) for i in range(8)])]
    ppermute x18 -> x5, waiting for transfers between devices: 21.9 us -> 11.3 us  [the longest x3 11.3 us: body(): lax.ppermute(query_line, 'x', ring(nx, s))]
    all_to_all x0 -> x1, waiting for transfers between devices: none -> 7.61 us  [body(): pair_blocks = lax.all_to_all(pair_line, 'x', 0, 0)]
    all_gather x0 -> x1, waiting for transfers between devices: none -> 6.63 us  [body(): line = lax.all_gather(line, 'z', axis=0)]
    all_gather x1, blocking collectives: 3.45 us -> 8.53 us  [body(): lax.all_gather(jnp.concatenate([weight_store, riders], axis=0), 'c', axis=0)]
    all_to_all x0 -> x1, starting transfers between devices: none -> 4.87 us  [body(): pair_blocks = lax.all_to_all(pair_line, 'x', 0, 0)]
  transfers between devices with their start and end apart: 31 -> 17, of which waited for: 13 -> 10; matrix products, arithmetic and copies ran while one was open for 5% -> 3% of each run, Pallas kernels for 5% -> 5%
where the time goes in v5:
time: 220 us; the launch traced here: 217 us
  starting transfers between devices  64.8 us (29%)
  blocking collectives  58.8 us (27%)
  waiting for transfers between devices  40 us (18%)
  Pallas kernels  19.8 us (9%)
  between operations  16.4 us (7%)
  local copies, waits for them, and re-layouts  11.6 us (5%)
  other arithmetic  5.24 us (2%)
    all_gather x2, blocking collectives, body(): own = [lax.all_gather(halves[i], 'y', axis=0) for i in range(2)]  25.4 us
    all_gather x1, blocking collectives, body(): halves = lax.all_gather(hidden, 'w', axis=0)  24.9 us
    ppermute x3, starting transfers between devices, across(): return lax.ppermute(v, 'z', [(i, i ^ bit) for i in range(8)])  19.9 us
    ppermute x3, waiting for transfers between devices, body(): lax.ppermute(query_line, 'x', ring(nx, s))  11.3 us
    ppermute x2, starting transfers between devices, body(): other = [lax.ppermute(v, 'c', swap) for v in own]  9.94 us
    ppermute x2, starting transfers between devices, body(): other = [lax.ppermute(v, 'c', swap) for v in mine]  8.72 us
    all_gather x1, blocking collectives, body(): lax.all_gather(jnp.concatenate([weight_store, riders], axis=0), 'c', axis=0)  8.53 us
    ppermute x3, starting transfers between devices, body(): lax.ppermute(query_line, 'x', ring(nx, s))  8.42 us
  transfers between devices with their start and end apart: 17, of which 10 were waited for; matrix products, arithmetic and copies ran while one was open for 3% of the time, Pallas kernels for 5%

profile of v5, /device:TPU:1, one launch (start us, length us, event | category | flops | bytes accessed | tf_op | source)
XLA Modules:
  0.0 216.6 jit_solution(1498614204114826112)
XLA Ops:
  8.9 8.5 %all-gather = bf16[192,768]{1,0:T(8,128)(2,1)S(1)} all-gather(bf16[96,768]{1,0:T(8,128)(2,1)S(1)} %fusion.2), channel_id=2, replica_groups=mesh['x'=4,'z'=8,'c'=2,'y'=4,'w'=2] {'c'}, dimensions={0}, use_global_device_ids=true | all-gather | bytes 442368 | tf_op jit(solution)/shard_map/all_gather | solution.py:266
  18.2 24.9 %all-gather.1 = bf16[384,640]{1,0:T(8,128)(2,1)S(1)} all-gather(bf16[192,640]{1,0:T(8,128)(2,1)S(1)} %copy-done.6), channel_id=3, replica_groups=mesh['x'=4,'z'=8,'c'=2,'y'=4,'w'=2] {'w'}, dimensions={0}, use_global_device_ids=true | all-gather | bytes 737280 | tf_op jit(solution)/shard_map/all_gather | solution.py:286
  43.1 12.0 %all-gather.3 = bf16[768,640]{1,0:T(8,128)(2,1)S(1)} all-gather(bf16[192,640]{1,0:T(8,128)(2,1)S(1)} %get-tuple-element.32), channel_id=5, replica_groups=mesh['x'=4,'z'=8,'c'=2,'y'=4,'w'=2] {'y'}, dimensions={0}, use_global_device_ids=true | all-gather | bytes 1228800 | tf_op jit(solution)/shard_map/all_gather | solution.py:287
  55.2 6.2 %collective-permute-start = (bf16[4,192,640]{2,1,0:T(8,128)(2,1)S(1)}, bf16[4,192,640]{2,1,0:T(8,128)(2,1)}, u32[]{:S(2)}, u32[]{:S(2)}) collective-permute-start(bf16[4,192,640]{2,1,0:T(8,128)(2,1)S(1)} %bitcast.49), channel_id=1, source_target_pairs={{0,8},{8,0},{1,9},{9,1},{2,10},{10,2},{3,11},{11,3},{4,12},{12,4},... | collective-permute-start | bytes 2949128 | tf_op jit(solution)/shard_map/ppermute | solution.py:288
  61.4 13.4 %all-gather.4 = bf16[768,640]{1,0:T(8,128)(2,1)S(1)} all-gather(bf16[192,640]{1,0:T(8,128)(2,1)S(1)} %get-tuple-element.31), channel_id=6, replica_groups=mesh['x'=4,'z'=8,'c'=2,'y'=4,'w'=2] {'y'}, dimensions={0}, use_global_device_ids=true | all-gather | bytes 1228800 | tf_op jit(solution)/shard_map/all_gather | solution.py:287
  74.7 3.8 %collective-permute-start.1 = (bf16[4,192,640]{2,1,0:T(8,128)(2,1)S(1)}, bf16[4,192,640]{2,1,0:T(8,128)(2,1)}, u32[]{:S(2)}, u32[]{:S(2)}) collective-permute-start(bf16[4,192,640]{2,1,0:T(8,128)(2,1)S(1)} %bitcast.51), channel_id=1, source_target_pairs={{0,8},{8,0},{1,9},{9,1},{2,10},{10,2},{3,11},{11,3},{4,12},{12,4},... | collective-permute-start | bytes 2949128 | tf_op jit(solution)/shard_map/ppermute | solution.py:288
  78.5 6.6 %all-gather.7.cloned.1.call-done = bf16[1408,384]{1,0:T(8,128)(2,1)} async-done(((bf16[176,384]{1,0:T(8,128)(2,1)}), bf16[1408,384]{1,0:T(8,128)(2,1)}) %all-gather.7.cloned.1.call-update) | async-done | bytes 1081360 | tf_op jit(solution)/shard_map/all_gather | solution.py:281
  87.5 4.9 %all-to-all-start = ((bf16[4,8,176,128]{3,2,1,0:T(8,128)(2,1)}), bf16[4,8,176,128]{3,2,1,0:T(8,128)(2,1)S(1)}, u32[]{:S(2)}, u32[]{:S(2)}) async-start(bf16[4,8,176,128]{3,2,1,0:T(8,128)(2,1)} %broadcast_in_dim.16), calls=%async_computation | async-start | bytes 2883584 | tf_op jit(solution)/shard_map/all_to_all | solution.py:283
  92.7 4.1 %shard_map.94.source = bf16[384,5120]{1,0:T(8,128)(2,1)S(1)} custom-call(s32[3]{0:T(128)S(1)} %pad_add_fusion.1.where, f32[1,5120]{1,0:T(1,128)S(1)} %bitcast.57, bf16[4,192,640]{2,1,0:T(8,128)(2,1)S(1)} %bitcast.50, bf16[4,192,640]{2,1,0:T(8,128)(2,1)S(1)} %bitcast.52, bf16[4,192,640]{2,1,0:T(8,128)(2,1)} %collective-permute-done.refs_2_, ...), custom_call_target="tpu_custom_call" | custom-call | flops 4000000000 | bytes 4194304 | tf_op jit(solution)/shard_map/pallas_call | solution.py:291
  98.7 7.6 %all-to-all-done.blocks = bf16[4,8,176,128]{3,2,1,0:T(8,128)(2,1)S(1)} async-done(((bf16[4,8,176,128]{3,2,1,0:T(8,128)(2,1)}), bf16[4,8,176,128]{3,2,1,0:T(8,128)(2,1)S(1)}, u32[]{:S(2)}, u32[]{:S(2)}) %all-to-all-start) | async-done | bytes 1441824 | tf_op jit(solution)/shard_map/all_to_all | solution.py:283
  108.1 2.1 copy-done.3
  110.2 2.3 %shard_map.95 = bf16[384,128]{1,0:T(8,128)(2,1)S(1)} custom-call(s32[64]{0:T(128)S(1)} %broadcast_multiply_fusion.offsets, s32[3]{0:T(128)S(1)} %pad_add_fusion.1.where, bf16[384,5120]{1,0:T(8,128)(2,1)S(1)} %copy-done.3, f32[1,128]{1,0:T(1,128)S(1)} %bitcast.58, f32[384,128]{1,0:T(8,128)S(1)} %get-tuple-element.48.cosine, ...), custom_call_target="tpu_custom_call" | custom-call | flops 2000000000 | bytes 4194304 | tf_op jit(solution)/shard_map/pallas_call | solution.py:331
  112.6 9.3 %collective-permute-start.2 = (bf16[384,128]{1,0:T(8,128)(2,1)S(1)}, bf16[384,128]{1,0:T(8,128)(2,1)S(1)}, u32[]{:S(2)}, u32[]{:S(2)}) collective-permute-start(bf16[384,128]{1,0:T(8,128)(2,1)S(1)} %shard_map.95), channel_id=1, source_target_pairs={{0,64},{16,80},{32,96},{48,112},{64,0},{80,16},{96,32},{112,48},{1... | collective-permute-start | bytes 294920 | tf_op jit(solution)/shard_map/ppermute | solution.py:247
  126.8 7.2 %collective-permute-start.3 = (bf16[2,384,128]{2,1,0:T(8,128)(2,1)S(1)}, bf16[2,384,128]{2,1,0:T(8,128)(2,1)S(1)}, u32[]{:S(2)}, u32[]{:S(2)}) collective-permute-start(bf16[2,384,128]{2,1,0:T(8,128)(2,1)S(1)} %pad_maximum_fusion.2), channel_id=1, source_target_pairs={{0,32},{16,48},{32,0},{48,16},{64,96},{80,112},{96,64},{112,80},{1... | collective-permute-start | bytes 589832 | tf_op jit(solution)/shard_map/ppermute | solution.py:247
  134.1 2.2 %collective-permute-start.5 = (bf16[8,160,256]{2,1,0:T(8,128)(2,1)S(1)}, bf16[8,160,256]{2,1,0:T(8,128)(2,1)S(1)}, u32[]{:S(2)}, u32[]{:S(2)}) collective-permute-start(bf16[8,160,256]{2,1,0:T(8,128)(2,1)S(1)} %slice.84.refs_0_), channel_id=1, source_target_pairs={{0,128},{128,256},{256,384},{384,0},{1,129},{129,257},{257,385},{3... | collective-permute-start | bytes 1966088 | tf_op jit(solution)/shard_map/ppermute | solution.py:346
  136.3 3.7 %collective-permute-start.6 = (bf16[8,160,256]{2,1,0:T(8,128)(2,1)S(1)}, bf16[8,160,256]{2,1,0:T(8,128)(2,1)}, u32[]{:S(2)}, u32[]{:S(2)}) collective-permute-start(bf16[8,160,256]{2,1,0:T(8,128)(2,1)S(1)} %slice.84.refs_0_), channel_id=1, source_target_pairs={{0,256},{128,384},{256,0},{384,128},{1,257},{129,385},{257,1},{385... | collective-permute-start | bytes 1966088 | tf_op jit(solution)/shard_map/ppermute | solution.py:346
  140.0 2.5 %collective-permute-start.7 = (bf16[8,160,256]{2,1,0:T(8,128)(2,1)S(1)}, bf16[8,160,256]{2,1,0:T(8,128)(2,1)}, u32[]{:S(2)}, u32[]{:S(2)}) collective-permute-start(bf16[8,160,256]{2,1,0:T(8,128)(2,1)S(1)} %slice.84.refs_0_), channel_id=1, source_target_pairs={{0,384},{128,0},{256,128},{384,256},{1,385},{129,1},{257,129},{385... | collective-permute-start | bytes 1966088 | tf_op jit(solution)/shard_map/ppermute | solution.py:346
  142.6 3.4 %collective-permute-start.9 = (bf16[4,384,128]{2,1,0:T(8,128)(2,1)S(1)}, bf16[4,384,128]{2,1,0:T(8,128)(2,1)}, u32[]{:S(2)}, u32[]{:S(2)}) collective-permute-start(bf16[4,384,128]{2,1,0:T(8,128)(2,1)S(1)} %constant_dynamic-update-slice_fusion.refs_0_), channel_id=1, source_target_pairs={{0,16},{16,0},{32,48},{48,32},{64,80},{80,64},{96,112},{112,96},{1... | collective-permute-start | bytes 1179656 | tf_op jit(solution)/shard_map/ppermute | solution.py:247
  146.0 3.6 %collective-permute-start.4 = (bf16[4,384,128]{2,1,0:T(8,128)(2,1)S(1)}, bf16[4,384,128]{2,1,0:T(8,128)(2,1)S(1)}, u32[]{:S(2)}, u32[]{:S(2)}) collective-permute-start(bf16[4,384,128]{2,1,0:T(8,128)(2,1)S(1)} %constant_dynamic-update-slice_fusion.refs_0_), channel_id=1, source_target_pairs={{0,8},{8,0},{1,9},{9,1},{2,10},{10,2},{3,11},{11,3},{4,12},{12,4},... | collective-permute-start | bytes 1179656 | tf_op jit(solution)/shard_map/ppermute | solution.py:361
  149.6 3.3 %collective-permute-done.9.refs_1_ = bf16[4,384,128]{2,1,0:T(8,128)(2,1)} collective-permute-done((bf16[4,384,128]{2,1,0:T(8,128)(2,1)S(1)}, bf16[4,384,128]{2,1,0:T(8,128)(2,1)}, u32[]{:S(2)}, u32[]{:S(2)}) %collective-permute-start.9) | collective-permute-done | bytes 393248 | tf_op jit(solution)/shard_map/ppermute | solution.py:247
  153.0 5.1 %collective-permute-start.10 = (bf16[4,384,128]{2,1,0:T(8,128)(2,1)}, bf16[4,384,128]{2,1,0:T(8,128)(2,1)}, u32[]{:S(2)}, u32[]{:S(2)}) collective-permute-start(bf16[4,384,128]{2,1,0:T(8,128)(2,1)} %collective-permute-done.9.refs_1_), channel_id=1, source_target_pairs={{0,8},{8,0},{1,9},{9,1},{2,10},{10,2},{3,11},{11,3},{4,12},{12,4},... | collective-permute-start | bytes 1179656 | tf_op jit(solution)/shard_map/ppermute | solution.py:361
  158.1 6.4 %collective-permute-done.6.refs_2_ = bf16[8,160,256]{2,1,0:T(8,128)(2,1)} collective-permute-done((bf16[8,160,256]{2,1,0:T(8,128)(2,1)S(1)}, bf16[8,160,256]{2,1,0:T(8,128)(2,1)}, u32[]{:S(2)}, u32[]{:S(2)}) %collective-permute-start.6) | collective-permute-done | bytes 655392 | tf_op jit(solution)/shard_map/ppermute | solution.py:346
  164.4 5.0 %collective-permute-done.7.refs_3_ = bf16[8,160,256]{2,1,0:T(8,128)(2,1)} collective-permute-done((bf16[8,160,256]{2,1,0:T(8,128)(2,1)S(1)}, bf16[8,160,256]{2,1,0:T(8,128)(2,1)}, u32[]{:S(2)}, u32[]{:S(2)}) %collective-permute-start.7) | collective-permute-done | bytes 655392 | tf_op jit(solution)/shard_map/ppermute | solution.py:346
  169.4 2.1 copy-done.4
  171.5 3.2 %shard_map.96 = bf16[2,2,192,128]{3,2,1,0:T(8,128)(2,1)S(1)} custom-call(s32[64]{0:T(128)S(1)} %broadcast_multiply_fusion.offsets, s32[3]{0:T(128)S(1)} %pad_add_fusion.1.where, bf16[384,5120]{1,0:T(8,128)(2,1)S(1)} %copy-done.4, f32[1,128]{1,0:T(1,128)S(1)} %bitcast.59, f32[384,128]{1,0:T(8,128)S(1)} %get-tuple-element.48.cosine, ...), custom_call_target="tpu_custom_call" | custom-call | flops 4000000000 | bytes 4194304 | tf_op jit(solution)/shard_map/pallas_call | solution.py:364
  174.7 3.6 %collective-permute-start.8 = (bf16[2,192,128]{2,1,0:T(8,128)(2,1)S(1)}, bf16[2,192,128]{2,1,0:T(8,128)(2,1)S(1)}, u32[]{:S(2)}, u32[]{:S(2)}) collective-permute-start(bf16[2,192,128]{2,1,0:T(8,128)(2,1)S(1)} %get-tuple-element.34), channel_id=1, source_target_pairs={{0,8},{8,0},{1,9},{9,1},{2,10},{10,2},{3,11},{11,3},{4,12},{12,4},... | collective-permute-start | bytes 294920 | tf_op jit(solution)/shard_map/ppermute | solution.py:380
  181.9 3.6 %shard_map.97 = (f32[768,128]{1,0:T(8,128)S(1)}, f32[768,1]{1,0:T(8,128)S(1)}, bf16[3072,128]{1,0:T(8,128)(2,1)S(1)}, bf16[3072,256]{1,0:T(8,128)(2,1)S(1)}) custom-call(s32[12]{0:T(128)S(1)} %stack.101.where, s32[3,192,1]{2,1,0:T(8,128)S(1)} %broadcast_subtract_fusion.begins, bf16[768,128]{1,0:T(8,128)(2,1)S(1)} %bitcast.56, ...), custom_call_target="tpu_custom_call" | custom-call | flops 10000000000 | bytes 4194304 | tf_op jit(solution)/shard_map/pallas_call | solution.py:386
  187.3 2.8 %collective-permute-done.12.far = bf16[768,128]{1,0:T(8,128)(2,1)S(1)} collective-permute-done((bf16[768,128]{1,0:T(8,128)(2,1)S(1)}, bf16[768,128]{1,0:T(8,128)(2,1)S(1)}, u32[]{:S(2)}, u32[]{:S(2)}) %collective-permute-start.12) | collective-permute-done | bytes 196640 | tf_op jit(solution)/shard_map/ppermute | solution.py:383
  190.1 4.5 %shard_map.98 = (bf16[816,128]{1,0:T(8,128)(2,1)S(1)}, bf16[816,128]{1,0:T(8,128)(2,1)S(1)}) custom-call(s32[12]{0:T(128)S(1)} %stack.101.where, s32[3,192,1]{2,1,0:T(8,128)S(1)} %broadcast_subtract_fusion.begins, bf16[768,128]{1,0:T(8,128)(2,1)S(1)} %collective-permute-done.11.near, bf16[768,128]{1,0:T(8,128)(2,1)S(1)} %collective-permute-done.12.far, ...), custom_call_target="tpu_custom_call" | custom-call | flops 10000000000 | bytes 4194304 | tf_op jit(solution)/shard_map/pallas_call | solution.py:399
  194.6 5.5 %collective-permute-start.13 = (bf16[816,128]{1,0:T(8,128)(2,1)S(1)}, bf16[816,128]{1,0:T(8,128)(2,1)S(1)}, u32[]{:S(2)}, u32[]{:S(2)}) collective-permute-start(bf16[816,128]{1,0:T(8,128)(2,1)S(1)} %get-tuple-element.27), channel_id=1, source_target_pairs={{0,128},{128,256},{256,384},{1,129},{129,257},{257,385},{2,130},{1... | collective-permute-start | bytes 626696 | tf_op jit(solution)/shard_map/ppermute | solution.py:407
  203.2 4.5 %collective-permute-done.14.r2 = bf16[816,128]{1,0:T(8,128)(2,1)S(1)} collective-permute-done((bf16[816,128]{1,0:T(8,128)(2,1)S(1)}, bf16[816,128]{1,0:T(8,128)(2,1)S(1)}, u32[]{:S(2)}, u32[]{:S(2)}) %collective-permute-start.14) | collective-permute-done | bytes 208928 | tf_op jit(solution)/shard_map/ppermute | solution.py:408
  207.7 2.0 shard_map.99
  (80 shorter events, 20.3 us)
Async XLA Ops:
  7.2 11.1 %copy-start.6 = (bf16[192,640]{1,0:T(8,128)(2,1)S(1)}, bf16[192,640]{1,0:T(8,128)(2,1)}, u32[]{:S(2)}) copy-start(bf16[192,640]{1,0:T(8,128)(2,1)} %param.7) | copy-start | bytes 737284
  7.2 78.0 %all-gather.7.cloned.1.call-start = ((), (), s32[]{:S(2)}) async-start(), calls=%async_computation.1 | async-start | bytes 1216512 | tf_op jit(solution)/shard_map/all_gather | solution.py:281
  55.2 37.5 %collective-permute-start = (bf16[4,192,640]{2,1,0:T(8,128)(2,1)S(1)}, bf16[4,192,640]{2,1,0:T(8,128)(2,1)}, u32[]{:S(2)}, u32[]{:S(2)}) collective-permute-start(bf16[4,192,640]{2,1,0:T(8,128)(2,1)S(1)} %bitcast.49), channel_id=1, source_target_pairs={{0,8},{8,0},{1,9},{9,1},{2,10},{10,2},{3,11},{11,3},{4,12},{12,4},... | collective-permute-start | bytes 2949128 | tf_op jit(solution)/shard_map/ppermute | solution.py:288
  74.7 17.9 %collective-permute-start.1 = (bf16[4,192,640]{2,1,0:T(8,128)(2,1)S(1)}, bf16[4,192,640]{2,1,0:T(8,128)(2,1)}, u32[]{:S(2)}, u32[]{:S(2)}) collective-permute-start(bf16[4,192,640]{2,1,0:T(8,128)(2,1)S(1)} %bitcast.51), channel_id=1, source_target_pairs={{0,8},{8,0},{1,9},{9,1},{2,10},{10,2},{3,11},{11,3},{4,12},{12,4},... | collective-permute-start | bytes 2949128 | tf_op jit(solution)/shard_map/ppermute | solution.py:288
  87.5 4.9 %copy-start.7 = (bf16[5120]{0:T(1024)(128)(2,1)S(1)}, bf16[5120]{0:T(1024)(128)(2,1)}, u32[]{:S(2)}) copy-start(bf16[5120]{0:T(1024)(128)(2,1)} %param.8) | copy-start | bytes 30724
  87.5 5.1 %copy-start.8 = (s32[64]{0:T(128)S(1)}, s32[64]{0:T(128)}, u32[]{:S(2)}) copy-start(s32[64]{0:T(128)} %param.13) | copy-start | bytes 772
  87.5 18.8 %all-to-all-start = ((bf16[4,8,176,128]{3,2,1,0:T(8,128)(2,1)}), bf16[4,8,176,128]{3,2,1,0:T(8,128)(2,1)S(1)}, u32[]{:S(2)}, u32[]{:S(2)}) async-start(bf16[4,8,176,128]{3,2,1,0:T(8,128)(2,1)} %broadcast_in_dim.16), calls=%async_computation | async-start | bytes 2883584 | tf_op jit(solution)/shard_map/all_to_all | solution.py:283
  96.8 1.9 copy-start.2
  98.7 9.4 %copy-start = (f32[128]{0:T(128)S(1)}, f32[128]{0:T(128)}, u32[]{:S(2)}) copy-start(f32[128]{0:T(128)} %param.10) | copy-start | bytes 1540
  108.1 2.1 copy-start.3
  112.6 21.5 %copy-start.5 = (bf16[1408,384]{1,0:T(8,128)(2,1)S(1)}, bf16[1408,384]{1,0:T(8,128)(2,1)}, u32[]{:S(2)}) copy-start(bf16[1408,384]{1,0:T(8,128)(2,1)} %all-gather.7.cloned.1.call-done) | copy-start | bytes 3244036
  112.6 14.2 %collective-permute-start.2 = (bf16[384,128]{1,0:T(8,128)(2,1)S(1)}, bf16[384,128]{1,0:T(8,128)(2,1)S(1)}, u32[]{:S(2)}, u32[]{:S(2)}) collective-permute-start(bf16[384,128]{1,0:T(8,128)(2,1)S(1)} %shard_map.95), channel_id=1, source_target_pairs={{0,64},{16,80},{32,96},{48,112},{64,0},{80,16},{96,32},{112,48},{1... | collective-permute-start | bytes 294920 | tf_op jit(solution)/shard_map/ppermute | solution.py:247
  122.3 47.1 %copy-start.1 = (f32[128]{0:T(128)S(1)}, f32[128]{0:T(128)}, u32[]{:S(2)}) copy-start(f32[128]{0:T(128)} %param.9) | copy-start | bytes 1540
  126.8 15.7 %collective-permute-start.3 = (bf16[2,384,128]{2,1,0:T(8,128)(2,1)S(1)}, bf16[2,384,128]{2,1,0:T(8,128)(2,1)S(1)}, u32[]{:S(2)}, u32[]{:S(2)}) collective-permute-start(bf16[2,384,128]{2,1,0:T(8,128)(2,1)S(1)} %pad_maximum_fusion.2), channel_id=1, source_target_pairs={{0,32},{16,48},{32,0},{48,16},{64,96},{80,112},{96,64},{112,80},{1... | collective-permute-start | bytes 589832 | tf_op jit(solution)/shard_map/ppermute | solution.py:247
  134.1 23.9 %collective-permute-start.5 = (bf16[8,160,256]{2,1,0:T(8,128)(2,1)S(1)}, bf16[8,160,256]{2,1,0:T(8,128)(2,1)S(1)}, u32[]{:S(2)}, u32[]{:S(2)}) collective-permute-start(bf16[8,160,256]{2,1,0:T(8,128)(2,1)S(1)} %slice.84.refs_0_), channel_id=1, source_target_pairs={{0,128},{128,256},{256,384},{384,0},{1,129},{129,257},{257,385},{3... | collective-permute-start | bytes 1966088 | tf_op jit(solution)/shard_map/ppermute | solution.py:346
  136.3 28.1 %collective-permute-start.6 = (bf16[8,160,256]{2,1,0:T(8,128)(2,1)S(1)}, bf16[8,160,256]{2,1,0:T(8,128)(2,1)}, u32[]{:S(2)}, u32[]{:S(2)}) collective-permute-start(bf16[8,160,256]{2,1,0:T(8,128)(2,1)S(1)} %slice.84.refs_0_), channel_id=1, source_target_pairs={{0,256},{128,384},{256,0},{384,128},{1,257},{129,385},{257,1},{385... | collective-permute-start | bytes 1966088 | tf_op jit(solution)/shard_map/ppermute | solution.py:346
  140.0 29.4 %collective-permute-start.7 = (bf16[8,160,256]{2,1,0:T(8,128)(2,1)S(1)}, bf16[8,160,256]{2,1,0:T(8,128)(2,1)}, u32[]{:S(2)}, u32[]{:S(2)}) collective-permute-start(bf16[8,160,256]{2,1,0:T(8,128)(2,1)S(1)} %slice.84.refs_0_), channel_id=1, source_target_pairs={{0,384},{128,0},{256,128},{384,256},{1,385},{129,1},{257,129},{385... | collective-permute-start | bytes 1966088 | tf_op jit(solution)/shard_map/ppermute | solution.py:346
  142.6 10.3 %collective-permute-start.9 = (bf16[4,384,128]{2,1,0:T(8,128)(2,1)S(1)}, bf16[4,384,128]{2,1,0:T(8,128)(2,1)}, u32[]{:S(2)}, u32[]{:S(2)}) collective-permute-start(bf16[4,384,128]{2,1,0:T(8,128)(2,1)S(1)} %constant_dynamic-update-slice_fusion.refs_0_), channel_id=1, source_target_pairs={{0,16},{16,0},{32,48},{48,32},{64,80},{80,64},{96,112},{112,96},{1... | collective-permute-start | bytes 1179656 | tf_op jit(solution)/shard_map/ppermute | solution.py:247
  146.0 35.9 %collective-permute-start.4 = (bf16[4,384,128]{2,1,0:T(8,128)(2,1)S(1)}, bf16[4,384,128]{2,1,0:T(8,128)(2,1)S(1)}, u32[]{:S(2)}, u32[]{:S(2)}) collective-permute-start(bf16[4,384,128]{2,1,0:T(8,128)(2,1)S(1)} %constant_dynamic-update-slice_fusion.refs_0_), channel_id=1, source_target_pairs={{0,8},{8,0},{1,9},{9,1},{2,10},{10,2},{3,11},{11,3},{4,12},{12,4},... | collective-permute-start | bytes 1179656 | tf_op jit(solution)/shard_map/ppermute | solution.py:361
  153.0 28.9 %collective-permute-start.10 = (bf16[4,384,128]{2,1,0:T(8,128)(2,1)}, bf16[4,384,128]{2,1,0:T(8,128)(2,1)}, u32[]{:S(2)}, u32[]{:S(2)}) collective-permute-start(bf16[4,384,128]{2,1,0:T(8,128)(2,1)} %collective-permute-done.9.refs_1_), channel_id=1, source_target_pairs={{0,8},{8,0},{1,9},{9,1},{2,10},{10,2},{3,11},{11,3},{4,12},{12,4},... | collective-permute-start | bytes 1179656 | tf_op jit(solution)/shard_map/ppermute | solution.py:361
  169.4 2.1 copy-start.4
  174.7 4.5 %collective-permute-start.8 = (bf16[2,192,128]{2,1,0:T(8,128)(2,1)S(1)}, bf16[2,192,128]{2,1,0:T(8,128)(2,1)S(1)}, u32[]{:S(2)}, u32[]{:S(2)}) collective-permute-start(bf16[2,192,128]{2,1,0:T(8,128)(2,1)S(1)} %get-tuple-element.34), channel_id=1, source_target_pairs={{0,8},{8,0},{1,9},{9,1},{2,10},{10,2},{3,11},{11,3},{4,12},{12,4},... | collective-permute-start | bytes 294920 | tf_op jit(solution)/shard_map/ppermute | solution.py:380
  179.3 8.0 %collective-permute-start.11 = (bf16[768,128]{1,0:T(8,128)(2,1)S(1)}, bf16[768,128]{1,0:T(8,128)(2,1)S(1)}, u32[]{:S(2)}, u32[]{:S(2)}) collective-permute-start(bf16[768,128]{1,0:T(8,128)(2,1)S(1)} %bitcast.54), channel_id=1, source_target_pairs={{128,0},{256,128},{384,256},{129,1},{257,129},{385,257},{130,2},{2... | collective-permute-start | bytes 589832 | tf_op jit(solution)/shard_map/ppermute | solution.py:382
  180.6 9.5 %collective-permute-start.12 = (bf16[768,128]{1,0:T(8,128)(2,1)S(1)}, bf16[768,128]{1,0:T(8,128)(2,1)S(1)}, u32[]{:S(2)}, u32[]{:S(2)}) collective-permute-start(bf16[768,128]{1,0:T(8,128)(2,1)S(1)} %bitcast.55), channel_id=1, source_target_pairs={{256,0},{384,128},{257,1},{385,129},{258,2},{386,130},{259,3},{387... | collective-permute-start | bytes 589832 | tf_op jit(solution)/shard_map/ppermute | solution.py:383
  194.6 8.6 %collective-permute-start.13 = (bf16[816,128]{1,0:T(8,128)(2,1)S(1)}, bf16[816,128]{1,0:T(8,128)(2,1)S(1)}, u32[]{:S(2)}, u32[]{:S(2)}) collective-permute-start(bf16[816,128]{1,0:T(8,128)(2,1)S(1)} %get-tuple-element.27), channel_id=1, source_target_pairs={{0,128},{128,256},{256,384},{1,129},{129,257},{257,385},{2,130},{1... | collective-permute-start | bytes 626696 | tf_op jit(solution)/shard_map/ppermute | solution.py:407
  200.1 7.6 %collective-permute-start.14 = (bf16[816,128]{1,0:T(8,128)(2,1)S(1)}, bf16[816,128]{1,0:T(8,128)(2,1)S(1)}, u32[]{:S(2)}, u32[]{:S(2)}) collective-permute-start(bf16[816,128]{1,0:T(8,128)(2,1)S(1)} %get-tuple-element.28), channel_id=1, source_target_pairs={{0,256},{128,384},{1,257},{129,385},{2,258},{130,386},{3,259},{131... | collective-permute-start | bytes 626696 | tf_op jit(solution)/shard_map/ppermute | solution.py:408
Sparse Core Ops, SparseCore 0:
  18.4 66.7 all-gather.6

commit v6 on v5

--- a/solution.py
+++ b/solution.py
@@ -43,12 +43,14 @@
     return v * cosine + pltpu.roll(v, 64, 1) * sine
 
 
-def collect(offsets, block, source, weights, panel):
-    for k in range(block.shape[0]):
-        for c in range(2):
-            slot = (source * block.shape[0] + k) * 2 + c
-            first = pl.multiple_of(offsets[slot], 16)
-            weights[pl.ds(first, panel), :] = block[k, c * panel : (c + 1) * panel, :]
+def collect(offsets, where, blocks, weights, panel):
+    nx, nz = blocks.shape[:2]
+    for s in range(nx):
+        for k, peer in enumerate(PEER):
+            for c in range(2):
+                slot = s * (2 * nz) + (where[1] ^ peer) * 2 + c
+                first = pl.multiple_of(offsets[slot], 16)
+                weights[pl.ds(first, panel), :] = blocks[s, k, c * panel : (c + 1) * panel, :]
 
 
 def norm_kernel(where, norm_gain, *refs):
@@ -67,7 +69,8 @@
         scale = lax.rsqrt(mean + epsilon)
         for half in range(2):
             for s in range(ny):
-                cols = pl.ds((s * 2 + half) * width, width)
+                source = s * 2 + (where[2] ^ half)
+                cols = pl.ds(pl.multiple_of(source * width, 128), width)
                 v = hidden[side * 2 + half][s].astype(jnp.float32)
                 v = v * scale * norm_gain[:, cols]
                 normed[pl.ds(first, rows), cols] = v.astype(jnp.bfloat16)
@@ -79,21 +82,17 @@
 def pair_kernel(panel, offsets, where, source, gain, cosine, sine, blocks, out, normed, weights, sem):
     copy = pltpu.make_async_copy(source, normed, sem)
     copy.start()
-    for s in range(blocks.shape[0]):
-        collect(offsets, blocks.at[s], s, weights, panel)
+    collect(offsets, where, blocks, weights, panel)
     copy.wait()
     v = jnp.dot(normed[...], weights[...], preferred_element_type=jnp.float32)
     keys = head_norm_rope(v, gain[...], cosine[...], sine[...])
     out[...] = jnp.where(where[0] == 0, keys, v).astype(jnp.bfloat16)
 
 
-def query_kernel(panel, offsets, where, source, gain, cosine, sine, *refs):
-    blocks, (out, normed, weights, sem) = refs[:-4], refs[-4:]
+def query_kernel(panel, offsets, where, source, gain, cosine, sine, blocks, out, normed, weights, sem):
     copy = pltpu.make_async_copy(source, normed, sem)
     copy.start()
-    nx = len(blocks)
-    for s in range(nx):
-        collect(offsets, blocks[s], lax.rem(where[2] + nx - s, nx), weights, panel)
+    collect(offsets, where, blocks, weights, panel)
     copy.wait()
     rows = out.shape[2]
     for side in range(2):
@@ -164,9 +163,18 @@
     return acc[:, :128] / safe, jnp.where(one > 0, top[...] * scale + jnp.log2(one), NEG)
 
 
-def own_kernel(where, begins, query, *refs):
+def own_kernel(where, begins, query, keys, values, out, log, acc, top):
+    rows = begins.shape[1]
+    index = where[2] + lax.broadcasted_iota(jnp.int32, (rows, 1), 0)
+    limits = [where[3 + i] for i in range(3)]
+    result, level = attend(query, keys, values, begins[0], index, *limits, acc, top)
+    out[...] = result
+    log[...] = level
+
+
+def remote_kernel(where, begins, near, far, *refs):
     mine, other = refs[:2], refs[2:4]
-    out, log, keys, values, acc, top = refs[4:]
+    out1, out2, keys, values, acc, top = refs[4:]
     block = mine[0].shape[1]
     values[:, 128:] = jnp.ones((values.shape[0], 128), values.dtype)
     for core, (first, second) in enumerate(((mine, other), (other, mine))):
@@ -178,15 +186,6 @@
                 keys[spot, :] = first[k // 4][k % 4]
                 values[spot, :128] = second[k // 4][k % 4]
 
-    rows = begins.shape[1]
-    index = where[2] + lax.broadcasted_iota(jnp.int32, (rows, 1), 0)
-    limits = [where[3 + i] for i in range(3)]
-    result, level = attend(query, keys, values, begins[0], index, *limits, acc, top)
-    out[...] = result
-    log[...] = level
-
-
-def remote_kernel(where, begins, near, far, keys, values, out1, out2, acc, top):
     eye = identity_mask()
     size = near.shape[0]
     for s, query, out in ((1, near, out1), (2, far, out2)):
@@ -239,10 +238,6 @@
             out[:, cols] = result[k * rows : (k + 1) * rows, :]
 
 
-def ring(size, shift):
-    return [(i, (i + shift) % size) for i in range(size)]
-
-
 def across(v, bit):
     return lax.ppermute(v, "z", [(i, i ^ bit) for i in range(8)])
 
@@ -252,7 +247,7 @@
 
 
 def body(hidden, norm_gain, query_gain, key_gain, weight_store, documents, owners):
-    x, z, c = (lax.axis_index(a) for a in ("x", "z", "c"))
+    x, z, c, w = (lax.axis_index(a) for a in ("x", "z", "c", "w"))
     nx, nz = (lax.axis_size(a) for a in ("x", "z"))
     rows = hidden.shape[0]
     slots = owners.shape[0]
@@ -277,16 +272,30 @@
     line = jnp.concatenate([columns, tail], axis=0)
     pair_docs = pair_docs[:, :rows].astype(jnp.int32)
 
-    hidden, line = lax.optimization_barrier((hidden, line))
-    line = lax.all_gather(line, "z", axis=0)
-    pair_line = jnp.broadcast_to(line[None, :, :, :128], (nx, nz, *line.shape[1:2], 128))
-    pair_blocks = lax.all_to_all(pair_line, "x", 0, 0)
-    query_line = line[:, : 2 * panel, 128:]
-
-    halves = lax.all_gather(hidden, "w", axis=0)
-    own = [lax.all_gather(halves[i], "y", axis=0) for i in range(2)]
-    other = [lax.ppermute(v, "c", swap) for v in own]
-    spot = jnp.stack([c, z, x]).astype(jnp.int32)
+    line = line[None]
+    step = across(line, 4)
+    far = lax.ppermute(hidden, "w", swap)
+    own_near = lax.all_gather(hidden, "y", axis=0)
+    step, far, own_near = lax.optimization_barrier((step, far, own_near))
+
+    line = jnp.concatenate([line, step], axis=0)
+    step = across(line, 2)
+    other_near = lax.ppermute(own_near, "c", swap)
+    own_far = lax.all_gather(far, "y", axis=0)
+    step, other_near, own_far = lax.optimization_barrier((step, other_near, own_far))
+
+    line = jnp.concatenate([line, step], axis=0)
+    step = across(line, 1)
+    other_far = lax.ppermute(own_far, "c", swap)
+    line = jnp.concatenate([line, step], axis=0)
+
+    def along_x(v):
+        return lax.all_to_all(jnp.broadcast_to(v[None], (nx, *v.shape)), "x", 0, 0)
+
+    pair_blocks = along_x(line[:, :, :128])
+    query_blocks = along_x(after(line[:, : 2 * panel, 128:], pair_blocks))
+
+    spot = jnp.stack([c, z, w]).astype(jnp.int32)
     features = norm_gain.shape[0]
     (normed,) = call(
         norm_kernel,
@@ -296,7 +305,7 @@
         [pltpu.VMEM((2 * rows, features), bf16), pltpu.SemaphoreType.DMA],
         4 * 10**9,
         out_hbm=True,
-    )(spot, norm_gain.astype(f32)[None, :], *own, *other)
+    )(spot, norm_gain.astype(f32)[None, :], own_near, own_far, other_near, other_far)
 
     riding = pair_blocks[:, :, 2 * panel : 2 * panel + 4, :].astype(f32)
     starts = jnp.sum(
@@ -320,7 +329,7 @@
     sine = jnp.concatenate([-sine, sine], axis=1)
     spread = [lax.dynamic_slice_in_dim(pair_begin, c * rows, rows, 0)]
     for s in (1, 2):
-        place = (jnp.minimum(x + s, nx - 1), z, 2 * c, 0)
+        place = (jnp.minimum(x + s, nx - 1), 0, 2 * c, 0)
         docs = lax.dynamic_slice(riding, place, (1, 1, 2, 128)).reshape(-1)[:rows]
         spread.append(begin_of(docs.astype(jnp.int32)))
     spread = jnp.stack(spread) - x * plane
@@ -341,10 +350,6 @@
         2 * 10**9,
         n_hbm=1,
     )(offsets, spot, normed, key_gain[None, :], cosine, sine, pair_blocks)
-    query_line = after(query_line, pair)
-    query_blocks = [query_line] + [
-        lax.ppermute(query_line, "x", ring(nx, s)) for s in range(1, nx)
-    ]
 
     inside = z * 2 * rows + c * rows
     low = [jnp.clip(spread[s, 0], 0, plane) for s in range(3)]
@@ -354,18 +359,19 @@
     begins = spread[:, :, None]
 
     mine0 = jnp.stack([pair, across(pair, 4)])
-    mine0, ranges, begins = lax.optimization_barrier((mine0, ranges, begins))
+    mine0, ranges, begins, query_blocks = lax.optimization_barrier(
+        (mine0, ranges, begins, query_blocks)
+    )
     mine0 = jnp.concatenate([mine0, across(mine0, 2)], axis=0)
     mine1 = across(mine0, 1)
     mine = [mine0, mine1]
     other = [lax.ppermute(v, "c", swap) for v in mine]
 
-    normed = after(normed, mine0)
     (query,) = call(
         functools.partial(query_kernel, panel),
         [jax.ShapeDtypeStruct((2, 2, rows, 128), bf16)],
         2,
-        3 + nx,
+        4,
         [
             pltpu.VMEM((2 * rows, features), bf16),
             pltpu.VMEM((features, 256), bf16),
@@ -373,7 +379,7 @@
         ],
         4 * 10**9,
         n_hbm=1,
-    )(offsets, spot, normed, query_gain[None, :], cosine, sine, *query_blocks)
+    )(offsets, spot, normed, query_gain[None, :], cosine, sine, query_blocks)
 
     own_query = lax.dynamic_index_in_dim(query, c, 0, keepdims=False)
     sent_query = lax.dynamic_index_in_dim(query, 1 - c, 0, keepdims=False)
@@ -383,29 +389,28 @@
     q2 = lax.ppermute(q0, "x", [(i, i - 2) for i in range(2, nx)])
 
     state = [pltpu.VMEM((4 * rows, 256), f32), pltpu.VMEM((4 * rows, 1), f32)]
-    o0, l0, keys, values = call(
+    r1, r2, keys, values = call(
+        remote_kernel,
+        [jax.ShapeDtypeStruct((4 * rows + 48, 128), bf16)] * 2
+        + [jax.ShapeDtypeStruct((plane, 128 * k), bf16) for k in (1, 2)],
+        1,
+        7,
+        state,
+        10**10,
+    )(ranges, begins, q1, q2, *mine, *other)
+    r1 = lax.ppermute(r1, "x", [(i, i + 1) for i in range(nx - 1)])
+    r2 = lax.ppermute(r2, "x", [(i, i + 2) for i in range(nx - 2)])
+    o0, l0 = call(
         own_kernel,
         [
             jax.ShapeDtypeStruct((4 * rows, 128), f32),
             jax.ShapeDtypeStruct((4 * rows, 1), f32),
-            jax.ShapeDtypeStruct((plane, 128), bf16),
-            jax.ShapeDtypeStruct((plane, 256), bf16),
         ],
         1,
-        6,
+        4,
         state,
         10**10,
-    )(ranges, begins, q0, *mine, *other)
-    r1, r2 = call(
-        remote_kernel,
-        [jax.ShapeDtypeStruct((4 * rows + 48, 128), bf16)] * 2,
-        1,
-        5,
-        state,
-        10**10,
-    )(ranges, begins, q1, q2, keys, values)
-    r1 = lax.ppermute(r1, "x", [(i, i + 1) for i in range(nx - 1)])
-    r2 = lax.ppermute(r2, "x", [(i, i + 2) for i in range(nx - 2)])
+    )(ranges, begins, q0, keys, values)
     came = jnp.stack([c, (x >= 1).astype(jnp.int32), (x >= 2).astype(jnp.int32)]).astype(jnp.int32)
     (context,) = call(combine_kernel, [jax.ShapeDtypeStruct((rows, 512), bf16)], 1, 4)(
         came, o0, l0, r1, r2

time: 220 us -> 215 us (0.977)
  blocking collectives: 58.8 us -> 37.6 us
  starting transfers between devices: 64.8 us -> 85.9 us
  between operations: 16.4 us -> 3.05 us
  local copies, waits for them, and re-layouts: 11.6 us -> 19.5 us
  Pallas kernels: 19.8 us -> 15.3 us
  other arithmetic: 5.24 us -> 8.51 us
    all_gather x3 -> x2, blocking collectives: 50.3 us -> 29.1 us  [the longest x1 15.9 us: body(): own_far = lax.all_gather(far, 'y', axis=0)]
    ppermute x3 -> x6, starting transfers between devices: 19.9 us -> 33.3 us  [across(): return lax.ppermute(v, 'z', [(i, i ^ bit) for i in range(8)])]
    ppermute x5 -> x3, waiting for transfers between devices: 11.3 us -> 0.01 us  [the longest x1 0.01 us: body(): other_near = lax.ppermute(own_near, 'c', swap)]
    all_to_all x1 -> x2, waiting for transfers between devices: 7.61 us -> 17.4 us  [along_x(): return lax.all_to_all(jnp.broadcast_to(v[None], (nx, *v.shape)), 'x', 0, 0)]
    ppermute x3 -> x6, waiting for transfers between devices: 3.33 us -> 12.7 us  [across(): return lax.ppermute(v, 'z', [(i, i ^ bit) for i in range(8)])]
    all_gather x1 -> x0, waiting for transfers between devices: 6.63 us -> none  [body(): line = lax.all_gather(line, 'z', axis=0)]
    ppermute x1, starting transfers between devices: 5.49 us -> 10.1 us  [body(): r1 = lax.ppermute(r1, 'x', [(i, i + 1) for i in range(nx - 1)])]
    unnamed x21 -> x35, local copies, waits for them, and re-layouts: 6.13 us -> 9.84 us
  transfers between devices with their start and end apart: 17 -> 18, of which waited for: 10 -> 8; matrix products, arithmetic and copies ran while one was open for 3% -> 6% of each run, Pallas kernels for 5% -> 5%
where the time goes in v6:
time: 215 us; the launch traced here: 212 us
  starting transfers between devices  85.9 us (40%)
  waiting for transfers between devices  41.9 us (19%)
  blocking collectives  37.6 us (17%)
  local copies, waits for them, and re-layouts  19.5 us (9%)
  Pallas kernels  15.3 us (7%)
  other arithmetic  8.51 us (4%)
  between operations  3.05 us (1%)
    ppermute x6, starting transfers between devices, across(): return lax.ppermute(v, 'z', [(i, i ^ bit) for i in range(8)])  33.3 us
    all_to_all x2, waiting for transfers between devices, along_x(): return lax.all_to_all(jnp.broadcast_to(v[None], (nx, *v.shape)), 'x', 0, 0)  17.4 us
    all_gather x1, blocking collectives, body(): own_far = lax.all_gather(far, 'y', axis=0)  15.9 us
    all_gather x1, blocking collectives, body(): own_near = lax.all_gather(hidden, 'y', axis=0)  13.2 us
    ppermute x6, waiting for transfers between devices, across(): return lax.ppermute(v, 'z', [(i, i ^ bit) for i in range(8)])  12.7 us
    ppermute x1, starting transfers between devices, body(): far = lax.ppermute(hidden, 'w', swap)  10.6 us
    ppermute x1, starting transfers between devices, body(): r1 = lax.ppermute(r1, 'x', [(i, i + 1) for i in range(nx - 1)])  10.1 us
    ppermute x2, starting transfers between devices, body(): other = [lax.ppermute(v, 'c', swap) for v in mine]  9.89 us
  transfers between devices with their start and end apart: 18, of which 8 were waited for; matrix products, arithmetic and copies ran while one was open for 6% of the time, Pallas kernels for 5%

profile of v6, /device:TPU:1, one launch (start us, length us, event | category | flops | bytes accessed | tf_op | source)
XLA Modules:
  0.0 211.8 jit_solution(15887520289597314019)
XLA Ops:
  2.3 8.5 %all-gather = bf16[192,768]{1,0:T(8,128)(2,1)S(1)} all-gather(bf16[96,768]{1,0:T(8,128)(2,1)S(1)} %fusion.2), channel_id=2, replica_groups=mesh['x'=4,'z'=8,'c'=2,'y'=4,'w'=2] {'c'}, dimensions={0}, use_global_device_ids=true | all-gather | bytes 442368 | tf_op jit(solution)/shard_map/all_gather | solution.py:261
  11.0 3.4 %collective-permute-start = (bf16[1,176,384]{2,1,0:T(8,128)(2,1)S(1)}, bf16[1,176,384]{2,1,0:T(8,128)(2,1)S(1)}, u32[]{:S(2)}, u32[]{:S(2)}) collective-permute-start(bf16[1,176,384]{2,1,0:T(8,128)(2,1)S(1)} %fusion.4), channel_id=1, source_target_pairs={{0,64},{16,80},{32,96},{48,112},{64,0},{80,16},{96,32},{112,48},{1... | collective-permute-start | bytes 405512 | tf_op jit(solution)/shard_map/ppermute | solution.py:242
  14.4 10.6 %collective-permute-start.1 = (bf16[192,640]{1,0:T(8,128)(2,1)S(1)}, bf16[192,640]{1,0:T(8,128)(2,1)S(1)}, u32[]{:S(2)}, u32[]{:S(2)}) collective-permute-start(bf16[192,640]{1,0:T(8,128)(2,1)S(1)} %copy-done.13), channel_id=1, source_target_pairs={{0,1},{1,0},{2,3},{3,2},{4,5},{5,4},{6,7},{7,6},{8,9},{9,8},{10,11... | collective-permute-start | bytes 737288 | tf_op jit(solution)/shard_map/ppermute | solution.py:277
  25.1 13.2 %all-gather.1 = bf16[768,640]{1,0:T(8,128)(2,1)S(1)} all-gather(bf16[192,640]{1,0:T(8,128)(2,1)S(1)} %copy-done.13), channel_id=3, replica_groups=mesh['x'=4,'z'=8,'c'=2,'y'=4,'w'=2] {'y'}, dimensions={0}, use_global_device_ids=true | all-gather | bytes 1228800 | tf_op jit(solution)/shard_map/all_gather | solution.py:278
  38.3 3.9 %collective-permute-start.3 = (bf16[4,192,640]{2,1,0:T(8,128)(2,1)S(1)}, bf16[4,192,640]{2,1,0:T(8,128)(2,1)S(1)}, u32[]{:S(2)}, u32[]{:S(2)}) collective-permute-start(bf16[4,192,640]{2,1,0:T(8,128)(2,1)S(1)} %bitcast.50), channel_id=1, source_target_pairs={{0,8},{8,0},{1,9},{9,1},{2,10},{10,2},{3,11},{11,3},{4,12},{12,4},... | collective-permute-start | bytes 2949128 | tf_op jit(solution)/shard_map/ppermute | solution.py:283
  42.2 14.7 %collective-permute-start.2 = (bf16[2,176,384]{2,1,0:T(8,128)(2,1)S(1)}, bf16[2,176,384]{2,1,0:T(8,128)(2,1)S(1)}, u32[]{:S(2)}, u32[]{:S(2)}) collective-permute-start(bf16[2,176,384]{2,1,0:T(8,128)(2,1)S(1)} %pad_maximum_fusion.5), channel_id=1, source_target_pairs={{0,32},{16,48},{32,0},{48,16},{64,96},{80,112},{96,64},{112,80},{1... | collective-permute-start | bytes 811016 | tf_op jit(solution)/shard_map/ppermute | solution.py:242
  56.9 15.9 %all-gather.2 = bf16[768,640]{1,0:T(8,128)(2,1)S(1)} all-gather(bf16[192,640]{1,0:T(8,128)(2,1)S(1)} %collective-permute-done.1), channel_id=4, replica_groups=mesh['x'=4,'z'=8,'c'=2,'y'=4,'w'=2] {'y'}, dimensions={0}, use_global_device_ids=true | all-gather | bytes 1228800 | tf_op jit(solution)/shard_map/all_gather | solution.py:284
  73.9 5.6 %collective-permute-start.5 = (bf16[4,176,384]{2,1,0:T(8,128)(2,1)S(1)}, bf16[4,176,384]{2,1,0:T(8,128)(2,1)S(1)}, u32[]{:S(2)}, u32[]{:S(2)}) collective-permute-start(bf16[4,176,384]{2,1,0:T(8,128)(2,1)S(1)} %pad_maximum_fusion.3), channel_id=1, source_target_pairs={{0,16},{16,0},{32,48},{48,32},{64,80},{80,64},{96,112},{112,96},{1... | collective-permute-start | bytes 1622024 | tf_op jit(solution)/shard_map/ppermute | solution.py:242
  79.6 4.3 %collective-permute-start.4 = (bf16[4,192,640]{2,1,0:T(8,128)(2,1)S(1)}, bf16[4,192,640]{2,1,0:T(8,128)(2,1)}, u32[]{:S(2)}, u32[]{:S(2)}) collective-permute-start(bf16[4,192,640]{2,1,0:T(8,128)(2,1)S(1)} %bitcast.52), channel_id=1, source_target_pairs={{0,8},{8,0},{1,9},{9,1},{2,10},{10,2},{3,11},{11,3},{4,12},{12,4},... | collective-permute-start | bytes 2949128 | tf_op jit(solution)/shard_map/ppermute | solution.py:289
  83.9 6.1 %collective-permute-done.5 = bf16[4,176,384]{2,1,0:T(8,128)(2,1)S(1)} collective-permute-done((bf16[4,176,384]{2,1,0:T(8,128)(2,1)S(1)}, bf16[4,176,384]{2,1,0:T(8,128)(2,1)S(1)}, u32[]{:S(2)}, u32[]{:S(2)}) %collective-permute-start.5) | collective-permute-done | bytes 540704 | tf_op jit(solution)/shard_map/ppermute | solution.py:242
  92.2 4.3 %all-to-all-start = ((bf16[4,8,176,128]{3,2,1,0:T(8,128)(2,1)}), bf16[4,8,176,128]{3,2,1,0:T(8,128)(2,1)S(1)}, u32[]{:S(2)}, u32[]{:S(2)}) async-start(bf16[4,8,176,128]{3,2,1,0:T(8,128)(2,1)} %broadcast_in_dim.21), calls=%async_computation | async-start | bytes 2883584 | tf_op jit(solution)/shard_map/all_to_all | solution.py:293
  96.8 2.1 %pad_maximum_fusion = bf16[8,160,256]{2,1,0:T(8,128)(2,1)} fusion(bf16[4,176,384]{2,1,0:T(8,128)(2,1)} %copy-done.11, bf16[2,176,384]{2,1,0:T(8,128)(2,1)} %copy-done.10, bf16[1,176,384]{2,1,0:T(8,128)(2,1)} %copy-done.12, bf16[1,176,384]{2,1,0:T(8,128)(2,1)} %copy-done.9), kind=kLoop, calls=%fused_computation.1 | loop fusion | flops 2621440 | bytes 1736704 | tf_op jit(solution)/shard_map/concatenate | solution.py:290
  98.9 3.8 %shard_map.94.source = bf16[384,5120]{1,0:T(8,128)(2,1)S(1)} custom-call(s32[3]{0:T(128)S(1)} %pad_add_fusion.1.where, f32[1,5120]{1,0:T(1,128)S(1)} %bitcast.58, bf16[4,192,640]{2,1,0:T(8,128)(2,1)S(1)} %bitcast.51, bf16[4,192,640]{2,1,0:T(8,128)(2,1)S(1)} %bitcast.53, bf16[4,192,640]{2,1,0:T(8,128)(2,1)S(1)} %copy-done.3, ...), custom_call_target="tpu_custom_call" | custom-call | flops 4000000000 | bytes 4194304 | tf_op jit(solution)/shard_map/pallas_call | solution.py:300
  104.6 8.2 %all-to-all-done.blocks = bf16[4,8,176,128]{3,2,1,0:T(8,128)(2,1)S(1)} async-done(((bf16[4,8,176,128]{3,2,1,0:T(8,128)(2,1)}), bf16[4,8,176,128]{3,2,1,0:T(8,128)(2,1)S(1)}, u32[]{:S(2)}, u32[]{:S(2)}) %all-to-all-start) | async-done | bytes 1441824 | tf_op jit(solution)/shard_map/all_to_all | solution.py:293
  113.6 2.9 %broadcast_in_dim.22 = bf16[4,8,160,256]{3,2,1,0:T(8,128)(2,1)} broadcast(bf16[8,160,256]{2,1,0:T(8,128)(2,1)} %pad_maximum_fusion), dimensions={1,2,3} | broadcast | bytes 3276800 | tf_op jit(solution)/shard_map/broadcast_in_dim | solution.py:293
  116.6 3.7 %all-to-all-start.1 = ((bf16[4,8,160,256]{3,2,1,0:T(8,128)(2,1)}), bf16[4,8,160,256]{3,2,1,0:T(8,128)(2,1)S(1)}, u32[]{:S(2)}, u32[]{:S(2)}) async-start(bf16[4,8,160,256]{3,2,1,0:T(8,128)(2,1)} %broadcast_in_dim.22), calls=%async_computation.1 | async-start | bytes 5242880 | tf_op jit(solution)/shard_map/all_to_all | solution.py:293
  121.6 2.1 copy-done.7
  123.7 2.3 %shard_map.95 = bf16[384,128]{1,0:T(8,128)(2,1)S(1)} custom-call(s32[64]{0:T(128)S(1)} %broadcast_multiply_fusion.offsets, s32[3]{0:T(128)S(1)} %pad_add_fusion.1.where, bf16[384,5120]{1,0:T(8,128)(2,1)S(1)} %copy-done.7, f32[1,128]{1,0:T(1,128)S(1)} %bitcast.59, f32[384,128]{1,0:T(8,128)S(1)} %get-tuple-element.54.cosine, ...), custom_call_target="tpu_custom_call" | custom-call | flops 2000000000 | bytes 4194304 | tf_op jit(solution)/shard_map/pallas_call | solution.py:340
  126.1 3.1 %collective-permute-start.6 = (bf16[384,128]{1,0:T(8,128)(2,1)S(1)}, bf16[384,128]{1,0:T(8,128)(2,1)S(1)}, u32[]{:S(2)}, u32[]{:S(2)}) collective-permute-start(bf16[384,128]{1,0:T(8,128)(2,1)S(1)} %shard_map.95), channel_id=1, source_target_pairs={{0,64},{16,80},{32,96},{48,112},{64,0},{80,16},{96,32},{112,48},{1... | collective-permute-start | bytes 294920 | tf_op jit(solution)/shard_map/ppermute | solution.py:242
  135.8 2.7 %collective-permute-done.6 = bf16[384,128]{1,0:T(8,128)(2,1)S(1)} collective-permute-done((bf16[384,128]{1,0:T(8,128)(2,1)S(1)}, bf16[384,128]{1,0:T(8,128)(2,1)S(1)}, u32[]{:S(2)}, u32[]{:S(2)}) %collective-permute-start.6) | collective-permute-done | bytes 98336 | tf_op jit(solution)/shard_map/ppermute | solution.py:242
  139.2 9.1 %all-to-all-done.1.blocks = bf16[4,8,160,256]{3,2,1,0:T(8,128)(2,1)S(1)} async-done(((bf16[4,8,160,256]{3,2,1,0:T(8,128)(2,1)}), bf16[4,8,160,256]{3,2,1,0:T(8,128)(2,1)S(1)}, u32[]{:S(2)}, u32[]{:S(2)}) %all-to-all-start.1) | async-done | bytes 2621472 | tf_op jit(solution)/shard_map/all_to_all | solution.py:293
  148.3 4.4 %collective-permute-start.7 = (bf16[2,384,128]{2,1,0:T(8,128)(2,1)}, bf16[2,384,128]{2,1,0:T(8,128)(2,1)}, u32[]{:S(2)}, u32[]{:S(2)}) collective-permute-start(bf16[2,384,128]{2,1,0:T(8,128)(2,1)} %pad_maximum_fusion.8), channel_id=1, source_target_pairs={{0,32},{16,48},{32,0},{48,16},{64,96},{80,112},{96,64},{112,80},{1... | collective-permute-start | bytes 589832 | tf_op jit(solution)/shard_map/ppermute | solution.py:242
  154.4 3.8 %collective-permute-done.7 = bf16[2,384,128]{2,1,0:T(8,128)(2,1)} collective-permute-done((bf16[2,384,128]{2,1,0:T(8,128)(2,1)}, bf16[2,384,128]{2,1,0:T(8,128)(2,1)}, u32[]{:S(2)}, u32[]{:S(2)}) %collective-permute-start.7) | collective-permute-done | bytes 196640 | tf_op jit(solution)/shard_map/ppermute | solution.py:242
  164.1 2.4 %shard_map.96 = bf16[2,2,192,128]{3,2,1,0:T(8,128)(2,1)S(1)} custom-call(s32[64]{0:T(128)S(1)} %broadcast_multiply_fusion.offsets, s32[3]{0:T(128)S(1)} %pad_add_fusion.1.where, bf16[384,5120]{1,0:T(8,128)(2,1)S(1)} %copy-done.8, f32[1,128]{1,0:T(1,128)S(1)} %bitcast.60, f32[384,128]{1,0:T(8,128)S(1)} %get-tuple-element.54.cosine, ...), custom_call_target="tpu_custom_call" | custom-call | flops 4000000000 | bytes 4194304 | tf_op jit(solution)/shard_map/pallas_call | solution.py:370
  166.5 7.5 %collective-permute-start.8 = (bf16[4,384,128]{2,1,0:T(8,128)(2,1)}, bf16[4,384,128]{2,1,0:T(8,128)(2,1)S(1)}, u32[]{:S(2)}, u32[]{:S(2)}) collective-permute-start(bf16[4,384,128]{2,1,0:T(8,128)(2,1)} %constant_dynamic-update-slice_fusion.refs_0_), channel_id=1, source_target_pairs={{0,8},{8,0},{1,9},{9,1},{2,10},{10,2},{3,11},{11,3},{4,12},{12,4},... | collective-permute-start | bytes 1179656 | tf_op jit(solution)/shard_map/ppermute | solution.py:368
  176.0 2.4 %collective-permute-start.13 = (bf16[4,384,128]{2,1,0:T(8,128)(2,1)}, bf16[4,384,128]{2,1,0:T(8,128)(2,1)S(1)}, u32[]{:S(2)}, u32[]{:S(2)}) collective-permute-start(bf16[4,384,128]{2,1,0:T(8,128)(2,1)} %collective-permute-done.12.refs_1_), channel_id=1, source_target_pairs={{0,8},{8,0},{1,9},{9,1},{2,10},{10,2},{3,11},{11,3},{4,12},{12,4},... | collective-permute-start | bytes 1179656 | tf_op jit(solution)/shard_map/ppermute | solution.py:368
  181.8 5.1 %collective-permute-done.10.near = bf16[768,128]{1,0:T(8,128)(2,1)S(1)} collective-permute-done((bf16[768,128]{1,0:T(8,128)(2,1)S(1)}, bf16[768,128]{1,0:T(8,128)(2,1)S(1)}, u32[]{:S(2)}, u32[]{:S(2)}) %collective-permute-start.10) | collective-permute-done | bytes 196640 | tf_op jit(solution)/shard_map/ppermute | solution.py:388
  186.8 2.8 %collective-permute-done.11.far = bf16[768,128]{1,0:T(8,128)(2,1)S(1)} collective-permute-done((bf16[768,128]{1,0:T(8,128)(2,1)S(1)}, bf16[768,128]{1,0:T(8,128)(2,1)S(1)}, u32[]{:S(2)}, u32[]{:S(2)}) %collective-permute-start.11) | collective-permute-done | bytes 196640 | tf_op jit(solution)/shard_map/ppermute | solution.py:389
  189.7 2.2 %shard_map.97 = (bf16[816,128]{1,0:T(8,128)(2,1)S(1)}, bf16[816,128]{1,0:T(8,128)(2,1)S(1)}, bf16[3072,128]{1,0:T(8,128)(2,1)S(1)}, bf16[3072,256]{1,0:T(8,128)(2,1)S(1)}) custom-call(s32[12]{0:T(128)S(1)} %stack.101.where, s32[3,192,1]{2,1,0:T(8,128)S(1)} %broadcast_subtract_fusion.begins, bf16[768,128]{1,0:T(8,128)(2,1)S(1)} %collective-permute-done.10.near, ...), custom_call_target="tpu_custom_call" | custom-call | flops 10000000000 | bytes 4194304 | tf_op jit(solution)/shard_map/pallas_call | solution.py:392
  191.8 10.1 %collective-permute-start.14 = (bf16[816,128]{1,0:T(8,128)(2,1)S(1)}, bf16[816,128]{1,0:T(8,128)(2,1)S(1)}, u32[]{:S(2)}, u32[]{:S(2)}) collective-permute-start(bf16[816,128]{1,0:T(8,128)(2,1)S(1)} %get-tuple-element.35), channel_id=1, source_target_pairs={{0,128},{128,256},{256,384},{1,129},{129,257},{257,385},{2,130},{1... | collective-permute-start | bytes 626696 | tf_op jit(solution)/shard_map/ppermute | solution.py:401
  203.2 2.5 %shard_map.98 = (f32[768,128]{1,0:T(8,128)S(1)}, f32[768,1]{1,0:T(8,128)S(1)}) custom-call(s32[12]{0:T(128)S(1)} %stack.101.where, s32[3,192,1]{2,1,0:T(8,128)S(1)} %broadcast_subtract_fusion.begins, bf16[768,128]{1,0:T(8,128)(2,1)S(1)} %bitcast.57, bf16[3072,128]{1,0:T(8,128)(2,1)S(1)} %get-tuple-element.31.keys, bf16[3072,256]{1,0:T(8,128)(2,1)S(1)} %get-tuple-element.32.values), custom_call_target="tpu_custom_call" | custom-call | flops 10000000000 | bytes 4194304 | tf_op jit(solution)/shard_map/pallas_call | solution.py:403
  205.7 4.0 %collective-permute-done.15.r2 = bf16[816,128]{1,0:T(8,128)(2,1)S(1)} collective-permute-done((bf16[816,128]{1,0:T(8,128)(2,1)S(1)}, bf16[816,128]{1,0:T(8,128)(2,1)S(1)}, u32[]{:S(2)}, u32[]{:S(2)}) %collective-permute-start.15) | collective-permute-done | bytes 208928 | tf_op jit(solution)/shard_map/ppermute | solution.py:402
  (96 shorter events, 30.8 us)
Async XLA Ops:
  0.6 13.8 %copy-start.13 = (bf16[192,640]{1,0:T(8,128)(2,1)S(1)}, bf16[192,640]{1,0:T(8,128)(2,1)}, u32[]{:S(2)}) copy-start(bf16[192,640]{1,0:T(8,128)(2,1)} %param.7) | copy-start | bytes 737284
  11.0 79.0 %copy-start.9 = (bf16[1,176,384]{2,1,0:T(8,128)(2,1)}, bf16[1,176,384]{2,1,0:T(8,128)(2,1)S(1)}, u32[]{:S(2)}) copy-start(bf16[1,176,384]{2,1,0:T(8,128)(2,1)S(1)} %fusion.4) | copy-start | bytes 405508
  11.0 27.3 %collective-permute-start = (bf16[1,176,384]{2,1,0:T(8,128)(2,1)S(1)}, bf16[1,176,384]{2,1,0:T(8,128)(2,1)S(1)}, u32[]{:S(2)}, u32[]{:S(2)}) collective-permute-start(bf16[1,176,384]{2,1,0:T(8,128)(2,1)S(1)} %fusion.4), channel_id=1, source_target_pairs={{0,64},{16,80},{32,96},{48,112},{64,0},{80,16},{96,32},{112,48},{1... | collective-permute-start | bytes 405512 | tf_op jit(solution)/shard_map/ppermute | solution.py:242
  14.4 23.8 %collective-permute-start.1 = (bf16[192,640]{1,0:T(8,128)(2,1)S(1)}, bf16[192,640]{1,0:T(8,128)(2,1)S(1)}, u32[]{:S(2)}, u32[]{:S(2)}) collective-permute-start(bf16[192,640]{1,0:T(8,128)(2,1)S(1)} %copy-done.13), channel_id=1, source_target_pairs={{0,1},{1,0},{2,3},{3,2},{4,5},{5,4},{6,7},{7,6},{8,9},{9,8},{10,11... | collective-permute-start | bytes 737288 | tf_op jit(solution)/shard_map/ppermute | solution.py:277
  38.3 51.7 %copy-start.12 = (bf16[1,176,384]{2,1,0:T(8,128)(2,1)}, bf16[1,176,384]{2,1,0:T(8,128)(2,1)S(1)}, u32[]{:S(2)}) copy-start(bf16[1,176,384]{2,1,0:T(8,128)(2,1)S(1)} %collective-permute-done) | copy-start | bytes 405508
  38.3 34.6 %collective-permute-start.3 = (bf16[4,192,640]{2,1,0:T(8,128)(2,1)S(1)}, bf16[4,192,640]{2,1,0:T(8,128)(2,1)S(1)}, u32[]{:S(2)}, u32[]{:S(2)}) collective-permute-start(bf16[4,192,640]{2,1,0:T(8,128)(2,1)S(1)} %bitcast.50), channel_id=1, source_target_pairs={{0,8},{8,0},{1,9},{9,1},{2,10},{10,2},{3,11},{11,3},{4,12},{12,4},... | collective-permute-start | bytes 2949128 | tf_op jit(solution)/shard_map/ppermute | solution.py:283
  42.2 30.6 %collective-permute-start.2 = (bf16[2,176,384]{2,1,0:T(8,128)(2,1)S(1)}, bf16[2,176,384]{2,1,0:T(8,128)(2,1)S(1)}, u32[]{:S(2)}, u32[]{:S(2)}) collective-permute-start(bf16[2,176,384]{2,1,0:T(8,128)(2,1)S(1)} %pad_maximum_fusion.5), channel_id=1, source_target_pairs={{0,32},{16,48},{32,0},{48,16},{64,96},{80,112},{96,64},{112,80},{1... | collective-permute-start | bytes 811016 | tf_op jit(solution)/shard_map/ppermute | solution.py:242
  72.8 17.1 %copy-start.10 = (bf16[2,176,384]{2,1,0:T(8,128)(2,1)}, bf16[2,176,384]{2,1,0:T(8,128)(2,1)S(1)}, u32[]{:S(2)}) copy-start(bf16[2,176,384]{2,1,0:T(8,128)(2,1)S(1)} %collective-permute-done.2) | copy-start | bytes 811012
  73.9 16.1 %collective-permute-start.5 = (bf16[4,176,384]{2,1,0:T(8,128)(2,1)S(1)}, bf16[4,176,384]{2,1,0:T(8,128)(2,1)S(1)}, u32[]{:S(2)}, u32[]{:S(2)}) collective-permute-start(bf16[4,176,384]{2,1,0:T(8,128)(2,1)S(1)} %pad_maximum_fusion.3), channel_id=1, source_target_pairs={{0,16},{16,0},{32,48},{48,32},{64,80},{80,64},{96,112},{112,96},{1... | collective-permute-start | bytes 1622024 | tf_op jit(solution)/shard_map/ppermute | solution.py:242
  79.6 19.4 %collective-permute-start.4 = (bf16[4,192,640]{2,1,0:T(8,128)(2,1)S(1)}, bf16[4,192,640]{2,1,0:T(8,128)(2,1)}, u32[]{:S(2)}, u32[]{:S(2)}) collective-permute-start(bf16[4,192,640]{2,1,0:T(8,128)(2,1)S(1)} %bitcast.52), channel_id=1, source_target_pairs={{0,8},{8,0},{1,9},{9,1},{2,10},{10,2},{3,11},{11,3},{4,12},{12,4},... | collective-permute-start | bytes 2949128 | tf_op jit(solution)/shard_map/ppermute | solution.py:289
  92.2 4.3 %copy-start.14 = (bf16[5120]{0:T(1024)(128)(2,1)S(1)}, bf16[5120]{0:T(1024)(128)(2,1)}, u32[]{:S(2)}) copy-start(bf16[5120]{0:T(1024)(128)(2,1)} %param.8) | copy-start | bytes 30724
  92.2 4.5 %copy-start.15 = (s32[64]{0:T(128)S(1)}, s32[64]{0:T(128)}, u32[]{:S(2)}) copy-start(s32[64]{0:T(128)} %param.13) | copy-start | bytes 772
  92.2 20.7 %all-to-all-start = ((bf16[4,8,176,128]{3,2,1,0:T(8,128)(2,1)}), bf16[4,8,176,128]{3,2,1,0:T(8,128)(2,1)S(1)}, u32[]{:S(2)}, u32[]{:S(2)}) async-start(bf16[4,8,176,128]{3,2,1,0:T(8,128)(2,1)} %broadcast_in_dim.21), calls=%async_computation | async-start | bytes 2883584 | tf_op jit(solution)/shard_map/all_to_all | solution.py:293
  96.6 2.3 %copy-start.3 = (bf16[4,192,640]{2,1,0:T(8,128)(2,1)S(1)}, bf16[4,192,640]{2,1,0:T(8,128)(2,1)}, u32[]{:S(2)}) copy-start(bf16[4,192,640]{2,1,0:T(8,128)(2,1)} %copy-done.2) | copy-start | bytes 2949124
  102.8 1.9 copy-start.6
  112.9 3.7 %copy-start = (bf16[4,8,176,128]{3,2,1,0:T(8,128)(2,1)}, bf16[4,8,176,128]{3,2,1,0:T(8,128)(2,1)S(1)}, u32[]{:S(2)}) copy-start(bf16[4,8,176,128]{3,2,1,0:T(8,128)(2,1)S(1)} %all-to-all-done.blocks) | copy-start | bytes 4325380
  116.6 31.8 %all-to-all-start.1 = ((bf16[4,8,160,256]{3,2,1,0:T(8,128)(2,1)}), bf16[4,8,160,256]{3,2,1,0:T(8,128)(2,1)S(1)}, u32[]{:S(2)}, u32[]{:S(2)}) async-start(bf16[4,8,160,256]{3,2,1,0:T(8,128)(2,1)} %broadcast_in_dim.22), calls=%async_computation.1 | async-start | bytes 5242880 | tf_op jit(solution)/shard_map/all_to_all | solution.py:293
  120.2 1.4 copy-start.1
  120.2 1.4 copy-start.4
  121.6 2.1 copy-start.7
  126.1 35.9 %copy-start.5 = (f32[128]{0:T(128)S(1)}, f32[128]{0:T(128)}, u32[]{:S(2)}) copy-start(f32[128]{0:T(128)} %param.9) | copy-start | bytes 1540
  126.1 12.4 %collective-permute-start.6 = (bf16[384,128]{1,0:T(8,128)(2,1)S(1)}, bf16[384,128]{1,0:T(8,128)(2,1)S(1)}, u32[]{:S(2)}, u32[]{:S(2)}) collective-permute-start(bf16[384,128]{1,0:T(8,128)(2,1)S(1)} %shard_map.95), channel_id=1, source_target_pairs={{0,64},{16,80},{32,96},{48,112},{64,0},{80,16},{96,32},{112,48},{1... | collective-permute-start | bytes 294920 | tf_op jit(solution)/shard_map/ppermute | solution.py:242
  148.3 9.9 %collective-permute-start.7 = (bf16[2,384,128]{2,1,0:T(8,128)(2,1)}, bf16[2,384,128]{2,1,0:T(8,128)(2,1)}, u32[]{:S(2)}, u32[]{:S(2)}) collective-permute-start(bf16[2,384,128]{2,1,0:T(8,128)(2,1)} %pad_maximum_fusion.8), channel_id=1, source_target_pairs={{0,32},{16,48},{32,0},{48,16},{64,96},{80,112},{96,64},{112,80},{1... | collective-permute-start | bytes 589832 | tf_op jit(solution)/shard_map/ppermute | solution.py:242
  159.9 16.1 %collective-permute-start.12 = (bf16[4,384,128]{2,1,0:T(8,128)(2,1)}, bf16[4,384,128]{2,1,0:T(8,128)(2,1)}, u32[]{:S(2)}, u32[]{:S(2)}) collective-permute-start(bf16[4,384,128]{2,1,0:T(8,128)(2,1)} %constant_dynamic-update-slice_fusion.refs_0_), channel_id=1, source_target_pairs={{0,16},{16,0},{32,48},{48,32},{64,80},{80,64},{96,112},{112,96},{1... | collective-permute-start | bytes 1179656 | tf_op jit(solution)/shard_map/ppermute | solution.py:242
  162.0 2.1 copy-start.8
  166.5 14.6 %collective-permute-start.8 = (bf16[4,384,128]{2,1,0:T(8,128)(2,1)}, bf16[4,384,128]{2,1,0:T(8,128)(2,1)S(1)}, u32[]{:S(2)}, u32[]{:S(2)}) collective-permute-start(bf16[4,384,128]{2,1,0:T(8,128)(2,1)} %constant_dynamic-update-slice_fusion.refs_0_), channel_id=1, source_target_pairs={{0,8},{8,0},{1,9},{9,1},{2,10},{10,2},{3,11},{11,3},{4,12},{12,4},... | collective-permute-start | bytes 1179656 | tf_op jit(solution)/shard_map/ppermute | solution.py:368
  174.0 4.4 %collective-permute-start.9 = (bf16[2,192,128]{2,1,0:T(8,128)(2,1)S(1)}, bf16[2,192,128]{2,1,0:T(8,128)(2,1)S(1)}, u32[]{:S(2)}, u32[]{:S(2)}) collective-permute-start(bf16[2,192,128]{2,1,0:T(8,128)(2,1)S(1)} %get-tuple-element.40), channel_id=1, source_target_pairs={{0,8},{8,0},{1,9},{9,1},{2,10},{10,2},{3,11},{11,3},{4,12},{12,4},... | collective-permute-start | bytes 294920 | tf_op jit(solution)/shard_map/ppermute | solution.py:386
  176.0 13.7 %collective-permute-start.13 = (bf16[4,384,128]{2,1,0:T(8,128)(2,1)}, bf16[4,384,128]{2,1,0:T(8,128)(2,1)S(1)}, u32[]{:S(2)}, u32[]{:S(2)}) collective-permute-start(bf16[4,384,128]{2,1,0:T(8,128)(2,1)} %collective-permute-done.12.refs_1_), channel_id=1, source_target_pairs={{0,8},{8,0},{1,9},{9,1},{2,10},{10,2},{3,11},{11,3},{4,12},{12,4},... | collective-permute-start | bytes 1179656 | tf_op jit(solution)/shard_map/ppermute | solution.py:368
  178.4 8.4 %collective-permute-start.10 = (bf16[768,128]{1,0:T(8,128)(2,1)S(1)}, bf16[768,128]{1,0:T(8,128)(2,1)S(1)}, u32[]{:S(2)}, u32[]{:S(2)}) collective-permute-start(bf16[768,128]{1,0:T(8,128)(2,1)S(1)} %bitcast.55), channel_id=1, source_target_pairs={{128,0},{256,128},{384,256},{129,1},{257,129},{385,257},{130,2},{2... | collective-permute-start | bytes 589832 | tf_op jit(solution)/shard_map/ppermute | solution.py:388
  179.7 9.9 %collective-permute-start.11 = (bf16[768,128]{1,0:T(8,128)(2,1)S(1)}, bf16[768,128]{1,0:T(8,128)(2,1)S(1)}, u32[]{:S(2)}, u32[]{:S(2)}) collective-permute-start(bf16[768,128]{1,0:T(8,128)(2,1)S(1)} %bitcast.56), channel_id=1, source_target_pairs={{256,0},{384,128},{257,1},{385,129},{258,2},{386,130},{259,3},{387... | collective-permute-start | bytes 589832 | tf_op jit(solution)/shard_map/ppermute | solution.py:389
  191.8 13.9 %collective-permute-start.14 = (bf16[816,128]{1,0:T(8,128)(2,1)S(1)}, bf16[816,128]{1,0:T(8,128)(2,1)S(1)}, u32[]{:S(2)}, u32[]{:S(2)}) collective-permute-start(bf16[816,128]{1,0:T(8,128)(2,1)S(1)} %get-tuple-element.35), channel_id=1, source_target_pairs={{0,128},{128,256},{256,384},{1,129},{129,257},{257,385},{2,130},{1... | collective-permute-start | bytes 626696 | tf_op jit(solution)/shard_map/ppermute | solution.py:401
  201.9 7.8 %collective-permute-start.15 = (bf16[816,128]{1,0:T(8,128)(2,1)S(1)}, bf16[816,128]{1,0:T(8,128)(2,1)S(1)}, u32[]{:S(2)}, u32[]{:S(2)}) collective-permute-start(bf16[816,128]{1,0:T(8,128)(2,1)S(1)} %get-tuple-element.36), channel_id=1, source_target_pairs={{0,256},{128,384},{1,257},{129,385},{2,258},{130,386},{3,259},{131... | collective-permute-start | bytes 626696 | tf_op jit(solution)/shard_map/ppermute | solution.py:402
  (2 other events, 1.8 us)

commit v7 on v6

--- a/solution.py
+++ b/solution.py
@@ -43,13 +43,12 @@
     return v * cosine + pltpu.roll(v, 64, 1) * sine
 
 
-def collect(offsets, where, blocks, weights, panel):
+def collect(offsets, blocks, weights, panel):
     nx, nz = blocks.shape[:2]
     for s in range(nx):
-        for k, peer in enumerate(PEER):
+        for k in range(nz):
             for c in range(2):
-                slot = s * (2 * nz) + (where[1] ^ peer) * 2 + c
-                first = pl.multiple_of(offsets[slot], 16)
+                first = pl.multiple_of(offsets[(s * nz + k) * 2 + c], 16)
                 weights[pl.ds(first, panel), :] = blocks[s, k, c * panel : (c + 1) * panel, :]
 
 
@@ -69,8 +68,7 @@
         scale = lax.rsqrt(mean + epsilon)
         for half in range(2):
             for s in range(ny):
-                source = s * 2 + (where[2] ^ half)
-                cols = pl.ds(pl.multiple_of(source * width, 128), width)
+                cols = pl.ds((s * 2 + half) * width, width)
                 v = hidden[side * 2 + half][s].astype(jnp.float32)
                 v = v * scale * norm_gain[:, cols]
                 normed[pl.ds(first, rows), cols] = v.astype(jnp.bfloat16)
@@ -82,7 +80,7 @@
 def pair_kernel(panel, offsets, where, source, gain, cosine, sine, blocks, out, normed, weights, sem):
     copy = pltpu.make_async_copy(source, normed, sem)
     copy.start()
-    collect(offsets, where, blocks, weights, panel)
+    collect(offsets, blocks, weights, panel)
     copy.wait()
     v = jnp.dot(normed[...], weights[...], preferred_element_type=jnp.float32)
     keys = head_norm_rope(v, gain[...], cosine[...], sine[...])
@@ -92,7 +90,7 @@
 def query_kernel(panel, offsets, where, source, gain, cosine, sine, blocks, out, normed, weights, sem):
     copy = pltpu.make_async_copy(source, normed, sem)
     copy.start()
-    collect(offsets, where, blocks, weights, panel)
+    collect(offsets, blocks, weights, panel)
     copy.wait()
     rows = out.shape[2]
     for side in range(2):
@@ -247,7 +245,7 @@
 
 
 def body(hidden, norm_gain, query_gain, key_gain, weight_store, documents, owners):
-    x, z, c, w = (lax.axis_index(a) for a in ("x", "z", "c", "w"))
+    x, z, c = (lax.axis_index(a) for a in ("x", "z", "c"))
     nx, nz = (lax.axis_size(a) for a in ("x", "z"))
     rows = hidden.shape[0]
     slots = owners.shape[0]
@@ -272,30 +270,19 @@
     line = jnp.concatenate([columns, tail], axis=0)
     pair_docs = pair_docs[:, :rows].astype(jnp.int32)
 
-    line = line[None]
-    step = across(line, 4)
-    far = lax.ppermute(hidden, "w", swap)
-    own_near = lax.all_gather(hidden, "y", axis=0)
-    step, far, own_near = lax.optimization_barrier((step, far, own_near))
-
-    line = jnp.concatenate([line, step], axis=0)
-    step = across(line, 2)
-    other_near = lax.ppermute(own_near, "c", swap)
-    own_far = lax.all_gather(far, "y", axis=0)
-    step, other_near, own_far = lax.optimization_barrier((step, other_near, own_far))
-
-    line = jnp.concatenate([line, step], axis=0)
-    step = across(line, 1)
-    other_far = lax.ppermute(own_far, "c", swap)
-    line = jnp.concatenate([line, step], axis=0)
-
-    def along_x(v):
-        return lax.all_to_all(jnp.broadcast_to(v[None], (nx, *v.shape)), "x", 0, 0)
-
-    pair_blocks = along_x(line[:, :, :128])
-    query_blocks = along_x(after(line[:, : 2 * panel, 128:], pair_blocks))
-
-    spot = jnp.stack([c, z, w]).astype(jnp.int32)
+    hidden, line = lax.optimization_barrier((hidden, line))
+    line = lax.all_gather(line, "z", axis=0)
+
+    halves = lax.all_gather(hidden, "w", axis=0)
+    own = [lax.all_gather(halves[i], "y", axis=0) for i in range(2)]
+    other = [lax.ppermute(v, "c", swap) for v in own]
+
+    pair_line = jnp.broadcast_to(line[None, :, :, :128], (nx, nz, *line.shape[1:2], 128))
+    query_line = jnp.broadcast_to(line[None, :, : 2 * panel, 128:], (nx, nz, 2 * panel, 256))
+    pair_blocks = lax.all_to_all(pair_line, "x", 0, 0)
+    query_blocks = lax.all_to_all(after(query_line, pair_blocks), "x", 0, 0)
+
+    spot = jnp.stack([c, z]).astype(jnp.int32)
     features = norm_gain.shape[0]
     (normed,) = call(
         norm_kernel,
@@ -305,7 +292,7 @@
         [pltpu.VMEM((2 * rows, features), bf16), pltpu.SemaphoreType.DMA],
         4 * 10**9,
         out_hbm=True,
-    )(spot, norm_gain.astype(f32)[None, :], own_near, own_far, other_near, other_far)
+    )(spot, norm_gain.astype(f32)[None, :], *own, *other)
 
     riding = pair_blocks[:, :, 2 * panel : 2 * panel + 4, :].astype(f32)
     starts = jnp.sum(
@@ -329,7 +316,7 @@
     sine = jnp.concatenate([-sine, sine], axis=1)
     spread = [lax.dynamic_slice_in_dim(pair_begin, c * rows, rows, 0)]
     for s in (1, 2):
-        place = (jnp.minimum(x + s, nx - 1), 0, 2 * c, 0)
+        place = (jnp.minimum(x + s, nx - 1), z, 2 * c, 0)
         docs = lax.dynamic_slice(riding, place, (1, 1, 2, 128)).reshape(-1)[:rows]
         spread.append(begin_of(docs.astype(jnp.int32)))
     spread = jnp.stack(spread) - x * plane
@@ -359,10 +346,9 @@
     begins = spread[:, :, None]
 
     mine0 = jnp.stack([pair, across(pair, 4)])
-    mine0, ranges, begins, query_blocks = lax.optimization_barrier(
-        (mine0, ranges, begins, query_blocks)
-    )
+    mine0, ranges, begins = lax.optimization_barrier((mine0, ranges, begins))
     mine0 = jnp.concatenate([mine0, across(mine0, 2)], axis=0)
+    mine0, query_blocks = lax.optimization_barrier((mine0, query_blocks))
     mine1 = across(mine0, 1)
     mine = [mine0, mine1]
     other = [lax.ppermute(v, "c", swap) for v in mine]

time: 215 us -> 220 us (1.023)
  blocking collectives: 37.6 us -> 59.2 us
  starting transfers between devices: 85.9 us -> 69.6 us
  between operations: 3.05 us -> 16.3 us
  waiting for transfers between devices: 41.9 us -> 31.7 us
    all_gather x2 -> x3, blocking collectives: 29.1 us -> 50.7 us  [the longest x1 25.3 us: body(): halves = lax.all_gather(hidden, 'w', axis=0)]
    ppermute x6 -> x3, starting transfers between devices: 33.3 us -> 17.3 us  [across(): return lax.ppermute(v, 'z', [(i, i ^ bit) for i in range(8)])]
    ppermute x3 -> x2, starting transfers between devices: 18.9 us -> 10.1 us  [body(): other = [lax.ppermute(v, 'c', swap) for v in own]]
    all_to_all x2, waiting for transfers between devices: 17.4 us -> 8.65 us  [the longest x1 8.65 us: body(): pair_blocks = lax.all_to_all(pair_line, 'x', 0, 0)]
    ppermute x6 -> x3, waiting for transfers between devices: 12.7 us -> 5.44 us  [across(): return lax.ppermute(v, 'z', [(i, i ^ bit) for i in range(8)])]
    all_gather x0 -> x1, waiting for transfers between devices: none -> 6.22 us  [body(): line = lax.all_gather(line, 'z', axis=0)]
    ppermute x1, starting transfers between devices: 10.1 us -> 14.8 us  [body(): r1 = lax.ppermute(r1, 'x', [(i, i + 1) for i in range(nx - 1)])]
    ppermute x2, starting transfers between devices: 9.89 us -> 12.7 us  [body(): other = [lax.ppermute(v, 'c', swap) for v in mine]]
  transfers between devices with their start and end apart: 18 -> 15, of which waited for: 8 -> 7; matrix products, arithmetic and copies ran while one was open for 6% -> 5% of each run, Pallas kernels for 5% -> 5%
where the time goes in v7:
time: 220 us; the launch traced here: 217 us
  starting transfers between devices  69.6 us (32%)
  blocking collectives  59.2 us (27%)
  waiting for transfers between devices  31.7 us (14%)
  local copies, waits for them, and re-layouts  17.8 us (8%)
  between operations  16.3 us (7%)
  Pallas kernels  15.7 us (7%)
  other arithmetic  7.13 us (3%)
    all_gather x1, blocking collectives, body(): halves = lax.all_gather(hidden, 'w', axis=0)  25.3 us
    all_gather x2, blocking collectives, body(): own = [lax.all_gather(halves[i], 'y', axis=0) for i in range(2)]  25.3 us
    ppermute x3, starting transfers between devices, across(): return lax.ppermute(v, 'z', [(i, i ^ bit) for i in range(8)])  17.3 us
    ppermute x1, starting transfers between devices, body(): r1 = lax.ppermute(r1, 'x', [(i, i + 1) for i in range(nx - 1)])  14.8 us
    ppermute x2, starting transfers between devices, body(): other = [lax.ppermute(v, 'c', swap) for v in mine]  12.7 us
    ppermute x2, starting transfers between devices, body(): other = [lax.ppermute(v, 'c', swap) for v in own]  10.1 us
    unnamed x32, local copies, waits for them, and re-layouts  9.47 us
    all_to_all x1, waiting for transfers between devices, body(): pair_blocks = lax.all_to_all(pair_line, 'x', 0, 0)  8.65 us
  transfers between devices with their start and end apart: 15, of which 7 were waited for; matrix products, arithmetic and copies ran while one was open for 5% of the time, Pallas kernels for 5%

profile of v7, /device:TPU:1, one launch (start us, length us, event | category | flops | bytes accessed | tf_op | source)
XLA Modules:
  0.0 217.4 jit_solution(898742194482296516)
XLA Ops:
  8.8 8.5 %all-gather = bf16[192,768]{1,0:T(8,128)(2,1)S(1)} all-gather(bf16[96,768]{1,0:T(8,128)(2,1)S(1)} %fusion.2), channel_id=2, replica_groups=mesh['x'=4,'z'=8,'c'=2,'y'=4,'w'=2] {'c'}, dimensions={0}, use_global_device_ids=true | all-gather | bytes 442368 | tf_op jit(solution)/shard_map/all_gather | solution.py:259
  18.2 25.3 %all-gather.1 = bf16[384,640]{1,0:T(8,128)(2,1)S(1)} all-gather(bf16[192,640]{1,0:T(8,128)(2,1)} %param.7), channel_id=3, replica_groups=mesh['x'=4,'z'=8,'c'=2,'y'=4,'w'=2] {'w'}, dimensions={0}, use_global_device_ids=true | all-gather | bytes 737280 | tf_op jit(solution)/shard_map/all_gather | solution.py:276
  43.5 12.0 %all-gather.3 = bf16[768,640]{1,0:T(8,128)(2,1)S(1)} all-gather(bf16[192,640]{1,0:T(8,128)(2,1)S(1)} %get-tuple-element.34), channel_id=5, replica_groups=mesh['x'=4,'z'=8,'c'=2,'y'=4,'w'=2] {'y'}, dimensions={0}, use_global_device_ids=true | all-gather | bytes 1228800 | tf_op jit(solution)/shard_map/all_gather | solution.py:277
  55.6 6.2 %collective-permute-start = (bf16[4,192,640]{2,1,0:T(8,128)(2,1)S(1)}, bf16[4,192,640]{2,1,0:T(8,128)(2,1)}, u32[]{:S(2)}, u32[]{:S(2)}) collective-permute-start(bf16[4,192,640]{2,1,0:T(8,128)(2,1)S(1)} %bitcast.48), channel_id=1, source_target_pairs={{0,8},{8,0},{1,9},{9,1},{2,10},{10,2},{3,11},{11,3},{4,12},{12,4},... | collective-permute-start | bytes 2949128 | tf_op jit(solution)/shard_map/ppermute | solution.py:278
  61.8 13.3 %all-gather.4 = bf16[768,640]{1,0:T(8,128)(2,1)S(1)} all-gather(bf16[192,640]{1,0:T(8,128)(2,1)S(1)} %get-tuple-element.33), channel_id=6, replica_groups=mesh['x'=4,'z'=8,'c'=2,'y'=4,'w'=2] {'y'}, dimensions={0}, use_global_device_ids=true | all-gather | bytes 1228800 | tf_op jit(solution)/shard_map/all_gather | solution.py:277
  75.1 3.8 %collective-permute-start.1 = (bf16[4,192,640]{2,1,0:T(8,128)(2,1)S(1)}, bf16[4,192,640]{2,1,0:T(8,128)(2,1)}, u32[]{:S(2)}, u32[]{:S(2)}) collective-permute-start(bf16[4,192,640]{2,1,0:T(8,128)(2,1)S(1)} %bitcast.50), channel_id=1, source_target_pairs={{0,8},{8,0},{1,9},{9,1},{2,10},{10,2},{3,11},{11,3},{4,12},{12,4},... | collective-permute-start | bytes 2949128 | tf_op jit(solution)/shard_map/ppermute | solution.py:278
  78.9 6.2 %all-gather.7.cloned.1.call-done = bf16[1408,384]{1,0:T(8,128)(2,1)} async-done(((bf16[176,384]{1,0:T(8,128)(2,1)}), bf16[1408,384]{1,0:T(8,128)(2,1)}) %all-gather.7.cloned.1.call-update) | async-done | bytes 1081360 | tf_op jit(solution)/shard_map/all_gather | solution.py:274
  87.5 4.8 %all-to-all-start = ((bf16[4,8,176,128]{3,2,1,0:T(8,128)(2,1)}), bf16[4,8,176,128]{3,2,1,0:T(8,128)(2,1)S(1)}, u32[]{:S(2)}, u32[]{:S(2)}) async-start(bf16[4,8,176,128]{3,2,1,0:T(8,128)(2,1)} %broadcast_in_dim.18), calls=%async_computation | async-start | bytes 2883584 | tf_op jit(solution)/shard_map/all_to_all | solution.py:282
  92.6 4.2 %shard_map.94.source = bf16[384,5120]{1,0:T(8,128)(2,1)S(1)} custom-call(s32[2]{0:T(128)S(1)} %pad_add_fusion.1.where, f32[1,5120]{1,0:T(1,128)S(1)} %bitcast.56, bf16[4,192,640]{2,1,0:T(8,128)(2,1)S(1)} %bitcast.49, bf16[4,192,640]{2,1,0:T(8,128)(2,1)S(1)} %bitcast.51, bf16[4,192,640]{2,1,0:T(8,128)(2,1)} %collective-permute-done.refs_2_, ...), custom_call_target="tpu_custom_call" | custom-call | flops 4000000000 | bytes 4194304 | tf_op jit(solution)/shard_map/pallas_call | solution.py:287
  96.9 1.9 copy-done.8
  98.8 8.7 %all-to-all-done.blocks = bf16[4,8,176,128]{3,2,1,0:T(8,128)(2,1)S(1)} async-done(((bf16[4,8,176,128]{3,2,1,0:T(8,128)(2,1)}), bf16[4,8,176,128]{3,2,1,0:T(8,128)(2,1)S(1)}, u32[]{:S(2)}, u32[]{:S(2)}) %all-to-all-start) | async-done | bytes 1441824 | tf_op jit(solution)/shard_map/all_to_all | solution.py:282
  110.1 3.8 %all-to-all-start.1 = ((bf16[4,8,160,256]{3,2,1,0:T(8,128)(2,1)}), bf16[4,8,160,256]{3,2,1,0:T(8,128)(2,1)S(1)}, u32[]{:S(2)}, u32[]{:S(2)}) async-start(bf16[4,8,160,256]{3,2,1,0:T(8,128)(2,1)} %broadcast_in_dim.19), calls=%async_computation.1 | async-start | bytes 5242880 | tf_op jit(solution)/shard_map/all_to_all | solution.py:283
  116.4 2.1 copy-done.9
  118.5 2.3 %shard_map.95 = bf16[384,128]{1,0:T(8,128)(2,1)S(1)} custom-call(s32[64]{0:T(128)S(1)} %broadcast_multiply_fusion.offsets, s32[2]{0:T(128)S(1)} %pad_add_fusion.1.where, bf16[384,5120]{1,0:T(8,128)(2,1)S(1)} %copy-done.9, f32[1,128]{1,0:T(1,128)S(1)} %bitcast.57, f32[384,128]{1,0:T(8,128)S(1)} %get-tuple-element.50.cosine, ...), custom_call_target="tpu_custom_call" | custom-call | flops 2000000000 | bytes 4194304 | tf_op jit(solution)/shard_map/pallas_call | solution.py:327
  120.9 8.1 %collective-permute-start.2 = (bf16[384,128]{1,0:T(8,128)(2,1)S(1)}, bf16[384,128]{1,0:T(8,128)(2,1)}, u32[]{:S(2)}, u32[]{:S(2)}) collective-permute-start(bf16[384,128]{1,0:T(8,128)(2,1)S(1)} %shard_map.95), channel_id=1, source_target_pairs={{0,64},{16,80},{32,96},{48,112},{64,0},{80,16},{96,32},{112,48},{1... | collective-permute-start | bytes 294920 | tf_op jit(solution)/shard_map/ppermute | solution.py:240
  131.9 2.1 stack.97.where
  134.9 7.2 %collective-permute-start.3 = (bf16[2,384,128]{2,1,0:T(8,128)(2,1)S(1)}, bf16[2,384,128]{2,1,0:T(8,128)(2,1)}, u32[]{:S(2)}, u32[]{:S(2)}) collective-permute-start(bf16[2,384,128]{2,1,0:T(8,128)(2,1)S(1)} %pad_maximum_fusion.3), channel_id=1, source_target_pairs={{0,32},{16,48},{32,0},{48,16},{64,96},{80,112},{96,64},{112,80},{1... | collective-permute-start | bytes 589832 | tf_op jit(solution)/shard_map/ppermute | solution.py:240
  142.2 3.3 %collective-permute-done.3 = bf16[2,384,128]{2,1,0:T(8,128)(2,1)} collective-permute-done((bf16[2,384,128]{2,1,0:T(8,128)(2,1)S(1)}, bf16[2,384,128]{2,1,0:T(8,128)(2,1)}, u32[]{:S(2)}, u32[]{:S(2)}) %collective-permute-start.3) | collective-permute-done | bytes 196640 | tf_op jit(solution)/shard_map/ppermute | solution.py:240
  146.6 10.0 %collective-permute-start.4 = (bf16[4,384,128]{2,1,0:T(8,128)(2,1)S(1)}, bf16[4,384,128]{2,1,0:T(8,128)(2,1)}, u32[]{:S(2)}, u32[]{:S(2)}) collective-permute-start(bf16[4,384,128]{2,1,0:T(8,128)(2,1)S(1)} %pad_maximum_fusion.refs_0_), channel_id=1, source_target_pairs={{0,8},{8,0},{1,9},{9,1},{2,10},{10,2},{3,11},{11,3},{4,12},{12,4},... | collective-permute-start | bytes 1179656 | tf_op jit(solution)/shard_map/ppermute | solution.py:354
  156.6 2.0 collective-permute-start.8
  160.4 2.1 copy-done.10
  162.6 2.4 %shard_map.96 = bf16[2,2,192,128]{3,2,1,0:T(8,128)(2,1)S(1)} custom-call(s32[64]{0:T(128)S(1)} %broadcast_multiply_fusion.offsets, s32[2]{0:T(128)S(1)} %pad_add_fusion.1.where, bf16[384,5120]{1,0:T(8,128)(2,1)S(1)} %copy-done.10, f32[1,128]{1,0:T(1,128)S(1)} %bitcast.58, f32[384,128]{1,0:T(8,128)S(1)} %copy-done.3, f32[384,128]{1,0:T(8,128)S(1)} %copy-done.5, ...), custom_call_target="tpu_custom_call" | custom-call | flops 4000000000 | bytes 4194304 | tf_op jit(solution)/shard_map/pallas_call | solution.py:356
  165.0 2.2 %collective-permute-start.5 = (bf16[2,192,128]{2,1,0:T(8,128)(2,1)S(1)}, bf16[2,192,128]{2,1,0:T(8,128)(2,1)S(1)}, u32[]{:S(2)}, u32[]{:S(2)}) collective-permute-start(bf16[2,192,128]{2,1,0:T(8,128)(2,1)S(1)} %get-tuple-element.36), channel_id=1, source_target_pairs={{0,8},{8,0},{1,9},{9,1},{2,10},{10,2},{3,11},{11,3},{4,12},{12,4},... | collective-permute-start | bytes 294920 | tf_op jit(solution)/shard_map/ppermute | solution.py:372
  167.2 2.1 collective-permute-done.8.refs_1_
  169.3 2.7 %collective-permute-start.9 = (bf16[4,384,128]{2,1,0:T(8,128)(2,1)}, bf16[4,384,128]{2,1,0:T(8,128)(2,1)S(1)}, u32[]{:S(2)}, u32[]{:S(2)}) collective-permute-start(bf16[4,384,128]{2,1,0:T(8,128)(2,1)} %collective-permute-done.8.refs_1_), channel_id=1, source_target_pairs={{0,8},{8,0},{1,9},{9,1},{2,10},{10,2},{3,11},{11,3},{4,12},{12,4},... | collective-permute-start | bytes 1179656 | tf_op jit(solution)/shard_map/ppermute | solution.py:354
  176.3 4.2 %collective-permute-done.6.near = bf16[768,128]{1,0:T(8,128)(2,1)S(1)} collective-permute-done((bf16[768,128]{1,0:T(8,128)(2,1)S(1)}, bf16[768,128]{1,0:T(8,128)(2,1)S(1)}, u32[]{:S(2)}, u32[]{:S(2)}) %collective-permute-start.6) | collective-permute-done | bytes 196640 | tf_op jit(solution)/shard_map/ppermute | solution.py:374
  180.5 2.8 %collective-permute-done.7.far = bf16[768,128]{1,0:T(8,128)(2,1)S(1)} collective-permute-done((bf16[768,128]{1,0:T(8,128)(2,1)S(1)}, bf16[768,128]{1,0:T(8,128)(2,1)S(1)}, u32[]{:S(2)}, u32[]{:S(2)}) %collective-permute-start.7) | collective-permute-done | bytes 196640 | tf_op jit(solution)/shard_map/ppermute | solution.py:375
  183.3 2.2 %shard_map.97 = (bf16[816,128]{1,0:T(8,128)(2,1)S(1)}, bf16[816,128]{1,0:T(8,128)(2,1)S(1)}, bf16[3072,128]{1,0:T(8,128)(2,1)S(1)}, bf16[3072,256]{1,0:T(8,128)(2,1)S(1)}) custom-call(s32[12]{0:T(128)S(1)} %stack.97.where, s32[3,192,1]{2,1,0:T(8,128)S(1)} %broadcast_subtract_fusion.begins, bf16[768,128]{1,0:T(8,128)(2,1)S(1)} %collective-permute-done.6.near, ...), custom_call_target="tpu_custom_call" | custom-call | flops 10000000000 | bytes 4194304 | tf_op jit(solution)/shard_map/pallas_call | solution.py:378
  185.5 14.8 %collective-permute-start.10 = (bf16[816,128]{1,0:T(8,128)(2,1)S(1)}, bf16[816,128]{1,0:T(8,128)(2,1)S(1)}, u32[]{:S(2)}, u32[]{:S(2)}) collective-permute-start(bf16[816,128]{1,0:T(8,128)(2,1)S(1)} %get-tuple-element.29), channel_id=1, source_target_pairs={{0,128},{128,256},{256,384},{1,129},{129,257},{257,385},{2,130},{1... | collective-permute-start | bytes 626696 | tf_op jit(solution)/shard_map/ppermute | solution.py:387
  201.6 2.5 %shard_map.98 = (f32[768,128]{1,0:T(8,128)S(1)}, f32[768,1]{1,0:T(8,128)S(1)}) custom-call(s32[12]{0:T(128)S(1)} %stack.97.where, s32[3,192,1]{2,1,0:T(8,128)S(1)} %broadcast_subtract_fusion.begins, bf16[768,128]{1,0:T(8,128)(2,1)S(1)} %bitcast.55, bf16[3072,128]{1,0:T(8,128)(2,1)S(1)} %get-tuple-element.25.keys, bf16[3072,256]{1,0:T(8,128)(2,1)S(1)} %get-tuple-element.26.values), custom_call_target="tpu_custom_call" | custom-call | flops 10000000000 | bytes 4194304 | tf_op jit(solution)/shard_map/pallas_call | solution.py:389
  204.1 4.4 %collective-permute-done.11.r2 = bf16[816,128]{1,0:T(8,128)(2,1)S(1)} collective-permute-done((bf16[816,128]{1,0:T(8,128)(2,1)S(1)}, bf16[816,128]{1,0:T(8,128)(2,1)S(1)}, u32[]{:S(2)}, u32[]{:S(2)}) %collective-permute-start.11) | collective-permute-done | bytes 208928 | tf_op jit(solution)/shard_map/ppermute | solution.py:388
  208.5 2.0 shard_map.99
  (88 shorter events, 20.8 us)
Async XLA Ops:
  7.2 78.0 %all-gather.7.cloned.1.call-start = ((), (), s32[]{:S(2)}) async-start(), calls=%async_computation.2 | async-start | bytes 1216512 | tf_op jit(solution)/shard_map/all_gather | solution.py:274
  55.6 37.0 %collective-permute-start = (bf16[4,192,640]{2,1,0:T(8,128)(2,1)S(1)}, bf16[4,192,640]{2,1,0:T(8,128)(2,1)}, u32[]{:S(2)}, u32[]{:S(2)}) collective-permute-start(bf16[4,192,640]{2,1,0:T(8,128)(2,1)S(1)} %bitcast.48), channel_id=1, source_target_pairs={{0,8},{8,0},{1,9},{9,1},{2,10},{10,2},{3,11},{11,3},{4,12},{12,4},... | collective-permute-start | bytes 2949128 | tf_op jit(solution)/shard_map/ppermute | solution.py:278
  75.1 17.5 %collective-permute-start.1 = (bf16[4,192,640]{2,1,0:T(8,128)(2,1)S(1)}, bf16[4,192,640]{2,1,0:T(8,128)(2,1)}, u32[]{:S(2)}, u32[]{:S(2)}) collective-permute-start(bf16[4,192,640]{2,1,0:T(8,128)(2,1)S(1)} %bitcast.50), channel_id=1, source_target_pairs={{0,8},{8,0},{1,9},{9,1},{2,10},{10,2},{3,11},{11,3},{4,12},{12,4},... | collective-permute-start | bytes 2949128 | tf_op jit(solution)/shard_map/ppermute | solution.py:278
  85.2 7.1 %copy-start.13 = (bf16[5120]{0:T(1024)(128)(2,1)S(1)}, bf16[5120]{0:T(1024)(128)(2,1)}, u32[]{:S(2)}) copy-start(bf16[5120]{0:T(1024)(128)(2,1)} %param.8) | copy-start | bytes 30724
  85.2 7.3 %copy-start.14 = (s32[64]{0:T(128)S(1)}, s32[64]{0:T(128)}, u32[]{:S(2)}) copy-start(s32[64]{0:T(128)} %param.13) | copy-start | bytes 772
  87.5 19.9 %all-to-all-start = ((bf16[4,8,176,128]{3,2,1,0:T(8,128)(2,1)}), bf16[4,8,176,128]{3,2,1,0:T(8,128)(2,1)S(1)}, u32[]{:S(2)}, u32[]{:S(2)}) async-start(bf16[4,8,176,128]{3,2,1,0:T(8,128)(2,1)} %broadcast_in_dim.18), calls=%async_computation | async-start | bytes 2883584 | tf_op jit(solution)/shard_map/all_to_all | solution.py:282
  92.6 6.1 %copy-start.11 = (bf16[1408,384]{1,0:T(8,128)(2,1)S(1)}, bf16[1408,384]{1,0:T(8,128)(2,1)}, u32[]{:S(2)}) copy-start(bf16[1408,384]{1,0:T(8,128)(2,1)} %all-gather.7.cloned.1.call-done) | copy-start | bytes 3244036
  96.9 1.9 copy-start.8
  107.5 2.6 %copy-start = (bf16[4,8,176,128]{3,2,1,0:T(8,128)(2,1)}, bf16[4,8,176,128]{3,2,1,0:T(8,128)(2,1)S(1)}, u32[]{:S(2)}) copy-start(bf16[4,8,176,128]{3,2,1,0:T(8,128)(2,1)S(1)} %all-to-all-done.blocks) | copy-start | bytes 4325380
  110.0 4.9 %copy-start.6 = (f32[128]{0:T(128)S(1)}, f32[128]{0:T(128)}, u32[]{:S(2)}) copy-start(f32[128]{0:T(128)} %param.10) | copy-start | bytes 1540
  110.1 36.5 %all-to-all-start.1 = ((bf16[4,8,160,256]{3,2,1,0:T(8,128)(2,1)}), bf16[4,8,160,256]{3,2,1,0:T(8,128)(2,1)S(1)}, u32[]{:S(2)}, u32[]{:S(2)}) async-start(bf16[4,8,160,256]{3,2,1,0:T(8,128)(2,1)} %broadcast_in_dim.19), calls=%async_computation.1 | async-start | bytes 5242880 | tf_op jit(solution)/shard_map/all_to_all | solution.py:283
  114.9 6.0 %copy-start.2 = (f32[384,128]{1,0:T(8,128)}, f32[384,128]{1,0:T(8,128)S(1)}, u32[]{:S(2)}) copy-start(f32[384,128]{1,0:T(8,128)S(1)} %get-tuple-element.50.cosine) | copy-start | bytes 589828
  114.9 6.0 %copy-start.4 = (f32[384,128]{1,0:T(8,128)}, f32[384,128]{1,0:T(8,128)S(1)}, u32[]{:S(2)}) copy-start(f32[384,128]{1,0:T(8,128)S(1)} %get-tuple-element.51.sine) | copy-start | bytes 589828
  114.9 1.5 copy-start.1
  116.4 2.1 copy-start.9
  118.5 40.0 %copy-start.7 = (f32[128]{0:T(128)S(1)}, f32[128]{0:T(128)}, u32[]{:S(2)}) copy-start(f32[128]{0:T(128)} %param.9) | copy-start | bytes 1540
  120.9 13.1 %collective-permute-start.2 = (bf16[384,128]{1,0:T(8,128)(2,1)S(1)}, bf16[384,128]{1,0:T(8,128)(2,1)}, u32[]{:S(2)}, u32[]{:S(2)}) collective-permute-start(bf16[384,128]{1,0:T(8,128)(2,1)S(1)} %shard_map.95), channel_id=1, source_target_pairs={{0,64},{16,80},{32,96},{48,112},{64,0},{80,16},{96,32},{112,48},{1... | collective-permute-start | bytes 294920 | tf_op jit(solution)/shard_map/ppermute | solution.py:240
  134.9 7.2 %copy-start.12 = (bf16[2,384,128]{2,1,0:T(8,128)(2,1)}, bf16[2,384,128]{2,1,0:T(8,128)(2,1)S(1)}, u32[]{:S(2)}) copy-start(bf16[2,384,128]{2,1,0:T(8,128)(2,1)S(1)} %pad_maximum_fusion.3) | copy-start | bytes 589828
  134.9 10.6 %collective-permute-start.3 = (bf16[2,384,128]{2,1,0:T(8,128)(2,1)S(1)}, bf16[2,384,128]{2,1,0:T(8,128)(2,1)}, u32[]{:S(2)}, u32[]{:S(2)}) collective-permute-start(bf16[2,384,128]{2,1,0:T(8,128)(2,1)S(1)} %pad_maximum_fusion.3), channel_id=1, source_target_pairs={{0,32},{16,48},{32,0},{48,16},{64,96},{80,112},{96,64},{112,80},{1... | collective-permute-start | bytes 589832 | tf_op jit(solution)/shard_map/ppermute | solution.py:240
  146.6 28.2 %collective-permute-start.4 = (bf16[4,384,128]{2,1,0:T(8,128)(2,1)S(1)}, bf16[4,384,128]{2,1,0:T(8,128)(2,1)}, u32[]{:S(2)}, u32[]{:S(2)}) collective-permute-start(bf16[4,384,128]{2,1,0:T(8,128)(2,1)S(1)} %pad_maximum_fusion.refs_0_), channel_id=1, source_target_pairs={{0,8},{8,0},{1,9},{9,1},{2,10},{10,2},{3,11},{11,3},{4,12},{12,4},... | collective-permute-start | bytes 1179656 | tf_op jit(solution)/shard_map/ppermute | solution.py:354
  156.6 12.7 %collective-permute-start.8 = (bf16[4,384,128]{2,1,0:T(8,128)(2,1)S(1)}, bf16[4,384,128]{2,1,0:T(8,128)(2,1)}, u32[]{:S(2)}, u32[]{:S(2)}) collective-permute-start(bf16[4,384,128]{2,1,0:T(8,128)(2,1)S(1)} %pad_maximum_fusion.refs_0_), channel_id=1, source_target_pairs={{0,16},{16,0},{32,48},{48,32},{64,80},{80,64},{96,112},{112,96},{1... | collective-permute-start | bytes 1179656 | tf_op jit(solution)/shard_map/ppermute | solution.py:240
  158.6 0.9 copy-start.3
  159.5 0.9 copy-start.5
  160.4 2.1 copy-start.10
  165.0 7.0 %collective-permute-start.5 = (bf16[2,192,128]{2,1,0:T(8,128)(2,1)S(1)}, bf16[2,192,128]{2,1,0:T(8,128)(2,1)S(1)}, u32[]{:S(2)}, u32[]{:S(2)}) collective-permute-start(bf16[2,192,128]{2,1,0:T(8,128)(2,1)S(1)} %get-tuple-element.36), channel_id=1, source_target_pairs={{0,8},{8,0},{1,9},{9,1},{2,10},{10,2},{3,11},{11,3},{4,12},{12,4},... | collective-permute-start | bytes 294920 | tf_op jit(solution)/shard_map/ppermute | solution.py:372
  169.3 14.0 %collective-permute-start.9 = (bf16[4,384,128]{2,1,0:T(8,128)(2,1)}, bf16[4,384,128]{2,1,0:T(8,128)(2,1)S(1)}, u32[]{:S(2)}, u32[]{:S(2)}) collective-permute-start(bf16[4,384,128]{2,1,0:T(8,128)(2,1)} %collective-permute-done.8.refs_1_), channel_id=1, source_target_pairs={{0,8},{8,0},{1,9},{9,1},{2,10},{10,2},{3,11},{11,3},{4,12},{12,4},... | collective-permute-start | bytes 1179656 | tf_op jit(solution)/shard_map/ppermute | solution.py:354
  172.1 8.4 %collective-permute-start.6 = (bf16[768,128]{1,0:T(8,128)(2,1)S(1)}, bf16[768,128]{1,0:T(8,128)(2,1)S(1)}, u32[]{:S(2)}, u32[]{:S(2)}) collective-permute-start(bf16[768,128]{1,0:T(8,128)(2,1)S(1)} %bitcast.53), channel_id=1, source_target_pairs={{128,0},{256,128},{384,256},{129,1},{257,129},{385,257},{130,2},{2... | collective-permute-start | bytes 589832 | tf_op jit(solution)/shard_map/ppermute | solution.py:374
  173.4 9.9 %collective-permute-start.7 = (bf16[768,128]{1,0:T(8,128)(2,1)S(1)}, bf16[768,128]{1,0:T(8,128)(2,1)S(1)}, u32[]{:S(2)}, u32[]{:S(2)}) collective-permute-start(bf16[768,128]{1,0:T(8,128)(2,1)S(1)} %bitcast.54), channel_id=1, source_target_pairs={{256,0},{384,128},{257,1},{385,129},{258,2},{386,130},{259,3},{387... | collective-permute-start | bytes 589832 | tf_op jit(solution)/shard_map/ppermute | solution.py:375
  185.5 18.6 %collective-permute-start.10 = (bf16[816,128]{1,0:T(8,128)(2,1)S(1)}, bf16[816,128]{1,0:T(8,128)(2,1)S(1)}, u32[]{:S(2)}, u32[]{:S(2)}) collective-permute-start(bf16[816,128]{1,0:T(8,128)(2,1)S(1)} %get-tuple-element.29), channel_id=1, source_target_pairs={{0,128},{128,256},{256,384},{1,129},{129,257},{257,385},{2,130},{1... | collective-permute-start | bytes 626696 | tf_op jit(solution)/shard_map/ppermute | solution.py:387
  200.3 8.2 %collective-permute-start.11 = (bf16[816,128]{1,0:T(8,128)(2,1)S(1)}, bf16[816,128]{1,0:T(8,128)(2,1)S(1)}, u32[]{:S(2)}, u32[]{:S(2)}) collective-permute-start(bf16[816,128]{1,0:T(8,128)(2,1)S(1)} %get-tuple-element.30), channel_id=1, source_target_pairs={{0,256},{128,384},{1,257},{129,385},{2,258},{130,386},{3,259},{131... | collective-permute-start | bytes 626696 | tf_op jit(solution)/shard_map/ppermute | solution.py:388
Sparse Core Ops, SparseCore 0:
  18.3 66.8 all-gather.6

commit v8 on v7

--- a/solution.py
+++ b/solution.py
@@ -32,9 +32,6 @@
         compiler_params=pltpu.CompilerParams(vmem_limit_bytes=VMEM_LIMIT),
         cost_estimate=pl.CostEstimate(flops=flops, bytes_accessed=4 << 20, transcendentals=0),
     )
-
-
-PEER = (0, 4, 2, 6, 1, 5, 3, 7)
 
 
 def head_norm_rope(v, gain, cosine, sine):
@@ -163,31 +160,27 @@
 
 def own_kernel(where, begins, query, keys, values, out, log, acc, top):
     rows = begins.shape[1]
-    index = where[2] + lax.broadcasted_iota(jnp.int32, (rows, 1), 0)
-    limits = [where[3 + i] for i in range(3)]
+    index = where[1] + lax.broadcasted_iota(jnp.int32, (rows, 1), 0)
+    limits = [where[2 + i] for i in range(3)]
     result, level = attend(query, keys, values, begins[0], index, *limits, acc, top)
     out[...] = result
     log[...] = level
 
 
 def remote_kernel(where, begins, near, far, *refs):
-    mine, other = refs[:2], refs[2:4]
-    out1, out2, keys, values, acc, top = refs[4:]
-    block = mine[0].shape[1]
+    mine, other, out1, out2, keys, values, acc, top = refs
     values[:, 128:] = jnp.ones((values.shape[0], 128), values.dtype)
     for core, (first, second) in enumerate(((mine, other), (other, mine))):
 
         @pl.when(where[0] == core)
         def _(first=first, second=second):
-            for k in range(8):
-                spot = pl.ds(pl.multiple_of((where[1] ^ PEER[k]) * block, block), block)
-                keys[spot, :] = first[k // 4][k % 4]
-                values[spot, :128] = second[k // 4][k % 4]
+            keys[...] = first[...]
+            values[:, :128] = second[...]
 
     eye = identity_mask()
     size = near.shape[0]
     for s, query, out in ((1, near, out1), (2, far, out2)):
-        limits = [where[3 + 3 * s + i] for i in range(3)]
+        limits = [where[2 + 3 * s + i] for i in range(3)]
         result, log = attend(query, keys, values, begins[s], None, *limits, acc, top)
         out[0:size, :] = result.astype(jnp.bfloat16)
         rest = jnp.concatenate(
@@ -236,8 +229,8 @@
             out[:, cols] = result[k * rows : (k + 1) * rows, :]
 
 
-def across(v, bit):
-    return lax.ppermute(v, "z", [(i, i ^ bit) for i in range(8)])
+def gather(v, axis):
+    return lax.all_to_all(jnp.broadcast_to(v[None], (lax.axis_size(axis), *v.shape)), axis, 0, 0)
 
 
 def after(v, *earlier):
@@ -259,30 +252,30 @@
     both = lax.all_gather(jnp.concatenate([weight_store, riders], axis=0), "c", axis=0)
     pair_docs = both[:, panel, :256]
     columns = both[:, :panel].reshape(2 * panel, -1)
-    columns = jnp.concatenate(
+    pair_line = jnp.concatenate(
         [
             lax.dynamic_slice_in_dim(columns, 512 + 128 * c, 128, 1),
-            lax.dynamic_slice_in_dim(columns, 256 * c, 256, 1),
+            jnp.pad(pair_docs.reshape(4, 128), ((0, 12), (0, 0))),
         ],
-        axis=1,
+        axis=0,
     )
-    tail = jnp.pad(pair_docs.reshape(4, 128), ((0, 12), (0, 256)))
-    line = jnp.concatenate([columns, tail], axis=0)
+    query_line = lax.dynamic_slice_in_dim(columns, 256 * c, 256, 1)
     pair_docs = pair_docs[:, :rows].astype(jnp.int32)
 
-    hidden, line = lax.optimization_barrier((hidden, line))
-    line = lax.all_gather(line, "z", axis=0)
-
+    hidden, pair_line, query_line = lax.optimization_barrier((hidden, pair_line, query_line))
+    pair_line = gather(pair_line, "z")
     halves = lax.all_gather(hidden, "w", axis=0)
+    halves, pair_line, query_line = lax.optimization_barrier((halves, pair_line, query_line))
+    pair_blocks = gather(pair_line, "x")
+    query_line = gather(query_line, "z")
     own = [lax.all_gather(halves[i], "y", axis=0) for i in range(2)]
     other = [lax.ppermute(v, "c", swap) for v in own]
-
-    pair_line = jnp.broadcast_to(line[None, :, :, :128], (nx, nz, *line.shape[1:2], 128))
-    query_line = jnp.broadcast_to(line[None, :, : 2 * panel, 128:], (nx, nz, 2 * panel, 256))
-    pair_blocks = lax.all_to_all(pair_line, "x", 0, 0)
-    query_blocks = lax.all_to_all(after(query_line, pair_blocks), "x", 0, 0)
-
-    spot = jnp.stack([c, z]).astype(jnp.int32)
+    own, other, pair_blocks, query_line = lax.optimization_barrier(
+        (own, other, pair_blocks, query_line)
+    )
+    query_blocks = gather(query_line, "x")
+
+    spot = jnp.stack([c]).astype(jnp.int32)
     features = norm_gain.shape[0]
     (normed,) = call(
         norm_kernel,
@@ -342,16 +335,11 @@
     low = [jnp.clip(spread[s, 0], 0, plane) for s in range(3)]
     high = [inside + rows] + [jnp.where(x + s < nx, plane, 0) for s in (1, 2)]
     limits = [v for s in range(3) for v in (low[s], high[s], spread[s, rows - 1])]
-    ranges = jnp.stack([c, z, inside] + limits).astype(jnp.int32)
+    ranges = jnp.stack([c, inside] + limits).astype(jnp.int32)
     begins = spread[:, :, None]
 
-    mine0 = jnp.stack([pair, across(pair, 4)])
-    mine0, ranges, begins = lax.optimization_barrier((mine0, ranges, begins))
-    mine0 = jnp.concatenate([mine0, across(mine0, 2)], axis=0)
-    mine0, query_blocks = lax.optimization_barrier((mine0, query_blocks))
-    mine1 = across(mine0, 1)
-    mine = [mine0, mine1]
-    other = [lax.ppermute(v, "c", swap) for v in mine]
+    mine = gather(pair, "z").reshape(plane, 128)
+    other = lax.ppermute(mine, "c", swap)
 
     (query,) = call(
         functools.partial(query_kernel, panel),
@@ -367,6 +355,7 @@
         n_hbm=1,
     )(offsets, spot, normed, query_gain[None, :], cosine, sine, query_blocks)
 
+    query, ranges, begins = lax.optimization_barrier((query, ranges, begins))
     own_query = lax.dynamic_index_in_dim(query, c, 0, keepdims=False)
     sent_query = lax.dynamic_index_in_dim(query, 1 - c, 0, keepdims=False)
     q0 = jnp.concatenate([own_query, lax.ppermute(sent_query, "c", swap)], axis=0)
@@ -380,10 +369,10 @@
         [jax.ShapeDtypeStruct((4 * rows + 48, 128), bf16)] * 2
         + [jax.ShapeDtypeStruct((plane, 128 * k), bf16) for k in (1, 2)],
         1,
-        7,
+        5,
         state,
         10**10,
-    )(ranges, begins, q1, q2, *mine, *other)
+    )(ranges, begins, q1, q2, mine, other)
     r1 = lax.ppermute(r1, "x", [(i, i + 1) for i in range(nx - 1)])
     r2 = lax.ppermute(r2, "x", [(i, i + 2) for i in range(nx - 2)])
     o0, l0 = call(
@@ -403,7 +392,7 @@
     )
 
     own_part = lax.dynamic_slice_in_dim(pair, c * rows, rows, 0)
-    other_part = lax.dynamic_slice_in_dim(other[0][0], c * rows, rows, 0)
+    other_part = lax.dynamic_slice_in_dim(other, inside, rows, 0)
     keys_fresh = jnp.where(c == 0, own_part, other_part)
     values_fresh = jnp.where(c == 0, other_part, own_part)
     return keys_fresh, values_fresh, context

time: 220 us -> 272 us (1.24)
  blocking collectives: 59.2 us -> 117 us
  between operations: 16.3 us -> 2.85 us
  waiting for transfers between devices: 31.7 us -> 42.1 us
  local copies, waits for them, and re-layouts: 17.8 us -> 14.4 us
    all_to_all x0 -> x2, blocking collectives: none -> 64.2 us  [gather(): lax.all_to_all(jnp.broadcast_to(v[None], (lax.axis_size(axis), *v.shape))...]
    all_to_all x2 -> x3, starting transfers between devices: 8.56 us -> 36.9 us  [gather(): lax.all_to_all(jnp.broadcast_to(v[None], (lax.axis_size(axis), *v.shape))...]
    ppermute x5 -> x1, starting transfers between devices: 30 us -> 3.72 us  [body(): other = lax.ppermute(mine, 'c', swap)]
    all_to_all x2 -> x3, waiting for transfers between devices: 8.65 us -> 28.9 us  [gather(): lax.all_to_all(jnp.broadcast_to(v[None], (lax.axis_size(axis), *v.shape))...]
    all_gather x1, blocking collectives: 25.3 us -> 19.1 us  [body(): halves = lax.all_gather(hidden, 'w', axis=0)]
    all_gather x1 -> x0, waiting for transfers between devices: 6.22 us -> none  [body(): line = lax.all_gather(line, 'z', axis=0)]
    ppermute x5 -> x1, waiting for transfers between devices: 5.44 us -> 0.01 us  [body(): other = lax.ppermute(mine, 'c', swap)]
    unnamed x32 -> x28, local copies, waits for them, and re-layouts: 9.47 us -> 4.98 us
  transfers between devices with their start and end apart: 15 -> 11, of which waited for: 7 -> 7; matrix products, arithmetic and copies ran while one was open for 5% -> 3% of each run, Pallas kernels for 5% -> 2%
where the time goes in v8:
time: 272 us; the launch traced here: 269 us
  blocking collectives  117 us (43%)
  starting transfers between devices  70.3 us (26%)
  waiting for transfers between devices  42.1 us (15%)
  Pallas kernels  15.8 us (6%)
  local copies, waits for them, and re-layouts  14.4 us (5%)
  other arithmetic  6.93 us (3%)
  between operations  2.85 us (1%)
    all_to_all x2, blocking collectives, gather(): lax.all_to_all(jnp.broadcast_to(v[None], (lax.axis_size(axis), *v.shape))...  64.2 us
    all_to_all x3, starting transfers between devices, gather(): lax.all_to_all(jnp.broadcast_to(v[None], (lax.axis_size(axis), *v.shape))...  36.9 us
    all_to_all x3, waiting for transfers between devices, gather(): lax.all_to_all(jnp.broadcast_to(v[None], (lax.axis_size(axis), *v.shape))...  28.9 us
    all_gather x2, blocking collectives, body(): own = [lax.all_gather(halves[i], 'y', axis=0) for i in range(2)]  25.3 us
    all_gather x1, blocking collectives, body(): halves = lax.all_gather(hidden, 'w', axis=0)  19.1 us
    ppermute x2, starting transfers between devices, body(): other = [lax.ppermute(v, 'c', swap) for v in own]  10.8 us
    ppermute x1, starting transfers between devices, body(): r1 = lax.ppermute(r1, 'x', [(i, i + 1) for i in range(nx - 1)])  10.4 us
    all_gather x1, blocking collectives, body(): lax.all_gather(jnp.concatenate([weight_store, riders], axis=0), 'c', axis=0)  8.53 us
  transfers between devices with their start and end apart: 11, of which 7 were waited for; matrix products, arithmetic and copies ran while one was open for 3% of the time, Pallas kernels for 2%

profile of v8, /device:TPU:1, one launch (start us, length us, event | category | flops | bytes accessed | tf_op | source)
XLA Modules:
  0.0 269.4 jit_solution(10035113511231373381)
XLA Ops:
  2.3 8.5 %all-gather = bf16[192,768]{1,0:T(8,128)(2,1)S(1)} all-gather(bf16[96,768]{1,0:T(8,128)(2,1)S(1)} %fusion.1), channel_id=2, replica_groups=mesh['x'=4,'z'=8,'c'=2,'y'=4,'w'=2] {'c'}, dimensions={0}, use_global_device_ids=true | all-gather | bytes 442368 | tf_op jit(solution)/shard_map/all_gather | solution.py:252
  11.7 6.9 %all-to-all-start = ((bf16[8,176,128]{2,1,0:T(8,128)(2,1)}), bf16[8,176,128]{2,1,0:T(8,128)(2,1)S(1)}, u32[]{:S(2)}, u32[]{:S(2)}) async-start(bf16[8,176,128]{2,1,0:T(8,128)(2,1)} %broadcast_in_dim.23), calls=%async_computation | async-start | bytes 720896 | tf_op jit(solution)/shard_map/all_to_all | solution.py:233
  18.6 19.1 %all-gather.1 = bf16[384,640]{1,0:T(8,128)(2,1)S(1)} all-gather(bf16[192,640]{1,0:T(8,128)(2,1)S(1)} %copy-done.10), channel_id=3, replica_groups=mesh['x'=4,'z'=8,'c'=2,'y'=4,'w'=2] {'w'}, dimensions={0}, use_global_device_ids=true | all-gather | bytes 737280 | tf_op jit(solution)/shard_map/all_gather | solution.py:267
  37.7 10.5 %all-to-all-done = bf16[8,176,128]{2,1,0:T(8,128)(2,1)S(1)} async-done(((bf16[8,176,128]{2,1,0:T(8,128)(2,1)}), bf16[8,176,128]{2,1,0:T(8,128)(2,1)S(1)}, u32[]{:S(2)}, u32[]{:S(2)}) %all-to-all-start) | async-done | bytes 360480 | tf_op jit(solution)/shard_map/all_to_all | solution.py:233
  48.3 15.7 %all_to_all.25.blocks = bf16[4,8,176,128]{3,2,1,0:T(8,128)(2,1)S(1)} all-to-all(bf16[4,8,176,128]{3,2,1,0:T(8,128)(2,1)S(1)} %broadcast_in_dim.24), channel_id=1, replica_groups=mesh['x'=4,'z'=8,'c'=2,'y'=4,'w'=2] {'x'}, dimensions={0} | all-to-all | bytes 2883584 | tf_op jit(solution)/shard_map/all_to_all | solution.py:233
  64.9 26.2 %all-to-all-start.2 = ((bf16[8,160,256]{2,1,0:T(8,128)(2,1)}), bf16[8,160,256]{2,1,0:T(8,128)(2,1)}, u32[]{:S(2)}, u32[]{:S(2)}) async-start(bf16[8,160,256]{2,1,0:T(8,128)(2,1)} %broadcast_in_dim.25), calls=%async_computation.2 | async-start | bytes 1310720 | tf_op jit(solution)/shard_map/all_to_all | solution.py:233
  91.2 12.0 %all_gather.22.refs_0_ = bf16[4,192,640]{2,1,0:T(8,128)(2,1)S(1)} all-gather(bf16[1,192,640]{2,1,0:T(8,128)(2,1)S(1)} %get-tuple-element.50), channel_id=1, replica_groups=mesh['x'=4,'z'=8,'c'=2,'y'=4,'w'=2] {'y'}, dimensions={0}, use_global_device_ids=true | all-gather | bytes 1228800 | tf_op jit(solution)/shard_map/all_gather | solution.py:271
  103.2 7.5 %collective-permute-start = (bf16[4,192,640]{2,1,0:T(8,128)(2,1)S(1)}, bf16[4,192,640]{2,1,0:T(8,128)(2,1)}, u32[]{:S(2)}, u32[]{:S(2)}) collective-permute-start(bf16[4,192,640]{2,1,0:T(8,128)(2,1)S(1)} %all_gather.22.refs_0_), channel_id=1, source_target_pairs={{0,8},{8,0},{1,9},{9,1},{2,10},{10,2},{3,11},{11,3},{4,12},{12,4},... | collective-permute-start | bytes 2949128 | tf_op jit(solution)/shard_map/ppermute | solution.py:272
  110.7 13.3 %all_gather.23.refs_1_ = bf16[4,192,640]{2,1,0:T(8,128)(2,1)S(1)} all-gather(bf16[1,192,640]{2,1,0:T(8,128)(2,1)S(1)} %get-tuple-element.49), channel_id=1, replica_groups=mesh['x'=4,'z'=8,'c'=2,'y'=4,'w'=2] {'y'}, dimensions={0}, use_global_device_ids=true | all-gather | bytes 1228800 | tf_op jit(solution)/shard_map/all_gather | solution.py:271
  124.0 3.3 %collective-permute-start.1 = (bf16[4,192,640]{2,1,0:T(8,128)(2,1)S(1)}, bf16[4,192,640]{2,1,0:T(8,128)(2,1)}, u32[]{:S(2)}, u32[]{:S(2)}) collective-permute-start(bf16[4,192,640]{2,1,0:T(8,128)(2,1)S(1)} %all_gather.23.refs_1_), channel_id=1, source_target_pairs={{0,8},{8,0},{1,9},{9,1},{2,10},{10,2},{3,11},{11,3},{4,12},{12,4},... | collective-permute-start | bytes 2949128 | tf_op jit(solution)/shard_map/ppermute | solution.py:272
  127.5 2.0 collective-permute-done.1.refs_3_
  131.4 4.3 %shard_map.94.source = bf16[384,5120]{1,0:T(8,128)(2,1)S(1)} custom-call(s32[1]{0:T(128)} %bitcast.where, f32[1,5120]{1,0:T(1,128)S(1)} %bitcast.46, bf16[4,192,640]{2,1,0:T(8,128)(2,1)S(1)} %all_gather.22.refs_0_, bf16[4,192,640]{2,1,0:T(8,128)(2,1)S(1)} %all_gather.23.refs_1_, bf16[4,192,640]{2,1,0:T(8,128)(2,1)} %collective-permute-done.refs_2_, ...), custom_call_target="tpu_custom_call" | custom-call | flops 4000000000 | bytes 4194304 | tf_op jit(solution)/shard_map/pallas_call | solution.py:280
  135.7 2.3 shard_map.95
  138.2 48.5 %all_to_all.26 = bf16[8,384,128]{2,1,0:T(8,128)(2,1)S(1)} all-to-all(bf16[8,384,128]{2,1,0:T(8,128)(2,1)S(1)} %broadcast_in_dim.27), channel_id=1, replica_groups=mesh['x'=4,'z'=8,'c'=2,'y'=4,'w'=2] {'z'}, dimensions={0} | all-to-all | bytes 1572864 | tf_op jit(solution)/shard_map/all_to_all | solution.py:233
  186.7 3.0 %broadcast_in_dim.29 = bf16[4,8,160,256]{3,2,1,0:T(8,128)(2,1)} broadcast(bf16[8,160,256]{2,1,0:T(8,128)(2,1)} %all-to-all-done.2), dimensions={1,2,3} | broadcast | bytes 3276800 | tf_op jit(solution)/shard_map/broadcast_in_dim | solution.py:233
  189.7 3.8 %all-to-all-start.4 = ((bf16[4,8,160,256]{3,2,1,0:T(8,128)(2,1)}), bf16[4,8,160,256]{3,2,1,0:T(8,128)(2,1)S(1)}, u32[]{:S(2)}, u32[]{:S(2)}) async-start(bf16[4,8,160,256]{3,2,1,0:T(8,128)(2,1)} %broadcast_in_dim.29), calls=%async_computation.4 | async-start | bytes 5242880 | tf_op jit(solution)/shard_map/all_to_all | solution.py:233
  197.7 2.0 stack.81.where
  199.7 1.7 broadcast_subtract_fusion.begins
  201.4 3.7 %collective-permute-start.2 = (bf16[3072,128]{1,0:T(8,128)(2,1)S(1)}, bf16[3072,128]{1,0:T(8,128)(2,1)}, u32[]{:S(2)}, u32[]{:S(2)}) collective-permute-start(bf16[3072,128]{1,0:T(8,128)(2,1)S(1)} %bitcast.41), channel_id=1, source_target_pairs={{0,8},{8,0},{1,9},{9,1},{2,10},{10,2},{3,11},{11,3},{4,12},{12,4},... | collective-permute-start | bytes 2359304 | tf_op jit(solution)/shard_map/ppermute | solution.py:342
  205.1 18.5 %all-to-all-done.4.blocks = bf16[4,8,160,256]{3,2,1,0:T(8,128)(2,1)S(1)} async-done(((bf16[4,8,160,256]{3,2,1,0:T(8,128)(2,1)}), bf16[4,8,160,256]{3,2,1,0:T(8,128)(2,1)S(1)}, u32[]{:S(2)}, u32[]{:S(2)}) %all-to-all-start.4) | async-done | bytes 2621472 | tf_op jit(solution)/shard_map/all_to_all | solution.py:233
  225.5 2.1 copy-done.8
  227.6 2.4 shard_map.96
  230.0 4.7 %collective-permute-start.3 = (bf16[2,192,128]{2,1,0:T(8,128)(2,1)S(1)}, bf16[2,192,128]{2,1,0:T(8,128)(2,1)S(1)}, u32[]{:S(2)}, u32[]{:S(2)}) collective-permute-start(bf16[2,192,128]{2,1,0:T(8,128)(2,1)S(1)} %get-tuple-element.52), channel_id=1, source_target_pairs={{0,8},{8,0},{1,9},{9,1},{2,10},{10,2},{3,11},{11,3},{4,12},{12,4},... | collective-permute-start | bytes 294920 | tf_op jit(solution)/shard_map/ppermute | solution.py:361
  238.3 5.3 %collective-permute-done.4.near = bf16[768,128]{1,0:T(8,128)(2,1)S(1)} collective-permute-done((bf16[768,128]{1,0:T(8,128)(2,1)S(1)}, bf16[768,128]{1,0:T(8,128)(2,1)S(1)}, u32[]{:S(2)}, u32[]{:S(2)}) %collective-permute-start.4) | collective-permute-done | bytes 196640 | tf_op jit(solution)/shard_map/ppermute | solution.py:363
  243.7 2.8 %collective-permute-done.5.far = bf16[768,128]{1,0:T(8,128)(2,1)S(1)} collective-permute-done((bf16[768,128]{1,0:T(8,128)(2,1)S(1)}, bf16[768,128]{1,0:T(8,128)(2,1)S(1)}, u32[]{:S(2)}, u32[]{:S(2)}) %collective-permute-start.5) | collective-permute-done | bytes 196640 | tf_op jit(solution)/shard_map/ppermute | solution.py:364
  247.4 2.2 shard_map.97
  249.6 10.4 %collective-permute-start.6 = (bf16[816,128]{1,0:T(8,128)(2,1)S(1)}, bf16[816,128]{1,0:T(8,128)(2,1)S(1)}, u32[]{:S(2)}, u32[]{:S(2)}) collective-permute-start(bf16[816,128]{1,0:T(8,128)(2,1)S(1)} %get-tuple-element.43), channel_id=1, source_target_pairs={{0,128},{128,256},{256,384},{1,129},{129,257},{257,385},{2,130},{1... | collective-permute-start | bytes 626696 | tf_op jit(solution)/shard_map/ppermute | solution.py:376
  260.0 1.3 collective-permute-start.7
  261.3 2.5 shard_map.98
  263.9 1.5 broadcast_select_fusion
  265.3 2.1 collective-permute-done.7.r2
  267.4 2.0 shard_map.99
  (74 shorter events, 14.6 us)
Async XLA Ops:
  0.6 18.0 %copy-start.10 = (bf16[192,640]{1,0:T(8,128)(2,1)S(1)}, bf16[192,640]{1,0:T(8,128)(2,1)}, u32[]{:S(2)}) copy-start(bf16[192,640]{1,0:T(8,128)(2,1)} %param.7) | copy-start | bytes 737284
  11.7 36.4 %all-to-all-start = ((bf16[8,176,128]{2,1,0:T(8,128)(2,1)}), bf16[8,176,128]{2,1,0:T(8,128)(2,1)S(1)}, u32[]{:S(2)}, u32[]{:S(2)}) async-start(bf16[8,176,128]{2,1,0:T(8,128)(2,1)} %broadcast_in_dim.23), calls=%async_computation | async-start | bytes 720896 | tf_op jit(solution)/shard_map/all_to_all | solution.py:233
  64.0 63.3 %copy-start.11 = (bf16[5120]{0:T(1024)(128)(2,1)S(1)}, bf16[5120]{0:T(1024)(128)(2,1)}, u32[]{:S(2)}) copy-start(bf16[5120]{0:T(1024)(128)(2,1)} %param.8) | copy-start | bytes 30724
  64.0 63.4 %copy-start.12 = (s32[64]{0:T(128)S(1)}, s32[64]{0:T(128)}, u32[]{:S(2)}) copy-start(s32[64]{0:T(128)} %param.13) | copy-start | bytes 772
  64.9 64.7 %all-to-all-start.2 = ((bf16[8,160,256]{2,1,0:T(8,128)(2,1)}), bf16[8,160,256]{2,1,0:T(8,128)(2,1)}, u32[]{:S(2)}, u32[]{:S(2)}) async-start(bf16[8,160,256]{2,1,0:T(8,128)(2,1)} %broadcast_in_dim.25), calls=%async_computation.2 | async-start | bytes 1310720 | tf_op jit(solution)/shard_map/all_to_all | solution.py:233
  103.2 24.3 %collective-permute-start = (bf16[4,192,640]{2,1,0:T(8,128)(2,1)S(1)}, bf16[4,192,640]{2,1,0:T(8,128)(2,1)}, u32[]{:S(2)}, u32[]{:S(2)}) collective-permute-start(bf16[4,192,640]{2,1,0:T(8,128)(2,1)S(1)} %all_gather.22.refs_0_), channel_id=1, source_target_pairs={{0,8},{8,0},{1,9},{9,1},{2,10},{10,2},{3,11},{11,3},{4,12},{12,4},... | collective-permute-start | bytes 2949128 | tf_op jit(solution)/shard_map/ppermute | solution.py:272
  124.0 5.6 %collective-permute-start.1 = (bf16[4,192,640]{2,1,0:T(8,128)(2,1)S(1)}, bf16[4,192,640]{2,1,0:T(8,128)(2,1)}, u32[]{:S(2)}, u32[]{:S(2)}) collective-permute-start(bf16[4,192,640]{2,1,0:T(8,128)(2,1)S(1)} %all_gather.23.refs_1_), channel_id=1, source_target_pairs={{0,8},{8,0},{1,9},{9,1},{2,10},{10,2},{3,11},{11,3},{4,12},{12,4},... | collective-permute-start | bytes 2949128 | tf_op jit(solution)/shard_map/ppermute | solution.py:272
  129.5 6.1 %copy-start.9 = (f32[4,8,4,128]{3,2,1,0:T(4,128)}, f32[4,8,4,128]{3,2,1,0:T(4,128)S(1)}, u32[]{:S(2)}) copy-start(f32[4,8,4,128]{3,2,1,0:T(4,128)S(1)} %slice_convert_fusion) | copy-start | bytes 196612
  131.3 4.3 %copy-start.1 = (f32[384,128]{1,0:T(8,128)}, f32[384,128]{1,0:T(8,128)S(1)}, u32[]{:S(2)}) copy-start(f32[384,128]{1,0:T(8,128)S(1)} %get-tuple-element.64.cosine) | copy-start | bytes 589828
  131.4 4.3 %copy-start.3 = (f32[384,128]{1,0:T(8,128)}, f32[384,128]{1,0:T(8,128)S(1)}, u32[]{:S(2)}) copy-start(f32[384,128]{1,0:T(8,128)S(1)} %get-tuple-element.65.sine) | copy-start | bytes 589828
  131.4 4.3 %copy-start.5 = (f32[128]{0:T(128)S(1)}, f32[128]{0:T(128)}, u32[]{:S(2)}) copy-start(f32[128]{0:T(128)} %param.10) | copy-start | bytes 1540
  135.7 2.4 copy-start.7
  189.7 33.9 %copy-start.6 = (f32[128]{0:T(128)S(1)}, f32[128]{0:T(128)}, u32[]{:S(2)}) copy-start(f32[128]{0:T(128)} %param.9) | copy-start | bytes 1540
  189.7 33.9 %all-to-all-start.4 = ((bf16[4,8,160,256]{3,2,1,0:T(8,128)(2,1)}), bf16[4,8,160,256]{3,2,1,0:T(8,128)(2,1)S(1)}, u32[]{:S(2)}, u32[]{:S(2)}) async-start(bf16[4,8,160,256]{3,2,1,0:T(8,128)(2,1)} %broadcast_in_dim.29), calls=%async_computation.4 | async-start | bytes 5242880 | tf_op jit(solution)/shard_map/all_to_all | solution.py:233
  201.4 45.0 %collective-permute-start.2 = (bf16[3072,128]{1,0:T(8,128)(2,1)S(1)}, bf16[3072,128]{1,0:T(8,128)(2,1)}, u32[]{:S(2)}, u32[]{:S(2)}) collective-permute-start(bf16[3072,128]{1,0:T(8,128)(2,1)S(1)} %bitcast.41), channel_id=1, source_target_pairs={{0,8},{8,0},{1,9},{9,1},{2,10},{10,2},{3,11},{11,3},{4,12},{12,4},... | collective-permute-start | bytes 2359304 | tf_op jit(solution)/shard_map/ppermute | solution.py:342
  223.6 0.9 copy-start.2
  224.5 0.9 copy-start.4
  225.5 2.1 copy-start.8
  230.0 5.6 %collective-permute-start.3 = (bf16[2,192,128]{2,1,0:T(8,128)(2,1)S(1)}, bf16[2,192,128]{2,1,0:T(8,128)(2,1)S(1)}, u32[]{:S(2)}, u32[]{:S(2)}) collective-permute-start(bf16[2,192,128]{2,1,0:T(8,128)(2,1)S(1)} %get-tuple-element.52), channel_id=1, source_target_pairs={{0,8},{8,0},{1,9},{9,1},{2,10},{10,2},{3,11},{11,3},{4,12},{12,4},... | collective-permute-start | bytes 294920 | tf_op jit(solution)/shard_map/ppermute | solution.py:361
  235.6 8.0 %collective-permute-start.4 = (bf16[768,128]{1,0:T(8,128)(2,1)S(1)}, bf16[768,128]{1,0:T(8,128)(2,1)S(1)}, u32[]{:S(2)}, u32[]{:S(2)}) collective-permute-start(bf16[768,128]{1,0:T(8,128)(2,1)S(1)} %bitcast.43), channel_id=1, source_target_pairs={{128,0},{256,128},{384,256},{129,1},{257,129},{385,257},{130,2},{2... | collective-permute-start | bytes 589832 | tf_op jit(solution)/shard_map/ppermute | solution.py:363
  236.9 9.5 %collective-permute-start.5 = (bf16[768,128]{1,0:T(8,128)(2,1)S(1)}, bf16[768,128]{1,0:T(8,128)(2,1)S(1)}, u32[]{:S(2)}, u32[]{:S(2)}) collective-permute-start(bf16[768,128]{1,0:T(8,128)(2,1)S(1)} %bitcast.44), channel_id=1, source_target_pairs={{256,0},{384,128},{257,1},{385,129},{258,2},{386,130},{259,3},{387... | collective-permute-start | bytes 589832 | tf_op jit(solution)/shard_map/ppermute | solution.py:364
  246.5 1.0 copy-start
  249.6 15.7 %collective-permute-start.6 = (bf16[816,128]{1,0:T(8,128)(2,1)S(1)}, bf16[816,128]{1,0:T(8,128)(2,1)S(1)}, u32[]{:S(2)}, u32[]{:S(2)}) collective-permute-start(bf16[816,128]{1,0:T(8,128)(2,1)S(1)} %get-tuple-element.43), channel_id=1, source_target_pairs={{0,128},{128,256},{256,384},{1,129},{129,257},{257,385},{2,130},{1... | collective-permute-start | bytes 626696 | tf_op jit(solution)/shard_map/ppermute | solution.py:376
  260.0 7.4 %collective-permute-start.7 = (bf16[816,128]{1,0:T(8,128)(2,1)S(1)}, bf16[816,128]{1,0:T(8,128)(2,1)S(1)}, u32[]{:S(2)}, u32[]{:S(2)}) collective-permute-start(bf16[816,128]{1,0:T(8,128)(2,1)S(1)} %get-tuple-element.44), channel_id=1, source_target_pairs={{0,256},{128,384},{1,257},{129,385},{2,258},{130,386},{3,259},{131... | collective-permute-start | bytes 626696 | tf_op jit(solution)/shard_map/ppermute | solution.py:377

commit v9 on v7

--- a/solution.py
+++ b/solution.py
@@ -15,7 +15,7 @@
 MASKED = -3e38
 KEY_BLOCK = 1024
 NO_SEGMENT = 100.0
-VMEM_LIMIT = 20 * 1024 * 1024
+VMEM_LIMIT = 14 * 1024 * 1024
 
 
 def call(kernel, out_shape, n_smem, n_vmem, scratch=(), flops=0, n_hbm=0, out_hbm=False):
@@ -271,7 +271,7 @@
     pair_docs = pair_docs[:, :rows].astype(jnp.int32)
 
     hidden, line = lax.optimization_barrier((hidden, line))
-    line = lax.all_gather(line, "z", axis=0)
+    line = lax.all_to_all(jnp.broadcast_to(line[None], (nz, *line.shape)), "z", 0, 0)
 
     halves = lax.all_gather(hidden, "w", axis=0)
     own = [lax.all_gather(halves[i], "y", axis=0) for i in range(2)]

time: 220 us -> 248 us (1.13)
  starting transfers between devices: 69.6 us -> 100 us
  blocking collectives: 59.2 us -> 74.3 us
  between operations: 16.3 us -> 3.21 us
  waiting for transfers between devices: 31.7 us -> 28.4 us
    ppermute x3, starting transfers between devices: 17.3 us -> 45.7 us  [across(): return lax.ppermute(v, 'z', [(i, i ^ bit) for i in range(8)])]
    all_gather x1, blocking collectives: 25.3 us -> 37.7 us  [body(): halves = lax.all_gather(hidden, 'w', axis=0)]
    all_to_all x0 -> x1, starting transfers between devices: none -> 6.87 us  [body(): lax.all_to_all(jnp.broadcast_to(line[None], (nz, *line.shape)), 'z', 0, 0)]
    all_gather x1 -> x0, waiting for transfers between devices: 6.22 us -> none  [body(): line = lax.all_gather(line, 'z', axis=0)]
    ppermute x2, starting transfers between devices: 10.1 us -> 7.12 us  [body(): other = [lax.ppermute(v, 'c', swap) for v in own]]
    all_gather x2, blocking collectives: 25.3 us -> 28.1 us  [body(): own = [lax.all_gather(halves[i], 'y', axis=0) for i in range(2)]]
    unnamed x32 -> x36, local copies, waits for them, and re-layouts: 9.47 us -> 9.49 us
  transfers between devices with their start and end apart: 15 -> 15, of which waited for: 7 -> 7; matrix products, arithmetic and copies ran while one was open for 5% -> 3% of each run, Pallas kernels for 5% -> 5%
where the time goes in v9:
time: 248 us; the launch traced here: 245 us
  starting transfers between devices  100 us (40%)
  blocking collectives  74.3 us (30%)
  waiting for transfers between devices  28.4 us (11%)
  local copies, waits for them, and re-layouts  17.8 us (7%)
  Pallas kernels  15.7 us (6%)
  other arithmetic  5.63 us (2%)
  between operations  3.21 us (1%)
    ppermute x3, starting transfers between devices, across(): return lax.ppermute(v, 'z', [(i, i ^ bit) for i in range(8)])  45.7 us
    all_gather x1, blocking collectives, body(): halves = lax.all_gather(hidden, 'w', axis=0)  37.7 us
    all_gather x2, blocking collectives, body(): own = [lax.all_gather(halves[i], 'y', axis=0) for i in range(2)]  28.1 us
    ppermute x1, starting transfers between devices, body(): r1 = lax.ppermute(r1, 'x', [(i, i + 1) for i in range(nx - 1)])  14.9 us
    ppermute x2, starting transfers between devices, body(): other = [lax.ppermute(v, 'c', swap) for v in mine]  11.8 us
    all_to_all x1, waiting for transfers between devices, body(): pair_blocks = lax.all_to_all(pair_line, 'x', 0, 0)  11 us
    unnamed x36, local copies, waits for them, and re-layouts  9.49 us
    all_gather x1, blocking collectives, body(): lax.all_gather(jnp.concatenate([weight_store, riders], axis=0), 'c', axis=0)  8.53 us
  transfers between devices with their start and end apart: 15, of which 7 were waited for; matrix products, arithmetic and copies ran while one was open for 3% of the time, Pallas kernels for 5%

profile of v9, /device:TPU:1, one launch (start us, length us, event | category | flops | bytes accessed | tf_op | source)
XLA Modules:
  0.0 245.4 jit_solution(12752886343304189154)
XLA Ops:
  2.3 8.5 %all-gather = bf16[192,768]{1,0:T(8,128)(2,1)S(1)} all-gather(bf16[96,768]{1,0:T(8,128)(2,1)S(1)} %fusion.2), channel_id=2, replica_groups=mesh['x'=4,'z'=8,'c'=2,'y'=4,'w'=2] {'c'}, dimensions={0}, use_global_device_ids=true | all-gather | bytes 442368 | tf_op jit(solution)/shard_map/all_gather | solution.py:259
  12.0 6.9 %all-to-all-start = ((bf16[8,176,384]{2,1,0:T(8,128)(2,1)}), bf16[8,176,384]{2,1,0:T(8,128)(2,1)S(1)}, u32[]{:S(2)}, u32[]{:S(2)}) async-start(bf16[8,176,384]{2,1,0:T(8,128)(2,1)} %broadcast_in_dim.20), calls=%async_computation | async-start | bytes 2162688 | tf_op jit(solution)/shard_map/all_to_all | solution.py:274
  18.9 37.7 %all-gather.1 = bf16[384,640]{1,0:T(8,128)(2,1)S(1)} all-gather(bf16[192,640]{1,0:T(8,128)(2,1)S(1)} %copy-done.14), channel_id=3, replica_groups=mesh['x'=4,'z'=8,'c'=2,'y'=4,'w'=2] {'w'}, dimensions={0}, use_global_device_ids=true | all-gather | bytes 737280 | tf_op jit(solution)/shard_map/all_gather | solution.py:276
  56.6 13.6 %all-gather.2 = bf16[768,640]{1,0:T(8,128)(2,1)S(1)} all-gather(bf16[192,640]{1,0:T(8,128)(2,1)S(1)} %get-tuple-element.34), channel_id=4, replica_groups=mesh['x'=4,'z'=8,'c'=2,'y'=4,'w'=2] {'y'}, dimensions={0}, use_global_device_ids=true | all-gather | bytes 1228800 | tf_op jit(solution)/shard_map/all_gather | solution.py:277
  70.3 4.1 %collective-permute-start = (bf16[4,192,640]{2,1,0:T(8,128)(2,1)S(1)}, bf16[4,192,640]{2,1,0:T(8,128)(2,1)}, u32[]{:S(2)}, u32[]{:S(2)}) collective-permute-start(bf16[4,192,640]{2,1,0:T(8,128)(2,1)S(1)} %bitcast.47), channel_id=1, source_target_pairs={{0,8},{8,0},{1,9},{9,1},{2,10},{10,2},{3,11},{11,3},{4,12},{12,4},... | collective-permute-start | bytes 2949128 | tf_op jit(solution)/shard_map/ppermute | solution.py:278
  74.4 14.5 %all-gather.3 = bf16[768,640]{1,0:T(8,128)(2,1)S(1)} all-gather(bf16[192,640]{1,0:T(8,128)(2,1)S(1)} %get-tuple-element.33), channel_id=5, replica_groups=mesh['x'=4,'z'=8,'c'=2,'y'=4,'w'=2] {'y'}, dimensions={0}, use_global_device_ids=true | all-gather | bytes 1228800 | tf_op jit(solution)/shard_map/all_gather | solution.py:277
  88.9 3.0 %collective-permute-start.1 = (bf16[4,192,640]{2,1,0:T(8,128)(2,1)S(1)}, bf16[4,192,640]{2,1,0:T(8,128)(2,1)}, u32[]{:S(2)}, u32[]{:S(2)}) collective-permute-start(bf16[4,192,640]{2,1,0:T(8,128)(2,1)S(1)} %bitcast.49), channel_id=1, source_target_pairs={{0,8},{8,0},{1,9},{9,1},{2,10},{10,2},{3,11},{11,3},{4,12},{12,4},... | collective-permute-start | bytes 2949128 | tf_op jit(solution)/shard_map/ppermute | solution.py:278
  93.5 4.0 %all-to-all-start.1 = ((bf16[4,8,176,128]{3,2,1,0:T(8,128)(2,1)}), bf16[4,8,176,128]{3,2,1,0:T(8,128)(2,1)S(1)}, u32[]{:S(2)}, u32[]{:S(2)}) async-start(bf16[4,8,176,128]{3,2,1,0:T(8,128)(2,1)} %broadcast_in_dim.21), calls=%async_computation.1 | async-start | bytes 2883584 | tf_op jit(solution)/shard_map/all_to_all | solution.py:282
  97.9 4.2 %shard_map.94.source = bf16[384,5120]{1,0:T(8,128)(2,1)S(1)} custom-call(s32[2]{0:T(128)S(1)} %pad_add_fusion.1.where, f32[1,5120]{1,0:T(1,128)S(1)} %bitcast.55, bf16[4,192,640]{2,1,0:T(8,128)(2,1)S(1)} %bitcast.48, bf16[4,192,640]{2,1,0:T(8,128)(2,1)S(1)} %bitcast.50, bf16[4,192,640]{2,1,0:T(8,128)(2,1)} %collective-permute-done.refs_2_, ...), custom_call_target="tpu_custom_call" | custom-call | flops 4000000000 | bytes 4194304 | tf_op jit(solution)/shard_map/pallas_call | solution.py:287
  102.1 1.9 copy-done.8
  104.1 11.0 %all-to-all-done.1.blocks = bf16[4,8,176,128]{3,2,1,0:T(8,128)(2,1)S(1)} async-done(((bf16[4,8,176,128]{3,2,1,0:T(8,128)(2,1)}), bf16[4,8,176,128]{3,2,1,0:T(8,128)(2,1)S(1)}, u32[]{:S(2)}, u32[]{:S(2)}) %all-to-all-start.1) | async-done | bytes 1441824 | tf_op jit(solution)/shard_map/all_to_all | solution.py:282
  117.7 3.8 %all-to-all-start.2 = ((bf16[4,8,160,256]{3,2,1,0:T(8,128)(2,1)}), bf16[4,8,160,256]{3,2,1,0:T(8,128)(2,1)S(1)}, u32[]{:S(2)}, u32[]{:S(2)}) async-start(bf16[4,8,160,256]{3,2,1,0:T(8,128)(2,1)} %broadcast_in_dim.22), calls=%async_computation.2 | async-start | bytes 5242880 | tf_op jit(solution)/shard_map/all_to_all | solution.py:283
  124.1 2.1 copy-done.9
  126.2 2.3 shard_map.95
  128.5 32.2 %collective-permute-start.2 = (bf16[384,128]{1,0:T(8,128)(2,1)S(1)}, bf16[384,128]{1,0:T(8,128)(2,1)S(1)}, u32[]{:S(2)}, u32[]{:S(2)}) collective-permute-start(bf16[384,128]{1,0:T(8,128)(2,1)S(1)} %shard_map.95), channel_id=1, source_target_pairs={{0,64},{16,80},{32,96},{48,112},{64,0},{80,16},{96,32},{112,48},{1... | collective-permute-start | bytes 294920 | tf_op jit(solution)/shard_map/ppermute | solution.py:240
  163.9 1.9 stack.97.where
  165.8 11.5 %collective-permute-start.3 = (bf16[2,384,128]{2,1,0:T(8,128)(2,1)S(1)}, bf16[2,384,128]{2,1,0:T(8,128)(2,1)}, u32[]{:S(2)}, u32[]{:S(2)}) collective-permute-start(bf16[2,384,128]{2,1,0:T(8,128)(2,1)S(1)} %pad_maximum_fusion.3), channel_id=1, source_target_pairs={{0,32},{16,48},{32,0},{48,16},{64,96},{80,112},{96,64},{112,80},{1... | collective-permute-start | bytes 589832 | tf_op jit(solution)/shard_map/ppermute | solution.py:240
  177.3 3.1 %collective-permute-done.3 = bf16[2,384,128]{2,1,0:T(8,128)(2,1)} collective-permute-done((bf16[2,384,128]{2,1,0:T(8,128)(2,1)S(1)}, bf16[2,384,128]{2,1,0:T(8,128)(2,1)}, u32[]{:S(2)}, u32[]{:S(2)}) %collective-permute-start.3) | collective-permute-done | bytes 196640 | tf_op jit(solution)/shard_map/ppermute | solution.py:240
  181.6 9.2 %collective-permute-start.4 = (bf16[4,384,128]{2,1,0:T(8,128)(2,1)S(1)}, bf16[4,384,128]{2,1,0:T(8,128)(2,1)}, u32[]{:S(2)}, u32[]{:S(2)}) collective-permute-start(bf16[4,384,128]{2,1,0:T(8,128)(2,1)S(1)} %pad_maximum_fusion.refs_0_), channel_id=1, source_target_pairs={{0,8},{8,0},{1,9},{9,1},{2,10},{10,2},{3,11},{11,3},{4,12},{12,4},... | collective-permute-start | bytes 1179656 | tf_op jit(solution)/shard_map/ppermute | solution.py:354
  190.7 2.0 collective-permute-start.8
  194.6 2.1 copy-done.10
  196.7 2.4 shard_map.96
  199.2 2.2 collective-permute-start.5
  201.4 2.1 collective-permute-done.8.refs_1_
  203.5 2.7 %collective-permute-start.9 = (bf16[4,384,128]{2,1,0:T(8,128)(2,1)}, bf16[4,384,128]{2,1,0:T(8,128)(2,1)S(1)}, u32[]{:S(2)}, u32[]{:S(2)}) collective-permute-start(bf16[4,384,128]{2,1,0:T(8,128)(2,1)} %collective-permute-done.8.refs_1_), channel_id=1, source_target_pairs={{0,8},{8,0},{1,9},{9,1},{2,10},{10,2},{3,11},{11,3},{4,12},{12,4},... | collective-permute-start | bytes 1179656 | tf_op jit(solution)/shard_map/ppermute | solution.py:354
  210.5 4.7 %collective-permute-done.6.near = bf16[768,128]{1,0:T(8,128)(2,1)S(1)} collective-permute-done((bf16[768,128]{1,0:T(8,128)(2,1)S(1)}, bf16[768,128]{1,0:T(8,128)(2,1)S(1)}, u32[]{:S(2)}, u32[]{:S(2)}) %collective-permute-start.6) | collective-permute-done | bytes 196640 | tf_op jit(solution)/shard_map/ppermute | solution.py:374
  215.2 2.9 %collective-permute-done.7.far = bf16[768,128]{1,0:T(8,128)(2,1)S(1)} collective-permute-done((bf16[768,128]{1,0:T(8,128)(2,1)S(1)}, bf16[768,128]{1,0:T(8,128)(2,1)S(1)}, u32[]{:S(2)}, u32[]{:S(2)}) %collective-permute-start.7) | collective-permute-done | bytes 196640 | tf_op jit(solution)/shard_map/ppermute | solution.py:375
  218.1 2.2 shard_map.97
  220.2 14.9 %collective-permute-start.10 = (bf16[816,128]{1,0:T(8,128)(2,1)S(1)}, bf16[816,128]{1,0:T(8,128)(2,1)S(1)}, u32[]{:S(2)}, u32[]{:S(2)}) collective-permute-start(bf16[816,128]{1,0:T(8,128)(2,1)S(1)} %get-tuple-element.29), channel_id=1, source_target_pairs={{0,128},{128,256},{256,384},{1,129},{129,257},{257,385},{2,130},{1... | collective-permute-start | bytes 626696 | tf_op jit(solution)/shard_map/ppermute | solution.py:387
  236.5 2.5 %shard_map.98 = (f32[768,128]{1,0:T(8,128)S(1)}, f32[768,1]{1,0:T(8,128)S(1)}) custom-call(s32[12]{0:T(128)S(1)} %stack.97.where, s32[3,192,1]{2,1,0:T(8,128)S(1)} %broadcast_subtract_fusion.begins, bf16[768,128]{1,0:T(8,128)(2,1)S(1)} %bitcast.54, bf16[3072,128]{1,0:T(8,128)(2,1)S(1)} %get-tuple-element.25.keys, bf16[3072,256]{1,0:T(8,128)(2,1)S(1)} %get-tuple-element.26.values), custom_call_target="tpu_custom_call" | custom-call | flops 10000000000 | bytes 4194304 | tf_op jit(solution)/shard_map/pallas_call | solution.py:389
  239.0 4.3 %collective-permute-done.11.r2 = bf16[816,128]{1,0:T(8,128)(2,1)S(1)} collective-permute-done((bf16[816,128]{1,0:T(8,128)(2,1)S(1)}, bf16[816,128]{1,0:T(8,128)(2,1)S(1)}, u32[]{:S(2)}, u32[]{:S(2)}) %collective-permute-start.11) | collective-permute-done | bytes 208928 | tf_op jit(solution)/shard_map/ppermute | solution.py:388
  243.3 2.0 shard_map.99
  (92 shorter events, 19.5 us)
Async XLA Ops:
  0.6 18.3 %copy-start.14 = (bf16[192,640]{1,0:T(8,128)(2,1)S(1)}, bf16[192,640]{1,0:T(8,128)(2,1)}, u32[]{:S(2)}) copy-start(bf16[192,640]{1,0:T(8,128)(2,1)} %param.7) | copy-start | bytes 737284
  12.0 80.0 %all-to-all-start = ((bf16[8,176,384]{2,1,0:T(8,128)(2,1)}), bf16[8,176,384]{2,1,0:T(8,128)(2,1)S(1)}, u32[]{:S(2)}, u32[]{:S(2)}) async-start(bf16[8,176,384]{2,1,0:T(8,128)(2,1)} %broadcast_in_dim.20), calls=%async_computation | async-start | bytes 2162688 | tf_op jit(solution)/shard_map/all_to_all | solution.py:274
  70.3 27.6 %collective-permute-start = (bf16[4,192,640]{2,1,0:T(8,128)(2,1)S(1)}, bf16[4,192,640]{2,1,0:T(8,128)(2,1)}, u32[]{:S(2)}, u32[]{:S(2)}) collective-permute-start(bf16[4,192,640]{2,1,0:T(8,128)(2,1)S(1)} %bitcast.47), channel_id=1, source_target_pairs={{0,8},{8,0},{1,9},{9,1},{2,10},{10,2},{3,11},{11,3},{4,12},{12,4},... | collective-permute-start | bytes 2949128 | tf_op jit(solution)/shard_map/ppermute | solution.py:278
  88.9 9.0 %collective-permute-start.1 = (bf16[4,192,640]{2,1,0:T(8,128)(2,1)S(1)}, bf16[4,192,640]{2,1,0:T(8,128)(2,1)}, u32[]{:S(2)}, u32[]{:S(2)}) collective-permute-start(bf16[4,192,640]{2,1,0:T(8,128)(2,1)S(1)} %bitcast.49), channel_id=1, source_target_pairs={{0,8},{8,0},{1,9},{9,1},{2,10},{10,2},{3,11},{11,3},{4,12},{12,4},... | collective-permute-start | bytes 2949128 | tf_op jit(solution)/shard_map/ppermute | solution.py:278
  91.9 5.6 %copy-start.15 = (bf16[5120]{0:T(1024)(128)(2,1)S(1)}, bf16[5120]{0:T(1024)(128)(2,1)}, u32[]{:S(2)}) copy-start(bf16[5120]{0:T(1024)(128)(2,1)} %param.8) | copy-start | bytes 30724
  91.9 5.8 %copy-start.16 = (s32[64]{0:T(128)S(1)}, s32[64]{0:T(128)}, u32[]{:S(2)}) copy-start(s32[64]{0:T(128)} %param.13) | copy-start | bytes 772
  92.1 1.5 copy-start.11
  93.5 21.6 %all-to-all-start.1 = ((bf16[4,8,176,128]{3,2,1,0:T(8,128)(2,1)}), bf16[4,8,176,128]{3,2,1,0:T(8,128)(2,1)S(1)}, u32[]{:S(2)}, u32[]{:S(2)}) async-start(bf16[4,8,176,128]{3,2,1,0:T(8,128)(2,1)} %broadcast_in_dim.21), calls=%async_computation.1 | async-start | bytes 2883584 | tf_op jit(solution)/shard_map/all_to_all | solution.py:282
  97.9 6.1 %copy-start.12 = (bf16[8,176,384]{2,1,0:T(8,128)(2,1)S(1)}, bf16[8,176,384]{2,1,0:T(8,128)(2,1)}, u32[]{:S(2)}) copy-start(bf16[8,176,384]{2,1,0:T(8,128)(2,1)} %copy-done.11) | copy-start | bytes 3244036
  102.1 1.9 copy-start.8
  115.1 2.6 %copy-start = (bf16[4,8,176,128]{3,2,1,0:T(8,128)(2,1)}, bf16[4,8,176,128]{3,2,1,0:T(8,128)(2,1)S(1)}, u32[]{:S(2)}) copy-start(bf16[4,8,176,128]{3,2,1,0:T(8,128)(2,1)S(1)} %all-to-all-done.1.blocks) | copy-start | bytes 4325380
  117.7 4.9 %copy-start.6 = (f32[128]{0:T(128)S(1)}, f32[128]{0:T(128)}, u32[]{:S(2)}) copy-start(f32[128]{0:T(128)} %param.10) | copy-start | bytes 1540
  117.7 63.9 %all-to-all-start.2 = ((bf16[4,8,160,256]{3,2,1,0:T(8,128)(2,1)}), bf16[4,8,160,256]{3,2,1,0:T(8,128)(2,1)S(1)}, u32[]{:S(2)}, u32[]{:S(2)}) async-start(bf16[4,8,160,256]{3,2,1,0:T(8,128)(2,1)} %broadcast_in_dim.22), calls=%async_computation.2 | async-start | bytes 5242880 | tf_op jit(solution)/shard_map/all_to_all | solution.py:283
  122.5 6.0 %copy-start.2 = (f32[384,128]{1,0:T(8,128)}, f32[384,128]{1,0:T(8,128)S(1)}, u32[]{:S(2)}) copy-start(f32[384,128]{1,0:T(8,128)S(1)} %get-tuple-element.50.cosine) | copy-start | bytes 589828
  122.5 6.0 %copy-start.4 = (f32[384,128]{1,0:T(8,128)}, f32[384,128]{1,0:T(8,128)S(1)}, u32[]{:S(2)}) copy-start(f32[384,128]{1,0:T(8,128)S(1)} %get-tuple-element.51.sine) | copy-start | bytes 589828
  122.6 1.5 copy-start.1
  124.1 2.1 copy-start.9
  126.2 66.6 %copy-start.7 = (f32[128]{0:T(128)S(1)}, f32[128]{0:T(128)}, u32[]{:S(2)}) copy-start(f32[128]{0:T(128)} %param.9) | copy-start | bytes 1540
  128.5 37.2 %collective-permute-start.2 = (bf16[384,128]{1,0:T(8,128)(2,1)S(1)}, bf16[384,128]{1,0:T(8,128)(2,1)S(1)}, u32[]{:S(2)}, u32[]{:S(2)}) collective-permute-start(bf16[384,128]{1,0:T(8,128)(2,1)S(1)} %shard_map.95), channel_id=1, source_target_pairs={{0,64},{16,80},{32,96},{48,112},{64,0},{80,16},{96,32},{112,48},{1... | collective-permute-start | bytes 294920 | tf_op jit(solution)/shard_map/ppermute | solution.py:240
  165.8 11.5 %copy-start.13 = (bf16[2,384,128]{2,1,0:T(8,128)(2,1)}, bf16[2,384,128]{2,1,0:T(8,128)(2,1)S(1)}, u32[]{:S(2)}) copy-start(bf16[2,384,128]{2,1,0:T(8,128)(2,1)S(1)} %pad_maximum_fusion.3) | copy-start | bytes 589828
  165.8 14.7 %collective-permute-start.3 = (bf16[2,384,128]{2,1,0:T(8,128)(2,1)S(1)}, bf16[2,384,128]{2,1,0:T(8,128)(2,1)}, u32[]{:S(2)}, u32[]{:S(2)}) collective-permute-start(bf16[2,384,128]{2,1,0:T(8,128)(2,1)S(1)} %pad_maximum_fusion.3), channel_id=1, source_target_pairs={{0,32},{16,48},{32,0},{48,16},{64,96},{80,112},{96,64},{112,80},{1... | collective-permute-start | bytes 589832 | tf_op jit(solution)/shard_map/ppermute | solution.py:240
  181.6 27.3 %collective-permute-start.4 = (bf16[4,384,128]{2,1,0:T(8,128)(2,1)S(1)}, bf16[4,384,128]{2,1,0:T(8,128)(2,1)}, u32[]{:S(2)}, u32[]{:S(2)}) collective-permute-start(bf16[4,384,128]{2,1,0:T(8,128)(2,1)S(1)} %pad_maximum_fusion.refs_0_), channel_id=1, source_target_pairs={{0,8},{8,0},{1,9},{9,1},{2,10},{10,2},{3,11},{11,3},{4,12},{12,4},... | collective-permute-start | bytes 1179656 | tf_op jit(solution)/shard_map/ppermute | solution.py:354
  190.7 12.7 %collective-permute-start.8 = (bf16[4,384,128]{2,1,0:T(8,128)(2,1)S(1)}, bf16[4,384,128]{2,1,0:T(8,128)(2,1)}, u32[]{:S(2)}, u32[]{:S(2)}) collective-permute-start(bf16[4,384,128]{2,1,0:T(8,128)(2,1)S(1)} %pad_maximum_fusion.refs_0_), channel_id=1, source_target_pairs={{0,16},{16,0},{32,48},{48,32},{64,80},{80,64},{96,112},{112,96},{1... | collective-permute-start | bytes 1179656 | tf_op jit(solution)/shard_map/ppermute | solution.py:240
  192.7 0.9 copy-start.3
  193.7 0.9 copy-start.5
  194.6 2.1 copy-start.10
  199.2 7.0 %collective-permute-start.5 = (bf16[2,192,128]{2,1,0:T(8,128)(2,1)S(1)}, bf16[2,192,128]{2,1,0:T(8,128)(2,1)S(1)}, u32[]{:S(2)}, u32[]{:S(2)}) collective-permute-start(bf16[2,192,128]{2,1,0:T(8,128)(2,1)S(1)} %get-tuple-element.36), channel_id=1, source_target_pairs={{0,8},{8,0},{1,9},{9,1},{2,10},{10,2},{3,11},{11,3},{4,12},{12,4},... | collective-permute-start | bytes 294920 | tf_op jit(solution)/shard_map/ppermute | solution.py:372
  203.5 14.6 %collective-permute-start.9 = (bf16[4,384,128]{2,1,0:T(8,128)(2,1)}, bf16[4,384,128]{2,1,0:T(8,128)(2,1)S(1)}, u32[]{:S(2)}, u32[]{:S(2)}) collective-permute-start(bf16[4,384,128]{2,1,0:T(8,128)(2,1)} %collective-permute-done.8.refs_1_), channel_id=1, source_target_pairs={{0,8},{8,0},{1,9},{9,1},{2,10},{10,2},{3,11},{11,3},{4,12},{12,4},... | collective-permute-start | bytes 1179656 | tf_op jit(solution)/shard_map/ppermute | solution.py:354
  206.2 9.0 %collective-permute-start.6 = (bf16[768,128]{1,0:T(8,128)(2,1)S(1)}, bf16[768,128]{1,0:T(8,128)(2,1)S(1)}, u32[]{:S(2)}, u32[]{:S(2)}) collective-permute-start(bf16[768,128]{1,0:T(8,128)(2,1)S(1)} %bitcast.52), channel_id=1, source_target_pairs={{128,0},{256,128},{384,256},{129,1},{257,129},{385,257},{130,2},{2... | collective-permute-start | bytes 589832 | tf_op jit(solution)/shard_map/ppermute | solution.py:374
  207.5 10.5 %collective-permute-start.7 = (bf16[768,128]{1,0:T(8,128)(2,1)S(1)}, bf16[768,128]{1,0:T(8,128)(2,1)S(1)}, u32[]{:S(2)}, u32[]{:S(2)}) collective-permute-start(bf16[768,128]{1,0:T(8,128)(2,1)S(1)} %bitcast.53), channel_id=1, source_target_pairs={{256,0},{384,128},{257,1},{385,129},{258,2},{386,130},{259,3},{387... | collective-permute-start | bytes 589832 | tf_op jit(solution)/shard_map/ppermute | solution.py:375
  220.2 18.7 %collective-permute-start.10 = (bf16[816,128]{1,0:T(8,128)(2,1)S(1)}, bf16[816,128]{1,0:T(8,128)(2,1)S(1)}, u32[]{:S(2)}, u32[]{:S(2)}) collective-permute-start(bf16[816,128]{1,0:T(8,128)(2,1)S(1)} %get-tuple-element.29), channel_id=1, source_target_pairs={{0,128},{128,256},{256,384},{1,129},{129,257},{257,385},{2,130},{1... | collective-permute-start | bytes 626696 | tf_op jit(solution)/shard_map/ppermute | solution.py:387
  235.2 8.1 %collective-permute-start.11 = (bf16[816,128]{1,0:T(8,128)(2,1)S(1)}, bf16[816,128]{1,0:T(8,128)(2,1)S(1)}, u32[]{:S(2)}, u32[]{:S(2)}) collective-permute-start(bf16[816,128]{1,0:T(8,128)(2,1)S(1)} %get-tuple-element.30), channel_id=1, source_target_pairs={{0,256},{128,384},{1,257},{129,385},{2,258},{130,386},{3,259},{131... | collective-permute-start | bytes 626696 | tf_op jit(solution)/shard_map/ppermute | solution.py:388

commit v10 on v6

--- a/solution.py
+++ b/solution.py
@@ -15,7 +15,7 @@
 MASKED = -3e38
 KEY_BLOCK = 1024
 NO_SEGMENT = 100.0
-VMEM_LIMIT = 20 * 1024 * 1024
+VMEM_LIMIT = 14 * 1024 * 1024
 
 
 def call(kernel, out_shape, n_smem, n_vmem, scratch=(), flops=0, n_hbm=0, out_hbm=False):
@@ -289,11 +289,13 @@
     other_far = lax.ppermute(own_far, "c", swap)
     line = jnp.concatenate([line, step], axis=0)
 
-    def along_x(v):
-        return lax.all_to_all(jnp.broadcast_to(v[None], (nx, *v.shape)), "x", 0, 0)
-
-    pair_blocks = along_x(line[:, :, :128])
-    query_blocks = along_x(after(line[:, : 2 * panel, 128:], pair_blocks))
+    def copies(v):
+        return jnp.broadcast_to(v[None], (nx, *v.shape))
+
+    pair_blocks = lax.all_to_all(copies(line[:, :, :128]), "x", 0, 0)
+    query_line = copies(line[:, : 2 * panel, 128:])
+    other_far, query_line = lax.optimization_barrier((other_far, query_line))
+    query_blocks = lax.all_to_all(after(query_line, pair_blocks), "x", 0, 0)
 
     spot = jnp.stack([c, z, w]).astype(jnp.int32)
     features = norm_gain.shape[0]
@@ -359,10 +361,9 @@
     begins = spread[:, :, None]
 
     mine0 = jnp.stack([pair, across(pair, 4)])
-    mine0, ranges, begins, query_blocks = lax.optimization_barrier(
-        (mine0, ranges, begins, query_blocks)
-    )
+    mine0, ranges, begins = lax.optimization_barrier((mine0, ranges, begins))
     mine0 = jnp.concatenate([mine0, across(mine0, 2)], axis=0)
+    mine0, query_blocks = lax.optimization_barrier((mine0, query_blocks))
     mine1 = across(mine0, 1)
     mine = [mine0, mine1]
     other = [lax.ppermute(v, "c", swap) for v in mine]

time: 215 us -> 207 us (0.963)
  starting transfers between devices: 85.9 us -> 81.7 us
  Pallas kernels: 15.3 us -> 18.6 us
  waiting for transfers between devices: 41.9 us -> 38.7 us
    all_to_all x2, waiting for transfers between devices: 17.4 us -> 7.33 us  [the longest x1 7.16 us: body(): pair_blocks = lax.all_to_all(copies(line[:, :, :128]), 'x', 0, 0)]
    ppermute x6, waiting for transfers between devices: 12.7 us -> 19.5 us  [across(): return lax.ppermute(v, 'z', [(i, i ^ bit) for i in range(8)])]
    pallas_call x1, Pallas kernels: 2.18 us -> 5.46 us  [body(): call(remote_kernel, [jax.ShapeDtypeStruct((4 * rows + 48, 128), bf16)] *...]
    ppermute x1, starting transfers between devices: 10.1 us -> 6.82 us  [body(): r1 = lax.ppermute(r1, 'x', [(i, i + 1) for i in range(nx - 1)])]
    ppermute x6, starting transfers between devices: 33.3 us -> 30.6 us  [across(): return lax.ppermute(v, 'z', [(i, i ^ bit) for i in range(8)])]
    unnamed x35 -> x44, local copies, waits for them, and re-layouts: 9.84 us -> 11.2 us
  transfers between devices with their start and end apart: 18 -> 18, of which waited for: 8 -> 9; matrix products, arithmetic and copies ran while one was open for 6% -> 6% of each run, Pallas kernels for 5% -> 5%
where the time goes in v10:
time: 207 us; the launch traced here: 205 us
  starting transfers between devices  81.7 us (39%)
  waiting for transfers between devices  38.7 us (19%)
  blocking collectives  37.6 us (18%)
  Pallas kernels  18.6 us (9%)
  local copies, waits for them, and re-layouts  18.4 us (9%)
  other arithmetic  7.13 us (3%)
  between operations  3.11 us (2%)
    ppermute x6, starting transfers between devices, across(): return lax.ppermute(v, 'z', [(i, i ^ bit) for i in range(8)])  30.6 us
    ppermute x6, waiting for transfers between devices, across(): return lax.ppermute(v, 'z', [(i, i ^ bit) for i in range(8)])  19.5 us
    all_gather x1, blocking collectives, body(): own_far = lax.all_gather(far, 'y', axis=0)  15.9 us
    all_gather x1, blocking collectives, body(): own_near = lax.all_gather(hidden, 'y', axis=0)  13.2 us
    ppermute x2, starting transfers between devices, body(): other = [lax.ppermute(v, 'c', swap) for v in mine]  11.6 us
    unnamed x44, local copies, waits for them, and re-layouts  11.2 us
    ppermute x1, starting transfers between devices, body(): far = lax.ppermute(hidden, 'w', swap)  10.6 us
    all_gather x1, blocking collectives, body(): lax.all_gather(jnp.concatenate([weight_store, riders], axis=0), 'c', axis=0)  8.53 us
  transfers between devices with their start and end apart: 18, of which 9 were waited for; matrix products, arithmetic and copies ran while one was open for 6% of the time, Pallas kernels for 5%

profile of v10, /device:TPU:1, one launch (start us, length us, event | category | flops | bytes accessed | tf_op | source)
XLA Modules:
  0.0 205.2 jit_solution(12904079022431203192)
XLA Ops:
  2.3 8.5 %all-gather = bf16[192,768]{1,0:T(8,128)(2,1)S(1)} all-gather(bf16[96,768]{1,0:T(8,128)(2,1)S(1)} %fusion.2), channel_id=2, replica_groups=mesh['x'=4,'z'=8,'c'=2,'y'=4,'w'=2] {'c'}, dimensions={0}, use_global_device_ids=true | all-gather | bytes 442368 | tf_op jit(solution)/shard_map/all_gather | solution.py:261
  11.0 3.4 %collective-permute-start = (bf16[1,176,384]{2,1,0:T(8,128)(2,1)S(1)}, bf16[1,176,384]{2,1,0:T(8,128)(2,1)S(1)}, u32[]{:S(2)}, u32[]{:S(2)}) collective-permute-start(bf16[1,176,384]{2,1,0:T(8,128)(2,1)S(1)} %fusion.4), channel_id=1, source_target_pairs={{0,64},{16,80},{32,96},{48,112},{64,0},{80,16},{96,32},{112,48},{1... | collective-permute-start | bytes 405512 | tf_op jit(solution)/shard_map/ppermute | solution.py:242
  14.4 10.6 %collective-permute-start.1 = (bf16[192,640]{1,0:T(8,128)(2,1)S(1)}, bf16[192,640]{1,0:T(8,128)(2,1)S(1)}, u32[]{:S(2)}, u32[]{:S(2)}) collective-permute-start(bf16[192,640]{1,0:T(8,128)(2,1)S(1)} %copy-done.18), channel_id=1, source_target_pairs={{0,1},{1,0},{2,3},{3,2},{4,5},{5,4},{6,7},{7,6},{8,9},{9,8},{10,11... | collective-permute-start | bytes 737288 | tf_op jit(solution)/shard_map/ppermute | solution.py:277
  25.1 13.2 %all-gather.1 = bf16[768,640]{1,0:T(8,128)(2,1)S(1)} all-gather(bf16[192,640]{1,0:T(8,128)(2,1)S(1)} %copy-done.18), channel_id=3, replica_groups=mesh['x'=4,'z'=8,'c'=2,'y'=4,'w'=2] {'y'}, dimensions={0}, use_global_device_ids=true | all-gather | bytes 1228800 | tf_op jit(solution)/shard_map/all_gather | solution.py:278
  38.3 3.9 %collective-permute-start.3 = (bf16[4,192,640]{2,1,0:T(8,128)(2,1)S(1)}, bf16[4,192,640]{2,1,0:T(8,128)(2,1)S(1)}, u32[]{:S(2)}, u32[]{:S(2)}) collective-permute-start(bf16[4,192,640]{2,1,0:T(8,128)(2,1)S(1)} %bitcast.50), channel_id=1, source_target_pairs={{0,8},{8,0},{1,9},{9,1},{2,10},{10,2},{3,11},{11,3},{4,12},{12,4},... | collective-permute-start | bytes 2949128 | tf_op jit(solution)/shard_map/ppermute | solution.py:283
  42.2 14.7 %collective-permute-start.2 = (bf16[2,176,384]{2,1,0:T(8,128)(2,1)S(1)}, bf16[2,176,384]{2,1,0:T(8,128)(2,1)S(1)}, u32[]{:S(2)}, u32[]{:S(2)}) collective-permute-start(bf16[2,176,384]{2,1,0:T(8,128)(2,1)S(1)} %pad_maximum_fusion.4), channel_id=1, source_target_pairs={{0,32},{16,48},{32,0},{48,16},{64,96},{80,112},{96,64},{112,80},{1... | collective-permute-start | bytes 811016 | tf_op jit(solution)/shard_map/ppermute | solution.py:242
  56.9 15.9 %all-gather.2 = bf16[768,640]{1,0:T(8,128)(2,1)S(1)} all-gather(bf16[192,640]{1,0:T(8,128)(2,1)S(1)} %collective-permute-done.1), channel_id=4, replica_groups=mesh['x'=4,'z'=8,'c'=2,'y'=4,'w'=2] {'y'}, dimensions={0}, use_global_device_ids=true | all-gather | bytes 1228800 | tf_op jit(solution)/shard_map/all_gather | solution.py:284
  73.9 5.6 %collective-permute-start.5 = (bf16[4,176,384]{2,1,0:T(8,128)(2,1)S(1)}, bf16[4,176,384]{2,1,0:T(8,128)(2,1)S(1)}, u32[]{:S(2)}, u32[]{:S(2)}) collective-permute-start(bf16[4,176,384]{2,1,0:T(8,128)(2,1)S(1)} %pad_maximum_fusion.1), channel_id=1, source_target_pairs={{0,16},{16,0},{32,48},{48,32},{64,80},{80,64},{96,112},{112,96},{1... | collective-permute-start | bytes 1622024 | tf_op jit(solution)/shard_map/ppermute | solution.py:242
  79.6 4.3 %collective-permute-start.4 = (bf16[4,192,640]{2,1,0:T(8,128)(2,1)S(1)}, bf16[4,192,640]{2,1,0:T(8,128)(2,1)}, u32[]{:S(2)}, u32[]{:S(2)}) collective-permute-start(bf16[4,192,640]{2,1,0:T(8,128)(2,1)S(1)} %bitcast.52), channel_id=1, source_target_pairs={{0,8},{8,0},{1,9},{9,1},{2,10},{10,2},{3,11},{11,3},{4,12},{12,4},... | collective-permute-start | bytes 2949128 | tf_op jit(solution)/shard_map/ppermute | solution.py:289
  83.9 6.1 %collective-permute-done.5 = bf16[4,176,384]{2,1,0:T(8,128)(2,1)S(1)} collective-permute-done((bf16[4,176,384]{2,1,0:T(8,128)(2,1)S(1)}, bf16[4,176,384]{2,1,0:T(8,128)(2,1)S(1)}, u32[]{:S(2)}, u32[]{:S(2)}) %collective-permute-start.5) | collective-permute-done | bytes 540704 | tf_op jit(solution)/shard_map/ppermute | solution.py:242
  92.2 4.3 %all-to-all-start = ((bf16[4,8,176,128]{3,2,1,0:T(8,128)(2,1)}), bf16[4,8,176,128]{3,2,1,0:T(8,128)(2,1)S(1)}, u32[]{:S(2)}, u32[]{:S(2)}) async-start(bf16[4,8,176,128]{3,2,1,0:T(8,128)(2,1)} %broadcast_in_dim.22), calls=%async_computation | async-start | bytes 2883584 | tf_op jit(solution)/shard_map/all_to_all | solution.py:295
  100.0 3.8 %shard_map.94.source = bf16[384,5120]{1,0:T(8,128)(2,1)S(1)} custom-call(s32[3]{0:T(128)S(1)} %pad_add_fusion.1.where, f32[1,5120]{1,0:T(1,128)S(1)} %bitcast.58, bf16[4,192,640]{2,1,0:T(8,128)(2,1)S(1)} %bitcast.51, bf16[4,192,640]{2,1,0:T(8,128)(2,1)S(1)} %bitcast.53, bf16[4,192,640]{2,1,0:T(8,128)(2,1)S(1)} %copy-done.7, ...), custom_call_target="tpu_custom_call" | custom-call | flops 4000000000 | bytes 4194304 | tf_op jit(solution)/shard_map/pallas_call | solution.py:302
  105.7 7.2 %all-to-all-done.blocks = bf16[4,8,176,128]{3,2,1,0:T(8,128)(2,1)S(1)} async-done(((bf16[4,8,176,128]{3,2,1,0:T(8,128)(2,1)}), bf16[4,8,176,128]{3,2,1,0:T(8,128)(2,1)S(1)}, u32[]{:S(2)}, u32[]{:S(2)}) %all-to-all-start) | async-done | bytes 1441824 | tf_op jit(solution)/shard_map/all_to_all | solution.py:295
  114.8 3.7 %all-to-all-start.1 = ((bf16[4,8,160,256]{3,2,1,0:T(8,128)(2,1)}), bf16[4,8,160,256]{3,2,1,0:T(8,128)(2,1)S(1)}, u32[]{:S(2)}, u32[]{:S(2)}) async-start(bf16[4,8,160,256]{3,2,1,0:T(8,128)(2,1)} %broadcast_in_dim.20), calls=%async_computation.1 | async-start | bytes 5242880 | tf_op jit(solution)/shard_map/all_to_all | solution.py:298
  119.8 2.1 %copy-done.11 = bf16[384,5120]{1,0:T(8,128)(2,1)S(1)} copy-done((bf16[384,5120]{1,0:T(8,128)(2,1)S(1)}, bf16[384,5120]{1,0:T(8,128)(2,1)}, u32[]{:S(2)}) %copy-start.11) | copy-done | bytes 3932184
  121.9 2.3 %shard_map.95 = bf16[384,128]{1,0:T(8,128)(2,1)S(1)} custom-call(s32[64]{0:T(128)S(1)} %broadcast_multiply_fusion.offsets, s32[3]{0:T(128)S(1)} %pad_add_fusion.1.where, bf16[384,5120]{1,0:T(8,128)(2,1)S(1)} %copy-done.11, f32[1,128]{1,0:T(1,128)S(1)} %bitcast.59, f32[384,128]{1,0:T(8,128)S(1)} %get-tuple-element.60.cosine, ...), custom_call_target="tpu_custom_call" | custom-call | flops 2000000000 | bytes 4194304 | tf_op jit(solution)/shard_map/pallas_call | solution.py:342
  124.3 3.1 %collective-permute-start.6 = (bf16[384,128]{1,0:T(8,128)(2,1)S(1)}, bf16[384,128]{1,0:T(8,128)(2,1)S(1)}, u32[]{:S(2)}, u32[]{:S(2)}) collective-permute-start(bf16[384,128]{1,0:T(8,128)(2,1)S(1)} %shard_map.95), channel_id=1, source_target_pairs={{0,64},{16,80},{32,96},{48,112},{64,0},{80,16},{96,32},{112,48},{1... | collective-permute-start | bytes 294920 | tf_op jit(solution)/shard_map/ppermute | solution.py:242
  130.4 2.0 stack.101.where
  132.4 4.3 %collective-permute-done.6 = bf16[384,128]{1,0:T(8,128)(2,1)S(1)} collective-permute-done((bf16[384,128]{1,0:T(8,128)(2,1)S(1)}, bf16[384,128]{1,0:T(8,128)(2,1)S(1)}, u32[]{:S(2)}, u32[]{:S(2)}) %collective-permute-start.6) | collective-permute-done | bytes 98336 | tf_op jit(solution)/shard_map/ppermute | solution.py:242
  138.7 6.6 %collective-permute-done.7 = bf16[2,384,128]{2,1,0:T(8,128)(2,1)} collective-permute-done((bf16[2,384,128]{2,1,0:T(8,128)(2,1)S(1)}, bf16[2,384,128]{2,1,0:T(8,128)(2,1)}, u32[]{:S(2)}, u32[]{:S(2)}) %collective-permute-start.7) | collective-permute-done | bytes 196640 | tf_op jit(solution)/shard_map/ppermute | solution.py:242
  146.5 8.9 %collective-permute-start.8 = (bf16[4,384,128]{2,1,0:T(8,128)(2,1)S(1)}, bf16[4,384,128]{2,1,0:T(8,128)(2,1)}, u32[]{:S(2)}, u32[]{:S(2)}) collective-permute-start(bf16[4,384,128]{2,1,0:T(8,128)(2,1)S(1)} %pad_maximum_fusion.2.refs_0_), channel_id=1, source_target_pairs={{0,8},{8,0},{1,9},{9,1},{2,10},{10,2},{3,11},{11,3},{4,12},{12,4},... | collective-permute-start | bytes 1179656 | tf_op jit(solution)/shard_map/ppermute | solution.py:369
  159.3 2.1 %copy-done.12 = bf16[384,5120]{1,0:T(8,128)(2,1)S(1)} copy-done((bf16[384,5120]{1,0:T(8,128)(2,1)S(1)}, bf16[384,5120]{1,0:T(8,128)(2,1)}, u32[]{:S(2)}) %copy-start.12) | copy-done | bytes 3932184
  161.4 2.4 %shard_map.96 = bf16[2,2,192,128]{3,2,1,0:T(8,128)(2,1)S(1)} custom-call(s32[64]{0:T(128)S(1)} %broadcast_multiply_fusion.offsets, s32[3]{0:T(128)S(1)} %pad_add_fusion.1.where, bf16[384,5120]{1,0:T(8,128)(2,1)S(1)} %copy-done.12, f32[1,128]{1,0:T(1,128)S(1)} %bitcast.60, f32[384,128]{1,0:T(8,128)S(1)} %copy-done.3, f32[384,128]{1,0:T(8,128)S(1)} %copy-done.5, ...), custom_call_target="tpu_custom_call" | custom-call | flops 4000000000 | bytes 4194304 | tf_op jit(solution)/shard_map/pallas_call | solution.py:371
  165.8 2.4 %collective-permute-done.12.refs_1_ = bf16[4,384,128]{2,1,0:T(8,128)(2,1)} collective-permute-done((bf16[4,384,128]{2,1,0:T(8,128)(2,1)S(1)}, bf16[4,384,128]{2,1,0:T(8,128)(2,1)}, u32[]{:S(2)}, u32[]{:S(2)}) %collective-permute-start.12) | collective-permute-done | bytes 393248 | tf_op jit(solution)/shard_map/ppermute | solution.py:242
  168.2 2.7 %collective-permute-start.13 = (bf16[4,384,128]{2,1,0:T(8,128)(2,1)}, bf16[4,384,128]{2,1,0:T(8,128)(2,1)S(1)}, u32[]{:S(2)}, u32[]{:S(2)}) collective-permute-start(bf16[4,384,128]{2,1,0:T(8,128)(2,1)} %collective-permute-done.12.refs_1_), channel_id=1, source_target_pairs={{0,8},{8,0},{1,9},{9,1},{2,10},{10,2},{3,11},{11,3},{4,12},{12,4},... | collective-permute-start | bytes 1179656 | tf_op jit(solution)/shard_map/ppermute | solution.py:369
  175.2 4.6 %collective-permute-done.10.near = bf16[768,128]{1,0:T(8,128)(2,1)S(1)} collective-permute-done((bf16[768,128]{1,0:T(8,128)(2,1)S(1)}, bf16[768,128]{1,0:T(8,128)(2,1)S(1)}, u32[]{:S(2)}, u32[]{:S(2)}) %collective-permute-start.10) | collective-permute-done | bytes 196640 | tf_op jit(solution)/shard_map/ppermute | solution.py:389
  179.8 2.9 %collective-permute-done.11.far = bf16[768,128]{1,0:T(8,128)(2,1)S(1)} collective-permute-done((bf16[768,128]{1,0:T(8,128)(2,1)S(1)}, bf16[768,128]{1,0:T(8,128)(2,1)S(1)}, u32[]{:S(2)}, u32[]{:S(2)}) %collective-permute-start.11) | collective-permute-done | bytes 196640 | tf_op jit(solution)/shard_map/ppermute | solution.py:390
  182.7 5.5 %shard_map.97 = (bf16[816,128]{1,0:T(8,128)(2,1)S(1)}, bf16[816,128]{1,0:T(8,128)(2,1)S(1)}, bf16[3072,128]{1,0:T(8,128)(2,1)S(1)}, bf16[3072,256]{1,0:T(8,128)(2,1)S(1)}) custom-call(s32[12]{0:T(128)S(1)} %stack.101.where, s32[3,192,1]{2,1,0:T(8,128)S(1)} %broadcast_subtract_fusion.begins, bf16[768,128]{1,0:T(8,128)(2,1)S(1)} %collective-permute-done.10.near, ...), custom_call_target="tpu_custom_call" | custom-call | flops 10000000000 | bytes 4194304 | tf_op jit(solution)/shard_map/pallas_call | solution.py:393
  188.2 6.8 %collective-permute-start.14 = (bf16[816,128]{1,0:T(8,128)(2,1)S(1)}, bf16[816,128]{1,0:T(8,128)(2,1)S(1)}, u32[]{:S(2)}, u32[]{:S(2)}) collective-permute-start(bf16[816,128]{1,0:T(8,128)(2,1)S(1)} %get-tuple-element.41), channel_id=1, source_target_pairs={{0,128},{128,256},{256,384},{1,129},{129,257},{257,385},{2,130},{1... | collective-permute-start | bytes 626696 | tf_op jit(solution)/shard_map/ppermute | solution.py:402
  196.3 2.5 %shard_map.98 = (f32[768,128]{1,0:T(8,128)S(1)}, f32[768,1]{1,0:T(8,128)S(1)}) custom-call(s32[12]{0:T(128)S(1)} %stack.101.where, s32[3,192,1]{2,1,0:T(8,128)S(1)} %broadcast_subtract_fusion.begins, bf16[768,128]{1,0:T(8,128)(2,1)S(1)} %bitcast.57, bf16[3072,128]{1,0:T(8,128)(2,1)S(1)} %get-tuple-element.37.keys, bf16[3072,256]{1,0:T(8,128)(2,1)S(1)} %get-tuple-element.38.values), custom_call_target="tpu_custom_call" | custom-call | flops 10000000000 | bytes 4194304 | tf_op jit(solution)/shard_map/pallas_call | solution.py:404
  198.8 4.3 %collective-permute-done.15.r2 = bf16[816,128]{1,0:T(8,128)(2,1)S(1)} collective-permute-done((bf16[816,128]{1,0:T(8,128)(2,1)S(1)}, bf16[816,128]{1,0:T(8,128)(2,1)S(1)}, u32[]{:S(2)}, u32[]{:S(2)}) %collective-permute-start.15) | collective-permute-done | bytes 208928 | tf_op jit(solution)/shard_map/ppermute | solution.py:403
  203.2 2.0 shard_map.99
  (106 shorter events, 29.1 us)
Async XLA Ops:
  0.6 13.8 %copy-start.18 = (bf16[192,640]{1,0:T(8,128)(2,1)S(1)}, bf16[192,640]{1,0:T(8,128)(2,1)}, u32[]{:S(2)}) copy-start(bf16[192,640]{1,0:T(8,128)(2,1)} %param.7) | copy-start | bytes 737284
  11.0 79.0 %copy-start.13 = (bf16[1,176,384]{2,1,0:T(8,128)(2,1)}, bf16[1,176,384]{2,1,0:T(8,128)(2,1)S(1)}, u32[]{:S(2)}) copy-start(bf16[1,176,384]{2,1,0:T(8,128)(2,1)S(1)} %fusion.4) | copy-start | bytes 405508
  11.0 27.3 %collective-permute-start = (bf16[1,176,384]{2,1,0:T(8,128)(2,1)S(1)}, bf16[1,176,384]{2,1,0:T(8,128)(2,1)S(1)}, u32[]{:S(2)}, u32[]{:S(2)}) collective-permute-start(bf16[1,176,384]{2,1,0:T(8,128)(2,1)S(1)} %fusion.4), channel_id=1, source_target_pairs={{0,64},{16,80},{32,96},{48,112},{64,0},{80,16},{96,32},{112,48},{1... | collective-permute-start | bytes 405512 | tf_op jit(solution)/shard_map/ppermute | solution.py:242
  14.4 23.8 %collective-permute-start.1 = (bf16[192,640]{1,0:T(8,128)(2,1)S(1)}, bf16[192,640]{1,0:T(8,128)(2,1)S(1)}, u32[]{:S(2)}, u32[]{:S(2)}) collective-permute-start(bf16[192,640]{1,0:T(8,128)(2,1)S(1)} %copy-done.18), channel_id=1, source_target_pairs={{0,1},{1,0},{2,3},{3,2},{4,5},{5,4},{6,7},{7,6},{8,9},{9,8},{10,11... | collective-permute-start | bytes 737288 | tf_op jit(solution)/shard_map/ppermute | solution.py:277
  38.3 51.7 %copy-start.15 = (bf16[1,176,384]{2,1,0:T(8,128)(2,1)}, bf16[1,176,384]{2,1,0:T(8,128)(2,1)S(1)}, u32[]{:S(2)}) copy-start(bf16[1,176,384]{2,1,0:T(8,128)(2,1)S(1)} %collective-permute-done) | copy-start | bytes 405508
  38.3 34.6 %collective-permute-start.3 = (bf16[4,192,640]{2,1,0:T(8,128)(2,1)S(1)}, bf16[4,192,640]{2,1,0:T(8,128)(2,1)S(1)}, u32[]{:S(2)}, u32[]{:S(2)}) collective-permute-start(bf16[4,192,640]{2,1,0:T(8,128)(2,1)S(1)} %bitcast.50), channel_id=1, source_target_pairs={{0,8},{8,0},{1,9},{9,1},{2,10},{10,2},{3,11},{11,3},{4,12},{12,4},... | collective-permute-start | bytes 2949128 | tf_op jit(solution)/shard_map/ppermute | solution.py:283
  42.2 30.6 %collective-permute-start.2 = (bf16[2,176,384]{2,1,0:T(8,128)(2,1)S(1)}, bf16[2,176,384]{2,1,0:T(8,128)(2,1)S(1)}, u32[]{:S(2)}, u32[]{:S(2)}) collective-permute-start(bf16[2,176,384]{2,1,0:T(8,128)(2,1)S(1)} %pad_maximum_fusion.4), channel_id=1, source_target_pairs={{0,32},{16,48},{32,0},{48,16},{64,96},{80,112},{96,64},{112,80},{1... | collective-permute-start | bytes 811016 | tf_op jit(solution)/shard_map/ppermute | solution.py:242
  72.8 17.1 %copy-start.14 = (bf16[2,176,384]{2,1,0:T(8,128)(2,1)}, bf16[2,176,384]{2,1,0:T(8,128)(2,1)S(1)}, u32[]{:S(2)}) copy-start(bf16[2,176,384]{2,1,0:T(8,128)(2,1)S(1)} %collective-permute-done.2) | copy-start | bytes 811012
  73.9 16.1 %collective-permute-start.5 = (bf16[4,176,384]{2,1,0:T(8,128)(2,1)S(1)}, bf16[4,176,384]{2,1,0:T(8,128)(2,1)S(1)}, u32[]{:S(2)}, u32[]{:S(2)}) collective-permute-start(bf16[4,176,384]{2,1,0:T(8,128)(2,1)S(1)} %pad_maximum_fusion.1), channel_id=1, source_target_pairs={{0,16},{16,0},{32,48},{48,32},{64,80},{80,64},{96,112},{112,96},{1... | collective-permute-start | bytes 1622024 | tf_op jit(solution)/shard_map/ppermute | solution.py:242
  79.6 18.6 %collective-permute-start.4 = (bf16[4,192,640]{2,1,0:T(8,128)(2,1)S(1)}, bf16[4,192,640]{2,1,0:T(8,128)(2,1)}, u32[]{:S(2)}, u32[]{:S(2)}) collective-permute-start(bf16[4,192,640]{2,1,0:T(8,128)(2,1)S(1)} %bitcast.52), channel_id=1, source_target_pairs={{0,8},{8,0},{1,9},{9,1},{2,10},{10,2},{3,11},{11,3},{4,12},{12,4},... | collective-permute-start | bytes 2949128 | tf_op jit(solution)/shard_map/ppermute | solution.py:289
  92.2 4.3 %copy-start.19 = (bf16[5120]{0:T(1024)(128)(2,1)S(1)}, bf16[5120]{0:T(1024)(128)(2,1)}, u32[]{:S(2)}) copy-start(bf16[5120]{0:T(1024)(128)(2,1)} %param.8) | copy-start | bytes 30724
  92.2 4.5 %copy-start.20 = (s32[64]{0:T(128)S(1)}, s32[64]{0:T(128)}, u32[]{:S(2)}) copy-start(s32[64]{0:T(128)} %param.13) | copy-start | bytes 772
  92.2 20.7 %all-to-all-start = ((bf16[4,8,176,128]{3,2,1,0:T(8,128)(2,1)}), bf16[4,8,176,128]{3,2,1,0:T(8,128)(2,1)S(1)}, u32[]{:S(2)}, u32[]{:S(2)}) async-start(bf16[4,8,176,128]{3,2,1,0:T(8,128)(2,1)} %broadcast_in_dim.22), calls=%async_computation | async-start | bytes 2883584 | tf_op jit(solution)/shard_map/all_to_all | solution.py:295
  98.2 1.8 copy-start.7
  103.9 1.9 copy-start.10
  114.8 31.8 %all-to-all-start.1 = ((bf16[4,8,160,256]{3,2,1,0:T(8,128)(2,1)}), bf16[4,8,160,256]{3,2,1,0:T(8,128)(2,1)S(1)}, u32[]{:S(2)}, u32[]{:S(2)}) async-start(bf16[4,8,160,256]{3,2,1,0:T(8,128)(2,1)} %broadcast_in_dim.20), calls=%async_computation.1 | async-start | bytes 5242880 | tf_op jit(solution)/shard_map/all_to_all | solution.py:298
  119.5 4.8 %copy-start.2 = (f32[384,128]{1,0:T(8,128)}, f32[384,128]{1,0:T(8,128)S(1)}, u32[]{:S(2)}) copy-start(f32[384,128]{1,0:T(8,128)S(1)} %get-tuple-element.60.cosine) | copy-start | bytes 589828
  119.5 4.8 %copy-start.4 = (f32[384,128]{1,0:T(8,128)}, f32[384,128]{1,0:T(8,128)S(1)}, u32[]{:S(2)}) copy-start(f32[384,128]{1,0:T(8,128)S(1)} %get-tuple-element.61.sine) | copy-start | bytes 589828
  119.8 2.1 %copy-start.11 = (bf16[384,5120]{1,0:T(8,128)(2,1)S(1)}, bf16[384,5120]{1,0:T(8,128)(2,1)}, u32[]{:S(2)}) copy-start(bf16[384,5120]{1,0:T(8,128)(2,1)} %copy-done.10) | copy-start | bytes 11796484
  124.3 33.1 %copy-start.9 = (f32[128]{0:T(128)S(1)}, f32[128]{0:T(128)}, u32[]{:S(2)}) copy-start(f32[128]{0:T(128)} %param.9) | copy-start | bytes 1540
  124.3 12.4 %collective-permute-start.6 = (bf16[384,128]{1,0:T(8,128)(2,1)S(1)}, bf16[384,128]{1,0:T(8,128)(2,1)S(1)}, u32[]{:S(2)}, u32[]{:S(2)}) collective-permute-start(bf16[384,128]{1,0:T(8,128)(2,1)S(1)} %shard_map.95), channel_id=1, source_target_pairs={{0,64},{16,80},{32,96},{48,112},{64,0},{80,16},{96,32},{112,48},{1... | collective-permute-start | bytes 294920 | tf_op jit(solution)/shard_map/ppermute | solution.py:242
  136.8 1.9 copy-start.17
  136.8 8.5 %collective-permute-start.7 = (bf16[2,384,128]{2,1,0:T(8,128)(2,1)S(1)}, bf16[2,384,128]{2,1,0:T(8,128)(2,1)}, u32[]{:S(2)}, u32[]{:S(2)}) collective-permute-start(bf16[2,384,128]{2,1,0:T(8,128)(2,1)S(1)} %pad_maximum_fusion.7), channel_id=1, source_target_pairs={{0,32},{16,48},{32,0},{48,16},{64,96},{80,112},{96,64},{112,80},{1... | collective-permute-start | bytes 589832 | tf_op jit(solution)/shard_map/ppermute | solution.py:242
  146.5 27.1 %collective-permute-start.8 = (bf16[4,384,128]{2,1,0:T(8,128)(2,1)S(1)}, bf16[4,384,128]{2,1,0:T(8,128)(2,1)}, u32[]{:S(2)}, u32[]{:S(2)}) collective-permute-start(bf16[4,384,128]{2,1,0:T(8,128)(2,1)S(1)} %pad_maximum_fusion.2.refs_0_), channel_id=1, source_target_pairs={{0,8},{8,0},{1,9},{9,1},{2,10},{10,2},{3,11},{11,3},{4,12},{12,4},... | collective-permute-start | bytes 1179656 | tf_op jit(solution)/shard_map/ppermute | solution.py:369
  155.5 12.7 %collective-permute-start.12 = (bf16[4,384,128]{2,1,0:T(8,128)(2,1)S(1)}, bf16[4,384,128]{2,1,0:T(8,128)(2,1)}, u32[]{:S(2)}, u32[]{:S(2)}) collective-permute-start(bf16[4,384,128]{2,1,0:T(8,128)(2,1)S(1)} %pad_maximum_fusion.2.refs_0_), channel_id=1, source_target_pairs={{0,16},{16,0},{32,48},{48,32},{64,80},{80,64},{96,112},{112,96},{1... | collective-permute-start | bytes 1179656 | tf_op jit(solution)/shard_map/ppermute | solution.py:242
  159.3 2.1 %copy-start.12 = (bf16[384,5120]{1,0:T(8,128)(2,1)S(1)}, bf16[384,5120]{1,0:T(8,128)(2,1)}, u32[]{:S(2)}) copy-start(bf16[384,5120]{1,0:T(8,128)(2,1)} %copy-done.10) | copy-start | bytes 11796484
  163.8 7.1 %collective-permute-start.9 = (bf16[2,192,128]{2,1,0:T(8,128)(2,1)S(1)}, bf16[2,192,128]{2,1,0:T(8,128)(2,1)S(1)}, u32[]{:S(2)}, u32[]{:S(2)}) collective-permute-start(bf16[2,192,128]{2,1,0:T(8,128)(2,1)S(1)} %get-tuple-element.46), channel_id=1, source_target_pairs={{0,8},{8,0},{1,9},{9,1},{2,10},{10,2},{3,11},{11,3},{4,12},{12,4},... | collective-permute-start | bytes 294920 | tf_op jit(solution)/shard_map/ppermute | solution.py:387
  168.2 14.5 %collective-permute-start.13 = (bf16[4,384,128]{2,1,0:T(8,128)(2,1)}, bf16[4,384,128]{2,1,0:T(8,128)(2,1)S(1)}, u32[]{:S(2)}, u32[]{:S(2)}) collective-permute-start(bf16[4,384,128]{2,1,0:T(8,128)(2,1)} %collective-permute-done.12.refs_1_), channel_id=1, source_target_pairs={{0,8},{8,0},{1,9},{9,1},{2,10},{10,2},{3,11},{11,3},{4,12},{12,4},... | collective-permute-start | bytes 1179656 | tf_op jit(solution)/shard_map/ppermute | solution.py:369
  171.0 8.8 %collective-permute-start.10 = (bf16[768,128]{1,0:T(8,128)(2,1)S(1)}, bf16[768,128]{1,0:T(8,128)(2,1)S(1)}, u32[]{:S(2)}, u32[]{:S(2)}) collective-permute-start(bf16[768,128]{1,0:T(8,128)(2,1)S(1)} %bitcast.55), channel_id=1, source_target_pairs={{128,0},{256,128},{384,256},{129,1},{257,129},{385,257},{130,2},{2... | collective-permute-start | bytes 589832 | tf_op jit(solution)/shard_map/ppermute | solution.py:389
  172.3 10.4 %collective-permute-start.11 = (bf16[768,128]{1,0:T(8,128)(2,1)S(1)}, bf16[768,128]{1,0:T(8,128)(2,1)S(1)}, u32[]{:S(2)}, u32[]{:S(2)}) collective-permute-start(bf16[768,128]{1,0:T(8,128)(2,1)S(1)} %bitcast.56), channel_id=1, source_target_pairs={{256,0},{384,128},{257,1},{385,129},{258,2},{386,130},{259,3},{387... | collective-permute-start | bytes 589832 | tf_op jit(solution)/shard_map/ppermute | solution.py:390
  188.2 10.6 %collective-permute-start.14 = (bf16[816,128]{1,0:T(8,128)(2,1)S(1)}, bf16[816,128]{1,0:T(8,128)(2,1)S(1)}, u32[]{:S(2)}, u32[]{:S(2)}) collective-permute-start(bf16[816,128]{1,0:T(8,128)(2,1)S(1)} %get-tuple-element.41), channel_id=1, source_target_pairs={{0,128},{128,256},{256,384},{1,129},{129,257},{257,385},{2,130},{1... | collective-permute-start | bytes 626696 | tf_op jit(solution)/shard_map/ppermute | solution.py:402
  195.0 8.1 %collective-permute-start.15 = (bf16[816,128]{1,0:T(8,128)(2,1)S(1)}, bf16[816,128]{1,0:T(8,128)(2,1)S(1)}, u32[]{:S(2)}, u32[]{:S(2)}) collective-permute-start(bf16[816,128]{1,0:T(8,128)(2,1)S(1)} %get-tuple-element.42), channel_id=1, source_target_pairs={{0,256},{128,384},{1,257},{129,385},{2,258},{130,386},{3,259},{131... | collective-permute-start | bytes 626696 | tf_op jit(solution)/shard_map/ppermute | solution.py:403
  (7 other events, 7.5 us)

commit v11 on v10

--- a/solution.py
+++ b/solution.py
@@ -43,14 +43,16 @@
     return v * cosine + pltpu.roll(v, 64, 1) * sine
 
 
-def collect(offsets, where, blocks, weights, panel):
-    nx, nz = blocks.shape[:2]
-    for s in range(nx):
-        for k, peer in enumerate(PEER):
-            for c in range(2):
-                slot = s * (2 * nz) + (where[1] ^ peer) * 2 + c
-                first = pl.multiple_of(offsets[slot], 16)
-                weights[pl.ds(first, panel), :] = blocks[s, k, c * panel : (c + 1) * panel, :]
+def collect(offsets, where, parts, weights, panel):
+    peers = iter(PEER)
+    for blocks in parts:
+        for k in range(blocks.shape[1]):
+            peer = next(peers)
+            for s in range(blocks.shape[0]):
+                for c in range(2):
+                    slot = s * (2 * len(PEER)) + (where[1] ^ peer) * 2 + c
+                    first = pl.multiple_of(offsets[slot], 16)
+                    weights[pl.ds(first, panel), :] = blocks[s, k, c * panel : (c + 1) * panel, :]
 
 
 def norm_kernel(where, norm_gain, *refs):
@@ -79,10 +81,10 @@
     copy.wait()
 
 
-def pair_kernel(panel, offsets, where, source, gain, cosine, sine, blocks, out, normed, weights, sem):
+def pair_kernel(panel, offsets, where, source, gain, cosine, sine, near, far, out, normed, weights, sem):
     copy = pltpu.make_async_copy(source, normed, sem)
     copy.start()
-    collect(offsets, where, blocks, weights, panel)
+    collect(offsets, where, (near, far), weights, panel)
     copy.wait()
     v = jnp.dot(normed[...], weights[...], preferred_element_type=jnp.float32)
     keys = head_norm_rope(v, gain[...], cosine[...], sine[...])
@@ -92,7 +94,7 @@
 def query_kernel(panel, offsets, where, source, gain, cosine, sine, blocks, out, normed, weights, sem):
     copy = pltpu.make_async_copy(source, normed, sem)
     copy.start()
-    collect(offsets, where, blocks, weights, panel)
+    collect(offsets, where, (blocks,), weights, panel)
     copy.wait()
     rows = out.shape[2]
     for side in range(2):
@@ -284,18 +286,20 @@
     own_far = lax.all_gather(far, "y", axis=0)
     step, other_near, own_far = lax.optimization_barrier((step, other_near, own_far))
 
+    def copies(v):
+        return jnp.broadcast_to(v[None], (nx, *v.shape))
+
     line = jnp.concatenate([line, step], axis=0)
     step = across(line, 1)
     other_far = lax.ppermute(own_far, "c", swap)
+    pair_near = lax.all_to_all(copies(line[:, :, :128]), "x", 0, 0)
+    step, pair_near = lax.optimization_barrier((step, pair_near))
+
+    pair_far = lax.all_to_all(copies(step[:, :, :128]), "x", 0, 0)
     line = jnp.concatenate([line, step], axis=0)
-
-    def copies(v):
-        return jnp.broadcast_to(v[None], (nx, *v.shape))
-
-    pair_blocks = lax.all_to_all(copies(line[:, :, :128]), "x", 0, 0)
     query_line = copies(line[:, : 2 * panel, 128:])
     other_far, query_line = lax.optimization_barrier((other_far, query_line))
-    query_blocks = lax.all_to_all(after(query_line, pair_blocks), "x", 0, 0)
+    query_blocks = lax.all_to_all(after(query_line, pair_far), "x", 0, 0)
 
     spot = jnp.stack([c, z, w]).astype(jnp.int32)
     features = norm_gain.shape[0]
@@ -309,7 +313,8 @@
         out_hbm=True,
     )(spot, norm_gain.astype(f32)[None, :], own_near, own_far, other_near, other_far)
 
-    riding = pair_blocks[:, :, 2 * panel : 2 * panel + 4, :].astype(f32)
+    riding = [v[:, :, 2 * panel : 2 * panel + 4, :] for v in (pair_near, pair_far)]
+    riding = jnp.concatenate(riding, axis=1).astype(f32)
     starts = jnp.sum(
         (riding.reshape(-1, 1) < table.astype(f32)[None, :]).astype(f32), axis=0
     ).astype(jnp.int32)
@@ -343,7 +348,7 @@
         functools.partial(pair_kernel, panel),
         [jax.ShapeDtypeStruct((2 * rows, 128), bf16)],
         2,
-        4,
+        5,
         [
             pltpu.VMEM((2 * rows, features), bf16),
             pltpu.VMEM((features, 128), bf16),
@@ -351,7 +356,7 @@
         ],
         2 * 10**9,
         n_hbm=1,
-    )(offsets, spot, normed, key_gain[None, :], cosine, sine, pair_blocks)
+    )(offsets, spot, normed, key_gain[None, :], cosine, sine, pair_near, pair_far)
 
     inside = z * 2 * rows + c * rows
     low = [jnp.clip(spread[s, 0], 0, plane) for s in range(3)]
@@ -363,11 +368,6 @@
     mine0 = jnp.stack([pair, across(pair, 4)])
     mine0, ranges, begins = lax.optimization_barrier((mine0, ranges, begins))
     mine0 = jnp.concatenate([mine0, across(mine0, 2)], axis=0)
-    mine0, query_blocks = lax.optimization_barrier((mine0, query_blocks))
-    mine1 = across(mine0, 1)
-    mine = [mine0, mine1]
-    other = [lax.ppermute(v, "c", swap) for v in mine]
-
     (query,) = call(
         functools.partial(query_kernel, panel),
         [jax.ShapeDtypeStruct((2, 2, rows, 128), bf16)],
@@ -382,6 +382,10 @@
         n_hbm=1,
     )(offsets, spot, normed, query_gain[None, :], cosine, sine, query_blocks)
 
+    mine0, query = lax.optimization_barrier((mine0, query))
+    mine1 = across(mine0, 1)
+    mine = [mine0, mine1]
+    other = [lax.ppermute(v, "c", swap) for v in mine]
     own_query = lax.dynamic_index_in_dim(query, c, 0, keepdims=False)
     sent_query = lax.dynamic_index_in_dim(query, 1 - c, 0, keepdims=False)
     q0 = jnp.concatenate([own_query, lax.ppermute(sent_query, "c", swap)], axis=0)

time: 207 us -> 215 us (1.039)
  waiting for transfers between devices: 38.7 us -> 46.2 us
    ppermute x6, waiting for transfers between devices: 19.5 us -> 28.6 us  [across(): return lax.ppermute(v, 'z', [(i, i ^ bit) for i in range(8)])]
    ppermute x2, starting transfers between devices: 11.6 us -> 5.63 us  [body(): other = [lax.ppermute(v, 'c', swap) for v in mine]]
    all_to_all x2 -> x3, starting transfers between devices: 7.94 us -> 11.7 us  [the longest x1 4.19 us: body(): pair_far = lax.all_to_all(copies(step[:, :, :128]), 'x', 0, 0)]
    slice x1 -> x4, local copies, waits for them, and re-layouts: 0.04 us -> 2.65 us  [the longest x1 0.94 us: body(): pair_near = lax.all_to_all(copies(line[:, :, :128]), 'x', 0, 0)]
    all_to_all x2 -> x3, waiting for transfers between devices: 7.33 us -> 5.14 us  [the longest x1 3.96 us: body(): pair_near = lax.all_to_all(copies(line[:, :, :128]), 'x', 0, 0)]
    unnamed x44 -> x32, local copies, waits for them, and re-layouts: 11.2 us -> 9.77 us
  transfers between devices with their start and end apart: 18 -> 19, of which waited for: 9 -> 9; matrix products, arithmetic and copies ran while one was open for 6% -> 7% of each run, Pallas kernels for 5% -> 4%
where the time goes in v11:
time: 215 us; the launch traced here: 212 us
  starting transfers between devices  79.8 us (37%)
  waiting for transfers between devices  46.2 us (21%)
  blocking collectives  37.6 us (17%)
  local copies, waits for them, and re-layouts  20.3 us (9%)
  Pallas kernels  18.7 us (9%)
  other arithmetic  6.56 us (3%)
  between operations  3.12 us (1%)
    ppermute x6, starting transfers between devices, across(): return lax.ppermute(v, 'z', [(i, i ^ bit) for i in range(8)])  31.3 us
    ppermute x6, waiting for transfers between devices, across(): return lax.ppermute(v, 'z', [(i, i ^ bit) for i in range(8)])  28.6 us
    all_gather x1, blocking collectives, body(): own_far = lax.all_gather(far, 'y', axis=0)  15.9 us
    all_gather x1, blocking collectives, body(): own_near = lax.all_gather(hidden, 'y', axis=0)  13.2 us
    ppermute x1, starting transfers between devices, body(): far = lax.ppermute(hidden, 'w', swap)  10.6 us
    unnamed x32, local copies, waits for them, and re-layouts  9.77 us
    all_gather x1, blocking collectives, body(): lax.all_gather(jnp.concatenate([weight_store, riders], axis=0), 'c', axis=0)  8.53 us
    ppermute x1, starting transfers between devices, body(): r1 = lax.ppermute(r1, 'x', [(i, i + 1) for i in range(nx - 1)])  6.87 us
  transfers between devices with their start and end apart: 19, of which 9 were waited for; matrix products, arithmetic and copies ran while one was open for 7% of the time, Pallas kernels for 4%

profile of v11, /device:TPU:1, one launch (start us, length us, event | category | flops | bytes accessed | tf_op | source)
XLA Modules:
  0.0 212.4 jit_solution(10779283424917533633)
XLA Ops:
  2.3 8.5 %all-gather = bf16[192,768]{1,0:T(8,128)(2,1)S(1)} all-gather(bf16[96,768]{1,0:T(8,128)(2,1)S(1)} %fusion.2), channel_id=2, replica_groups=mesh['x'=4,'z'=8,'c'=2,'y'=4,'w'=2] {'c'}, dimensions={0}, use_global_device_ids=true | all-gather | bytes 442368 | tf_op jit(solution)/shard_map/all_gather | solution.py:263
  11.0 3.4 %collective-permute-start = (bf16[1,176,384]{2,1,0:T(8,128)(2,1)S(1)}, bf16[1,176,384]{2,1,0:T(8,128)(2,1)S(1)}, u32[]{:S(2)}, u32[]{:S(2)}) collective-permute-start(bf16[1,176,384]{2,1,0:T(8,128)(2,1)S(1)} %fusion.4), channel_id=1, source_target_pairs={{0,64},{16,80},{32,96},{48,112},{64,0},{80,16},{96,32},{112,48},{1... | collective-permute-start | bytes 405512 | tf_op jit(solution)/shard_map/ppermute | solution.py:244
  14.4 10.6 %collective-permute-start.1 = (bf16[192,640]{1,0:T(8,128)(2,1)S(1)}, bf16[192,640]{1,0:T(8,128)(2,1)S(1)}, u32[]{:S(2)}, u32[]{:S(2)}) collective-permute-start(bf16[192,640]{1,0:T(8,128)(2,1)S(1)} %copy-done.12), channel_id=1, source_target_pairs={{0,1},{1,0},{2,3},{3,2},{4,5},{5,4},{6,7},{7,6},{8,9},{9,8},{10,11... | collective-permute-start | bytes 737288 | tf_op jit(solution)/shard_map/ppermute | solution.py:279
  25.1 13.2 %all-gather.1 = bf16[768,640]{1,0:T(8,128)(2,1)S(1)} all-gather(bf16[192,640]{1,0:T(8,128)(2,1)S(1)} %copy-done.12), channel_id=3, replica_groups=mesh['x'=4,'z'=8,'c'=2,'y'=4,'w'=2] {'y'}, dimensions={0}, use_global_device_ids=true | all-gather | bytes 1228800 | tf_op jit(solution)/shard_map/all_gather | solution.py:280
  38.3 3.9 %collective-permute-start.3 = (bf16[4,192,640]{2,1,0:T(8,128)(2,1)S(1)}, bf16[4,192,640]{2,1,0:T(8,128)(2,1)S(1)}, u32[]{:S(2)}, u32[]{:S(2)}) collective-permute-start(bf16[4,192,640]{2,1,0:T(8,128)(2,1)S(1)} %bitcast.50), channel_id=1, source_target_pairs={{0,8},{8,0},{1,9},{9,1},{2,10},{10,2},{3,11},{11,3},{4,12},{12,4},... | collective-permute-start | bytes 2949128 | tf_op jit(solution)/shard_map/ppermute | solution.py:285
  42.3 14.7 %collective-permute-start.2 = (bf16[2,176,384]{2,1,0:T(8,128)(2,1)S(1)}, bf16[2,176,384]{2,1,0:T(8,128)(2,1)S(1)}, u32[]{:S(2)}, u32[]{:S(2)}) collective-permute-start(bf16[2,176,384]{2,1,0:T(8,128)(2,1)S(1)} %pad_maximum_fusion.5), channel_id=1, source_target_pairs={{0,32},{16,48},{32,0},{48,16},{64,96},{80,112},{96,64},{112,80},{1... | collective-permute-start | bytes 811016 | tf_op jit(solution)/shard_map/ppermute | solution.py:244
  57.0 15.9 %all-gather.2 = bf16[768,640]{1,0:T(8,128)(2,1)S(1)} all-gather(bf16[192,640]{1,0:T(8,128)(2,1)S(1)} %collective-permute-done.1), channel_id=4, replica_groups=mesh['x'=4,'z'=8,'c'=2,'y'=4,'w'=2] {'y'}, dimensions={0}, use_global_device_ids=true | all-gather | bytes 1228800 | tf_op jit(solution)/shard_map/all_gather | solution.py:286
  73.9 3.9 %collective-permute-start.4 = (bf16[4,192,640]{2,1,0:T(8,128)(2,1)S(1)}, bf16[4,192,640]{2,1,0:T(8,128)(2,1)}, u32[]{:S(2)}, u32[]{:S(2)}) collective-permute-start(bf16[4,192,640]{2,1,0:T(8,128)(2,1)S(1)} %bitcast.52), channel_id=1, source_target_pairs={{0,8},{8,0},{1,9},{9,1},{2,10},{10,2},{3,11},{11,3},{4,12},{12,4},... | collective-permute-start | bytes 2949128 | tf_op jit(solution)/shard_map/ppermute | solution.py:294
  78.7 5.7 %collective-permute-start.5 = (bf16[4,176,384]{2,1,0:T(8,128)(2,1)}, bf16[4,176,384]{2,1,0:T(8,128)(2,1)}, u32[]{:S(2)}, u32[]{:S(2)}) collective-permute-start(bf16[4,176,384]{2,1,0:T(8,128)(2,1)} %pad_maximum_fusion.3), channel_id=1, source_target_pairs={{0,16},{16,0},{32,48},{48,32},{64,80},{80,64},{96,112},{112,96},{1... | collective-permute-start | bytes 1622024 | tf_op jit(solution)/shard_map/ppermute | solution.py:244
  86.4 3.9 %all-to-all-start = ((bf16[4,4,176,128]{3,2,1,0:T(8,128)(2,1)}), bf16[4,4,176,128]{3,2,1,0:T(8,128)(2,1)S(1)}, u32[]{:S(2)}, u32[]{:S(2)}) async-start(bf16[4,4,176,128]{3,2,1,0:T(8,128)(2,1)} %broadcast_in_dim.22), calls=%async_computation | async-start | bytes 1441792 | tf_op jit(solution)/shard_map/all_to_all | solution.py:295
  90.3 7.1 %collective-permute-done.5 = bf16[4,176,384]{2,1,0:T(8,128)(2,1)} collective-permute-done((bf16[4,176,384]{2,1,0:T(8,128)(2,1)}, bf16[4,176,384]{2,1,0:T(8,128)(2,1)}, u32[]{:S(2)}, u32[]{:S(2)}) %collective-permute-start.5) | collective-permute-done | bytes 540704 | tf_op jit(solution)/shard_map/ppermute | solution.py:244
  97.4 4.0 %all-to-all-done.near = bf16[4,4,176,128]{3,2,1,0:T(8,128)(2,1)S(1)} async-done(((bf16[4,4,176,128]{3,2,1,0:T(8,128)(2,1)}), bf16[4,4,176,128]{3,2,1,0:T(8,128)(2,1)S(1)}, u32[]{:S(2)}, u32[]{:S(2)}) %all-to-all-start) | async-done | bytes 720928 | tf_op jit(solution)/shard_map/all_to_all | solution.py:295
  103.3 4.2 %all-to-all-start.1 = ((bf16[4,4,176,128]{3,2,1,0:T(8,128)(2,1)}), bf16[4,4,176,128]{3,2,1,0:T(8,128)(2,1)}, u32[]{:S(2)}, u32[]{:S(2)}) async-start(bf16[4,4,176,128]{3,2,1,0:T(8,128)(2,1)} %broadcast_in_dim.25), calls=%async_computation.1 | async-start | bytes 1441792 | tf_op jit(solution)/shard_map/all_to_all | solution.py:298
  110.6 3.8 %shard_map.94.source = bf16[384,5120]{1,0:T(8,128)(2,1)S(1)} custom-call(s32[3]{0:T(128)S(1)} %pad_add_fusion.1.where, f32[1,5120]{1,0:T(1,128)S(1)} %bitcast.58, bf16[4,192,640]{2,1,0:T(8,128)(2,1)S(1)} %bitcast.51, bf16[4,192,640]{2,1,0:T(8,128)(2,1)S(1)} %bitcast.53, bf16[4,192,640]{2,1,0:T(8,128)(2,1)S(1)} %copy-done.6, ...), custom_call_target="tpu_custom_call" | custom-call | flops 4000000000 | bytes 4194304 | tf_op jit(solution)/shard_map/pallas_call | solution.py:306
  119.0 3.7 %all-to-all-start.2 = ((bf16[4,8,160,256]{3,2,1,0:T(8,128)(2,1)}), bf16[4,8,160,256]{3,2,1,0:T(8,128)(2,1)S(1)}, u32[]{:S(2)}, u32[]{:S(2)}) async-start(bf16[4,8,160,256]{3,2,1,0:T(8,128)(2,1)} %broadcast_in_dim.23), calls=%async_computation.2 | async-start | bytes 5242880 | tf_op jit(solution)/shard_map/all_to_all | solution.py:302
  123.8 2.2 %copy-done.10 = bf16[384,5120]{1,0:T(8,128)(2,1)S(1)} copy-done((bf16[384,5120]{1,0:T(8,128)(2,1)S(1)}, bf16[384,5120]{1,0:T(8,128)(2,1)}, u32[]{:S(2)}) %copy-start.10) | copy-done | bytes 3932184
  126.0 2.9 %shard_map.95 = bf16[384,128]{1,0:T(8,128)(2,1)S(1)} custom-call(s32[64]{0:T(128)S(1)} %broadcast_multiply_fusion.offsets, s32[3]{0:T(128)S(1)} %pad_add_fusion.1.where, bf16[384,5120]{1,0:T(8,128)(2,1)S(1)} %copy-done.10, f32[1,128]{1,0:T(1,128)S(1)} %bitcast.59, f32[384,128]{1,0:T(8,128)S(1)} %get-tuple-element.64.cosine, ...), custom_call_target="tpu_custom_call" | custom-call | flops 2000000000 | bytes 4194304 | tf_op jit(solution)/shard_map/pallas_call | solution.py:347
  129.0 3.6 %collective-permute-start.6 = (bf16[384,128]{1,0:T(8,128)(2,1)S(1)}, bf16[384,128]{1,0:T(8,128)(2,1)S(1)}, u32[]{:S(2)}, u32[]{:S(2)}) collective-permute-start(bf16[384,128]{1,0:T(8,128)(2,1)S(1)} %shard_map.95), channel_id=1, source_target_pairs={{0,64},{16,80},{32,96},{48,112},{64,0},{80,16},{96,32},{112,48},{1... | collective-permute-start | bytes 294920 | tf_op jit(solution)/shard_map/ppermute | solution.py:244
  137.7 7.8 %collective-permute-done.6 = bf16[384,128]{1,0:T(8,128)(2,1)S(1)} collective-permute-done((bf16[384,128]{1,0:T(8,128)(2,1)S(1)}, bf16[384,128]{1,0:T(8,128)(2,1)S(1)}, u32[]{:S(2)}, u32[]{:S(2)}) %collective-permute-start.6) | collective-permute-done | bytes 98336 | tf_op jit(solution)/shard_map/ppermute | solution.py:244
  147.5 8.7 %collective-permute-done.7 = bf16[2,384,128]{2,1,0:T(8,128)(2,1)S(1)} collective-permute-done((bf16[2,384,128]{2,1,0:T(8,128)(2,1)S(1)}, bf16[2,384,128]{2,1,0:T(8,128)(2,1)S(1)}, u32[]{:S(2)}, u32[]{:S(2)}) %collective-permute-start.7) | collective-permute-done | bytes 196640 | tf_op jit(solution)/shard_map/ppermute | solution.py:244
  158.1 2.1 copy-done.11
  160.2 2.4 %shard_map.96 = bf16[2,2,192,128]{3,2,1,0:T(8,128)(2,1)S(1)} custom-call(s32[64]{0:T(128)S(1)} %broadcast_multiply_fusion.offsets, s32[3]{0:T(128)S(1)} %pad_add_fusion.1.where, bf16[384,5120]{1,0:T(8,128)(2,1)S(1)} %copy-done.11, f32[1,128]{1,0:T(1,128)S(1)} %bitcast.60, f32[384,128]{1,0:T(8,128)S(1)} %copy-done.2, f32[384,128]{1,0:T(8,128)S(1)} %copy-done.4, ...), custom_call_target="tpu_custom_call" | custom-call | flops 4000000000 | bytes 4194304 | tf_op jit(solution)/shard_map/pallas_call | solution.py:371
  165.3 2.4 %collective-permute-start.8 = (bf16[4,384,128]{2,1,0:T(8,128)(2,1)S(1)}, bf16[4,384,128]{2,1,0:T(8,128)(2,1)S(1)}, u32[]{:S(2)}, u32[]{:S(2)}) collective-permute-start(bf16[4,384,128]{2,1,0:T(8,128)(2,1)S(1)} %pad_maximum_fusion.4.refs_0_), channel_id=1, source_target_pairs={{0,8},{8,0},{1,9},{9,1},{2,10},{10,2},{3,11},{11,3},{4,12},{12,4},... | collective-permute-start | bytes 1179656 | tf_op jit(solution)/shard_map/ppermute | solution.py:388
  170.6 4.9 %collective-permute-done.12.refs_1_ = bf16[4,384,128]{2,1,0:T(8,128)(2,1)S(1)} collective-permute-done((bf16[4,384,128]{2,1,0:T(8,128)(2,1)S(1)}, bf16[4,384,128]{2,1,0:T(8,128)(2,1)S(1)}, u32[]{:S(2)}, u32[]{:S(2)}) %collective-permute-start.12) | collective-permute-done | bytes 393248 | tf_op jit(solution)/shard_map/ppermute | solution.py:244
  175.4 3.2 %collective-permute-start.13 = (bf16[4,384,128]{2,1,0:T(8,128)(2,1)S(1)}, bf16[4,384,128]{2,1,0:T(8,128)(2,1)S(1)}, u32[]{:S(2)}, u32[]{:S(2)}) collective-permute-start(bf16[4,384,128]{2,1,0:T(8,128)(2,1)S(1)} %collective-permute-done.12.refs_1_), channel_id=1, source_target_pairs={{0,8},{8,0},{1,9},{9,1},{2,10},{10,2},{3,11},{11,3},{4,12},{12,4},... | collective-permute-start | bytes 1179656 | tf_op jit(solution)/shard_map/ppermute | solution.py:388
  182.1 5.2 %collective-permute-done.10.near = bf16[768,128]{1,0:T(8,128)(2,1)S(1)} collective-permute-done((bf16[768,128]{1,0:T(8,128)(2,1)S(1)}, bf16[768,128]{1,0:T(8,128)(2,1)S(1)}, u32[]{:S(2)}, u32[]{:S(2)}) %collective-permute-start.10) | collective-permute-done | bytes 196640 | tf_op jit(solution)/shard_map/ppermute | solution.py:393
  187.3 3.0 %collective-permute-done.11.far = bf16[768,128]{1,0:T(8,128)(2,1)S(1)} collective-permute-done((bf16[768,128]{1,0:T(8,128)(2,1)S(1)}, bf16[768,128]{1,0:T(8,128)(2,1)S(1)}, u32[]{:S(2)}, u32[]{:S(2)}) %collective-permute-start.11) | collective-permute-done | bytes 196640 | tf_op jit(solution)/shard_map/ppermute | solution.py:394
  190.3 5.0 %shard_map.97 = (bf16[816,128]{1,0:T(8,128)(2,1)S(1)}, bf16[816,128]{1,0:T(8,128)(2,1)S(1)}, bf16[3072,128]{1,0:T(8,128)(2,1)S(1)}, bf16[3072,256]{1,0:T(8,128)(2,1)S(1)}) custom-call(s32[12]{0:T(128)S(1)} %stack.101.where, s32[3,192,1]{2,1,0:T(8,128)S(1)} %broadcast_subtract_fusion.begins, bf16[768,128]{1,0:T(8,128)(2,1)S(1)} %collective-permute-done.10.near, ...), custom_call_target="tpu_custom_call" | custom-call | flops 10000000000 | bytes 4194304 | tf_op jit(solution)/shard_map/pallas_call | solution.py:397
  195.3 6.9 %collective-permute-start.14 = (bf16[816,128]{1,0:T(8,128)(2,1)S(1)}, bf16[816,128]{1,0:T(8,128)(2,1)S(1)}, u32[]{:S(2)}, u32[]{:S(2)}) collective-permute-start(bf16[816,128]{1,0:T(8,128)(2,1)S(1)} %get-tuple-element.45), channel_id=1, source_target_pairs={{0,128},{128,256},{256,384},{1,129},{129,257},{257,385},{2,130},{1... | collective-permute-start | bytes 626696 | tf_op jit(solution)/shard_map/ppermute | solution.py:406
  203.5 2.5 %shard_map.98 = (f32[768,128]{1,0:T(8,128)S(1)}, f32[768,1]{1,0:T(8,128)S(1)}) custom-call(s32[12]{0:T(128)S(1)} %stack.101.where, s32[3,192,1]{2,1,0:T(8,128)S(1)} %broadcast_subtract_fusion.begins, bf16[768,128]{1,0:T(8,128)(2,1)S(1)} %bitcast.57, bf16[3072,128]{1,0:T(8,128)(2,1)S(1)} %get-tuple-element.41.keys, bf16[3072,256]{1,0:T(8,128)(2,1)S(1)} %get-tuple-element.42.values), custom_call_target="tpu_custom_call" | custom-call | flops 10000000000 | bytes 4194304 | tf_op jit(solution)/shard_map/pallas_call | solution.py:408
  206.0 4.3 %collective-permute-done.15.r2 = bf16[816,128]{1,0:T(8,128)(2,1)S(1)} collective-permute-done((bf16[816,128]{1,0:T(8,128)(2,1)S(1)}, bf16[816,128]{1,0:T(8,128)(2,1)S(1)}, u32[]{:S(2)}, u32[]{:S(2)}) %collective-permute-start.15) | collective-permute-done | bytes 208928 | tf_op jit(solution)/shard_map/ppermute | solution.py:407
  210.3 2.1 shard_map.99
  (99 shorter events, 33.3 us)
Async XLA Ops:
  0.6 13.8 %copy-start.12 = (bf16[192,640]{1,0:T(8,128)(2,1)S(1)}, bf16[192,640]{1,0:T(8,128)(2,1)}, u32[]{:S(2)}) copy-start(bf16[192,640]{1,0:T(8,128)(2,1)} %param.7) | copy-start | bytes 737284
  0.6 41.6 %copy-start.14 = (s32[64]{0:T(128)S(1)}, s32[64]{0:T(128)}, u32[]{:S(2)}) copy-start(s32[64]{0:T(128)} %param.13) | copy-start | bytes 772
  11.0 27.3 %collective-permute-start = (bf16[1,176,384]{2,1,0:T(8,128)(2,1)S(1)}, bf16[1,176,384]{2,1,0:T(8,128)(2,1)S(1)}, u32[]{:S(2)}, u32[]{:S(2)}) collective-permute-start(bf16[1,176,384]{2,1,0:T(8,128)(2,1)S(1)} %fusion.4), channel_id=1, source_target_pairs={{0,64},{16,80},{32,96},{48,112},{64,0},{80,16},{96,32},{112,48},{1... | collective-permute-start | bytes 405512 | tf_op jit(solution)/shard_map/ppermute | solution.py:244
  14.4 23.8 %collective-permute-start.1 = (bf16[192,640]{1,0:T(8,128)(2,1)S(1)}, bf16[192,640]{1,0:T(8,128)(2,1)S(1)}, u32[]{:S(2)}, u32[]{:S(2)}) collective-permute-start(bf16[192,640]{1,0:T(8,128)(2,1)S(1)} %copy-done.12), channel_id=1, source_target_pairs={{0,1},{1,0},{2,3},{3,2},{4,5},{5,4},{6,7},{7,6},{8,9},{9,8},{10,11... | collective-permute-start | bytes 737288 | tf_op jit(solution)/shard_map/ppermute | solution.py:279
  38.3 34.7 %collective-permute-start.3 = (bf16[4,192,640]{2,1,0:T(8,128)(2,1)S(1)}, bf16[4,192,640]{2,1,0:T(8,128)(2,1)S(1)}, u32[]{:S(2)}, u32[]{:S(2)}) collective-permute-start(bf16[4,192,640]{2,1,0:T(8,128)(2,1)S(1)} %bitcast.50), channel_id=1, source_target_pairs={{0,8},{8,0},{1,9},{9,1},{2,10},{10,2},{3,11},{11,3},{4,12},{12,4},... | collective-permute-start | bytes 2949128 | tf_op jit(solution)/shard_map/ppermute | solution.py:285
  42.3 30.6 %collective-permute-start.2 = (bf16[2,176,384]{2,1,0:T(8,128)(2,1)S(1)}, bf16[2,176,384]{2,1,0:T(8,128)(2,1)S(1)}, u32[]{:S(2)}, u32[]{:S(2)}) collective-permute-start(bf16[2,176,384]{2,1,0:T(8,128)(2,1)S(1)} %pad_maximum_fusion.5), channel_id=1, source_target_pairs={{0,32},{16,48},{32,0},{48,16},{64,96},{80,112},{96,64},{112,80},{1... | collective-permute-start | bytes 811016 | tf_op jit(solution)/shard_map/ppermute | solution.py:244
  72.9 1.0 copy-start.5
  73.9 34.8 %collective-permute-start.4 = (bf16[4,192,640]{2,1,0:T(8,128)(2,1)S(1)}, bf16[4,192,640]{2,1,0:T(8,128)(2,1)}, u32[]{:S(2)}, u32[]{:S(2)}) collective-permute-start(bf16[4,192,640]{2,1,0:T(8,128)(2,1)S(1)} %bitcast.52), channel_id=1, source_target_pairs={{0,8},{8,0},{1,9},{9,1},{2,10},{10,2},{3,11},{11,3},{4,12},{12,4},... | collective-permute-start | bytes 2949128 | tf_op jit(solution)/shard_map/ppermute | solution.py:294
  78.7 18.7 %collective-permute-start.5 = (bf16[4,176,384]{2,1,0:T(8,128)(2,1)}, bf16[4,176,384]{2,1,0:T(8,128)(2,1)}, u32[]{:S(2)}, u32[]{:S(2)}) collective-permute-start(bf16[4,176,384]{2,1,0:T(8,128)(2,1)} %pad_maximum_fusion.3), channel_id=1, source_target_pairs={{0,16},{16,0},{32,48},{48,32},{64,80},{80,64},{96,112},{112,96},{1... | collective-permute-start | bytes 1622024 | tf_op jit(solution)/shard_map/ppermute | solution.py:244
  86.4 15.0 %all-to-all-start = ((bf16[4,4,176,128]{3,2,1,0:T(8,128)(2,1)}), bf16[4,4,176,128]{3,2,1,0:T(8,128)(2,1)S(1)}, u32[]{:S(2)}, u32[]{:S(2)}) async-start(bf16[4,4,176,128]{3,2,1,0:T(8,128)(2,1)} %broadcast_in_dim.22), calls=%async_computation | async-start | bytes 1441792 | tf_op jit(solution)/shard_map/all_to_all | solution.py:295
  90.3 17.3 %copy-start.13 = (bf16[5120]{0:T(1024)(128)(2,1)S(1)}, bf16[5120]{0:T(1024)(128)(2,1)}, u32[]{:S(2)}) copy-start(bf16[5120]{0:T(1024)(128)(2,1)} %param.8) | copy-start | bytes 30724
  103.3 14.1 %all-to-all-start.1 = ((bf16[4,4,176,128]{3,2,1,0:T(8,128)(2,1)}), bf16[4,4,176,128]{3,2,1,0:T(8,128)(2,1)}, u32[]{:S(2)}, u32[]{:S(2)}) async-start(bf16[4,4,176,128]{3,2,1,0:T(8,128)(2,1)} %broadcast_in_dim.25), calls=%async_computation.1 | async-start | bytes 1441792 | tf_op jit(solution)/shard_map/all_to_all | solution.py:298
  108.7 1.8 copy-start.6
  114.4 1.9 copy-start.9
  119.0 37.3 %all-to-all-start.2 = ((bf16[4,8,160,256]{3,2,1,0:T(8,128)(2,1)}), bf16[4,8,160,256]{3,2,1,0:T(8,128)(2,1)S(1)}, u32[]{:S(2)}, u32[]{:S(2)}) async-start(bf16[4,8,160,256]{3,2,1,0:T(8,128)(2,1)} %broadcast_in_dim.23), calls=%async_computation.2 | async-start | bytes 5242880 | tf_op jit(solution)/shard_map/all_to_all | solution.py:302
  122.7 1.1 copy-start.7
  123.7 5.2 %copy-start.1 = (f32[384,128]{1,0:T(8,128)}, f32[384,128]{1,0:T(8,128)S(1)}, u32[]{:S(2)}) copy-start(f32[384,128]{1,0:T(8,128)S(1)} %get-tuple-element.64.cosine) | copy-start | bytes 589828
  123.7 5.2 %copy-start.3 = (f32[384,128]{1,0:T(8,128)}, f32[384,128]{1,0:T(8,128)S(1)}, u32[]{:S(2)}) copy-start(f32[384,128]{1,0:T(8,128)S(1)} %get-tuple-element.65.sine) | copy-start | bytes 589828
  123.8 2.2 %copy-start.10 = (bf16[384,5120]{1,0:T(8,128)(2,1)S(1)}, bf16[384,5120]{1,0:T(8,128)(2,1)}, u32[]{:S(2)}) copy-start(bf16[384,5120]{1,0:T(8,128)(2,1)} %copy-done.9) | copy-start | bytes 11796484
  129.0 27.3 %copy-start.8 = (f32[128]{0:T(128)S(1)}, f32[128]{0:T(128)}, u32[]{:S(2)}) copy-start(f32[128]{0:T(128)} %param.9) | copy-start | bytes 1540
  129.0 16.6 %collective-permute-start.6 = (bf16[384,128]{1,0:T(8,128)(2,1)S(1)}, bf16[384,128]{1,0:T(8,128)(2,1)S(1)}, u32[]{:S(2)}, u32[]{:S(2)}) collective-permute-start(bf16[384,128]{1,0:T(8,128)(2,1)S(1)} %shard_map.95), channel_id=1, source_target_pairs={{0,64},{16,80},{32,96},{48,112},{64,0},{80,16},{96,32},{112,48},{1... | collective-permute-start | bytes 294920 | tf_op jit(solution)/shard_map/ppermute | solution.py:244
  145.5 10.7 %collective-permute-start.7 = (bf16[2,384,128]{2,1,0:T(8,128)(2,1)S(1)}, bf16[2,384,128]{2,1,0:T(8,128)(2,1)S(1)}, u32[]{:S(2)}, u32[]{:S(2)}) collective-permute-start(bf16[2,384,128]{2,1,0:T(8,128)(2,1)S(1)} %pad_maximum_fusion.8), channel_id=1, source_target_pairs={{0,32},{16,48},{32,0},{48,16},{64,96},{80,112},{96,64},{112,80},{1... | collective-permute-start | bytes 589832 | tf_op jit(solution)/shard_map/ppermute | solution.py:244
  156.3 0.9 copy-start.2
  158.1 2.1 copy-start.11
  163.4 12.1 %collective-permute-start.12 = (bf16[4,384,128]{2,1,0:T(8,128)(2,1)S(1)}, bf16[4,384,128]{2,1,0:T(8,128)(2,1)S(1)}, u32[]{:S(2)}, u32[]{:S(2)}) collective-permute-start(bf16[4,384,128]{2,1,0:T(8,128)(2,1)S(1)} %pad_maximum_fusion.4.refs_0_), channel_id=1, source_target_pairs={{0,16},{16,0},{32,48},{48,32},{64,80},{80,64},{96,112},{112,96},{1... | collective-permute-start | bytes 1179656 | tf_op jit(solution)/shard_map/ppermute | solution.py:244
  165.3 16.1 %collective-permute-start.8 = (bf16[4,384,128]{2,1,0:T(8,128)(2,1)S(1)}, bf16[4,384,128]{2,1,0:T(8,128)(2,1)S(1)}, u32[]{:S(2)}, u32[]{:S(2)}) collective-permute-start(bf16[4,384,128]{2,1,0:T(8,128)(2,1)S(1)} %pad_maximum_fusion.4.refs_0_), channel_id=1, source_target_pairs={{0,8},{8,0},{1,9},{9,1},{2,10},{10,2},{3,11},{11,3},{4,12},{12,4},... | collective-permute-start | bytes 1179656 | tf_op jit(solution)/shard_map/ppermute | solution.py:388
  168.6 10.0 %collective-permute-start.9 = (bf16[2,192,128]{2,1,0:T(8,128)(2,1)S(1)}, bf16[2,192,128]{2,1,0:T(8,128)(2,1)S(1)}, u32[]{:S(2)}, u32[]{:S(2)}) collective-permute-start(bf16[2,192,128]{2,1,0:T(8,128)(2,1)S(1)} %get-tuple-element.50), channel_id=1, source_target_pairs={{0,8},{8,0},{1,9},{9,1},{2,10},{10,2},{3,11},{11,3},{4,12},{12,4},... | collective-permute-start | bytes 294920 | tf_op jit(solution)/shard_map/ppermute | solution.py:391
  175.4 14.9 %collective-permute-start.13 = (bf16[4,384,128]{2,1,0:T(8,128)(2,1)S(1)}, bf16[4,384,128]{2,1,0:T(8,128)(2,1)S(1)}, u32[]{:S(2)}, u32[]{:S(2)}) collective-permute-start(bf16[4,384,128]{2,1,0:T(8,128)(2,1)S(1)} %collective-permute-done.12.refs_1_), channel_id=1, source_target_pairs={{0,8},{8,0},{1,9},{9,1},{2,10},{10,2},{3,11},{11,3},{4,12},{12,4},... | collective-permute-start | bytes 1179656 | tf_op jit(solution)/shard_map/ppermute | solution.py:388
  178.7 8.6 %collective-permute-start.10 = (bf16[768,128]{1,0:T(8,128)(2,1)S(1)}, bf16[768,128]{1,0:T(8,128)(2,1)S(1)}, u32[]{:S(2)}, u32[]{:S(2)}) collective-permute-start(bf16[768,128]{1,0:T(8,128)(2,1)S(1)} %bitcast.55), channel_id=1, source_target_pairs={{128,0},{256,128},{384,256},{129,1},{257,129},{385,257},{130,2},{2... | collective-permute-start | bytes 589832 | tf_op jit(solution)/shard_map/ppermute | solution.py:393
  180.0 10.3 %collective-permute-start.11 = (bf16[768,128]{1,0:T(8,128)(2,1)S(1)}, bf16[768,128]{1,0:T(8,128)(2,1)S(1)}, u32[]{:S(2)}, u32[]{:S(2)}) collective-permute-start(bf16[768,128]{1,0:T(8,128)(2,1)S(1)} %bitcast.56), channel_id=1, source_target_pairs={{256,0},{384,128},{257,1},{385,129},{258,2},{386,130},{259,3},{387... | collective-permute-start | bytes 589832 | tf_op jit(solution)/shard_map/ppermute | solution.py:394
  195.3 10.7 %collective-permute-start.14 = (bf16[816,128]{1,0:T(8,128)(2,1)S(1)}, bf16[816,128]{1,0:T(8,128)(2,1)S(1)}, u32[]{:S(2)}, u32[]{:S(2)}) collective-permute-start(bf16[816,128]{1,0:T(8,128)(2,1)S(1)} %get-tuple-element.45), channel_id=1, source_target_pairs={{0,128},{128,256},{256,384},{1,129},{129,257},{257,385},{2,130},{1... | collective-permute-start | bytes 626696 | tf_op jit(solution)/shard_map/ppermute | solution.py:406
  202.2 8.2 %collective-permute-start.15 = (bf16[816,128]{1,0:T(8,128)(2,1)S(1)}, bf16[816,128]{1,0:T(8,128)(2,1)S(1)}, u32[]{:S(2)}, u32[]{:S(2)}) collective-permute-start(bf16[816,128]{1,0:T(8,128)(2,1)S(1)} %get-tuple-element.46), channel_id=1, source_target_pairs={{0,256},{128,384},{1,257},{129,385},{2,258},{130,386},{3,259},{131... | collective-permute-start | bytes 626696 | tf_op jit(solution)/shard_map/ppermute | solution.py:407
  (2 other events, 1.6 us)

commit v12 on v10

--- a/solution.py
+++ b/solution.py
@@ -363,11 +363,6 @@
     mine0 = jnp.stack([pair, across(pair, 4)])
     mine0, ranges, begins = lax.optimization_barrier((mine0, ranges, begins))
     mine0 = jnp.concatenate([mine0, across(mine0, 2)], axis=0)
-    mine0, query_blocks = lax.optimization_barrier((mine0, query_blocks))
-    mine1 = across(mine0, 1)
-    mine = [mine0, mine1]
-    other = [lax.ppermute(v, "c", swap) for v in mine]
-
     (query,) = call(
         functools.partial(query_kernel, panel),
         [jax.ShapeDtypeStruct((2, 2, rows, 128), bf16)],
@@ -382,10 +377,14 @@
         n_hbm=1,
     )(offsets, spot, normed, query_gain[None, :], cosine, sine, query_blocks)
 
+    mine0, query = lax.optimization_barrier((mine0, query))
+    mine1 = across(mine0, 1)
     own_query = lax.dynamic_index_in_dim(query, c, 0, keepdims=False)
     sent_query = lax.dynamic_index_in_dim(query, 1 - c, 0, keepdims=False)
     q0 = jnp.concatenate([own_query, lax.ppermute(sent_query, "c", swap)], axis=0)
     q0 = q0.reshape(4 * rows, 128)
+    mine = [mine0, mine1]
+    other = [lax.ppermute(v, "c", swap) for v in (after(mine0, q0), mine1)]
     q1 = lax.ppermute(q0, "x", [(i, i - 1) for i in range(1, nx)])
     q2 = lax.ppermute(q0, "x", [(i, i - 2) for i in range(2, nx)])
 

time: 207 us -> 206 us (level)
  starting transfers between devices: 81.7 us -> 85.7 us
  Pallas kernels: 18.6 us -> 14.7 us
    ppermute x1, starting transfers between devices: 1.92 us -> 8.35 us  [body(): lax.ppermute(sent_query, 'c', swap)]
    ppermute x2, starting transfers between devices: 11.6 us -> 6.73 us  [body(): other = [lax.ppermute(v, 'c', swap) for v in (after(mine0, q0), mine1)]]
    pallas_call x1, Pallas kernels: 5.46 us -> 1.6 us  [body(): call(remote_kernel, [jax.ShapeDtypeStruct((4 * rows + 48, 128), bf16)] *...]
    ppermute x6, waiting for transfers between devices: 19.5 us -> 17 us  [across(): return lax.ppermute(v, 'z', [(i, i ^ bit) for i in range(8)])]
  transfers between devices with their start and end apart: 18 -> 18, of which waited for: 9 -> 9; matrix products, arithmetic and copies ran while one was open for 6% -> 5% of each run, Pallas kernels for 5% -> 4%
where the time goes in v12:
time: 206 us; the launch traced here: 204 us
  starting transfers between devices  85.7 us (42%)
  waiting for transfers between devices  38 us (18%)
  blocking collectives  37.6 us (18%)
  local copies, waits for them, and re-layouts  17.5 us (8%)
  Pallas kernels  14.7 us (7%)
  other arithmetic  7.13 us (3%)
  between operations  3.09 us (2%)
    ppermute x6, starting transfers between devices, across(): return lax.ppermute(v, 'z', [(i, i ^ bit) for i in range(8)])  31.2 us
    ppermute x6, waiting for transfers between devices, across(): return lax.ppermute(v, 'z', [(i, i ^ bit) for i in range(8)])  17 us
    all_gather x1, blocking collectives, body(): own_far = lax.all_gather(far, 'y', axis=0)  15.9 us
    all_gather x1, blocking collectives, body(): own_near = lax.all_gather(hidden, 'y', axis=0)  13.2 us
    unnamed x44, local copies, waits for them, and re-layouts  11.2 us
    ppermute x1, starting transfers between devices, body(): far = lax.ppermute(hidden, 'w', swap)  10.6 us
    ppermute x1, starting transfers between devices, body(): r1 = lax.ppermute(r1, 'x', [(i, i + 1) for i in range(nx - 1)])  8.65 us
    all_gather x1, blocking collectives, body(): lax.all_gather(jnp.concatenate([weight_store, riders], axis=0), 'c', axis=0)  8.53 us
  transfers between devices with their start and end apart: 18, of which 9 were waited for; matrix products, arithmetic and copies ran while one was open for 5% of the time, Pallas kernels for 4%

profile of v12, /device:TPU:1, one launch (start us, length us, event | category | flops | bytes accessed | tf_op | source)
XLA Modules:
  0.0 203.8 jit_solution(8301457467612750728)
XLA Ops:
  2.3 8.5 %all-gather = bf16[192,768]{1,0:T(8,128)(2,1)S(1)} all-gather(bf16[96,768]{1,0:T(8,128)(2,1)S(1)} %fusion.2), channel_id=2, replica_groups=mesh['x'=4,'z'=8,'c'=2,'y'=4,'w'=2] {'c'}, dimensions={0}, use_global_device_ids=true | all-gather | bytes 442368 | tf_op jit(solution)/shard_map/all_gather | solution.py:261
  11.0 3.4 %collective-permute-start = (bf16[1,176,384]{2,1,0:T(8,128)(2,1)S(1)}, bf16[1,176,384]{2,1,0:T(8,128)(2,1)S(1)}, u32[]{:S(2)}, u32[]{:S(2)}) collective-permute-start(bf16[1,176,384]{2,1,0:T(8,128)(2,1)S(1)} %fusion.4), channel_id=1, source_target_pairs={{0,64},{16,80},{32,96},{48,112},{64,0},{80,16},{96,32},{112,48},{1... | collective-permute-start | bytes 405512 | tf_op jit(solution)/shard_map/ppermute | solution.py:242
  14.4 10.6 %collective-permute-start.1 = (bf16[192,640]{1,0:T(8,128)(2,1)S(1)}, bf16[192,640]{1,0:T(8,128)(2,1)S(1)}, u32[]{:S(2)}, u32[]{:S(2)}) collective-permute-start(bf16[192,640]{1,0:T(8,128)(2,1)S(1)} %copy-done.18), channel_id=1, source_target_pairs={{0,1},{1,0},{2,3},{3,2},{4,5},{5,4},{6,7},{7,6},{8,9},{9,8},{10,11... | collective-permute-start | bytes 737288 | tf_op jit(solution)/shard_map/ppermute | solution.py:277
  25.1 13.2 %all-gather.1 = bf16[768,640]{1,0:T(8,128)(2,1)S(1)} all-gather(bf16[192,640]{1,0:T(8,128)(2,1)S(1)} %copy-done.18), channel_id=3, replica_groups=mesh['x'=4,'z'=8,'c'=2,'y'=4,'w'=2] {'y'}, dimensions={0}, use_global_device_ids=true | all-gather | bytes 1228800 | tf_op jit(solution)/shard_map/all_gather | solution.py:278
  38.3 3.9 %collective-permute-start.3 = (bf16[4,192,640]{2,1,0:T(8,128)(2,1)S(1)}, bf16[4,192,640]{2,1,0:T(8,128)(2,1)S(1)}, u32[]{:S(2)}, u32[]{:S(2)}) collective-permute-start(bf16[4,192,640]{2,1,0:T(8,128)(2,1)S(1)} %bitcast.50), channel_id=1, source_target_pairs={{0,8},{8,0},{1,9},{9,1},{2,10},{10,2},{3,11},{11,3},{4,12},{12,4},... | collective-permute-start | bytes 2949128 | tf_op jit(solution)/shard_map/ppermute | solution.py:283
  42.2 14.7 %collective-permute-start.2 = (bf16[2,176,384]{2,1,0:T(8,128)(2,1)S(1)}, bf16[2,176,384]{2,1,0:T(8,128)(2,1)S(1)}, u32[]{:S(2)}, u32[]{:S(2)}) collective-permute-start(bf16[2,176,384]{2,1,0:T(8,128)(2,1)S(1)} %pad_maximum_fusion.4), channel_id=1, source_target_pairs={{0,32},{16,48},{32,0},{48,16},{64,96},{80,112},{96,64},{112,80},{1... | collective-permute-start | bytes 811016 | tf_op jit(solution)/shard_map/ppermute | solution.py:242
  56.9 15.9 %all-gather.2 = bf16[768,640]{1,0:T(8,128)(2,1)S(1)} all-gather(bf16[192,640]{1,0:T(8,128)(2,1)S(1)} %collective-permute-done.1), channel_id=4, replica_groups=mesh['x'=4,'z'=8,'c'=2,'y'=4,'w'=2] {'y'}, dimensions={0}, use_global_device_ids=true | all-gather | bytes 1228800 | tf_op jit(solution)/shard_map/all_gather | solution.py:284
  73.9 5.6 %collective-permute-start.5 = (bf16[4,176,384]{2,1,0:T(8,128)(2,1)S(1)}, bf16[4,176,384]{2,1,0:T(8,128)(2,1)S(1)}, u32[]{:S(2)}, u32[]{:S(2)}) collective-permute-start(bf16[4,176,384]{2,1,0:T(8,128)(2,1)S(1)} %pad_maximum_fusion.1), channel_id=1, source_target_pairs={{0,16},{16,0},{32,48},{48,32},{64,80},{80,64},{96,112},{112,96},{1... | collective-permute-start | bytes 1622024 | tf_op jit(solution)/shard_map/ppermute | solution.py:242
  79.6 4.3 %collective-permute-start.4 = (bf16[4,192,640]{2,1,0:T(8,128)(2,1)S(1)}, bf16[4,192,640]{2,1,0:T(8,128)(2,1)}, u32[]{:S(2)}, u32[]{:S(2)}) collective-permute-start(bf16[4,192,640]{2,1,0:T(8,128)(2,1)S(1)} %bitcast.52), channel_id=1, source_target_pairs={{0,8},{8,0},{1,9},{9,1},{2,10},{10,2},{3,11},{11,3},{4,12},{12,4},... | collective-permute-start | bytes 2949128 | tf_op jit(solution)/shard_map/ppermute | solution.py:289
  83.9 6.1 %collective-permute-done.5 = bf16[4,176,384]{2,1,0:T(8,128)(2,1)S(1)} collective-permute-done((bf16[4,176,384]{2,1,0:T(8,128)(2,1)S(1)}, bf16[4,176,384]{2,1,0:T(8,128)(2,1)S(1)}, u32[]{:S(2)}, u32[]{:S(2)}) %collective-permute-start.5) | collective-permute-done | bytes 540704 | tf_op jit(solution)/shard_map/ppermute | solution.py:242
  92.2 4.3 %all-to-all-start = ((bf16[4,8,176,128]{3,2,1,0:T(8,128)(2,1)}), bf16[4,8,176,128]{3,2,1,0:T(8,128)(2,1)S(1)}, u32[]{:S(2)}, u32[]{:S(2)}) async-start(bf16[4,8,176,128]{3,2,1,0:T(8,128)(2,1)} %broadcast_in_dim.22), calls=%async_computation | async-start | bytes 2883584 | tf_op jit(solution)/shard_map/all_to_all | solution.py:295
  100.0 3.8 %shard_map.94.source = bf16[384,5120]{1,0:T(8,128)(2,1)S(1)} custom-call(s32[3]{0:T(128)S(1)} %pad_add_fusion.1.where, f32[1,5120]{1,0:T(1,128)S(1)} %bitcast.58, bf16[4,192,640]{2,1,0:T(8,128)(2,1)S(1)} %bitcast.51, bf16[4,192,640]{2,1,0:T(8,128)(2,1)S(1)} %bitcast.53, bf16[4,192,640]{2,1,0:T(8,128)(2,1)S(1)} %copy-done.7, ...), custom_call_target="tpu_custom_call" | custom-call | flops 4000000000 | bytes 4194304 | tf_op jit(solution)/shard_map/pallas_call | solution.py:302
  105.7 7.2 %all-to-all-done.blocks = bf16[4,8,176,128]{3,2,1,0:T(8,128)(2,1)S(1)} async-done(((bf16[4,8,176,128]{3,2,1,0:T(8,128)(2,1)}), bf16[4,8,176,128]{3,2,1,0:T(8,128)(2,1)S(1)}, u32[]{:S(2)}, u32[]{:S(2)}) %all-to-all-start) | async-done | bytes 1441824 | tf_op jit(solution)/shard_map/all_to_all | solution.py:295
  114.8 3.7 %all-to-all-start.1 = ((bf16[4,8,160,256]{3,2,1,0:T(8,128)(2,1)}), bf16[4,8,160,256]{3,2,1,0:T(8,128)(2,1)S(1)}, u32[]{:S(2)}, u32[]{:S(2)}) async-start(bf16[4,8,160,256]{3,2,1,0:T(8,128)(2,1)} %broadcast_in_dim.20), calls=%async_computation.1 | async-start | bytes 5242880 | tf_op jit(solution)/shard_map/all_to_all | solution.py:298
  119.8 2.1 %copy-done.11 = bf16[384,5120]{1,0:T(8,128)(2,1)S(1)} copy-done((bf16[384,5120]{1,0:T(8,128)(2,1)S(1)}, bf16[384,5120]{1,0:T(8,128)(2,1)}, u32[]{:S(2)}) %copy-start.11) | copy-done | bytes 3932184
  121.9 2.3 %shard_map.95 = bf16[384,128]{1,0:T(8,128)(2,1)S(1)} custom-call(s32[64]{0:T(128)S(1)} %broadcast_multiply_fusion.offsets, s32[3]{0:T(128)S(1)} %pad_add_fusion.1.where, bf16[384,5120]{1,0:T(8,128)(2,1)S(1)} %copy-done.11, f32[1,128]{1,0:T(1,128)S(1)} %bitcast.59, f32[384,128]{1,0:T(8,128)S(1)} %get-tuple-element.62.cosine, ...), custom_call_target="tpu_custom_call" | custom-call | flops 2000000000 | bytes 4194304 | tf_op jit(solution)/shard_map/pallas_call | solution.py:342
  124.3 3.1 %collective-permute-start.6 = (bf16[384,128]{1,0:T(8,128)(2,1)S(1)}, bf16[384,128]{1,0:T(8,128)(2,1)S(1)}, u32[]{:S(2)}, u32[]{:S(2)}) collective-permute-start(bf16[384,128]{1,0:T(8,128)(2,1)S(1)} %shard_map.95), channel_id=1, source_target_pairs={{0,64},{16,80},{32,96},{48,112},{64,0},{80,16},{96,32},{112,48},{1... | collective-permute-start | bytes 294920 | tf_op jit(solution)/shard_map/ppermute | solution.py:242
  130.4 2.0 stack.101.where
  132.4 4.3 %collective-permute-done.6 = bf16[384,128]{1,0:T(8,128)(2,1)S(1)} collective-permute-done((bf16[384,128]{1,0:T(8,128)(2,1)S(1)}, bf16[384,128]{1,0:T(8,128)(2,1)S(1)}, u32[]{:S(2)}, u32[]{:S(2)}) %collective-permute-start.6) | collective-permute-done | bytes 98336 | tf_op jit(solution)/shard_map/ppermute | solution.py:242
  138.7 6.6 %collective-permute-done.7 = bf16[2,384,128]{2,1,0:T(8,128)(2,1)} collective-permute-done((bf16[2,384,128]{2,1,0:T(8,128)(2,1)S(1)}, bf16[2,384,128]{2,1,0:T(8,128)(2,1)}, u32[]{:S(2)}, u32[]{:S(2)}) %collective-permute-start.7) | collective-permute-done | bytes 196640 | tf_op jit(solution)/shard_map/ppermute | solution.py:242
  148.4 2.1 %copy-done.12 = bf16[384,5120]{1,0:T(8,128)(2,1)S(1)} copy-done((bf16[384,5120]{1,0:T(8,128)(2,1)S(1)}, bf16[384,5120]{1,0:T(8,128)(2,1)}, u32[]{:S(2)}) %copy-start.12) | copy-done | bytes 3932184
  150.5 2.4 %shard_map.96 = bf16[2,2,192,128]{3,2,1,0:T(8,128)(2,1)S(1)} custom-call(s32[64]{0:T(128)S(1)} %broadcast_multiply_fusion.offsets, s32[3]{0:T(128)S(1)} %pad_add_fusion.1.where, bf16[384,5120]{1,0:T(8,128)(2,1)S(1)} %copy-done.12, f32[1,128]{1,0:T(1,128)S(1)} %bitcast.60, f32[384,128]{1,0:T(8,128)S(1)} %copy-done.3, f32[384,128]{1,0:T(8,128)S(1)} %copy-done.5, ...), custom_call_target="tpu_custom_call" | custom-call | flops 4000000000 | bytes 4194304 | tf_op jit(solution)/shard_map/pallas_call | solution.py:366
  152.9 2.5 %collective-permute-start.12 = (bf16[4,384,128]{2,1,0:T(8,128)(2,1)S(1)}, bf16[4,384,128]{2,1,0:T(8,128)(2,1)S(1)}, u32[]{:S(2)}, u32[]{:S(2)}) collective-permute-start(bf16[4,384,128]{2,1,0:T(8,128)(2,1)S(1)} %pad_maximum_fusion.2.refs_0_), channel_id=1, source_target_pairs={{0,16},{16,0},{32,48},{48,32},{64,80},{80,64},{96,112},{112,96},{1... | collective-permute-start | bytes 1179656 | tf_op jit(solution)/shard_map/ppermute | solution.py:242
  155.5 8.3 %collective-permute-start.8 = (bf16[2,192,128]{2,1,0:T(8,128)(2,1)S(1)}, bf16[2,192,128]{2,1,0:T(8,128)(2,1)S(1)}, u32[]{:S(2)}, u32[]{:S(2)}) collective-permute-start(bf16[2,192,128]{2,1,0:T(8,128)(2,1)S(1)} %get-tuple-element.50), channel_id=1, source_target_pairs={{0,8},{8,0},{1,9},{9,1},{2,10},{10,2},{3,11},{11,3},{4,12},{12,4},... | collective-permute-start | bytes 294920 | tf_op jit(solution)/shard_map/ppermute | solution.py:384
  164.8 2.3 %collective-permute-start.9 = (bf16[4,384,128]{2,1,0:T(8,128)(2,1)S(1)}, bf16[4,384,128]{2,1,0:T(8,128)(2,1)S(1)}, u32[]{:S(2)}, u32[]{:S(2)}) collective-permute-start(bf16[4,384,128]{2,1,0:T(8,128)(2,1)S(1)} %pad_maximum_fusion.2.refs_0_), channel_id=1, source_target_pairs={{0,8},{8,0},{1,9},{9,1},{2,10},{10,2},{3,11},{11,3},{4,12},{12,4},... | collective-permute-start | bytes 1179656 | tf_op jit(solution)/shard_map/ppermute | solution.py:387
  167.1 4.5 %collective-permute-start.13 = (bf16[4,384,128]{2,1,0:T(8,128)(2,1)S(1)}, bf16[4,384,128]{2,1,0:T(8,128)(2,1)S(1)}, u32[]{:S(2)}, u32[]{:S(2)}) collective-permute-start(bf16[4,384,128]{2,1,0:T(8,128)(2,1)S(1)} %collective-permute-done.12.refs_1_), channel_id=1, source_target_pairs={{0,8},{8,0},{1,9},{9,1},{2,10},{10,2},{3,11},{11,3},{4,12},{12,4},... | collective-permute-start | bytes 1179656 | tf_op jit(solution)/shard_map/ppermute | solution.py:387
  174.9 5.5 %collective-permute-done.10.near = bf16[768,128]{1,0:T(8,128)(2,1)S(1)} collective-permute-done((bf16[768,128]{1,0:T(8,128)(2,1)S(1)}, bf16[768,128]{1,0:T(8,128)(2,1)S(1)}, u32[]{:S(2)}, u32[]{:S(2)}) %collective-permute-start.10) | collective-permute-done | bytes 196640 | tf_op jit(solution)/shard_map/ppermute | solution.py:388
  180.4 2.9 %collective-permute-done.11.far = bf16[768,128]{1,0:T(8,128)(2,1)S(1)} collective-permute-done((bf16[768,128]{1,0:T(8,128)(2,1)S(1)}, bf16[768,128]{1,0:T(8,128)(2,1)S(1)}, u32[]{:S(2)}, u32[]{:S(2)}) %collective-permute-start.11) | collective-permute-done | bytes 196640 | tf_op jit(solution)/shard_map/ppermute | solution.py:389
  184.9 8.6 %collective-permute-start.14 = (bf16[816,128]{1,0:T(8,128)(2,1)S(1)}, bf16[816,128]{1,0:T(8,128)(2,1)S(1)}, u32[]{:S(2)}, u32[]{:S(2)}) collective-permute-start(bf16[816,128]{1,0:T(8,128)(2,1)S(1)} %get-tuple-element.43), channel_id=1, source_target_pairs={{0,128},{128,256},{256,384},{1,129},{129,257},{257,385},{2,130},{1... | collective-permute-start | bytes 626696 | tf_op jit(solution)/shard_map/ppermute | solution.py:401
  194.9 2.5 %shard_map.98 = (f32[768,128]{1,0:T(8,128)S(1)}, f32[768,1]{1,0:T(8,128)S(1)}) custom-call(s32[12]{0:T(128)S(1)} %stack.101.where, s32[3,192,1]{2,1,0:T(8,128)S(1)} %broadcast_subtract_fusion.begins, bf16[768,128]{1,0:T(8,128)(2,1)S(1)} %bitcast.57, bf16[3072,128]{1,0:T(8,128)(2,1)S(1)} %get-tuple-element.39.keys, bf16[3072,256]{1,0:T(8,128)(2,1)S(1)} %get-tuple-element.40.values), custom_call_target="tpu_custom_call" | custom-call | flops 10000000000 | bytes 4194304 | tf_op jit(solution)/shard_map/pallas_call | solution.py:403
  197.4 4.4 %collective-permute-done.15.r2 = bf16[816,128]{1,0:T(8,128)(2,1)S(1)} collective-permute-done((bf16[816,128]{1,0:T(8,128)(2,1)S(1)}, bf16[816,128]{1,0:T(8,128)(2,1)S(1)}, u32[]{:S(2)}, u32[]{:S(2)}) %collective-permute-start.15) | collective-permute-done | bytes 208928 | tf_op jit(solution)/shard_map/ppermute | solution.py:402
  201.7 2.1 %shard_map.99 = bf16[192,512]{1,0:T(8,128)(2,1)} custom-call(s32[3]{0:T(128)S(1)} %pad_add_fusion.2.where, f32[768,128]{1,0:T(8,128)S(1)} %get-tuple-element.41.o0, f32[768,1]{1,0:T(8,128)S(1)} %get-tuple-element.42.l0, bf16[816,128]{1,0:T(8,128)(2,1)S(1)} %collective-permute-done.14.r1, bf16[816,128]{1,0:T(8,128)(2,1)S(1)} %collective-permute-done.15.r2), custom_call_target="tpu_custom_call" | custom-call | bytes 4194304 | tf_op jit(solution)/shard_map/pallas_call | solution.py:415
  (106 shorter events, 26.9 us)
Async XLA Ops:
  0.6 13.8 %copy-start.18 = (bf16[192,640]{1,0:T(8,128)(2,1)S(1)}, bf16[192,640]{1,0:T(8,128)(2,1)}, u32[]{:S(2)}) copy-start(bf16[192,640]{1,0:T(8,128)(2,1)} %param.7) | copy-start | bytes 737284
  11.0 79.0 %copy-start.13 = (bf16[1,176,384]{2,1,0:T(8,128)(2,1)}, bf16[1,176,384]{2,1,0:T(8,128)(2,1)S(1)}, u32[]{:S(2)}) copy-start(bf16[1,176,384]{2,1,0:T(8,128)(2,1)S(1)} %fusion.4) | copy-start | bytes 405508
  11.0 27.3 %collective-permute-start = (bf16[1,176,384]{2,1,0:T(8,128)(2,1)S(1)}, bf16[1,176,384]{2,1,0:T(8,128)(2,1)S(1)}, u32[]{:S(2)}, u32[]{:S(2)}) collective-permute-start(bf16[1,176,384]{2,1,0:T(8,128)(2,1)S(1)} %fusion.4), channel_id=1, source_target_pairs={{0,64},{16,80},{32,96},{48,112},{64,0},{80,16},{96,32},{112,48},{1... | collective-permute-start | bytes 405512 | tf_op jit(solution)/shard_map/ppermute | solution.py:242
  14.4 23.8 %collective-permute-start.1 = (bf16[192,640]{1,0:T(8,128)(2,1)S(1)}, bf16[192,640]{1,0:T(8,128)(2,1)S(1)}, u32[]{:S(2)}, u32[]{:S(2)}) collective-permute-start(bf16[192,640]{1,0:T(8,128)(2,1)S(1)} %copy-done.18), channel_id=1, source_target_pairs={{0,1},{1,0},{2,3},{3,2},{4,5},{5,4},{6,7},{7,6},{8,9},{9,8},{10,11... | collective-permute-start | bytes 737288 | tf_op jit(solution)/shard_map/ppermute | solution.py:277
  38.3 51.7 %copy-start.15 = (bf16[1,176,384]{2,1,0:T(8,128)(2,1)}, bf16[1,176,384]{2,1,0:T(8,128)(2,1)S(1)}, u32[]{:S(2)}) copy-start(bf16[1,176,384]{2,1,0:T(8,128)(2,1)S(1)} %collective-permute-done) | copy-start | bytes 405508
  38.3 34.6 %collective-permute-start.3 = (bf16[4,192,640]{2,1,0:T(8,128)(2,1)S(1)}, bf16[4,192,640]{2,1,0:T(8,128)(2,1)S(1)}, u32[]{:S(2)}, u32[]{:S(2)}) collective-permute-start(bf16[4,192,640]{2,1,0:T(8,128)(2,1)S(1)} %bitcast.50), channel_id=1, source_target_pairs={{0,8},{8,0},{1,9},{9,1},{2,10},{10,2},{3,11},{11,3},{4,12},{12,4},... | collective-permute-start | bytes 2949128 | tf_op jit(solution)/shard_map/ppermute | solution.py:283
  42.2 30.6 %collective-permute-start.2 = (bf16[2,176,384]{2,1,0:T(8,128)(2,1)S(1)}, bf16[2,176,384]{2,1,0:T(8,128)(2,1)S(1)}, u32[]{:S(2)}, u32[]{:S(2)}) collective-permute-start(bf16[2,176,384]{2,1,0:T(8,128)(2,1)S(1)} %pad_maximum_fusion.4), channel_id=1, source_target_pairs={{0,32},{16,48},{32,0},{48,16},{64,96},{80,112},{96,64},{112,80},{1... | collective-permute-start | bytes 811016 | tf_op jit(solution)/shard_map/ppermute | solution.py:242
  72.8 17.1 %copy-start.14 = (bf16[2,176,384]{2,1,0:T(8,128)(2,1)}, bf16[2,176,384]{2,1,0:T(8,128)(2,1)S(1)}, u32[]{:S(2)}) copy-start(bf16[2,176,384]{2,1,0:T(8,128)(2,1)S(1)} %collective-permute-done.2) | copy-start | bytes 811012
  73.9 16.1 %collective-permute-start.5 = (bf16[4,176,384]{2,1,0:T(8,128)(2,1)S(1)}, bf16[4,176,384]{2,1,0:T(8,128)(2,1)S(1)}, u32[]{:S(2)}, u32[]{:S(2)}) collective-permute-start(bf16[4,176,384]{2,1,0:T(8,128)(2,1)S(1)} %pad_maximum_fusion.1), channel_id=1, source_target_pairs={{0,16},{16,0},{32,48},{48,32},{64,80},{80,64},{96,112},{112,96},{1... | collective-permute-start | bytes 1622024 | tf_op jit(solution)/shard_map/ppermute | solution.py:242
  79.6 18.6 %collective-permute-start.4 = (bf16[4,192,640]{2,1,0:T(8,128)(2,1)S(1)}, bf16[4,192,640]{2,1,0:T(8,128)(2,1)}, u32[]{:S(2)}, u32[]{:S(2)}) collective-permute-start(bf16[4,192,640]{2,1,0:T(8,128)(2,1)S(1)} %bitcast.52), channel_id=1, source_target_pairs={{0,8},{8,0},{1,9},{9,1},{2,10},{10,2},{3,11},{11,3},{4,12},{12,4},... | collective-permute-start | bytes 2949128 | tf_op jit(solution)/shard_map/ppermute | solution.py:289
  92.2 4.3 %copy-start.19 = (bf16[5120]{0:T(1024)(128)(2,1)S(1)}, bf16[5120]{0:T(1024)(128)(2,1)}, u32[]{:S(2)}) copy-start(bf16[5120]{0:T(1024)(128)(2,1)} %param.8) | copy-start | bytes 30724
  92.2 4.5 %copy-start.20 = (s32[64]{0:T(128)S(1)}, s32[64]{0:T(128)}, u32[]{:S(2)}) copy-start(s32[64]{0:T(128)} %param.13) | copy-start | bytes 772
  92.2 20.7 %all-to-all-start = ((bf16[4,8,176,128]{3,2,1,0:T(8,128)(2,1)}), bf16[4,8,176,128]{3,2,1,0:T(8,128)(2,1)S(1)}, u32[]{:S(2)}, u32[]{:S(2)}) async-start(bf16[4,8,176,128]{3,2,1,0:T(8,128)(2,1)} %broadcast_in_dim.22), calls=%async_computation | async-start | bytes 2883584 | tf_op jit(solution)/shard_map/all_to_all | solution.py:295
  98.2 1.8 copy-start.7
  103.9 1.9 copy-start.10
  114.8 31.8 %all-to-all-start.1 = ((bf16[4,8,160,256]{3,2,1,0:T(8,128)(2,1)}), bf16[4,8,160,256]{3,2,1,0:T(8,128)(2,1)S(1)}, u32[]{:S(2)}, u32[]{:S(2)}) async-start(bf16[4,8,160,256]{3,2,1,0:T(8,128)(2,1)} %broadcast_in_dim.20), calls=%async_computation.1 | async-start | bytes 5242880 | tf_op jit(solution)/shard_map/all_to_all | solution.py:298
  119.5 4.8 %copy-start.2 = (f32[384,128]{1,0:T(8,128)}, f32[384,128]{1,0:T(8,128)S(1)}, u32[]{:S(2)}) copy-start(f32[384,128]{1,0:T(8,128)S(1)} %get-tuple-element.62.cosine) | copy-start | bytes 589828
  119.5 4.8 %copy-start.4 = (f32[384,128]{1,0:T(8,128)}, f32[384,128]{1,0:T(8,128)S(1)}, u32[]{:S(2)}) copy-start(f32[384,128]{1,0:T(8,128)S(1)} %get-tuple-element.63.sine) | copy-start | bytes 589828
  119.8 2.1 %copy-start.11 = (bf16[384,5120]{1,0:T(8,128)(2,1)S(1)}, bf16[384,5120]{1,0:T(8,128)(2,1)}, u32[]{:S(2)}) copy-start(bf16[384,5120]{1,0:T(8,128)(2,1)} %copy-done.10) | copy-start | bytes 11796484
  124.3 22.3 %copy-start.9 = (f32[128]{0:T(128)S(1)}, f32[128]{0:T(128)}, u32[]{:S(2)}) copy-start(f32[128]{0:T(128)} %param.9) | copy-start | bytes 1540
  124.3 12.4 %collective-permute-start.6 = (bf16[384,128]{1,0:T(8,128)(2,1)S(1)}, bf16[384,128]{1,0:T(8,128)(2,1)S(1)}, u32[]{:S(2)}, u32[]{:S(2)}) collective-permute-start(bf16[384,128]{1,0:T(8,128)(2,1)S(1)} %shard_map.95), channel_id=1, source_target_pairs={{0,64},{16,80},{32,96},{48,112},{64,0},{80,16},{96,32},{112,48},{1... | collective-permute-start | bytes 294920 | tf_op jit(solution)/shard_map/ppermute | solution.py:242
  136.8 1.9 copy-start.17
  136.8 8.5 %collective-permute-start.7 = (bf16[2,384,128]{2,1,0:T(8,128)(2,1)S(1)}, bf16[2,384,128]{2,1,0:T(8,128)(2,1)}, u32[]{:S(2)}, u32[]{:S(2)}) collective-permute-start(bf16[2,384,128]{2,1,0:T(8,128)(2,1)S(1)} %pad_maximum_fusion.7), channel_id=1, source_target_pairs={{0,32},{16,48},{32,0},{48,16},{64,96},{80,112},{96,64},{112,80},{1... | collective-permute-start | bytes 589832 | tf_op jit(solution)/shard_map/ppermute | solution.py:242
  148.4 2.1 %copy-start.12 = (bf16[384,5120]{1,0:T(8,128)(2,1)S(1)}, bf16[384,5120]{1,0:T(8,128)(2,1)}, u32[]{:S(2)}) copy-start(bf16[384,5120]{1,0:T(8,128)(2,1)} %copy-done.10) | copy-start | bytes 11796484
  152.9 14.1 %collective-permute-start.12 = (bf16[4,384,128]{2,1,0:T(8,128)(2,1)S(1)}, bf16[4,384,128]{2,1,0:T(8,128)(2,1)S(1)}, u32[]{:S(2)}, u32[]{:S(2)}) collective-permute-start(bf16[4,384,128]{2,1,0:T(8,128)(2,1)S(1)} %pad_maximum_fusion.2.refs_0_), channel_id=1, source_target_pairs={{0,16},{16,0},{32,48},{48,32},{64,80},{80,64},{96,112},{112,96},{1... | collective-permute-start | bytes 1179656 | tf_op jit(solution)/shard_map/ppermute | solution.py:242
  155.5 9.3 %collective-permute-start.8 = (bf16[2,192,128]{2,1,0:T(8,128)(2,1)S(1)}, bf16[2,192,128]{2,1,0:T(8,128)(2,1)S(1)}, u32[]{:S(2)}, u32[]{:S(2)}) collective-permute-start(bf16[2,192,128]{2,1,0:T(8,128)(2,1)S(1)} %get-tuple-element.50), channel_id=1, source_target_pairs={{0,8},{8,0},{1,9},{9,1},{2,10},{10,2},{3,11},{11,3},{4,12},{12,4},... | collective-permute-start | bytes 294920 | tf_op jit(solution)/shard_map/ppermute | solution.py:384
  164.8 9.4 %collective-permute-start.9 = (bf16[4,384,128]{2,1,0:T(8,128)(2,1)S(1)}, bf16[4,384,128]{2,1,0:T(8,128)(2,1)S(1)}, u32[]{:S(2)}, u32[]{:S(2)}) collective-permute-start(bf16[4,384,128]{2,1,0:T(8,128)(2,1)S(1)} %pad_maximum_fusion.2.refs_0_), channel_id=1, source_target_pairs={{0,8},{8,0},{1,9},{9,1},{2,10},{10,2},{3,11},{11,3},{4,12},{12,4},... | collective-permute-start | bytes 1179656 | tf_op jit(solution)/shard_map/ppermute | solution.py:387
  167.1 16.2 %collective-permute-start.13 = (bf16[4,384,128]{2,1,0:T(8,128)(2,1)S(1)}, bf16[4,384,128]{2,1,0:T(8,128)(2,1)S(1)}, u32[]{:S(2)}, u32[]{:S(2)}) collective-permute-start(bf16[4,384,128]{2,1,0:T(8,128)(2,1)S(1)} %collective-permute-done.12.refs_1_), channel_id=1, source_target_pairs={{0,8},{8,0},{1,9},{9,1},{2,10},{10,2},{3,11},{11,3},{4,12},{12,4},... | collective-permute-start | bytes 1179656 | tf_op jit(solution)/shard_map/ppermute | solution.py:387
  171.6 8.8 %collective-permute-start.10 = (bf16[768,128]{1,0:T(8,128)(2,1)S(1)}, bf16[768,128]{1,0:T(8,128)(2,1)S(1)}, u32[]{:S(2)}, u32[]{:S(2)}) collective-permute-start(bf16[768,128]{1,0:T(8,128)(2,1)S(1)} %bitcast.55), channel_id=1, source_target_pairs={{128,0},{256,128},{384,256},{129,1},{257,129},{385,257},{130,2},{2... | collective-permute-start | bytes 589832 | tf_op jit(solution)/shard_map/ppermute | solution.py:388
  172.9 10.4 %collective-permute-start.11 = (bf16[768,128]{1,0:T(8,128)(2,1)S(1)}, bf16[768,128]{1,0:T(8,128)(2,1)S(1)}, u32[]{:S(2)}, u32[]{:S(2)}) collective-permute-start(bf16[768,128]{1,0:T(8,128)(2,1)S(1)} %bitcast.56), channel_id=1, source_target_pairs={{256,0},{384,128},{257,1},{385,129},{258,2},{386,130},{259,3},{387... | collective-permute-start | bytes 589832 | tf_op jit(solution)/shard_map/ppermute | solution.py:389
  184.9 12.4 %collective-permute-start.14 = (bf16[816,128]{1,0:T(8,128)(2,1)S(1)}, bf16[816,128]{1,0:T(8,128)(2,1)S(1)}, u32[]{:S(2)}, u32[]{:S(2)}) collective-permute-start(bf16[816,128]{1,0:T(8,128)(2,1)S(1)} %get-tuple-element.43), channel_id=1, source_target_pairs={{0,128},{128,256},{256,384},{1,129},{129,257},{257,385},{2,130},{1... | collective-permute-start | bytes 626696 | tf_op jit(solution)/shard_map/ppermute | solution.py:401
  193.6 8.2 %collective-permute-start.15 = (bf16[816,128]{1,0:T(8,128)(2,1)S(1)}, bf16[816,128]{1,0:T(8,128)(2,1)S(1)}, u32[]{:S(2)}, u32[]{:S(2)}) collective-permute-start(bf16[816,128]{1,0:T(8,128)(2,1)S(1)} %get-tuple-element.44), channel_id=1, source_target_pairs={{0,256},{128,384},{1,257},{129,385},{2,258},{130,386},{3,259},{131... | collective-permute-start | bytes 626696 | tf_op jit(solution)/shard_map/ppermute | solution.py:402
  (7 other events, 7.5 us)

commit v13 on v12

--- a/solution.py
+++ b/solution.py
@@ -16,9 +16,10 @@
 KEY_BLOCK = 1024
 NO_SEGMENT = 100.0
 VMEM_LIMIT = 14 * 1024 * 1024
-
-
-def call(kernel, out_shape, n_smem, n_vmem, scratch=(), flops=0, n_hbm=0, out_hbm=False):
+WIDE_LIMIT = 44 * 1024 * 1024
+
+
+def call(kernel, out_shape, n_smem, n_vmem, scratch=(), flops=0, n_hbm=0, out_hbm=False, limit=VMEM_LIMIT):
     specs = [pl.BlockSpec(memory_space=pltpu.SMEM)] * n_smem
     specs += [pl.BlockSpec(memory_space=pltpu.HBM)] * n_hbm
     specs += [pl.BlockSpec(memory_space=pltpu.VMEM)] * n_vmem
@@ -29,7 +30,7 @@
         in_specs=specs,
         out_specs=[out] * len(out_shape),
         scratch_shapes=list(scratch),
-        compiler_params=pltpu.CompilerParams(vmem_limit_bytes=VMEM_LIMIT),
+        compiler_params=pltpu.CompilerParams(vmem_limit_bytes=limit),
         cost_estimate=pl.CostEstimate(flops=flops, bytes_accessed=4 << 20, transcendentals=0),
     )
 
@@ -79,21 +80,32 @@
     copy.wait()
 
 
-def pair_kernel(panel, offsets, where, source, gain, cosine, sine, blocks, out, normed, weights, sem):
-    copy = pltpu.make_async_copy(source, normed, sem)
-    copy.start()
-    collect(offsets, where, blocks, weights, panel)
-    copy.wait()
+def fetch(offsets, where, sources, buffers, weights, sems, panel):
+    copies = [
+        pltpu.make_async_copy(source, buffer, sems.at[i])
+        for i, (source, buffer) in enumerate(zip(sources, buffers, strict=True))
+    ]
+    for copy in copies[::-1]:
+        copy.start()
+    copies[3].wait()
+    collect(offsets, where, buffers[3], weights, panel)
+    for copy in copies[:3]:
+        copy.wait()
+
+
+def pair_kernel(panel, offsets, where, *refs):
+    sources, (gain, out, weights, sems), buffers = refs[:4], refs[4:8], refs[8:]
+    fetch(offsets, where, sources, buffers, weights, sems, panel)
+    normed, cosine, sine, _ = buffers
     v = jnp.dot(normed[...], weights[...], preferred_element_type=jnp.float32)
     keys = head_norm_rope(v, gain[...], cosine[...], sine[...])
     out[...] = jnp.where(where[0] == 0, keys, v).astype(jnp.bfloat16)
 
 
-def query_kernel(panel, offsets, where, source, gain, cosine, sine, blocks, out, normed, weights, sem):
-    copy = pltpu.make_async_copy(source, normed, sem)
-    copy.start()
-    collect(offsets, where, blocks, weights, panel)
-    copy.wait()
+def query_kernel(panel, offsets, where, *refs):
+    sources, (gain, out, weights, sems), buffers = refs[:4], refs[4:8], refs[8:]
+    fetch(offsets, where, sources, buffers, weights, sems, panel)
+    normed, cosine, sine, _ = buffers
     rows = out.shape[2]
     for side in range(2):
         span = pl.ds(side * rows, rows)
@@ -339,19 +351,28 @@
     offsets = panel * jnp.sum(
         table[:, None] * (owners[:, None] == table[None, :]).astype(jnp.int32), axis=0
     )
-    (pair,) = call(
-        functools.partial(pair_kernel, panel),
-        [jax.ShapeDtypeStruct((2 * rows, 128), bf16)],
-        2,
-        4,
-        [
-            pltpu.VMEM((2 * rows, features), bf16),
-            pltpu.VMEM((features, 128), bf16),
-            pltpu.SemaphoreType.DMA,
-        ],
-        2 * 10**9,
-        n_hbm=1,
-    )(offsets, spot, normed, key_gain[None, :], cosine, sine, pair_blocks)
+    def project(kernel, out_shape, gain, blocks):
+        scratch = [
+            pltpu.VMEM((features, blocks.shape[-1]), bf16),
+            pltpu.SemaphoreType.DMA((4,)),
+            pltpu.VMEM(normed.shape, bf16),
+            pltpu.VMEM(cosine.shape, f32),
+            pltpu.VMEM(sine.shape, f32),
+            pltpu.VMEM(blocks.shape, bf16),
+        ]
+        (result,) = call(
+            functools.partial(kernel, panel),
+            [jax.ShapeDtypeStruct(out_shape, bf16)],
+            2,
+            1,
+            scratch,
+            3 * 10**9,
+            n_hbm=4,
+            limit=WIDE_LIMIT,
+        )(offsets, spot, normed, cosine, sine, blocks, gain[None, :])
+        return result
+
+    pair = project(pair_kernel, (2 * rows, 128), key_gain, pair_blocks)
 
     inside = z * 2 * rows + c * rows
     low = [jnp.clip(spread[s, 0], 0, plane) for s in range(3)]
@@ -363,19 +384,7 @@
     mine0 = jnp.stack([pair, across(pair, 4)])
     mine0, ranges, begins = lax.optimization_barrier((mine0, ranges, begins))
     mine0 = jnp.concatenate([mine0, across(mine0, 2)], axis=0)
-    (query,) = call(
-        functools.partial(query_kernel, panel),
-        [jax.ShapeDtypeStruct((2, 2, rows, 128), bf16)],
-        2,
-        4,
-        [
-            pltpu.VMEM((2 * rows, features), bf16),
-            pltpu.VMEM((features, 256), bf16),
-            pltpu.SemaphoreType.DMA,
-        ],
-        4 * 10**9,
-        n_hbm=1,
-    )(offsets, spot, normed, query_gain[None, :], cosine, sine, query_blocks)
+    query = project(query_kernel, (2, 2, rows, 128), query_gain, query_blocks)
 
     mine0, query = lax.optimization_barrier((mine0, query))
     mine1 = across(mine0, 1)
@@ -384,9 +393,9 @@
     q0 = jnp.concatenate([own_query, lax.ppermute(sent_query, "c", swap)], axis=0)
     q0 = q0.reshape(4 * rows, 128)
     mine = [mine0, mine1]
-    other = [lax.ppermute(v, "c", swap) for v in (after(mine0, q0), mine1)]
     q1 = lax.ppermute(q0, "x", [(i, i - 1) for i in range(1, nx)])
     q2 = lax.ppermute(q0, "x", [(i, i - 2) for i in range(2, nx)])
+    other = [lax.ppermute(v, "c", swap) for v in (after(mine0, q0), after(mine1, q1, q2))]
 
     state = [pltpu.VMEM((4 * rows, 256), f32), pltpu.VMEM((4 * rows, 1), f32)]
     r1, r2, keys, values = call(

time: 206 us -> 206 us (level)
  Pallas kernels: 14.7 us -> 25.6 us
  starting transfers between devices: 85.7 us -> 76.3 us
    pallas_call x1, Pallas kernels: 1.6 us -> 11 us  [body(): call(remote_kernel, [jax.ShapeDtypeStruct((4 * rows + 48, 128), bf16)] *...]
    ppermute x1, starting transfers between devices: 8.65 us -> 1.3 us  [body(): r1 = lax.ppermute(r1, 'x', [(i, i + 1) for i in range(nx - 1)])]
    ppermute x2, starting transfers between devices: 6.73 us -> 4.61 us  [body(): lax.ppermute(v, 'c', swap)]
  transfers between devices with their start and end apart: 18 -> 18, of which waited for: 9 -> 9; matrix products, arithmetic and copies ran while one was open for 5% -> 5% of each run, Pallas kernels for 4% -> 5%
where the time goes in v13:
time: 206 us; the launch traced here: 205 us
  starting transfers between devices  76.3 us (37%)
  blocking collectives  37.6 us (18%)
  waiting for transfers between devices  37.1 us (18%)
  Pallas kernels  25.6 us (12%)
  local copies, waits for them, and re-layouts  17.5 us (8%)
  other arithmetic  7.13 us (3%)
  between operations  3.11 us (2%)
    ppermute x6, starting transfers between devices, across(): return lax.ppermute(v, 'z', [(i, i ^ bit) for i in range(8)])  30.6 us
    ppermute x6, waiting for transfers between devices, across(): return lax.ppermute(v, 'z', [(i, i ^ bit) for i in range(8)])  17 us
    all_gather x1, blocking collectives, body(): own_far = lax.all_gather(far, 'y', axis=0)  15.9 us
    all_gather x1, blocking collectives, body(): own_near = lax.all_gather(hidden, 'y', axis=0)  13.2 us
    unnamed x44, local copies, waits for them, and re-layouts  11.2 us
    pallas_call x1, Pallas kernels, body(): call(remote_kernel, [jax.ShapeDtypeStruct((4 * rows + 48, 128), bf16)] *...  11 us
    ppermute x1, starting transfers between devices, body(): far = lax.ppermute(hidden, 'w', swap)  10.6 us
    ppermute x1, starting transfers between devices, body(): lax.ppermute(sent_query, 'c', swap)  9.08 us
  transfers between devices with their start and end apart: 18, of which 9 were waited for; matrix products, arithmetic and copies ran while one was open for 5% of the time, Pallas kernels for 5%

profile of v13, /device:TPU:1, one launch (start us, length us, event | category | flops | bytes accessed | tf_op | source)
XLA Modules:
  0.0 204.5 jit_solution(1672694881055049769)
XLA Ops:
  2.3 8.5 %all-gather = bf16[192,768]{1,0:T(8,128)(2,1)S(1)} all-gather(bf16[96,768]{1,0:T(8,128)(2,1)S(1)} %fusion.2), channel_id=2, replica_groups=mesh['x'=4,'z'=8,'c'=2,'y'=4,'w'=2] {'c'}, dimensions={0}, use_global_device_ids=true | all-gather | bytes 442368 | tf_op jit(solution)/shard_map/all_gather | solution.py:273
  11.0 3.4 %collective-permute-start = (bf16[1,176,384]{2,1,0:T(8,128)(2,1)S(1)}, bf16[1,176,384]{2,1,0:T(8,128)(2,1)S(1)}, u32[]{:S(2)}, u32[]{:S(2)}) collective-permute-start(bf16[1,176,384]{2,1,0:T(8,128)(2,1)S(1)} %fusion.4), channel_id=1, source_target_pairs={{0,64},{16,80},{32,96},{48,112},{64,0},{80,16},{96,32},{112,48},{1... | collective-permute-start | bytes 405512 | tf_op jit(solution)/shard_map/ppermute | solution.py:254
  14.4 10.6 %collective-permute-start.1 = (bf16[192,640]{1,0:T(8,128)(2,1)S(1)}, bf16[192,640]{1,0:T(8,128)(2,1)S(1)}, u32[]{:S(2)}, u32[]{:S(2)}) collective-permute-start(bf16[192,640]{1,0:T(8,128)(2,1)S(1)} %copy-done.18), channel_id=1, source_target_pairs={{0,1},{1,0},{2,3},{3,2},{4,5},{5,4},{6,7},{7,6},{8,9},{9,8},{10,11... | collective-permute-start | bytes 737288 | tf_op jit(solution)/shard_map/ppermute | solution.py:289
  25.1 13.2 %all-gather.1 = bf16[768,640]{1,0:T(8,128)(2,1)S(1)} all-gather(bf16[192,640]{1,0:T(8,128)(2,1)S(1)} %copy-done.18), channel_id=3, replica_groups=mesh['x'=4,'z'=8,'c'=2,'y'=4,'w'=2] {'y'}, dimensions={0}, use_global_device_ids=true | all-gather | bytes 1228800 | tf_op jit(solution)/shard_map/all_gather | solution.py:290
  38.3 3.9 %collective-permute-start.3 = (bf16[4,192,640]{2,1,0:T(8,128)(2,1)S(1)}, bf16[4,192,640]{2,1,0:T(8,128)(2,1)S(1)}, u32[]{:S(2)}, u32[]{:S(2)}) collective-permute-start(bf16[4,192,640]{2,1,0:T(8,128)(2,1)S(1)} %bitcast.50), channel_id=1, source_target_pairs={{0,8},{8,0},{1,9},{9,1},{2,10},{10,2},{3,11},{11,3},{4,12},{12,4},... | collective-permute-start | bytes 2949128 | tf_op jit(solution)/shard_map/ppermute | solution.py:295
  42.2 14.7 %collective-permute-start.2 = (bf16[2,176,384]{2,1,0:T(8,128)(2,1)S(1)}, bf16[2,176,384]{2,1,0:T(8,128)(2,1)S(1)}, u32[]{:S(2)}, u32[]{:S(2)}) collective-permute-start(bf16[2,176,384]{2,1,0:T(8,128)(2,1)S(1)} %pad_maximum_fusion.4), channel_id=1, source_target_pairs={{0,32},{16,48},{32,0},{48,16},{64,96},{80,112},{96,64},{112,80},{1... | collective-permute-start | bytes 811016 | tf_op jit(solution)/shard_map/ppermute | solution.py:254
  56.9 15.9 %all-gather.2 = bf16[768,640]{1,0:T(8,128)(2,1)S(1)} all-gather(bf16[192,640]{1,0:T(8,128)(2,1)S(1)} %collective-permute-done.1), channel_id=4, replica_groups=mesh['x'=4,'z'=8,'c'=2,'y'=4,'w'=2] {'y'}, dimensions={0}, use_global_device_ids=true | all-gather | bytes 1228800 | tf_op jit(solution)/shard_map/all_gather | solution.py:296
  73.9 5.6 %collective-permute-start.5 = (bf16[4,176,384]{2,1,0:T(8,128)(2,1)S(1)}, bf16[4,176,384]{2,1,0:T(8,128)(2,1)S(1)}, u32[]{:S(2)}, u32[]{:S(2)}) collective-permute-start(bf16[4,176,384]{2,1,0:T(8,128)(2,1)S(1)} %pad_maximum_fusion.1), channel_id=1, source_target_pairs={{0,16},{16,0},{32,48},{48,32},{64,80},{80,64},{96,112},{112,96},{1... | collective-permute-start | bytes 1622024 | tf_op jit(solution)/shard_map/ppermute | solution.py:254
  79.6 4.3 %collective-permute-start.4 = (bf16[4,192,640]{2,1,0:T(8,128)(2,1)S(1)}, bf16[4,192,640]{2,1,0:T(8,128)(2,1)}, u32[]{:S(2)}, u32[]{:S(2)}) collective-permute-start(bf16[4,192,640]{2,1,0:T(8,128)(2,1)S(1)} %bitcast.52), channel_id=1, source_target_pairs={{0,8},{8,0},{1,9},{9,1},{2,10},{10,2},{3,11},{11,3},{4,12},{12,4},... | collective-permute-start | bytes 2949128 | tf_op jit(solution)/shard_map/ppermute | solution.py:301
  83.9 6.1 %collective-permute-done.5 = bf16[4,176,384]{2,1,0:T(8,128)(2,1)S(1)} collective-permute-done((bf16[4,176,384]{2,1,0:T(8,128)(2,1)S(1)}, bf16[4,176,384]{2,1,0:T(8,128)(2,1)S(1)}, u32[]{:S(2)}, u32[]{:S(2)}) %collective-permute-start.5) | collective-permute-done | bytes 540704 | tf_op jit(solution)/shard_map/ppermute | solution.py:254
  92.2 4.3 %all-to-all-start = ((bf16[4,8,176,128]{3,2,1,0:T(8,128)(2,1)}), bf16[4,8,176,128]{3,2,1,0:T(8,128)(2,1)S(1)}, u32[]{:S(2)}, u32[]{:S(2)}) async-start(bf16[4,8,176,128]{3,2,1,0:T(8,128)(2,1)} %broadcast_in_dim.21), calls=%async_computation | async-start | bytes 2883584 | tf_op jit(solution)/shard_map/all_to_all | solution.py:307
  100.0 3.8 %shard_map.94.refs_0_ = bf16[384,5120]{1,0:T(8,128)(2,1)S(1)} custom-call(s32[3]{0:T(128)S(1)} %pad_add_fusion.1.where, f32[1,5120]{1,0:T(1,128)S(1)} %bitcast.58, bf16[4,192,640]{2,1,0:T(8,128)(2,1)S(1)} %bitcast.51, bf16[4,192,640]{2,1,0:T(8,128)(2,1)S(1)} %bitcast.53, bf16[4,192,640]{2,1,0:T(8,128)(2,1)S(1)} %copy-done.7, ...), custom_call_target="tpu_custom_call" | custom-call | flops 4000000000 | bytes 4194304 | tf_op jit(solution)/shard_map/pallas_call | solution.py:314
  105.7 7.2 %all-to-all-done.refs_3_ = bf16[4,8,176,128]{3,2,1,0:T(8,128)(2,1)S(1)} async-done(((bf16[4,8,176,128]{3,2,1,0:T(8,128)(2,1)}), bf16[4,8,176,128]{3,2,1,0:T(8,128)(2,1)S(1)}, u32[]{:S(2)}, u32[]{:S(2)}) %all-to-all-start) | async-done | bytes 1441824 | tf_op jit(solution)/shard_map/all_to_all | solution.py:307
  114.8 3.7 %all-to-all-start.1 = ((bf16[4,8,160,256]{3,2,1,0:T(8,128)(2,1)}), bf16[4,8,160,256]{3,2,1,0:T(8,128)(2,1)S(1)}, u32[]{:S(2)}, u32[]{:S(2)}) async-start(bf16[4,8,160,256]{3,2,1,0:T(8,128)(2,1)} %broadcast_in_dim.20), calls=%async_computation.1 | async-start | bytes 5242880 | tf_op jit(solution)/shard_map/all_to_all | solution.py:310
  119.8 2.1 %copy-done.11 = bf16[384,5120]{1,0:T(8,128)(2,1)S(1)} copy-done((bf16[384,5120]{1,0:T(8,128)(2,1)S(1)}, bf16[384,5120]{1,0:T(8,128)(2,1)}, u32[]{:S(2)}) %copy-start.11) | copy-done | bytes 3932184
  121.9 3.1 %shard_map.95 = bf16[384,128]{1,0:T(8,128)(2,1)S(1)} custom-call(s32[64]{0:T(128)S(1)} %broadcast_multiply_fusion.offsets, s32[3]{0:T(128)S(1)} %pad_add_fusion.1.where, bf16[384,5120]{1,0:T(8,128)(2,1)S(1)} %copy-done.11, f32[384,128]{1,0:T(8,128)S(1)} %get-tuple-element.64.refs_1_, f32[384,128]{1,0:T(8,128)S(1)} %get-tuple-element.65.refs_2_, ...), custom_call_target="tpu_custom_call" | custom-call | flops 3000000000 | bytes 4194304 | tf_op jit(solution)/shard_map/pallas_call | solution.py:363
  125.1 3.1 %collective-permute-start.6 = (bf16[384,128]{1,0:T(8,128)(2,1)S(1)}, bf16[384,128]{1,0:T(8,128)(2,1)S(1)}, u32[]{:S(2)}, u32[]{:S(2)}) collective-permute-start(bf16[384,128]{1,0:T(8,128)(2,1)S(1)} %shard_map.95), channel_id=1, source_target_pairs={{0,64},{16,80},{32,96},{48,112},{64,0},{80,16},{96,32},{112,48},{1... | collective-permute-start | bytes 294920 | tf_op jit(solution)/shard_map/ppermute | solution.py:254
  131.2 2.0 stack.101.where
  133.2 4.3 %collective-permute-done.6 = bf16[384,128]{1,0:T(8,128)(2,1)S(1)} collective-permute-done((bf16[384,128]{1,0:T(8,128)(2,1)S(1)}, bf16[384,128]{1,0:T(8,128)(2,1)S(1)}, u32[]{:S(2)}, u32[]{:S(2)}) %collective-permute-start.6) | collective-permute-done | bytes 98336 | tf_op jit(solution)/shard_map/ppermute | solution.py:254
  137.6 1.9 collective-permute-start.7
  139.5 6.6 %collective-permute-done.7 = bf16[2,384,128]{2,1,0:T(8,128)(2,1)} collective-permute-done((bf16[2,384,128]{2,1,0:T(8,128)(2,1)S(1)}, bf16[2,384,128]{2,1,0:T(8,128)(2,1)}, u32[]{:S(2)}, u32[]{:S(2)}) %collective-permute-start.7) | collective-permute-done | bytes 196640 | tf_op jit(solution)/shard_map/ppermute | solution.py:254
  149.1 2.1 %copy-done.12 = bf16[384,5120]{1,0:T(8,128)(2,1)S(1)} copy-done((bf16[384,5120]{1,0:T(8,128)(2,1)S(1)}, bf16[384,5120]{1,0:T(8,128)(2,1)}, u32[]{:S(2)}) %copy-start.12) | copy-done | bytes 3932184
  151.2 3.1 %shard_map.96 = bf16[2,2,192,128]{3,2,1,0:T(8,128)(2,1)S(1)} custom-call(s32[64]{0:T(128)S(1)} %broadcast_multiply_fusion.offsets, s32[3]{0:T(128)S(1)} %pad_add_fusion.1.where, bf16[384,5120]{1,0:T(8,128)(2,1)S(1)} %copy-done.12, f32[384,128]{1,0:T(8,128)S(1)} %copy-done.3, f32[384,128]{1,0:T(8,128)S(1)} %copy-done.5, ...), custom_call_target="tpu_custom_call" | custom-call | flops 3000000000 | bytes 4194304 | tf_op jit(solution)/shard_map/pallas_call | solution.py:363
  154.3 9.1 %collective-permute-start.8 = (bf16[2,192,128]{2,1,0:T(8,128)(2,1)S(1)}, bf16[2,192,128]{2,1,0:T(8,128)(2,1)S(1)}, u32[]{:S(2)}, u32[]{:S(2)}) collective-permute-start(bf16[2,192,128]{2,1,0:T(8,128)(2,1)S(1)} %get-tuple-element.52), channel_id=1, source_target_pairs={{0,8},{8,0},{1,9},{9,1},{2,10},{10,2},{3,11},{11,3},{4,12},{12,4},... | collective-permute-start | bytes 294920 | tf_op jit(solution)/shard_map/ppermute | solution.py:393
  168.0 1.9 collective-permute-start.9
  169.9 4.3 %collective-permute-done.10.near = bf16[768,128]{1,0:T(8,128)(2,1)S(1)} collective-permute-done((bf16[768,128]{1,0:T(8,128)(2,1)S(1)}, bf16[768,128]{1,0:T(8,128)(2,1)S(1)}, u32[]{:S(2)}, u32[]{:S(2)}) %collective-permute-start.10) | collective-permute-done | bytes 196640 | tf_op jit(solution)/shard_map/ppermute | solution.py:396
  174.2 2.9 %collective-permute-done.11.far = bf16[768,128]{1,0:T(8,128)(2,1)S(1)} collective-permute-done((bf16[768,128]{1,0:T(8,128)(2,1)S(1)}, bf16[768,128]{1,0:T(8,128)(2,1)S(1)}, u32[]{:S(2)}, u32[]{:S(2)}) %collective-permute-start.11) | collective-permute-done | bytes 196640 | tf_op jit(solution)/shard_map/ppermute | solution.py:397
  177.1 2.7 %collective-permute-start.13 = (bf16[4,384,128]{2,1,0:T(8,128)(2,1)S(1)}, bf16[4,384,128]{2,1,0:T(8,128)(2,1)S(1)}, u32[]{:S(2)}, u32[]{:S(2)}) collective-permute-start(bf16[4,384,128]{2,1,0:T(8,128)(2,1)S(1)} %collective-permute-done.12.refs_1_), channel_id=1, source_target_pairs={{0,8},{8,0},{1,9},{9,1},{2,10},{10,2},{3,11},{11,3},{4,12},{12,4},... | collective-permute-start | bytes 1179656 | tf_op jit(solution)/shard_map/ppermute | solution.py:398
  181.2 11.0 %shard_map.97 = (bf16[816,128]{1,0:T(8,128)(2,1)S(1)}, bf16[816,128]{1,0:T(8,128)(2,1)S(1)}, bf16[3072,128]{1,0:T(8,128)(2,1)S(1)}, bf16[3072,256]{1,0:T(8,128)(2,1)S(1)}) custom-call(s32[12]{0:T(128)S(1)} %stack.101.where, s32[3,192,1]{2,1,0:T(8,128)S(1)} %broadcast_subtract_fusion.begins, bf16[768,128]{1,0:T(8,128)(2,1)S(1)} %collective-permute-done.10.near, ...), custom_call_target="tpu_custom_call" | custom-call | flops 10000000000 | bytes 4194304 | tf_op jit(solution)/shard_map/pallas_call | solution.py:401
  194.8 2.5 %shard_map.98 = (f32[768,128]{1,0:T(8,128)S(1)}, f32[768,1]{1,0:T(8,128)S(1)}) custom-call(s32[12]{0:T(128)S(1)} %stack.101.where, s32[3,192,1]{2,1,0:T(8,128)S(1)} %broadcast_subtract_fusion.begins, bf16[768,128]{1,0:T(8,128)(2,1)S(1)} %bitcast.57, bf16[3072,128]{1,0:T(8,128)(2,1)S(1)} %get-tuple-element.41.keys, bf16[3072,256]{1,0:T(8,128)(2,1)S(1)} %get-tuple-element.42.values), custom_call_target="tpu_custom_call" | custom-call | flops 10000000000 | bytes 4194304 | tf_op jit(solution)/shard_map/pallas_call | solution.py:412
  198.0 4.5 %collective-permute-done.15.r2 = bf16[816,128]{1,0:T(8,128)(2,1)S(1)} collective-permute-done((bf16[816,128]{1,0:T(8,128)(2,1)S(1)}, bf16[816,128]{1,0:T(8,128)(2,1)S(1)}, u32[]{:S(2)}, u32[]{:S(2)}) %collective-permute-start.15) | collective-permute-done | bytes 208928 | tf_op jit(solution)/shard_map/ppermute | solution.py:411
  202.5 2.1 %shard_map.99 = bf16[192,512]{1,0:T(8,128)(2,1)} custom-call(s32[3]{0:T(128)S(1)} %pad_add_fusion.2.where, f32[768,128]{1,0:T(8,128)S(1)} %get-tuple-element.43.o0, f32[768,1]{1,0:T(8,128)S(1)} %get-tuple-element.44.l0, bf16[816,128]{1,0:T(8,128)(2,1)S(1)} %collective-permute-done.14.r1, bf16[816,128]{1,0:T(8,128)(2,1)S(1)} %collective-permute-done.15.r2), custom_call_target="tpu_custom_call" | custom-call | bytes 4194304 | tf_op jit(solution)/shard_map/pallas_call | solution.py:424
  (106 shorter events, 26.8 us)
Async XLA Ops:
  0.6 13.8 %copy-start.18 = (bf16[192,640]{1,0:T(8,128)(2,1)S(1)}, bf16[192,640]{1,0:T(8,128)(2,1)}, u32[]{:S(2)}) copy-start(bf16[192,640]{1,0:T(8,128)(2,1)} %param.7) | copy-start | bytes 737284
  11.0 79.0 %copy-start.13 = (bf16[1,176,384]{2,1,0:T(8,128)(2,1)}, bf16[1,176,384]{2,1,0:T(8,128)(2,1)S(1)}, u32[]{:S(2)}) copy-start(bf16[1,176,384]{2,1,0:T(8,128)(2,1)S(1)} %fusion.4) | copy-start | bytes 405508
  11.0 27.3 %collective-permute-start = (bf16[1,176,384]{2,1,0:T(8,128)(2,1)S(1)}, bf16[1,176,384]{2,1,0:T(8,128)(2,1)S(1)}, u32[]{:S(2)}, u32[]{:S(2)}) collective-permute-start(bf16[1,176,384]{2,1,0:T(8,128)(2,1)S(1)} %fusion.4), channel_id=1, source_target_pairs={{0,64},{16,80},{32,96},{48,112},{64,0},{80,16},{96,32},{112,48},{1... | collective-permute-start | bytes 405512 | tf_op jit(solution)/shard_map/ppermute | solution.py:254
  14.4 23.8 %collective-permute-start.1 = (bf16[192,640]{1,0:T(8,128)(2,1)S(1)}, bf16[192,640]{1,0:T(8,128)(2,1)S(1)}, u32[]{:S(2)}, u32[]{:S(2)}) collective-permute-start(bf16[192,640]{1,0:T(8,128)(2,1)S(1)} %copy-done.18), channel_id=1, source_target_pairs={{0,1},{1,0},{2,3},{3,2},{4,5},{5,4},{6,7},{7,6},{8,9},{9,8},{10,11... | collective-permute-start | bytes 737288 | tf_op jit(solution)/shard_map/ppermute | solution.py:289
  38.3 51.7 %copy-start.15 = (bf16[1,176,384]{2,1,0:T(8,128)(2,1)}, bf16[1,176,384]{2,1,0:T(8,128)(2,1)S(1)}, u32[]{:S(2)}) copy-start(bf16[1,176,384]{2,1,0:T(8,128)(2,1)S(1)} %collective-permute-done) | copy-start | bytes 405508
  38.3 34.6 %collective-permute-start.3 = (bf16[4,192,640]{2,1,0:T(8,128)(2,1)S(1)}, bf16[4,192,640]{2,1,0:T(8,128)(2,1)S(1)}, u32[]{:S(2)}, u32[]{:S(2)}) collective-permute-start(bf16[4,192,640]{2,1,0:T(8,128)(2,1)S(1)} %bitcast.50), channel_id=1, source_target_pairs={{0,8},{8,0},{1,9},{9,1},{2,10},{10,2},{3,11},{11,3},{4,12},{12,4},... | collective-permute-start | bytes 2949128 | tf_op jit(solution)/shard_map/ppermute | solution.py:295
  42.2 30.6 %collective-permute-start.2 = (bf16[2,176,384]{2,1,0:T(8,128)(2,1)S(1)}, bf16[2,176,384]{2,1,0:T(8,128)(2,1)S(1)}, u32[]{:S(2)}, u32[]{:S(2)}) collective-permute-start(bf16[2,176,384]{2,1,0:T(8,128)(2,1)S(1)} %pad_maximum_fusion.4), channel_id=1, source_target_pairs={{0,32},{16,48},{32,0},{48,16},{64,96},{80,112},{96,64},{112,80},{1... | collective-permute-start | bytes 811016 | tf_op jit(solution)/shard_map/ppermute | solution.py:254
  72.8 17.1 %copy-start.14 = (bf16[2,176,384]{2,1,0:T(8,128)(2,1)}, bf16[2,176,384]{2,1,0:T(8,128)(2,1)S(1)}, u32[]{:S(2)}) copy-start(bf16[2,176,384]{2,1,0:T(8,128)(2,1)S(1)} %collective-permute-done.2) | copy-start | bytes 811012
  73.9 16.1 %collective-permute-start.5 = (bf16[4,176,384]{2,1,0:T(8,128)(2,1)S(1)}, bf16[4,176,384]{2,1,0:T(8,128)(2,1)S(1)}, u32[]{:S(2)}, u32[]{:S(2)}) collective-permute-start(bf16[4,176,384]{2,1,0:T(8,128)(2,1)S(1)} %pad_maximum_fusion.1), channel_id=1, source_target_pairs={{0,16},{16,0},{32,48},{48,32},{64,80},{80,64},{96,112},{112,96},{1... | collective-permute-start | bytes 1622024 | tf_op jit(solution)/shard_map/ppermute | solution.py:254
  79.6 18.6 %collective-permute-start.4 = (bf16[4,192,640]{2,1,0:T(8,128)(2,1)S(1)}, bf16[4,192,640]{2,1,0:T(8,128)(2,1)}, u32[]{:S(2)}, u32[]{:S(2)}) collective-permute-start(bf16[4,192,640]{2,1,0:T(8,128)(2,1)S(1)} %bitcast.52), channel_id=1, source_target_pairs={{0,8},{8,0},{1,9},{9,1},{2,10},{10,2},{3,11},{11,3},{4,12},{12,4},... | collective-permute-start | bytes 2949128 | tf_op jit(solution)/shard_map/ppermute | solution.py:301
  92.2 4.3 %copy-start.19 = (bf16[5120]{0:T(1024)(128)(2,1)S(1)}, bf16[5120]{0:T(1024)(128)(2,1)}, u32[]{:S(2)}) copy-start(bf16[5120]{0:T(1024)(128)(2,1)} %param.8) | copy-start | bytes 30724
  92.2 4.5 %copy-start.20 = (s32[64]{0:T(128)S(1)}, s32[64]{0:T(128)}, u32[]{:S(2)}) copy-start(s32[64]{0:T(128)} %param.13) | copy-start | bytes 772
  92.2 20.7 %all-to-all-start = ((bf16[4,8,176,128]{3,2,1,0:T(8,128)(2,1)}), bf16[4,8,176,128]{3,2,1,0:T(8,128)(2,1)S(1)}, u32[]{:S(2)}, u32[]{:S(2)}) async-start(bf16[4,8,176,128]{3,2,1,0:T(8,128)(2,1)} %broadcast_in_dim.21), calls=%async_computation | async-start | bytes 2883584 | tf_op jit(solution)/shard_map/all_to_all | solution.py:307
  98.2 1.8 copy-start.7
  103.9 1.9 copy-start.10
  114.8 32.4 %all-to-all-start.1 = ((bf16[4,8,160,256]{3,2,1,0:T(8,128)(2,1)}), bf16[4,8,160,256]{3,2,1,0:T(8,128)(2,1)S(1)}, u32[]{:S(2)}, u32[]{:S(2)}) async-start(bf16[4,8,160,256]{3,2,1,0:T(8,128)(2,1)} %broadcast_in_dim.20), calls=%async_computation.1 | async-start | bytes 5242880 | tf_op jit(solution)/shard_map/all_to_all | solution.py:310
  119.5 5.5 %copy-start.2 = (f32[384,128]{1,0:T(8,128)}, f32[384,128]{1,0:T(8,128)S(1)}, u32[]{:S(2)}) copy-start(f32[384,128]{1,0:T(8,128)S(1)} %get-tuple-element.64.refs_1_) | copy-start | bytes 589828
  119.5 5.5 %copy-start.4 = (f32[384,128]{1,0:T(8,128)}, f32[384,128]{1,0:T(8,128)S(1)}, u32[]{:S(2)}) copy-start(f32[384,128]{1,0:T(8,128)S(1)} %get-tuple-element.65.refs_2_) | copy-start | bytes 589828
  119.8 2.1 %copy-start.11 = (bf16[384,5120]{1,0:T(8,128)(2,1)S(1)}, bf16[384,5120]{1,0:T(8,128)(2,1)}, u32[]{:S(2)}) copy-start(bf16[384,5120]{1,0:T(8,128)(2,1)} %copy-done.10) | copy-start | bytes 11796484
  125.1 22.1 %copy-start.9 = (f32[128]{0:T(128)S(1)}, f32[128]{0:T(128)}, u32[]{:S(2)}) copy-start(f32[128]{0:T(128)} %param.9) | copy-start | bytes 1540
  125.1 12.4 %collective-permute-start.6 = (bf16[384,128]{1,0:T(8,128)(2,1)S(1)}, bf16[384,128]{1,0:T(8,128)(2,1)S(1)}, u32[]{:S(2)}, u32[]{:S(2)}) collective-permute-start(bf16[384,128]{1,0:T(8,128)(2,1)S(1)} %shard_map.95), channel_id=1, source_target_pairs={{0,64},{16,80},{32,96},{48,112},{64,0},{80,16},{96,32},{112,48},{1... | collective-permute-start | bytes 294920 | tf_op jit(solution)/shard_map/ppermute | solution.py:254
  137.6 1.9 copy-start.17
  137.6 8.5 %collective-permute-start.7 = (bf16[2,384,128]{2,1,0:T(8,128)(2,1)S(1)}, bf16[2,384,128]{2,1,0:T(8,128)(2,1)}, u32[]{:S(2)}, u32[]{:S(2)}) collective-permute-start(bf16[2,384,128]{2,1,0:T(8,128)(2,1)S(1)} %pad_maximum_fusion.7), channel_id=1, source_target_pairs={{0,32},{16,48},{32,0},{48,16},{64,96},{80,112},{96,64},{112,80},{1... | collective-permute-start | bytes 589832 | tf_op jit(solution)/shard_map/ppermute | solution.py:254
  149.1 2.1 %copy-start.12 = (bf16[384,5120]{1,0:T(8,128)(2,1)S(1)}, bf16[384,5120]{1,0:T(8,128)(2,1)}, u32[]{:S(2)}) copy-start(bf16[384,5120]{1,0:T(8,128)(2,1)} %copy-done.10) | copy-start | bytes 11796484
  154.3 11.0 %collective-permute-start.8 = (bf16[2,192,128]{2,1,0:T(8,128)(2,1)S(1)}, bf16[2,192,128]{2,1,0:T(8,128)(2,1)S(1)}, u32[]{:S(2)}, u32[]{:S(2)}) collective-permute-start(bf16[2,192,128]{2,1,0:T(8,128)(2,1)S(1)} %get-tuple-element.52), channel_id=1, source_target_pairs={{0,8},{8,0},{1,9},{9,1},{2,10},{10,2},{3,11},{11,3},{4,12},{12,4},... | collective-permute-start | bytes 294920 | tf_op jit(solution)/shard_map/ppermute | solution.py:393
  163.4 13.7 %collective-permute-start.12 = (bf16[4,384,128]{2,1,0:T(8,128)(2,1)S(1)}, bf16[4,384,128]{2,1,0:T(8,128)(2,1)S(1)}, u32[]{:S(2)}, u32[]{:S(2)}) collective-permute-start(bf16[4,384,128]{2,1,0:T(8,128)(2,1)S(1)} %pad_maximum_fusion.2.refs_0_), channel_id=1, source_target_pairs={{0,16},{16,0},{32,48},{48,32},{64,80},{80,64},{96,112},{112,96},{1... | collective-permute-start | bytes 1179656 | tf_op jit(solution)/shard_map/ppermute | solution.py:254
  165.4 8.8 %collective-permute-start.10 = (bf16[768,128]{1,0:T(8,128)(2,1)S(1)}, bf16[768,128]{1,0:T(8,128)(2,1)S(1)}, u32[]{:S(2)}, u32[]{:S(2)}) collective-permute-start(bf16[768,128]{1,0:T(8,128)(2,1)S(1)} %bitcast.55), channel_id=1, source_target_pairs={{128,0},{256,128},{384,256},{129,1},{257,129},{385,257},{130,2},{2... | collective-permute-start | bytes 589832 | tf_op jit(solution)/shard_map/ppermute | solution.py:396
  166.7 10.4 %collective-permute-start.11 = (bf16[768,128]{1,0:T(8,128)(2,1)S(1)}, bf16[768,128]{1,0:T(8,128)(2,1)S(1)}, u32[]{:S(2)}, u32[]{:S(2)}) collective-permute-start(bf16[768,128]{1,0:T(8,128)(2,1)S(1)} %bitcast.56), channel_id=1, source_target_pairs={{256,0},{384,128},{257,1},{385,129},{258,2},{386,130},{259,3},{387... | collective-permute-start | bytes 589832 | tf_op jit(solution)/shard_map/ppermute | solution.py:397
  168.0 11.9 %collective-permute-start.9 = (bf16[4,384,128]{2,1,0:T(8,128)(2,1)S(1)}, bf16[4,384,128]{2,1,0:T(8,128)(2,1)S(1)}, u32[]{:S(2)}, u32[]{:S(2)}) collective-permute-start(bf16[4,384,128]{2,1,0:T(8,128)(2,1)S(1)} %pad_maximum_fusion.2.refs_0_), channel_id=1, source_target_pairs={{0,8},{8,0},{1,9},{9,1},{2,10},{10,2},{3,11},{11,3},{4,12},{12,4},... | collective-permute-start | bytes 1179656 | tf_op jit(solution)/shard_map/ppermute | solution.py:398
  177.1 4.0 %collective-permute-start.13 = (bf16[4,384,128]{2,1,0:T(8,128)(2,1)S(1)}, bf16[4,384,128]{2,1,0:T(8,128)(2,1)S(1)}, u32[]{:S(2)}, u32[]{:S(2)}) collective-permute-start(bf16[4,384,128]{2,1,0:T(8,128)(2,1)S(1)} %collective-permute-done.12.refs_1_), channel_id=1, source_target_pairs={{0,8},{8,0},{1,9},{9,1},{2,10},{10,2},{3,11},{11,3},{4,12},{12,4},... | collective-permute-start | bytes 1179656 | tf_op jit(solution)/shard_map/ppermute | solution.py:398
  192.2 5.8 %collective-permute-start.14 = (bf16[816,128]{1,0:T(8,128)(2,1)S(1)}, bf16[816,128]{1,0:T(8,128)(2,1)S(1)}, u32[]{:S(2)}, u32[]{:S(2)}) collective-permute-start(bf16[816,128]{1,0:T(8,128)(2,1)S(1)} %get-tuple-element.45), channel_id=1, source_target_pairs={{0,128},{128,256},{256,384},{1,129},{129,257},{257,385},{2,130},{1... | collective-permute-start | bytes 626696 | tf_op jit(solution)/shard_map/ppermute | solution.py:410
  193.5 9.0 %collective-permute-start.15 = (bf16[816,128]{1,0:T(8,128)(2,1)S(1)}, bf16[816,128]{1,0:T(8,128)(2,1)S(1)}, u32[]{:S(2)}, u32[]{:S(2)}) collective-permute-start(bf16[816,128]{1,0:T(8,128)(2,1)S(1)} %get-tuple-element.46), channel_id=1, source_target_pairs={{0,256},{128,384},{1,257},{129,385},{2,258},{130,386},{3,259},{131... | collective-permute-start | bytes 626696 | tf_op jit(solution)/shard_map/ppermute | solution.py:411
  (7 other events, 7.5 us)

commit v14 on v13

--- a/solution.py
+++ b/solution.py
@@ -16,7 +16,7 @@
 KEY_BLOCK = 1024
 NO_SEGMENT = 100.0
 VMEM_LIMIT = 14 * 1024 * 1024
-WIDE_LIMIT = 44 * 1024 * 1024
+WIDE_LIMIT = 60 * 1024 * 1024
 
 
 def call(kernel, out_shape, n_smem, n_vmem, scratch=(), flops=0, n_hbm=0, out_hbm=False, limit=VMEM_LIMIT):

time: 206 us -> 212 us (1.029)
  starting transfers between devices: 76.3 us -> 90.7 us
  local copies, waits for them, and re-layouts: 17.5 us -> 11.4 us
  Pallas kernels: 25.6 us -> 21.3 us
  other arithmetic: 7.13 us -> 9.87 us
    ppermute x1, starting transfers between devices: 1.3 us -> 14.7 us  [body(): r1 = lax.ppermute(r1, 'x', [(i, i + 1) for i in range(nx - 1)])]
    pallas_call x1, Pallas kernels: 11 us -> 1.6 us  [body(): call(remote_kernel, [jax.ShapeDtypeStruct((4 * rows + 48, 128), bf16)] *...]
    unnamed x44 -> x18, local copies, waits for them, and re-layouts: 11.2 us -> 4.24 us
    pallas_call x2, Pallas kernels: 6.25 us -> 11.4 us  [project(): call(functools.partial(kernel, panel), [jax.ShapeDtypeStruct(out_shape, b...]
  transfers between devices with their start and end apart: 18 -> 18, of which waited for: 9 -> 9; matrix products, arithmetic and copies ran while one was open for 5% -> 6% of each run, Pallas kernels for 5% -> 6%
where the time goes in v14:
time: 212 us; the launch traced here: 210 us
  starting transfers between devices  90.7 us (43%)
  blocking collectives  37.6 us (18%)
  waiting for transfers between devices  36.2 us (17%)
  Pallas kernels  21.3 us (10%)
  local copies, waits for them, and re-layouts  11.4 us (5%)
  other arithmetic  9.87 us (5%)
  between operations  2.97 us (1%)
    ppermute x6, starting transfers between devices, across(): return lax.ppermute(v, 'z', [(i, i ^ bit) for i in range(8)])  31.2 us
    ppermute x6, waiting for transfers between devices, across(): return lax.ppermute(v, 'z', [(i, i ^ bit) for i in range(8)])  16.5 us
    all_gather x1, blocking collectives, body(): own_far = lax.all_gather(far, 'y', axis=0)  15.9 us
    ppermute x1, starting transfers between devices, body(): r1 = lax.ppermute(r1, 'x', [(i, i + 1) for i in range(nx - 1)])  14.7 us
    all_gather x1, blocking collectives, body(): own_near = lax.all_gather(hidden, 'y', axis=0)  13.2 us
    pallas_call x2, Pallas kernels, project(): call(functools.partial(kernel, panel), [jax.ShapeDtypeStruct(out_shape, b...  11.4 us
    ppermute x1, starting transfers between devices, body(): far = lax.ppermute(hidden, 'w', swap)  10.6 us
    ppermute x1, starting transfers between devices, body(): lax.ppermute(sent_query, 'c', swap)  9.31 us
  transfers between devices with their start and end apart: 18, of which 9 were waited for; matrix products, arithmetic and copies ran while one was open for 6% of the time, Pallas kernels for 6%

profile of v14, /device:TPU:1, one launch (start us, length us, event | category | flops | bytes accessed | tf_op | source)
XLA Modules:
  0.0 210.1 jit_solution(14632686508831373581)
XLA Ops:
  2.3 8.5 %all-gather = bf16[192,768]{1,0:T(8,128)(2,1)S(1)} all-gather(bf16[96,768]{1,0:T(8,128)(2,1)S(1)} %fusion.2), channel_id=2, replica_groups=mesh['x'=4,'z'=8,'c'=2,'y'=4,'w'=2] {'c'}, dimensions={0}, use_global_device_ids=true | all-gather | bytes 442368 | tf_op jit(solution)/shard_map/all_gather | solution.py:273
  11.0 3.4 %collective-permute-start = (bf16[1,176,384]{2,1,0:T(8,128)(2,1)S(1)}, bf16[1,176,384]{2,1,0:T(8,128)(2,1)S(1)}, u32[]{:S(2)}, u32[]{:S(2)}) collective-permute-start(bf16[1,176,384]{2,1,0:T(8,128)(2,1)S(1)} %fusion.4), channel_id=1, source_target_pairs={{0,64},{16,80},{32,96},{48,112},{64,0},{80,16},{96,32},{112,48},{1... | collective-permute-start | bytes 405512 | tf_op jit(solution)/shard_map/ppermute | solution.py:254
  14.4 10.6 %collective-permute-start.1 = (bf16[192,640]{1,0:T(8,128)(2,1)S(1)}, bf16[192,640]{1,0:T(8,128)(2,1)S(1)}, u32[]{:S(2)}, u32[]{:S(2)}) collective-permute-start(bf16[192,640]{1,0:T(8,128)(2,1)S(1)} %copy-done.4), channel_id=1, source_target_pairs={{0,1},{1,0},{2,3},{3,2},{4,5},{5,4},{6,7},{7,6},{8,9},{9,8},{10,11... | collective-permute-start | bytes 737288 | tf_op jit(solution)/shard_map/ppermute | solution.py:289
  25.1 13.2 %all-gather.1 = bf16[768,640]{1,0:T(8,128)(2,1)S(1)} all-gather(bf16[192,640]{1,0:T(8,128)(2,1)S(1)} %copy-done.4), channel_id=3, replica_groups=mesh['x'=4,'z'=8,'c'=2,'y'=4,'w'=2] {'y'}, dimensions={0}, use_global_device_ids=true | all-gather | bytes 1228800 | tf_op jit(solution)/shard_map/all_gather | solution.py:290
  38.3 3.9 %collective-permute-start.3 = (bf16[4,192,640]{2,1,0:T(8,128)(2,1)S(1)}, bf16[4,192,640]{2,1,0:T(8,128)(2,1)S(1)}, u32[]{:S(2)}, u32[]{:S(2)}) collective-permute-start(bf16[4,192,640]{2,1,0:T(8,128)(2,1)S(1)} %bitcast.50), channel_id=1, source_target_pairs={{0,8},{8,0},{1,9},{9,1},{2,10},{10,2},{3,11},{11,3},{4,12},{12,4},... | collective-permute-start | bytes 2949128 | tf_op jit(solution)/shard_map/ppermute | solution.py:295
  42.2 14.7 %collective-permute-start.2 = (bf16[2,176,384]{2,1,0:T(8,128)(2,1)S(1)}, bf16[2,176,384]{2,1,0:T(8,128)(2,1)S(1)}, u32[]{:S(2)}, u32[]{:S(2)}) collective-permute-start(bf16[2,176,384]{2,1,0:T(8,128)(2,1)S(1)} %pad_maximum_fusion.4), channel_id=1, source_target_pairs={{0,32},{16,48},{32,0},{48,16},{64,96},{80,112},{96,64},{112,80},{1... | collective-permute-start | bytes 811016 | tf_op jit(solution)/shard_map/ppermute | solution.py:254
  56.9 15.9 %all-gather.2 = bf16[768,640]{1,0:T(8,128)(2,1)S(1)} all-gather(bf16[192,640]{1,0:T(8,128)(2,1)S(1)} %collective-permute-done.1), channel_id=4, replica_groups=mesh['x'=4,'z'=8,'c'=2,'y'=4,'w'=2] {'y'}, dimensions={0}, use_global_device_ids=true | all-gather | bytes 1228800 | tf_op jit(solution)/shard_map/all_gather | solution.py:296
  72.9 5.6 %collective-permute-start.5 = (bf16[4,176,384]{2,1,0:T(8,128)(2,1)S(1)}, bf16[4,176,384]{2,1,0:T(8,128)(2,1)S(1)}, u32[]{:S(2)}, u32[]{:S(2)}) collective-permute-start(bf16[4,176,384]{2,1,0:T(8,128)(2,1)S(1)} %pad_maximum_fusion.1), channel_id=1, source_target_pairs={{0,16},{16,0},{32,48},{48,32},{64,80},{80,64},{96,112},{112,96},{1... | collective-permute-start | bytes 1622024 | tf_op jit(solution)/shard_map/ppermute | solution.py:254
  78.6 4.3 %collective-permute-start.4 = (bf16[4,192,640]{2,1,0:T(8,128)(2,1)S(1)}, bf16[4,192,640]{2,1,0:T(8,128)(2,1)}, u32[]{:S(2)}, u32[]{:S(2)}) collective-permute-start(bf16[4,192,640]{2,1,0:T(8,128)(2,1)S(1)} %bitcast.52), channel_id=1, source_target_pairs={{0,8},{8,0},{1,9},{9,1},{2,10},{10,2},{3,11},{11,3},{4,12},{12,4},... | collective-permute-start | bytes 2949128 | tf_op jit(solution)/shard_map/ppermute | solution.py:301
  82.9 6.1 %collective-permute-done.5 = bf16[4,176,384]{2,1,0:T(8,128)(2,1)S(1)} collective-permute-done((bf16[4,176,384]{2,1,0:T(8,128)(2,1)S(1)}, bf16[4,176,384]{2,1,0:T(8,128)(2,1)S(1)}, u32[]{:S(2)}, u32[]{:S(2)}) %collective-permute-start.5) | collective-permute-done | bytes 540704 | tf_op jit(solution)/shard_map/ppermute | solution.py:254
  91.2 4.5 %all-to-all-start = ((bf16[4,8,176,128]{3,2,1,0:T(8,128)(2,1)}), bf16[4,8,176,128]{3,2,1,0:T(8,128)(2,1)}, u32[]{:S(2)}, u32[]{:S(2)}) async-start(bf16[4,8,176,128]{3,2,1,0:T(8,128)(2,1)} %broadcast_in_dim.21), calls=%async_computation | async-start | bytes 2883584 | tf_op jit(solution)/shard_map/all_to_all | solution.py:307
  99.6 3.8 %shard_map.94.refs_0_ = bf16[384,5120]{1,0:T(8,128)(2,1)S(1)} custom-call(s32[3]{0:T(128)S(1)} %pad_add_fusion.1.where, f32[1,5120]{1,0:T(1,128)S(1)} %bitcast.57, bf16[4,192,640]{2,1,0:T(8,128)(2,1)S(1)} %bitcast.51, bf16[4,192,640]{2,1,0:T(8,128)(2,1)S(1)} %bitcast.53, bf16[4,192,640]{2,1,0:T(8,128)(2,1)S(1)} %collective-permute-done.3.refs_2_, ...), custom_call_target="tpu_custom_call" | custom-call | flops 4000000000 | bytes 4194304 | tf_op jit(solution)/shard_map/pallas_call | solution.py:314
  103.5 1.9 copy-done.1
  105.3 7.0 %all-to-all-done.refs_3_ = bf16[4,8,176,128]{3,2,1,0:T(8,128)(2,1)} async-done(((bf16[4,8,176,128]{3,2,1,0:T(8,128)(2,1)}), bf16[4,8,176,128]{3,2,1,0:T(8,128)(2,1)}, u32[]{:S(2)}, u32[]{:S(2)}) %all-to-all-start) | async-done | bytes 1441824 | tf_op jit(solution)/shard_map/all_to_all | solution.py:307
  113.9 3.7 %all-to-all-start.1 = ((bf16[4,8,160,256]{3,2,1,0:T(8,128)(2,1)}), bf16[4,8,160,256]{3,2,1,0:T(8,128)(2,1)S(1)}, u32[]{:S(2)}, u32[]{:S(2)}) async-start(bf16[4,8,160,256]{3,2,1,0:T(8,128)(2,1)} %broadcast_in_dim.20), calls=%async_computation.1 | async-start | bytes 5242880 | tf_op jit(solution)/shard_map/all_to_all | solution.py:310
  119.4 5.4 %shard_map.95 = bf16[384,128]{1,0:T(8,128)(2,1)} custom-call(s32[64]{0:T(128)} %broadcast_multiply_fusion.offsets, s32[3]{0:T(128)} %copy-done, bf16[384,5120]{1,0:T(8,128)(2,1)} %copy-done.1, f32[384,128]{1,0:T(8,128)} %get-tuple-element.64.refs_1_, f32[384,128]{1,0:T(8,128)} %get-tuple-element.65.refs_2_, bf16[4,8,176,128]{3,2,1,0:T(8,128)(2,1)} %all-to-all-done.refs_3_, ...), custom_call_target="tpu_custom_call" | custom-call | flops 3000000000 | bytes 4194304 | tf_op jit(solution)/shard_map/pallas_call | solution.py:363
  124.8 3.5 %collective-permute-start.6 = (bf16[384,128]{1,0:T(8,128)(2,1)}, bf16[384,128]{1,0:T(8,128)(2,1)S(1)}, u32[]{:S(2)}, u32[]{:S(2)}) collective-permute-start(bf16[384,128]{1,0:T(8,128)(2,1)} %shard_map.95), channel_id=1, source_target_pairs={{0,64},{16,80},{32,96},{48,112},{64,0},{80,16},{96,32},{112,48},{1... | collective-permute-start | bytes 294920 | tf_op jit(solution)/shard_map/ppermute | solution.py:254
  131.3 1.9 stack.101.where
  133.1 4.3 %collective-permute-done.6 = bf16[384,128]{1,0:T(8,128)(2,1)S(1)} collective-permute-done((bf16[384,128]{1,0:T(8,128)(2,1)}, bf16[384,128]{1,0:T(8,128)(2,1)S(1)}, u32[]{:S(2)}, u32[]{:S(2)}) %collective-permute-start.6) | collective-permute-done | bytes 98336 | tf_op jit(solution)/shard_map/ppermute | solution.py:254
  138.4 2.0 collective-permute-start.7
  140.4 6.1 %collective-permute-done.7 = bf16[2,384,128]{2,1,0:T(8,128)(2,1)} collective-permute-done((bf16[2,384,128]{2,1,0:T(8,128)(2,1)S(1)}, bf16[2,384,128]{2,1,0:T(8,128)(2,1)}, u32[]{:S(2)}, u32[]{:S(2)}) %collective-permute-start.7) | collective-permute-done | bytes 196640 | tf_op jit(solution)/shard_map/ppermute | solution.py:254
  149.0 6.0 %shard_map.96 = bf16[2,2,192,128]{3,2,1,0:T(8,128)(2,1)} custom-call(s32[64]{0:T(128)} %broadcast_multiply_fusion.offsets, s32[3]{0:T(128)} %copy-done, bf16[384,5120]{1,0:T(8,128)(2,1)} %copy-done.1, f32[384,128]{1,0:T(8,128)} %get-tuple-element.64.refs_1_, f32[384,128]{1,0:T(8,128)} %get-tuple-element.65.refs_2_, bf16[4,8,160,256]{3,2,1,0:T(8,128)(2,1)} %copy-done.2, ...), custom_call_target="tpu_custom_call" | custom-call | flops 3000000000 | bytes 4194304 | tf_op jit(solution)/shard_map/pallas_call | solution.py:363
  155.9 9.3 %collective-permute-start.8 = (bf16[2,192,128]{2,1,0:T(8,128)(2,1)S(1)}, bf16[2,192,128]{2,1,0:T(8,128)(2,1)S(1)}, u32[]{:S(2)}, u32[]{:S(2)}) collective-permute-start(bf16[2,192,128]{2,1,0:T(8,128)(2,1)S(1)} %get-tuple-element.52), channel_id=1, source_target_pairs={{0,8},{8,0},{1,9},{9,1},{2,10},{10,2},{3,11},{11,3},{4,12},{12,4},... | collective-permute-start | bytes 294920 | tf_op jit(solution)/shard_map/ppermute | solution.py:393
  165.2 1.9 collective-permute-start.12
  169.8 1.9 collective-permute-start.9
  171.7 4.4 %collective-permute-done.10.near = bf16[768,128]{1,0:T(8,128)(2,1)S(1)} collective-permute-done((bf16[768,128]{1,0:T(8,128)(2,1)S(1)}, bf16[768,128]{1,0:T(8,128)(2,1)S(1)}, u32[]{:S(2)}, u32[]{:S(2)}) %collective-permute-start.10) | collective-permute-done | bytes 196640 | tf_op jit(solution)/shard_map/ppermute | solution.py:396
  176.1 2.9 %collective-permute-done.11.far = bf16[768,128]{1,0:T(8,128)(2,1)S(1)} collective-permute-done((bf16[768,128]{1,0:T(8,128)(2,1)S(1)}, bf16[768,128]{1,0:T(8,128)(2,1)S(1)}, u32[]{:S(2)}, u32[]{:S(2)}) %collective-permute-start.11) | collective-permute-done | bytes 196640 | tf_op jit(solution)/shard_map/ppermute | solution.py:397
  179.0 2.7 %collective-permute-start.13 = (bf16[4,384,128]{2,1,0:T(8,128)(2,1)S(1)}, bf16[4,384,128]{2,1,0:T(8,128)(2,1)S(1)}, u32[]{:S(2)}, u32[]{:S(2)}) collective-permute-start(bf16[4,384,128]{2,1,0:T(8,128)(2,1)S(1)} %collective-permute-done.12.refs_1_), channel_id=1, source_target_pairs={{0,8},{8,0},{1,9},{9,1},{2,10},{10,2},{3,11},{11,3},{4,12},{12,4},... | collective-permute-start | bytes 1179656 | tf_op jit(solution)/shard_map/ppermute | solution.py:398
  184.6 14.7 %collective-permute-start.14 = (bf16[816,128]{1,0:T(8,128)(2,1)S(1)}, bf16[816,128]{1,0:T(8,128)(2,1)S(1)}, u32[]{:S(2)}, u32[]{:S(2)}) collective-permute-start(bf16[816,128]{1,0:T(8,128)(2,1)S(1)} %get-tuple-element.45), channel_id=1, source_target_pairs={{0,128},{128,256},{256,384},{1,129},{129,257},{257,385},{2,130},{1... | collective-permute-start | bytes 626696 | tf_op jit(solution)/shard_map/ppermute | solution.py:410
  200.7 2.4 %shard_map.98 = (f32[768,128]{1,0:T(8,128)S(1)}, f32[768,1]{1,0:T(8,128)S(1)}) custom-call(s32[12]{0:T(128)S(1)} %stack.101.where, s32[3,192,1]{2,1,0:T(8,128)S(1)} %broadcast_subtract_fusion.begins, bf16[768,128]{1,0:T(8,128)(2,1)S(1)} %bitcast.56, bf16[3072,128]{1,0:T(8,128)(2,1)S(1)} %get-tuple-element.41.keys, bf16[3072,256]{1,0:T(8,128)(2,1)S(1)} %get-tuple-element.42.values), custom_call_target="tpu_custom_call" | custom-call | flops 10000000000 | bytes 4194304 | tf_op jit(solution)/shard_map/pallas_call | solution.py:412
  203.5 4.5 %collective-permute-done.15.r2 = bf16[816,128]{1,0:T(8,128)(2,1)S(1)} collective-permute-done((bf16[816,128]{1,0:T(8,128)(2,1)S(1)}, bf16[816,128]{1,0:T(8,128)(2,1)S(1)}, u32[]{:S(2)}, u32[]{:S(2)}) %collective-permute-start.15) | collective-permute-done | bytes 208928 | tf_op jit(solution)/shard_map/ppermute | solution.py:411
  208.0 2.0 shard_map.99
  (80 shorter events, 24.0 us)
Async XLA Ops:
  0.6 13.8 %copy-start.4 = (bf16[192,640]{1,0:T(8,128)(2,1)S(1)}, bf16[192,640]{1,0:T(8,128)(2,1)}, u32[]{:S(2)}) copy-start(bf16[192,640]{1,0:T(8,128)(2,1)} %param.7) | copy-start | bytes 737284
  11.0 27.3 %collective-permute-start = (bf16[1,176,384]{2,1,0:T(8,128)(2,1)S(1)}, bf16[1,176,384]{2,1,0:T(8,128)(2,1)S(1)}, u32[]{:S(2)}, u32[]{:S(2)}) collective-permute-start(bf16[1,176,384]{2,1,0:T(8,128)(2,1)S(1)} %fusion.4), channel_id=1, source_target_pairs={{0,64},{16,80},{32,96},{48,112},{64,0},{80,16},{96,32},{112,48},{1... | collective-permute-start | bytes 405512 | tf_op jit(solution)/shard_map/ppermute | solution.py:254
  14.4 23.8 %collective-permute-start.1 = (bf16[192,640]{1,0:T(8,128)(2,1)S(1)}, bf16[192,640]{1,0:T(8,128)(2,1)S(1)}, u32[]{:S(2)}, u32[]{:S(2)}) collective-permute-start(bf16[192,640]{1,0:T(8,128)(2,1)S(1)} %copy-done.4), channel_id=1, source_target_pairs={{0,1},{1,0},{2,3},{3,2},{4,5},{5,4},{6,7},{7,6},{8,9},{9,8},{10,11... | collective-permute-start | bytes 737288 | tf_op jit(solution)/shard_map/ppermute | solution.py:289
  38.3 34.6 %collective-permute-start.3 = (bf16[4,192,640]{2,1,0:T(8,128)(2,1)S(1)}, bf16[4,192,640]{2,1,0:T(8,128)(2,1)S(1)}, u32[]{:S(2)}, u32[]{:S(2)}) collective-permute-start(bf16[4,192,640]{2,1,0:T(8,128)(2,1)S(1)} %bitcast.50), channel_id=1, source_target_pairs={{0,8},{8,0},{1,9},{9,1},{2,10},{10,2},{3,11},{11,3},{4,12},{12,4},... | collective-permute-start | bytes 2949128 | tf_op jit(solution)/shard_map/ppermute | solution.py:295
  42.2 30.6 %collective-permute-start.2 = (bf16[2,176,384]{2,1,0:T(8,128)(2,1)S(1)}, bf16[2,176,384]{2,1,0:T(8,128)(2,1)S(1)}, u32[]{:S(2)}, u32[]{:S(2)}) collective-permute-start(bf16[2,176,384]{2,1,0:T(8,128)(2,1)S(1)} %pad_maximum_fusion.4), channel_id=1, source_target_pairs={{0,32},{16,48},{32,0},{48,16},{64,96},{80,112},{96,64},{112,80},{1... | collective-permute-start | bytes 811016 | tf_op jit(solution)/shard_map/ppermute | solution.py:254
  72.9 16.1 %collective-permute-start.5 = (bf16[4,176,384]{2,1,0:T(8,128)(2,1)S(1)}, bf16[4,176,384]{2,1,0:T(8,128)(2,1)S(1)}, u32[]{:S(2)}, u32[]{:S(2)}) collective-permute-start(bf16[4,176,384]{2,1,0:T(8,128)(2,1)S(1)} %pad_maximum_fusion.1), channel_id=1, source_target_pairs={{0,16},{16,0},{32,48},{48,32},{64,80},{80,64},{96,112},{112,96},{1... | collective-permute-start | bytes 1622024 | tf_op jit(solution)/shard_map/ppermute | solution.py:254
  78.6 19.2 %collective-permute-start.4 = (bf16[4,192,640]{2,1,0:T(8,128)(2,1)S(1)}, bf16[4,192,640]{2,1,0:T(8,128)(2,1)}, u32[]{:S(2)}, u32[]{:S(2)}) collective-permute-start(bf16[4,192,640]{2,1,0:T(8,128)(2,1)S(1)} %bitcast.52), channel_id=1, source_target_pairs={{0,8},{8,0},{1,9},{9,1},{2,10},{10,2},{3,11},{11,3},{4,12},{12,4},... | collective-permute-start | bytes 2949128 | tf_op jit(solution)/shard_map/ppermute | solution.py:301
  89.0 0.8 copy-start.3
  91.2 4.5 %copy-start.6 = (bf16[5120]{0:T(1024)(128)(2,1)S(1)}, bf16[5120]{0:T(1024)(128)(2,1)}, u32[]{:S(2)}) copy-start(bf16[5120]{0:T(1024)(128)(2,1)} %param.8) | copy-start | bytes 30724
  91.2 4.7 %copy-start.7 = (s32[64]{0:T(128)S(1)}, s32[64]{0:T(128)}, u32[]{:S(2)}) copy-start(s32[64]{0:T(128)} %param.13) | copy-start | bytes 772
  91.2 21.1 %all-to-all-start = ((bf16[4,8,176,128]{3,2,1,0:T(8,128)(2,1)}), bf16[4,8,176,128]{3,2,1,0:T(8,128)(2,1)}, u32[]{:S(2)}, u32[]{:S(2)}) async-start(bf16[4,8,176,128]{3,2,1,0:T(8,128)(2,1)} %broadcast_in_dim.21), calls=%async_computation | async-start | bytes 2883584 | tf_op jit(solution)/shard_map/all_to_all | solution.py:307
  95.9 3.7 %copy-start = (s32[3]{0:T(128)}, s32[3]{0:T(128)S(1)}, u32[]{:S(2)}) copy-start(s32[3]{0:T(128)S(1)} %pad_add_fusion.1.where) | copy-start | bytes 40
  103.5 1.9 copy-start.1
  113.9 33.5 %all-to-all-start.1 = ((bf16[4,8,160,256]{3,2,1,0:T(8,128)(2,1)}), bf16[4,8,160,256]{3,2,1,0:T(8,128)(2,1)S(1)}, u32[]{:S(2)}, u32[]{:S(2)}) async-start(bf16[4,8,160,256]{3,2,1,0:T(8,128)(2,1)} %broadcast_in_dim.20), calls=%async_computation.1 | async-start | bytes 5242880 | tf_op jit(solution)/shard_map/all_to_all | solution.py:310
  124.8 12.6 %collective-permute-start.6 = (bf16[384,128]{1,0:T(8,128)(2,1)}, bf16[384,128]{1,0:T(8,128)(2,1)S(1)}, u32[]{:S(2)}, u32[]{:S(2)}) collective-permute-start(bf16[384,128]{1,0:T(8,128)(2,1)} %shard_map.95), channel_id=1, source_target_pairs={{0,64},{16,80},{32,96},{48,112},{64,0},{80,16},{96,32},{112,48},{1... | collective-permute-start | bytes 294920 | tf_op jit(solution)/shard_map/ppermute | solution.py:254
  138.4 8.1 %collective-permute-start.7 = (bf16[2,384,128]{2,1,0:T(8,128)(2,1)S(1)}, bf16[2,384,128]{2,1,0:T(8,128)(2,1)}, u32[]{:S(2)}, u32[]{:S(2)}) collective-permute-start(bf16[2,384,128]{2,1,0:T(8,128)(2,1)S(1)} %pad_maximum_fusion.7), channel_id=1, source_target_pairs={{0,32},{16,48},{32,0},{48,16},{64,96},{80,112},{96,64},{112,80},{1... | collective-permute-start | bytes 589832 | tf_op jit(solution)/shard_map/ppermute | solution.py:254
  147.4 1.5 copy-start.2
  149.0 32.9 %copy-start.5 = (bf16[384,128]{1,0:T(8,128)(2,1)S(1)}, bf16[384,128]{1,0:T(8,128)(2,1)}, u32[]{:S(2)}) copy-start(bf16[384,128]{1,0:T(8,128)(2,1)} %shard_map.95) | copy-start | bytes 294916
  155.9 11.2 %collective-permute-start.8 = (bf16[2,192,128]{2,1,0:T(8,128)(2,1)S(1)}, bf16[2,192,128]{2,1,0:T(8,128)(2,1)S(1)}, u32[]{:S(2)}, u32[]{:S(2)}) collective-permute-start(bf16[2,192,128]{2,1,0:T(8,128)(2,1)S(1)} %get-tuple-element.52), channel_id=1, source_target_pairs={{0,8},{8,0},{1,9},{9,1},{2,10},{10,2},{3,11},{11,3},{4,12},{12,4},... | collective-permute-start | bytes 294920 | tf_op jit(solution)/shard_map/ppermute | solution.py:393
  165.2 13.8 %collective-permute-start.12 = (bf16[4,384,128]{2,1,0:T(8,128)(2,1)S(1)}, bf16[4,384,128]{2,1,0:T(8,128)(2,1)S(1)}, u32[]{:S(2)}, u32[]{:S(2)}) collective-permute-start(bf16[4,384,128]{2,1,0:T(8,128)(2,1)S(1)} %pad_maximum_fusion.2.refs_0_), channel_id=1, source_target_pairs={{0,16},{16,0},{32,48},{48,32},{64,80},{80,64},{96,112},{112,96},{1... | collective-permute-start | bytes 1179656 | tf_op jit(solution)/shard_map/ppermute | solution.py:254
  167.2 8.9 %collective-permute-start.10 = (bf16[768,128]{1,0:T(8,128)(2,1)S(1)}, bf16[768,128]{1,0:T(8,128)(2,1)S(1)}, u32[]{:S(2)}, u32[]{:S(2)}) collective-permute-start(bf16[768,128]{1,0:T(8,128)(2,1)S(1)} %bitcast.54), channel_id=1, source_target_pairs={{128,0},{256,128},{384,256},{129,1},{257,129},{385,257},{130,2},{2... | collective-permute-start | bytes 589832 | tf_op jit(solution)/shard_map/ppermute | solution.py:396
  168.5 10.5 %collective-permute-start.11 = (bf16[768,128]{1,0:T(8,128)(2,1)S(1)}, bf16[768,128]{1,0:T(8,128)(2,1)S(1)}, u32[]{:S(2)}, u32[]{:S(2)}) collective-permute-start(bf16[768,128]{1,0:T(8,128)(2,1)S(1)} %bitcast.55), channel_id=1, source_target_pairs={{256,0},{384,128},{257,1},{385,129},{258,2},{386,130},{259,3},{387... | collective-permute-start | bytes 589832 | tf_op jit(solution)/shard_map/ppermute | solution.py:397
  169.8 12.0 %collective-permute-start.9 = (bf16[4,384,128]{2,1,0:T(8,128)(2,1)S(1)}, bf16[4,384,128]{2,1,0:T(8,128)(2,1)S(1)}, u32[]{:S(2)}, u32[]{:S(2)}) collective-permute-start(bf16[4,384,128]{2,1,0:T(8,128)(2,1)S(1)} %pad_maximum_fusion.2.refs_0_), channel_id=1, source_target_pairs={{0,8},{8,0},{1,9},{9,1},{2,10},{10,2},{3,11},{11,3},{4,12},{12,4},... | collective-permute-start | bytes 1179656 | tf_op jit(solution)/shard_map/ppermute | solution.py:398
  179.0 4.0 %collective-permute-start.13 = (bf16[4,384,128]{2,1,0:T(8,128)(2,1)S(1)}, bf16[4,384,128]{2,1,0:T(8,128)(2,1)S(1)}, u32[]{:S(2)}, u32[]{:S(2)}) collective-permute-start(bf16[4,384,128]{2,1,0:T(8,128)(2,1)S(1)} %collective-permute-done.12.refs_1_), channel_id=1, source_target_pairs={{0,8},{8,0},{1,9},{9,1},{2,10},{10,2},{3,11},{11,3},{4,12},{12,4},... | collective-permute-start | bytes 1179656 | tf_op jit(solution)/shard_map/ppermute | solution.py:398
  184.6 18.9 %collective-permute-start.14 = (bf16[816,128]{1,0:T(8,128)(2,1)S(1)}, bf16[816,128]{1,0:T(8,128)(2,1)S(1)}, u32[]{:S(2)}, u32[]{:S(2)}) collective-permute-start(bf16[816,128]{1,0:T(8,128)(2,1)S(1)} %get-tuple-element.45), channel_id=1, source_target_pairs={{0,128},{128,256},{256,384},{1,129},{129,257},{257,385},{2,130},{1... | collective-permute-start | bytes 626696 | tf_op jit(solution)/shard_map/ppermute | solution.py:410
  199.4 8.6 %collective-permute-start.15 = (bf16[816,128]{1,0:T(8,128)(2,1)S(1)}, bf16[816,128]{1,0:T(8,128)(2,1)S(1)}, u32[]{:S(2)}, u32[]{:S(2)}) collective-permute-start(bf16[816,128]{1,0:T(8,128)(2,1)S(1)} %get-tuple-element.46), channel_id=1, source_target_pairs={{0,256},{128,384},{1,257},{129,385},{2,258},{130,386},{3,259},{131... | collective-permute-start | bytes 626696 | tf_op jit(solution)/shard_map/ppermute | solution.py:411

commit v15 on v13

--- a/solution.py
+++ b/solution.py
@@ -384,10 +384,10 @@
     mine0 = jnp.stack([pair, across(pair, 4)])
     mine0, ranges, begins = lax.optimization_barrier((mine0, ranges, begins))
     mine0 = jnp.concatenate([mine0, across(mine0, 2)], axis=0)
+    mine0, query_blocks = lax.optimization_barrier((mine0, query_blocks))
+    mine1 = across(mine0, 1)
     query = project(query_kernel, (2, 2, rows, 128), query_gain, query_blocks)
 
-    mine0, query = lax.optimization_barrier((mine0, query))
-    mine1 = across(mine0, 1)
     own_query = lax.dynamic_index_in_dim(query, c, 0, keepdims=False)
     sent_query = lax.dynamic_index_in_dim(query, 1 - c, 0, keepdims=False)
     q0 = jnp.concatenate([own_query, lax.ppermute(sent_query, "c", swap)], axis=0)
@@ -395,7 +395,7 @@
     mine = [mine0, mine1]
     q1 = lax.ppermute(q0, "x", [(i, i - 1) for i in range(1, nx)])
     q2 = lax.ppermute(q0, "x", [(i, i - 2) for i in range(2, nx)])
-    other = [lax.ppermute(v, "c", swap) for v in (after(mine0, q0), after(mine1, q1, q2))]
+    other = [lax.ppermute(v, "c", swap) for v in (after(mine0, q0), after(mine1, q0))]
 
     state = [pltpu.VMEM((4 * rows, 256), f32), pltpu.VMEM((4 * rows, 1), f32)]
     r1, r2, keys, values = call(

time: 206 us -> 207 us (level)
  starting transfers between devices: 76.3 us -> 86.7 us
  Pallas kernels: 25.6 us -> 16.7 us
    ppermute x1, starting transfers between devices: 1.3 us -> 11.8 us  [body(): r1 = lax.ppermute(r1, 'x', [(i, i + 1) for i in range(nx - 1)])]
    pallas_call x1, Pallas kernels: 11 us -> 2.07 us  [body(): call(remote_kernel, [jax.ShapeDtypeStruct((4 * rows + 48, 128), bf16)] *...]
  transfers between devices with their start and end apart: 18 -> 18, of which waited for: 9 -> 8; matrix products, arithmetic and copies ran while one was open for 5% -> 5% of each run, Pallas kernels for 5% -> 6%
where the time goes in v15:
time: 207 us; the launch traced here: 206 us
  starting transfers between devices  86.7 us (42%)
  blocking collectives  37.6 us (18%)
  waiting for transfers between devices  37 us (18%)
  local copies, waits for them, and re-layouts  17.5 us (8%)
  Pallas kernels  16.7 us (8%)
  other arithmetic  7.13 us (3%)
  between operations  3.11 us (2%)
    ppermute x6, starting transfers between devices, across(): return lax.ppermute(v, 'z', [(i, i ^ bit) for i in range(8)])  30.6 us
    ppermute x6, waiting for transfers between devices, across(): return lax.ppermute(v, 'z', [(i, i ^ bit) for i in range(8)])  17 us
    all_gather x1, blocking collectives, body(): own_far = lax.all_gather(far, 'y', axis=0)  15.9 us
    all_gather x1, blocking collectives, body(): own_near = lax.all_gather(hidden, 'y', axis=0)  13.2 us
    ppermute x1, starting transfers between devices, body(): r1 = lax.ppermute(r1, 'x', [(i, i + 1) for i in range(nx - 1)])  11.8 us
    unnamed x44, local copies, waits for them, and re-layouts  11.2 us
    ppermute x1, starting transfers between devices, body(): far = lax.ppermute(hidden, 'w', swap)  10.6 us
    ppermute x1, starting transfers between devices, body(): lax.ppermute(sent_query, 'c', swap)  9.18 us
  transfers between devices with their start and end apart: 18, of which 8 were waited for; matrix products, arithmetic and copies ran while one was open for 5% of the time, Pallas kernels for 6%

profile of v15, /device:TPU:1, one launch (start us, length us, event | category | flops | bytes accessed | tf_op | source)
XLA Modules:
  0.0 205.8 jit_solution(16556435356953791981)
XLA Ops:
  2.3 8.5 %all-gather = bf16[192,768]{1,0:T(8,128)(2,1)S(1)} all-gather(bf16[96,768]{1,0:T(8,128)(2,1)S(1)} %fusion.2), channel_id=2, replica_groups=mesh['x'=4,'z'=8,'c'=2,'y'=4,'w'=2] {'c'}, dimensions={0}, use_global_device_ids=true | all-gather | bytes 442368 | tf_op jit(solution)/shard_map/all_gather | solution.py:273
  11.0 3.4 %collective-permute-start = (bf16[1,176,384]{2,1,0:T(8,128)(2,1)S(1)}, bf16[1,176,384]{2,1,0:T(8,128)(2,1)S(1)}, u32[]{:S(2)}, u32[]{:S(2)}) collective-permute-start(bf16[1,176,384]{2,1,0:T(8,128)(2,1)S(1)} %fusion.4), channel_id=1, source_target_pairs={{0,64},{16,80},{32,96},{48,112},{64,0},{80,16},{96,32},{112,48},{1... | collective-permute-start | bytes 405512 | tf_op jit(solution)/shard_map/ppermute | solution.py:254
  14.4 10.6 %collective-permute-start.1 = (bf16[192,640]{1,0:T(8,128)(2,1)S(1)}, bf16[192,640]{1,0:T(8,128)(2,1)S(1)}, u32[]{:S(2)}, u32[]{:S(2)}) collective-permute-start(bf16[192,640]{1,0:T(8,128)(2,1)S(1)} %copy-done.18), channel_id=1, source_target_pairs={{0,1},{1,0},{2,3},{3,2},{4,5},{5,4},{6,7},{7,6},{8,9},{9,8},{10,11... | collective-permute-start | bytes 737288 | tf_op jit(solution)/shard_map/ppermute | solution.py:289
  25.1 13.2 %all-gather.1 = bf16[768,640]{1,0:T(8,128)(2,1)S(1)} all-gather(bf16[192,640]{1,0:T(8,128)(2,1)S(1)} %copy-done.18), channel_id=3, replica_groups=mesh['x'=4,'z'=8,'c'=2,'y'=4,'w'=2] {'y'}, dimensions={0}, use_global_device_ids=true | all-gather | bytes 1228800 | tf_op jit(solution)/shard_map/all_gather | solution.py:290
  38.3 3.9 %collective-permute-start.3 = (bf16[4,192,640]{2,1,0:T(8,128)(2,1)S(1)}, bf16[4,192,640]{2,1,0:T(8,128)(2,1)S(1)}, u32[]{:S(2)}, u32[]{:S(2)}) collective-permute-start(bf16[4,192,640]{2,1,0:T(8,128)(2,1)S(1)} %bitcast.50), channel_id=1, source_target_pairs={{0,8},{8,0},{1,9},{9,1},{2,10},{10,2},{3,11},{11,3},{4,12},{12,4},... | collective-permute-start | bytes 2949128 | tf_op jit(solution)/shard_map/ppermute | solution.py:295
  42.2 14.7 %collective-permute-start.2 = (bf16[2,176,384]{2,1,0:T(8,128)(2,1)S(1)}, bf16[2,176,384]{2,1,0:T(8,128)(2,1)S(1)}, u32[]{:S(2)}, u32[]{:S(2)}) collective-permute-start(bf16[2,176,384]{2,1,0:T(8,128)(2,1)S(1)} %pad_maximum_fusion.4), channel_id=1, source_target_pairs={{0,32},{16,48},{32,0},{48,16},{64,96},{80,112},{96,64},{112,80},{1... | collective-permute-start | bytes 811016 | tf_op jit(solution)/shard_map/ppermute | solution.py:254
  56.9 15.9 %all-gather.2 = bf16[768,640]{1,0:T(8,128)(2,1)S(1)} all-gather(bf16[192,640]{1,0:T(8,128)(2,1)S(1)} %collective-permute-done.1), channel_id=4, replica_groups=mesh['x'=4,'z'=8,'c'=2,'y'=4,'w'=2] {'y'}, dimensions={0}, use_global_device_ids=true | all-gather | bytes 1228800 | tf_op jit(solution)/shard_map/all_gather | solution.py:296
  73.9 5.6 %collective-permute-start.5 = (bf16[4,176,384]{2,1,0:T(8,128)(2,1)S(1)}, bf16[4,176,384]{2,1,0:T(8,128)(2,1)S(1)}, u32[]{:S(2)}, u32[]{:S(2)}) collective-permute-start(bf16[4,176,384]{2,1,0:T(8,128)(2,1)S(1)} %pad_maximum_fusion.1), channel_id=1, source_target_pairs={{0,16},{16,0},{32,48},{48,32},{64,80},{80,64},{96,112},{112,96},{1... | collective-permute-start | bytes 1622024 | tf_op jit(solution)/shard_map/ppermute | solution.py:254
  79.6 4.3 %collective-permute-start.4 = (bf16[4,192,640]{2,1,0:T(8,128)(2,1)S(1)}, bf16[4,192,640]{2,1,0:T(8,128)(2,1)}, u32[]{:S(2)}, u32[]{:S(2)}) collective-permute-start(bf16[4,192,640]{2,1,0:T(8,128)(2,1)S(1)} %bitcast.52), channel_id=1, source_target_pairs={{0,8},{8,0},{1,9},{9,1},{2,10},{10,2},{3,11},{11,3},{4,12},{12,4},... | collective-permute-start | bytes 2949128 | tf_op jit(solution)/shard_map/ppermute | solution.py:301
  83.9 6.1 %collective-permute-done.5 = bf16[4,176,384]{2,1,0:T(8,128)(2,1)S(1)} collective-permute-done((bf16[4,176,384]{2,1,0:T(8,128)(2,1)S(1)}, bf16[4,176,384]{2,1,0:T(8,128)(2,1)S(1)}, u32[]{:S(2)}, u32[]{:S(2)}) %collective-permute-start.5) | collective-permute-done | bytes 540704 | tf_op jit(solution)/shard_map/ppermute | solution.py:254
  92.2 4.3 %all-to-all-start = ((bf16[4,8,176,128]{3,2,1,0:T(8,128)(2,1)}), bf16[4,8,176,128]{3,2,1,0:T(8,128)(2,1)S(1)}, u32[]{:S(2)}, u32[]{:S(2)}) async-start(bf16[4,8,176,128]{3,2,1,0:T(8,128)(2,1)} %broadcast_in_dim.21), calls=%async_computation | async-start | bytes 2883584 | tf_op jit(solution)/shard_map/all_to_all | solution.py:307
  100.0 3.8 %shard_map.94.refs_0_ = bf16[384,5120]{1,0:T(8,128)(2,1)S(1)} custom-call(s32[3]{0:T(128)S(1)} %pad_add_fusion.1.where, f32[1,5120]{1,0:T(1,128)S(1)} %bitcast.58, bf16[4,192,640]{2,1,0:T(8,128)(2,1)S(1)} %bitcast.51, bf16[4,192,640]{2,1,0:T(8,128)(2,1)S(1)} %bitcast.53, bf16[4,192,640]{2,1,0:T(8,128)(2,1)S(1)} %copy-done.7, ...), custom_call_target="tpu_custom_call" | custom-call | flops 4000000000 | bytes 4194304 | tf_op jit(solution)/shard_map/pallas_call | solution.py:314
  105.7 7.2 %all-to-all-done.refs_3_ = bf16[4,8,176,128]{3,2,1,0:T(8,128)(2,1)S(1)} async-done(((bf16[4,8,176,128]{3,2,1,0:T(8,128)(2,1)}), bf16[4,8,176,128]{3,2,1,0:T(8,128)(2,1)S(1)}, u32[]{:S(2)}, u32[]{:S(2)}) %all-to-all-start) | async-done | bytes 1441824 | tf_op jit(solution)/shard_map/all_to_all | solution.py:307
  114.8 3.7 %all-to-all-start.1 = ((bf16[4,8,160,256]{3,2,1,0:T(8,128)(2,1)}), bf16[4,8,160,256]{3,2,1,0:T(8,128)(2,1)S(1)}, u32[]{:S(2)}, u32[]{:S(2)}) async-start(bf16[4,8,160,256]{3,2,1,0:T(8,128)(2,1)} %broadcast_in_dim.20), calls=%async_computation.1 | async-start | bytes 5242880 | tf_op jit(solution)/shard_map/all_to_all | solution.py:310
  119.8 2.1 %copy-done.11 = bf16[384,5120]{1,0:T(8,128)(2,1)S(1)} copy-done((bf16[384,5120]{1,0:T(8,128)(2,1)S(1)}, bf16[384,5120]{1,0:T(8,128)(2,1)}, u32[]{:S(2)}) %copy-start.11) | copy-done | bytes 3932184
  121.9 3.1 %shard_map.95 = bf16[384,128]{1,0:T(8,128)(2,1)S(1)} custom-call(s32[64]{0:T(128)S(1)} %broadcast_multiply_fusion.offsets, s32[3]{0:T(128)S(1)} %pad_add_fusion.1.where, bf16[384,5120]{1,0:T(8,128)(2,1)S(1)} %copy-done.11, f32[384,128]{1,0:T(8,128)S(1)} %get-tuple-element.64.refs_1_, f32[384,128]{1,0:T(8,128)S(1)} %get-tuple-element.65.refs_2_, ...), custom_call_target="tpu_custom_call" | custom-call | flops 3000000000 | bytes 4194304 | tf_op jit(solution)/shard_map/pallas_call | solution.py:363
  125.1 3.1 %collective-permute-start.6 = (bf16[384,128]{1,0:T(8,128)(2,1)S(1)}, bf16[384,128]{1,0:T(8,128)(2,1)S(1)}, u32[]{:S(2)}, u32[]{:S(2)}) collective-permute-start(bf16[384,128]{1,0:T(8,128)(2,1)S(1)} %shard_map.95), channel_id=1, source_target_pairs={{0,64},{16,80},{32,96},{48,112},{64,0},{80,16},{96,32},{112,48},{1... | collective-permute-start | bytes 294920 | tf_op jit(solution)/shard_map/ppermute | solution.py:254
  131.2 2.0 stack.101.where
  133.2 4.3 %collective-permute-done.6 = bf16[384,128]{1,0:T(8,128)(2,1)S(1)} collective-permute-done((bf16[384,128]{1,0:T(8,128)(2,1)S(1)}, bf16[384,128]{1,0:T(8,128)(2,1)S(1)}, u32[]{:S(2)}, u32[]{:S(2)}) %collective-permute-start.6) | collective-permute-done | bytes 98336 | tf_op jit(solution)/shard_map/ppermute | solution.py:254
  139.5 6.6 %collective-permute-done.7 = bf16[2,384,128]{2,1,0:T(8,128)(2,1)} collective-permute-done((bf16[2,384,128]{2,1,0:T(8,128)(2,1)S(1)}, bf16[2,384,128]{2,1,0:T(8,128)(2,1)}, u32[]{:S(2)}, u32[]{:S(2)}) %collective-permute-start.7) | collective-permute-done | bytes 196640 | tf_op jit(solution)/shard_map/ppermute | solution.py:254
  151.0 2.1 %copy-done.12 = bf16[384,5120]{1,0:T(8,128)(2,1)S(1)} copy-done((bf16[384,5120]{1,0:T(8,128)(2,1)S(1)}, bf16[384,5120]{1,0:T(8,128)(2,1)}, u32[]{:S(2)}) %copy-start.12) | copy-done | bytes 3932184
  153.1 3.1 %shard_map.96 = bf16[2,2,192,128]{3,2,1,0:T(8,128)(2,1)S(1)} custom-call(s32[64]{0:T(128)S(1)} %broadcast_multiply_fusion.offsets, s32[3]{0:T(128)S(1)} %pad_add_fusion.1.where, bf16[384,5120]{1,0:T(8,128)(2,1)S(1)} %copy-done.12, f32[384,128]{1,0:T(8,128)S(1)} %copy-done.3, f32[384,128]{1,0:T(8,128)S(1)} %copy-done.5, ...), custom_call_target="tpu_custom_call" | custom-call | flops 3000000000 | bytes 4194304 | tf_op jit(solution)/shard_map/pallas_call | solution.py:363
  156.3 9.2 %collective-permute-start.8 = (bf16[2,192,128]{2,1,0:T(8,128)(2,1)S(1)}, bf16[2,192,128]{2,1,0:T(8,128)(2,1)S(1)}, u32[]{:S(2)}, u32[]{:S(2)}) collective-permute-start(bf16[2,192,128]{2,1,0:T(8,128)(2,1)S(1)} %get-tuple-element.52), channel_id=1, source_target_pairs={{0,8},{8,0},{1,9},{9,1},{2,10},{10,2},{3,11},{11,3},{4,12},{12,4},... | collective-permute-start | bytes 294920 | tf_op jit(solution)/shard_map/ppermute | solution.py:393
  166.4 2.3 %collective-permute-start.9 = (bf16[4,384,128]{2,1,0:T(8,128)(2,1)S(1)}, bf16[4,384,128]{2,1,0:T(8,128)(2,1)S(1)}, u32[]{:S(2)}, u32[]{:S(2)}) collective-permute-start(bf16[4,384,128]{2,1,0:T(8,128)(2,1)S(1)} %pad_maximum_fusion.2.refs_0_), channel_id=1, source_target_pairs={{0,8},{8,0},{1,9},{9,1},{2,10},{10,2},{3,11},{11,3},{4,12},{12,4},... | collective-permute-start | bytes 1179656 | tf_op jit(solution)/shard_map/ppermute | solution.py:398
  168.7 2.1 %collective-permute-start.13 = (bf16[4,384,128]{2,1,0:T(8,128)(2,1)}, bf16[4,384,128]{2,1,0:T(8,128)(2,1)S(1)}, u32[]{:S(2)}, u32[]{:S(2)}) collective-permute-start(bf16[4,384,128]{2,1,0:T(8,128)(2,1)} %collective-permute-done.12.refs_1_), channel_id=1, source_target_pairs={{0,8},{8,0},{1,9},{9,1},{2,10},{10,2},{3,11},{11,3},{4,12},{12,4},... | collective-permute-start | bytes 1179656 | tf_op jit(solution)/shard_map/ppermute | solution.py:398
  174.1 5.2 %collective-permute-done.10.near = bf16[768,128]{1,0:T(8,128)(2,1)S(1)} collective-permute-done((bf16[768,128]{1,0:T(8,128)(2,1)S(1)}, bf16[768,128]{1,0:T(8,128)(2,1)S(1)}, u32[]{:S(2)}, u32[]{:S(2)}) %collective-permute-start.10) | collective-permute-done | bytes 196640 | tf_op jit(solution)/shard_map/ppermute | solution.py:396
  179.3 2.8 %collective-permute-done.11.far = bf16[768,128]{1,0:T(8,128)(2,1)S(1)} collective-permute-done((bf16[768,128]{1,0:T(8,128)(2,1)S(1)}, bf16[768,128]{1,0:T(8,128)(2,1)S(1)}, u32[]{:S(2)}, u32[]{:S(2)}) %collective-permute-start.11) | collective-permute-done | bytes 196640 | tf_op jit(solution)/shard_map/ppermute | solution.py:397
  182.1 2.1 %shard_map.97 = (bf16[816,128]{1,0:T(8,128)(2,1)S(1)}, bf16[816,128]{1,0:T(8,128)(2,1)S(1)}, bf16[3072,128]{1,0:T(8,128)(2,1)S(1)}, bf16[3072,256]{1,0:T(8,128)(2,1)S(1)}) custom-call(s32[12]{0:T(128)S(1)} %stack.101.where, s32[3,192,1]{2,1,0:T(8,128)S(1)} %broadcast_subtract_fusion.begins, bf16[768,128]{1,0:T(8,128)(2,1)S(1)} %collective-permute-done.10.near, ...), custom_call_target="tpu_custom_call" | custom-call | flops 10000000000 | bytes 4194304 | tf_op jit(solution)/shard_map/pallas_call | solution.py:401
  184.2 11.8 %collective-permute-start.14 = (bf16[816,128]{1,0:T(8,128)(2,1)S(1)}, bf16[816,128]{1,0:T(8,128)(2,1)S(1)}, u32[]{:S(2)}, u32[]{:S(2)}) collective-permute-start(bf16[816,128]{1,0:T(8,128)(2,1)S(1)} %get-tuple-element.45), channel_id=1, source_target_pairs={{0,128},{128,256},{256,384},{1,129},{129,257},{257,385},{2,130},{1... | collective-permute-start | bytes 626696 | tf_op jit(solution)/shard_map/ppermute | solution.py:410
  197.3 2.5 %shard_map.98 = (f32[768,128]{1,0:T(8,128)S(1)}, f32[768,1]{1,0:T(8,128)S(1)}) custom-call(s32[12]{0:T(128)S(1)} %stack.101.where, s32[3,192,1]{2,1,0:T(8,128)S(1)} %broadcast_subtract_fusion.begins, bf16[768,128]{1,0:T(8,128)(2,1)S(1)} %bitcast.57, bf16[3072,128]{1,0:T(8,128)(2,1)S(1)} %get-tuple-element.41.keys, bf16[3072,256]{1,0:T(8,128)(2,1)S(1)} %get-tuple-element.42.values), custom_call_target="tpu_custom_call" | custom-call | flops 10000000000 | bytes 4194304 | tf_op jit(solution)/shard_map/pallas_call | solution.py:412
  199.8 3.9 %collective-permute-done.15.r2 = bf16[816,128]{1,0:T(8,128)(2,1)S(1)} collective-permute-done((bf16[816,128]{1,0:T(8,128)(2,1)S(1)}, bf16[816,128]{1,0:T(8,128)(2,1)S(1)}, u32[]{:S(2)}, u32[]{:S(2)}) %collective-permute-start.15) | collective-permute-done | bytes 208928 | tf_op jit(solution)/shard_map/ppermute | solution.py:411
  203.7 2.0 shard_map.99
  (106 shorter events, 27.1 us)
Async XLA Ops:
  0.6 13.8 %copy-start.18 = (bf16[192,640]{1,0:T(8,128)(2,1)S(1)}, bf16[192,640]{1,0:T(8,128)(2,1)}, u32[]{:S(2)}) copy-start(bf16[192,640]{1,0:T(8,128)(2,1)} %param.7) | copy-start | bytes 737284
  11.0 79.0 %copy-start.13 = (bf16[1,176,384]{2,1,0:T(8,128)(2,1)}, bf16[1,176,384]{2,1,0:T(8,128)(2,1)S(1)}, u32[]{:S(2)}) copy-start(bf16[1,176,384]{2,1,0:T(8,128)(2,1)S(1)} %fusion.4) | copy-start | bytes 405508
  11.0 27.3 %collective-permute-start = (bf16[1,176,384]{2,1,0:T(8,128)(2,1)S(1)}, bf16[1,176,384]{2,1,0:T(8,128)(2,1)S(1)}, u32[]{:S(2)}, u32[]{:S(2)}) collective-permute-start(bf16[1,176,384]{2,1,0:T(8,128)(2,1)S(1)} %fusion.4), channel_id=1, source_target_pairs={{0,64},{16,80},{32,96},{48,112},{64,0},{80,16},{96,32},{112,48},{1... | collective-permute-start | bytes 405512 | tf_op jit(solution)/shard_map/ppermute | solution.py:254
  14.4 23.8 %collective-permute-start.1 = (bf16[192,640]{1,0:T(8,128)(2,1)S(1)}, bf16[192,640]{1,0:T(8,128)(2,1)S(1)}, u32[]{:S(2)}, u32[]{:S(2)}) collective-permute-start(bf16[192,640]{1,0:T(8,128)(2,1)S(1)} %copy-done.18), channel_id=1, source_target_pairs={{0,1},{1,0},{2,3},{3,2},{4,5},{5,4},{6,7},{7,6},{8,9},{9,8},{10,11... | collective-permute-start | bytes 737288 | tf_op jit(solution)/shard_map/ppermute | solution.py:289
  38.3 51.7 %copy-start.15 = (bf16[1,176,384]{2,1,0:T(8,128)(2,1)}, bf16[1,176,384]{2,1,0:T(8,128)(2,1)S(1)}, u32[]{:S(2)}) copy-start(bf16[1,176,384]{2,1,0:T(8,128)(2,1)S(1)} %collective-permute-done) | copy-start | bytes 405508
  38.3 34.6 %collective-permute-start.3 = (bf16[4,192,640]{2,1,0:T(8,128)(2,1)S(1)}, bf16[4,192,640]{2,1,0:T(8,128)(2,1)S(1)}, u32[]{:S(2)}, u32[]{:S(2)}) collective-permute-start(bf16[4,192,640]{2,1,0:T(8,128)(2,1)S(1)} %bitcast.50), channel_id=1, source_target_pairs={{0,8},{8,0},{1,9},{9,1},{2,10},{10,2},{3,11},{11,3},{4,12},{12,4},... | collective-permute-start | bytes 2949128 | tf_op jit(solution)/shard_map/ppermute | solution.py:295
  42.2 30.6 %collective-permute-start.2 = (bf16[2,176,384]{2,1,0:T(8,128)(2,1)S(1)}, bf16[2,176,384]{2,1,0:T(8,128)(2,1)S(1)}, u32[]{:S(2)}, u32[]{:S(2)}) collective-permute-start(bf16[2,176,384]{2,1,0:T(8,128)(2,1)S(1)} %pad_maximum_fusion.4), channel_id=1, source_target_pairs={{0,32},{16,48},{32,0},{48,16},{64,96},{80,112},{96,64},{112,80},{1... | collective-permute-start | bytes 811016 | tf_op jit(solution)/shard_map/ppermute | solution.py:254
  72.8 17.1 %copy-start.14 = (bf16[2,176,384]{2,1,0:T(8,128)(2,1)}, bf16[2,176,384]{2,1,0:T(8,128)(2,1)S(1)}, u32[]{:S(2)}) copy-start(bf16[2,176,384]{2,1,0:T(8,128)(2,1)S(1)} %collective-permute-done.2) | copy-start | bytes 811012
  73.9 16.1 %collective-permute-start.5 = (bf16[4,176,384]{2,1,0:T(8,128)(2,1)S(1)}, bf16[4,176,384]{2,1,0:T(8,128)(2,1)S(1)}, u32[]{:S(2)}, u32[]{:S(2)}) collective-permute-start(bf16[4,176,384]{2,1,0:T(8,128)(2,1)S(1)} %pad_maximum_fusion.1), channel_id=1, source_target_pairs={{0,16},{16,0},{32,48},{48,32},{64,80},{80,64},{96,112},{112,96},{1... | collective-permute-start | bytes 1622024 | tf_op jit(solution)/shard_map/ppermute | solution.py:254
  79.6 18.6 %collective-permute-start.4 = (bf16[4,192,640]{2,1,0:T(8,128)(2,1)S(1)}, bf16[4,192,640]{2,1,0:T(8,128)(2,1)}, u32[]{:S(2)}, u32[]{:S(2)}) collective-permute-start(bf16[4,192,640]{2,1,0:T(8,128)(2,1)S(1)} %bitcast.52), channel_id=1, source_target_pairs={{0,8},{8,0},{1,9},{9,1},{2,10},{10,2},{3,11},{11,3},{4,12},{12,4},... | collective-permute-start | bytes 2949128 | tf_op jit(solution)/shard_map/ppermute | solution.py:301
  92.2 4.3 %copy-start.19 = (bf16[5120]{0:T(1024)(128)(2,1)S(1)}, bf16[5120]{0:T(1024)(128)(2,1)}, u32[]{:S(2)}) copy-start(bf16[5120]{0:T(1024)(128)(2,1)} %param.8) | copy-start | bytes 30724
  92.2 4.5 %copy-start.20 = (s32[64]{0:T(128)S(1)}, s32[64]{0:T(128)}, u32[]{:S(2)}) copy-start(s32[64]{0:T(128)} %param.13) | copy-start | bytes 772
  92.2 20.7 %all-to-all-start = ((bf16[4,8,176,128]{3,2,1,0:T(8,128)(2,1)}), bf16[4,8,176,128]{3,2,1,0:T(8,128)(2,1)S(1)}, u32[]{:S(2)}, u32[]{:S(2)}) async-start(bf16[4,8,176,128]{3,2,1,0:T(8,128)(2,1)} %broadcast_in_dim.21), calls=%async_computation | async-start | bytes 2883584 | tf_op jit(solution)/shard_map/all_to_all | solution.py:307
  98.2 1.8 copy-start.7
  103.9 1.9 copy-start.10
  114.8 32.4 %all-to-all-start.1 = ((bf16[4,8,160,256]{3,2,1,0:T(8,128)(2,1)}), bf16[4,8,160,256]{3,2,1,0:T(8,128)(2,1)S(1)}, u32[]{:S(2)}, u32[]{:S(2)}) async-start(bf16[4,8,160,256]{3,2,1,0:T(8,128)(2,1)} %broadcast_in_dim.20), calls=%async_computation.1 | async-start | bytes 5242880 | tf_op jit(solution)/shard_map/all_to_all | solution.py:310
  119.5 5.5 %copy-start.2 = (f32[384,128]{1,0:T(8,128)}, f32[384,128]{1,0:T(8,128)S(1)}, u32[]{:S(2)}) copy-start(f32[384,128]{1,0:T(8,128)S(1)} %get-tuple-element.64.refs_1_) | copy-start | bytes 589828
  119.5 5.5 %copy-start.4 = (f32[384,128]{1,0:T(8,128)}, f32[384,128]{1,0:T(8,128)S(1)}, u32[]{:S(2)}) copy-start(f32[384,128]{1,0:T(8,128)S(1)} %get-tuple-element.65.refs_2_) | copy-start | bytes 589828
  119.8 2.1 %copy-start.11 = (bf16[384,5120]{1,0:T(8,128)(2,1)S(1)}, bf16[384,5120]{1,0:T(8,128)(2,1)}, u32[]{:S(2)}) copy-start(bf16[384,5120]{1,0:T(8,128)(2,1)} %copy-done.10) | copy-start | bytes 11796484
  125.1 24.0 %copy-start.9 = (f32[128]{0:T(128)S(1)}, f32[128]{0:T(128)}, u32[]{:S(2)}) copy-start(f32[128]{0:T(128)} %param.9) | copy-start | bytes 1540
  125.1 12.4 %collective-permute-start.6 = (bf16[384,128]{1,0:T(8,128)(2,1)S(1)}, bf16[384,128]{1,0:T(8,128)(2,1)S(1)}, u32[]{:S(2)}, u32[]{:S(2)}) collective-permute-start(bf16[384,128]{1,0:T(8,128)(2,1)S(1)} %shard_map.95), channel_id=1, source_target_pairs={{0,64},{16,80},{32,96},{48,112},{64,0},{80,16},{96,32},{112,48},{1... | collective-permute-start | bytes 294920 | tf_op jit(solution)/shard_map/ppermute | solution.py:254
  137.6 1.9 copy-start.17
  137.6 8.5 %collective-permute-start.7 = (bf16[2,384,128]{2,1,0:T(8,128)(2,1)S(1)}, bf16[2,384,128]{2,1,0:T(8,128)(2,1)}, u32[]{:S(2)}, u32[]{:S(2)}) collective-permute-start(bf16[2,384,128]{2,1,0:T(8,128)(2,1)S(1)} %pad_maximum_fusion.7), channel_id=1, source_target_pairs={{0,32},{16,48},{32,0},{48,16},{64,96},{80,112},{96,64},{112,80},{1... | collective-permute-start | bytes 589832 | tf_op jit(solution)/shard_map/ppermute | solution.py:254
  147.2 21.5 %collective-permute-start.12 = (bf16[4,384,128]{2,1,0:T(8,128)(2,1)S(1)}, bf16[4,384,128]{2,1,0:T(8,128)(2,1)}, u32[]{:S(2)}, u32[]{:S(2)}) collective-permute-start(bf16[4,384,128]{2,1,0:T(8,128)(2,1)S(1)} %pad_maximum_fusion.2.refs_0_), channel_id=1, source_target_pairs={{0,16},{16,0},{32,48},{48,32},{64,80},{80,64},{96,112},{112,96},{1... | collective-permute-start | bytes 1179656 | tf_op jit(solution)/shard_map/ppermute | solution.py:254
  151.0 2.1 %copy-start.12 = (bf16[384,5120]{1,0:T(8,128)(2,1)S(1)}, bf16[384,5120]{1,0:T(8,128)(2,1)}, u32[]{:S(2)}) copy-start(bf16[384,5120]{1,0:T(8,128)(2,1)} %copy-done.10) | copy-start | bytes 11796484
  156.3 10.1 %collective-permute-start.8 = (bf16[2,192,128]{2,1,0:T(8,128)(2,1)S(1)}, bf16[2,192,128]{2,1,0:T(8,128)(2,1)S(1)}, u32[]{:S(2)}, u32[]{:S(2)}) collective-permute-start(bf16[2,192,128]{2,1,0:T(8,128)(2,1)S(1)} %get-tuple-element.52), channel_id=1, source_target_pairs={{0,8},{8,0},{1,9},{9,1},{2,10},{10,2},{3,11},{11,3},{4,12},{12,4},... | collective-permute-start | bytes 294920 | tf_op jit(solution)/shard_map/ppermute | solution.py:393
  166.4 7.0 %collective-permute-start.9 = (bf16[4,384,128]{2,1,0:T(8,128)(2,1)S(1)}, bf16[4,384,128]{2,1,0:T(8,128)(2,1)S(1)}, u32[]{:S(2)}, u32[]{:S(2)}) collective-permute-start(bf16[4,384,128]{2,1,0:T(8,128)(2,1)S(1)} %pad_maximum_fusion.2.refs_0_), channel_id=1, source_target_pairs={{0,8},{8,0},{1,9},{9,1},{2,10},{10,2},{3,11},{11,3},{4,12},{12,4},... | collective-permute-start | bytes 1179656 | tf_op jit(solution)/shard_map/ppermute | solution.py:398
  168.7 13.4 %collective-permute-start.13 = (bf16[4,384,128]{2,1,0:T(8,128)(2,1)}, bf16[4,384,128]{2,1,0:T(8,128)(2,1)S(1)}, u32[]{:S(2)}, u32[]{:S(2)}) collective-permute-start(bf16[4,384,128]{2,1,0:T(8,128)(2,1)} %collective-permute-done.12.refs_1_), channel_id=1, source_target_pairs={{0,8},{8,0},{1,9},{9,1},{2,10},{10,2},{3,11},{11,3},{4,12},{12,4},... | collective-permute-start | bytes 1179656 | tf_op jit(solution)/shard_map/ppermute | solution.py:398
  170.8 8.5 %collective-permute-start.10 = (bf16[768,128]{1,0:T(8,128)(2,1)S(1)}, bf16[768,128]{1,0:T(8,128)(2,1)S(1)}, u32[]{:S(2)}, u32[]{:S(2)}) collective-permute-start(bf16[768,128]{1,0:T(8,128)(2,1)S(1)} %bitcast.55), channel_id=1, source_target_pairs={{128,0},{256,128},{384,256},{129,1},{257,129},{385,257},{130,2},{2... | collective-permute-start | bytes 589832 | tf_op jit(solution)/shard_map/ppermute | solution.py:396
  172.1 10.0 %collective-permute-start.11 = (bf16[768,128]{1,0:T(8,128)(2,1)S(1)}, bf16[768,128]{1,0:T(8,128)(2,1)S(1)}, u32[]{:S(2)}, u32[]{:S(2)}) collective-permute-start(bf16[768,128]{1,0:T(8,128)(2,1)S(1)} %bitcast.56), channel_id=1, source_target_pairs={{256,0},{384,128},{257,1},{385,129},{258,2},{386,130},{259,3},{387... | collective-permute-start | bytes 589832 | tf_op jit(solution)/shard_map/ppermute | solution.py:397
  184.2 15.6 %collective-permute-start.14 = (bf16[816,128]{1,0:T(8,128)(2,1)S(1)}, bf16[816,128]{1,0:T(8,128)(2,1)S(1)}, u32[]{:S(2)}, u32[]{:S(2)}) collective-permute-start(bf16[816,128]{1,0:T(8,128)(2,1)S(1)} %get-tuple-element.45), channel_id=1, source_target_pairs={{0,128},{128,256},{256,384},{1,129},{129,257},{257,385},{2,130},{1... | collective-permute-start | bytes 626696 | tf_op jit(solution)/shard_map/ppermute | solution.py:410
  196.0 7.7 %collective-permute-start.15 = (bf16[816,128]{1,0:T(8,128)(2,1)S(1)}, bf16[816,128]{1,0:T(8,128)(2,1)S(1)}, u32[]{:S(2)}, u32[]{:S(2)}) collective-permute-start(bf16[816,128]{1,0:T(8,128)(2,1)S(1)} %get-tuple-element.46), channel_id=1, source_target_pairs={{0,256},{128,384},{1,257},{129,385},{2,258},{130,386},{3,259},{131... | collective-permute-start | bytes 626696 | tf_op jit(solution)/shard_map/ppermute | solution.py:411
  (7 other events, 7.5 us)
